TPU v7x, 32 devices: a whole 2x2x4 slice. The times are simulated.
32 devices in a mesh: step: 4 (over y, x), head: 4 (over z), fsdp: 2 (over core).
Axes of the slice: x: 2, y: 2, z: 4, core: 2. Of those that a mesh axis runs over, the one named last changes fastest.
Arguments:
- states: float32 [4, 2, 512, 5120], P('step', 'fsdp', 'head'), may hold values from -10.5 to 10.5
- timesteps: int32 [4, 2], P('step'), may hold values from 0 to 1000, as said below
- lengths: int32 [2], P('fsdp'), may hold values from 256 to 512, as said below
- modulation: float32 [4, 3, 5120], P('step'), may hold values from -4 to 4
- w_query: bfloat16 [5120, 3072], P(('step', 'fsdp'), 'head'), may hold values from -0.1118034 to 0.1118034
- w_key: bfloat16 [5120, 3072], P(('step', 'fsdp'), 'head'), may hold values from -0.1118034 to 0.1118034
- w_value: bfloat16 [5120, 3072], P(('step', 'fsdp'), 'head'), may hold values from -0.078125 to 0.078125
- w_out: bfloat16 [3072, 5120], P('head', ('step', 'fsdp')), may hold values from -0.109375 to 0.109375
- q_gain: float32 [3072], P('head'), may hold values from 0.5 to 12
- k_gain: float32 [3072], P('head'), may hold values from 0.5 to 12
Outputs:
- next_states: float32 [4, 2, 512, 5120], P('step', 'fsdp', 'head')
- update: bfloat16 [4, 2, 512, 5120], P('step', 'fsdp', 'head')
Inputs may be any that keep to these rules, and one draw needn't show every extreme that they name: `timesteps`: A row holds a step's start above its end; each row's end is the next row's start; the first row starts at 1000 and the last ends at 0. `lengths`: positions from a clip's length on are padding; at least one clip is full.
All inputs are finite; a program needn't handle non-finite values.
Results may differ from a plain program's by a relative error of at most 0.02.
The roundings to bfloat16 on the way count: a program that leaves them out, or rounds other values in their place, can miss the bound.
Values may be sent and summed in bfloat16 or wider, within the bound.
No kernel may reach another device: no remote copies, remote signals or barrier semaphores. Data moves between devices by JAX's collectives and lax.ppermute only.
A program may use at most 128 MiB of HBM per device.

v0:
```python
import math

import jax
import jax.numpy as jnp
from jax import lax
from jax.sharding import PartitionSpec as P

HD = 128


def prefix(x, axis, combine, identity):
    peers, position = (lax.axis_size(axis), lax.axis_index(axis))
    everything = lax.all_gather(x.astype(jnp.bfloat16), axis)
    start = jnp.broadcast_to(jnp.asarray(identity, x.dtype), x.shape)

    def lap(k, before):
        reached = k < position
        new = combine(before, everything[k].astype(x.dtype))
        return jnp.where(reached, new, before)

    return lax.fori_loop(0, peers, lap, start)


def normed_rows(current, shift_row, scale_row):
    centre = jnp.mean(current, axis=-1, keepdims=True)
    centred = current - centre
    spread = jnp.mean(centred * centred, axis=-1, keepdims=True)
    return (centred * lax.rsqrt(spread + 1e-06) * (1.0 + scale_row) + shift_row).astype(
        jnp.bfloat16
    )


def scaled_heads(values, square_sum, full_width, gain_vec):
    row_count = values.shape[0]
    square = (square_sum / full_width)[:, None]
    normed = (values * lax.rsqrt(square + 1e-06) * gain_vec).astype(jnp.bfloat16)
    return normed.reshape(row_count, values.shape[1] // HD, HD)


def add_terms(earlier, following):
    return earlier + following


def body(states, timesteps, lengths, modulation, w_query, w_key, w_value, w_out, q_gain, k_gain):
    current = states[0, 0]
    modulated = normed_rows(current, modulation[0, 0], modulation[0, 1])
    gathered = lax.all_gather(modulated, "head", axis=0, tiled=True)
    total_tokens = gathered.shape[0]
    local_inner = w_query.shape[1]
    pieces = (
        lax.all_gather(w_query, ("step", "fsdp"), axis=0, tiled=True),
        lax.all_gather(w_key, ("step", "fsdp"), axis=0, tiled=True),
        lax.all_gather(w_value, ("step", "fsdp"), axis=0, tiled=True),
    )
    query_raw, key_raw, value_raw = tuple(
        (jnp.dot(gathered, piece_rows, preferred_element_type=jnp.float32) for piece_rows in pieces)
    )
    full_width = float(local_inner * lax.axis_size("head"))
    query_square, key_square = lax.psum(
        (jnp.sum(query_raw * query_raw, axis=1), jnp.sum(key_raw * key_raw, axis=1)), "head"
    )
    queries = scaled_heads(query_raw, query_square, full_width, q_gain)
    keys_normed = scaled_heads(key_raw, key_square, full_width, k_gain)
    value_rows = value_raw.astype(jnp.bfloat16).reshape(total_tokens, -1, HD)
    scores = jnp.einsum(
        "qhd,khd->hqk", queries, keys_normed, preferred_element_type=jnp.float32
    ) * (1.0 / math.sqrt(HD))
    valid_keys = lax.iota(jnp.int32, total_tokens) < lengths[0]
    scores = jnp.where(valid_keys[None, None, :], scores, -jnp.inf)
    highest = jnp.max(scores, axis=-1, keepdims=True)
    raised = jnp.exp(scores - highest)
    soft_rows = (raised / jnp.sum(raised, axis=-1, keepdims=True)).astype(jnp.bfloat16)
    attended = jnp.einsum("hqk,khd->qhd", soft_rows, value_rows, preferred_element_type=jnp.float32)
    attended = attended.astype(jnp.bfloat16).reshape(total_tokens, local_inner)
    out_full = lax.all_gather(w_out, ("step", "fsdp"), axis=1, tiled=True)
    projected = lax.psum_scatter(
        jnp.dot(attended, out_full, preferred_element_type=jnp.float32).astype(jnp.bfloat16),
        "head",
        scatter_dimension=0,
        tiled=True,
    ).astype(jnp.float32)
    gate_row = modulation[0, 2]
    branch = gate_row * projected
    update = branch.astype(jnp.bfloat16)
    step_width = (timesteps[0, 1] - timesteps[0, 0]).astype(jnp.float32) / 1000.0
    drift_term = step_width * (current + branch)
    anchor = jnp.where(lax.axis_index("step") == 0, current, jnp.zeros_like(current))
    carried = drift_term + anchor
    before = prefix(carried, "step", add_terms, jnp.zeros_like(carried))
    reached = before + carried
    return (reached[None, None], update[None, None])


def solution(mesh):
    in_specs = (
        P("step", "fsdp", "head", None),
        P("step", None),
        P("fsdp"),
        P("step", None, None),
        P(("step", "fsdp"), "head"),
        P(("step", "fsdp"), "head"),
        P(("step", "fsdp"), "head"),
        P("head", ("step", "fsdp")),
        P("head"),
        P("head"),
    )
    out_specs = (P("step", "fsdp", "head", None), P("step", "fsdp", "head", None))
    return jax.shard_map(body, mesh=mesh, in_specs=in_specs, out_specs=out_specs, check_vma=False)
```

profile of v0, /device:TPU:0, one launch (start us, length us, event | category | flops | bytes accessed | tf_op | source)
XLA Modules:
  0.0 519.3 jit_solution(12100649105221211503)
XLA Ops:
  8.2 2.0 reduce_sum.45
  15.5 97.6 %all-gather.8.cloned.1.call-done = bf16[512,5120]{1,0:T(8,128)(2,1)} async-done(((bf16[128,5120]{1,0:T(8,128)(2,1)}), bf16[512,5120]{1,0:T(8,128)(2,1)}) %all-gather.8.cloned.1.call-update) | async-done | bytes 5242896 | tf_op jit(solution)/shard_map/all_gather | solution.py:47
  113.1 52.5 %all-gather.10.cloned.1.call-done = bf16[5120,768]{1,0:T(8,128)(2,1)} async-done(((bf16[640,768]{1,0:T(8,128)(2,1)}), bf16[5120,768]{1,0:T(8,128)(2,1)}) %all-gather.10.cloned.1.call-update) | async-done | bytes 7864336 | tf_op jit(solution)/shard_map/all_gather | solution.py:53
  165.5 9.0 %convolution_convert_fusion.1 = bf16[512,768]{1,0:T(8,128)(2,1)S(1)} fusion(bf16[512,5120]{1,0:T(8,128)(2,1)} %all-gather.8.cloned.1.call-done, bf16[5120,768]{1,0:T(8,128)(2,1)} %all-gather.10.cloned.1.call-done), kind=kOutput, calls=%fused_computation.26 | convolution fusion | flops 4026925056 | bytes 13893632 | tf_op jit(solution)/shard_map/dot_general | solution.py:56
  175.7 43.9 %all-gather.12.cloned.1.call-done = bf16[5120,768]{1,0:T(8,128)(2,1)} async-done(((bf16[640,768]{1,0:T(8,128)(2,1)}), bf16[5120,768]{1,0:T(8,128)(2,1)}) %all-gather.12.cloned.1.call-update) | async-done | bytes 7864336 | tf_op jit(solution)/shard_map/all_gather | solution.py:51
  219.6 10.2 %multiply_reduce_fusion.2 = (f32[512]{0:T(512)S(1)}, f32[512,768]{1,0:T(8,128)}) fusion(bf16[512,5120]{1,0:T(8,128)(2,1)} %all-gather.8.cloned.1.call-done, bf16[5120,768]{1,0:T(8,128)(2,1)} %all-gather.12.cloned.1.call-done), kind=kOutput, calls=%fused_computation.24 | convolution fusion | flops 4027317760 | bytes 14682112 | tf_op jit(solution)/shard_map/dot_general | solution.py:56
  229.8 43.8 %all-gather.14.cloned.1.call-done = bf16[5120,768]{1,0:T(8,128)(2,1)} async-done(((bf16[640,768]{1,0:T(8,128)(2,1)}), bf16[5120,768]{1,0:T(8,128)(2,1)}) %all-gather.14.cloned.1.call-update) | async-done | bytes 7864336 | tf_op jit(solution)/shard_map/all_gather | solution.py:52
  273.6 10.2 %multiply_reduce_fusion.1 = (f32[512]{0:T(512)S(1)}, f32[512,768]{1,0:T(8,128)}) fusion(bf16[512,5120]{1,0:T(8,128)(2,1)} %all-gather.8.cloned.1.call-done, bf16[5120,768]{1,0:T(8,128)(2,1)} %all-gather.14.cloned.1.call-done), kind=kOutput, calls=%fused_computation.22 | convolution fusion | flops 4027317760 | bytes 14682112 | tf_op jit(solution)/shard_map/dot_general | solution.py:56
  283.8 12.0 %all-reduce = (f32[512]{0:T(512)S(1)}, f32[512]{0:T(512)S(1)}) all-reduce(f32[512]{0:T(512)S(1)} %get-tuple-element.114, f32[512]{0:T(512)S(1)} %get-tuple-element.116), channel_id=1, replica_groups=mesh['step'=4,'head'=4,'fsdp'=2] {'head'}, use_global_device_ids=true, to_apply=%region_3.0 | all-reduce | flops 1024 | bytes 8192 | tf_op jit(solution)/shard_map/psum | solution.py:59
  295.7 1.6 multiply_convert_fusion.1
  298.5 1.6 multiply_convert_fusion
  301.3 6.7 %fusion.18 = (f32[6,512]{1,0:T(8,128)S(1)}, f32[6,512,512]{1,2,0:T(8,128)}) fusion(pred[512]{0:T(512)(128)(4,1)S(1)} %iota_compare_fusion, bf16[512,6,128]{0,2,1:T(8,128)(2,1)} %bitcast.55, bf16[512,6,128]{0,2,1:T(8,128)(2,1)} %bitcast.56), kind=kOutput, calls=%fused_computation.40 | convolution fusion | flops 408945152 | bytes 7877120 | tf_op jit(solution)/shard_map/sub | solution.py:71
  308.0 4.3 fusion.9
  312.3 15.1 %all-gather.16.cloned.1.call-done = bf16[768,5120]{1,0:T(8,128)(2,1)} async-done(((bf16[768,640]{1,0:T(8,128)(2,1)}), bf16[768,5120]{1,0:T(8,128)(2,1)}) %all-gather.16.cloned.1.call-update) | async-done | bytes 7864336 | tf_op jit(solution)/shard_map/all_gather | solution.py:75
  327.5 10.1 %convolution_convert_fusion = bf16[512,5120]{1,0:T(8,128)(2,1)} fusion(bf16[512,768]{0,1:T(8,128)(2,1)} %bitcast.61, bf16[768,5120]{1,0:T(8,128)(2,1)} %all-gather.16.cloned.1.call-done), kind=kOutput, calls=%fused_computation.2 | convolution fusion | flops 4029153280 | bytes 13893632 | tf_op jit(solution)/shard_map/dot_general | solution.py:77
  340.1 91.4 %reduce-scatter.2.cloned.1.call-done = bf16[128,5120]{1,0:T(8,128)(2,1)} async-done(((bf16[512,5120]{1,0:T(8,128)(2,1)}), bf16[128,5120]{1,0:T(8,128)(2,1)}) %reduce-scatter.2.cloned.1.call-update) | async-done | bytes 1310736 | tf_op jit(solution)/shard_map/reduce_scatter | solution.py:76
  431.5 2.9 fusion.11
  434.5 62.1 %all-gather.18.cloned.1.call-done = bf16[512,5120]{1,0:T(8,128)(2,1)} async-done(((bf16[128,5120]{1,0:T(8,128)(2,1)}), bf16[512,5120]{1,0:T(8,128)(2,1)}) %all-gather.18.cloned.1.call-update) | async-done | bytes 5242896 | tf_op jit(solution)/shard_map/all_gather | solution.py:13
  496.6 11.1 %while.14 = (s32[]{:T(128)}, f32[128,5120]{1,0:T(8,128)S(1)}, s32[]{:T(128)}, bf16[4,128,5120]{2,1,0:T(8,128)(2,1)}, s32[]{:T(128)}, /*index=5*/s32[]{:T(128)}) while((s32[]{:T(128)}, f32[128,5120]{1,0:T(8,128)S(1)}, s32[]{:T(128)}, bf16[4,128,5120]{2,1,0:T(8,128)(2,1)}, s32[]{:T(128)}, /*index=5*/s32[]{:T(128)}) %tuple.61), condition=%wide.region_10.11_spmd.clone, body=%wide.region_9.10_spmd.clone.sunk | while | flops 2621444 | bytes 6553701 | solution.py:21
  496.6 2.8 add_select_fusion.2
  499.4 2.8 add_select_fusion.2
  502.1 2.8 add_select_fusion.2
  504.9 2.8 add_select_fusion.2
  507.7 4.8 fusion.10
  (36 shorter events, 10.4 us)
Async XLA Ops:
  7.2 3.0 copy-start
  7.2 105.9 %all-gather.8.cloned.1.call-start = ((), (), s32[]{:S(2)}) async-start(), calls=%async_computation.1 | async-start | bytes 6553600 | tf_op jit(solution)/shard_map/all_gather | solution.py:47
  12.1 153.4 %all-gather.10.cloned.1.call-start = ((), (), s32[]{:S(2)}) async-start(), calls=%async_computation.2 | async-start | bytes 8847360 | tf_op jit(solution)/shard_map/all_gather | solution.py:53
  12.9 206.7 %all-gather.12.cloned.1.call-start = ((), (), s32[]{:S(2)}) async-start(), calls=%async_computation.3 | async-start | bytes 8847360 | tf_op jit(solution)/shard_map/all_gather | solution.py:51
  13.6 260.0 %all-gather.14.cloned.1.call-start = ((), (), s32[]{:S(2)}) async-start(), calls=%async_computation.4 | async-start | bytes 8847360 | tf_op jit(solution)/shard_map/all_gather | solution.py:52
  14.2 313.2 %all-gather.16.cloned.1.call-start = ((), (), s32[]{:S(2)}) async-start(), calls=%async_computation.5 | async-start | bytes 8847360 | tf_op jit(solution)/shard_map/all_gather | solution.py:75
  14.8 416.7 %reduce-scatter.2.cloned.1.call-start = ((), (), s32[]{:S(2)}) async-start(), calls=%async_computation.6 | async-start | bytes 6553600 | tf_op jit(solution)/shard_map/reduce_scatter | solution.py:76
  229.8 65.9 %copy-start.2 = (f32[768]{0:T(1024)S(1)}, f32[768]{0:T(1024)}, u32[]{:S(2)}) copy-start(f32[768]{0:T(1024)} %param.20) | copy-start | bytes 9220
  283.8 14.8 %copy-start.3 = (f32[768]{0:T(1024)S(1)}, f32[768]{0:T(1024)}, u32[]{:S(2)}) copy-start(f32[768]{0:T(1024)} %param.21) | copy-start | bytes 9220
  301.3 6.7 %copy-start.1 = (bf16[512,768]{0,1:T(8,128)(2,1)S(1)}, bf16[512,768]{0,1:T(8,128)(2,1)}, u32[]{:S(2)}) copy-start(bf16[512,768]{0,1:T(8,128)(2,1)} %copy.16) | copy-start | bytes 2359300
  337.6 0.7 copy-start.4
  337.6 159.0 %all-gather.18.cloned.1.call-start = ((), (), s32[]{:S(2)}) async-start(), calls=%async_computation.7 | async-start | bytes 6553600 | tf_op jit(solution)/shard_map/all_gather | solution.py:13
Sparse Core Ops, SparseCore 0:
  12.3 100.7 all-gather.7
  114.9 50.5 all-gather.9
  167.4 52.1 all-gather.11
  221.4 52.1 all-gather.13
  275.3 52.0 all-gather.15
  337.7 93.7 reduce-scatter.1
  434.6 61.9 all-gather.17
where the time goes:
time: 520 us; the launch traced here: 519 us
  waiting for transfers between devices  409 us (79%)
  matrix products  50.5 us (10%)
  other arithmetic  26.8 us (5%)
  between operations  16.2 us (3%)
  blocking collectives  12 us (2%)
    all_gather x1, waiting for transfers between devices, body(): gathered = lax.all_gather(modulated, 'head', axis=0, tiled=True)  97.6 us
    reduce_scatter x1, waiting for transfers between devices, body(): lax.psum_scatter(jnp.dot(attended, out_full, preferred_element_type=jnp.f...  91.4 us
    all_gather x1, waiting for transfers between devices, prefix(): everything = lax.all_gather(x.astype(jnp.bfloat16), axis)  62.1 us
    all_gather x1, waiting for transfers between devices, body(): lax.all_gather(w_value, ('step', 'fsdp'), axis=0, tiled=True)  52.5 us
    all_gather x1, waiting for transfers between devices, body(): lax.all_gather(w_query, ('step', 'fsdp'), axis=0, tiled=True)  43.9 us
    all_gather x1, waiting for transfers between devices, body(): lax.all_gather(w_key, ('step', 'fsdp'), axis=0, tiled=True)  43.8 us
    dot_general x3, matrix products, body(): jnp.dot(gathered, piece_rows, preferred_element_type=jnp.float32)  29.3 us
    all_gather x1, waiting for transfers between devices, body(): out_full = lax.all_gather(w_out, ('step', 'fsdp'), axis=1, tiled=True)  15.1 us
  transfers between devices with their start and end apart: 7, of which 7 were waited for; matrix products, arithmetic and copies ran while one was open for 9% of the time, Pallas kernels for 0%

commit v1 on v0

v1 whole, which is shorter than its diff:
```python
import functools
import math

import jax
import jax.numpy as jnp
from jax import lax
from jax.experimental import pallas as pl
from jax.experimental.pallas import tpu as pltpu
from jax.sharding import PartitionSpec as P

HD = 128
MIB = 1 << 20
SMEM = pl.BlockSpec(memory_space=pltpu.SMEM)
VMEM = pl.BlockSpec(memory_space=pltpu.VMEM)
ANY = pl.BlockSpec(memory_space=pl.ANY)


def swap(x, axis, offset):
    return lax.ppermute(x, axis, [(i, i ^ offset) for i in range(lax.axis_size(axis))])


def spread(x, turn):
    held = [x]
    for offset in range(1, lax.axis_size("step")):
        low, high = offset & -offset, 1 << (offset.bit_length() - 1)
        last = low if turn % 2 else high
        held.append(swap(held[offset ^ last], "step", last))
    return held


def along_line(x):
    size = lax.axis_size("head")
    below, above = [x], [x]
    for hop in range(1, size):
        below.append(lax.ppermute(below[-1], "head", [(i, i + 1) for i in range(hop - 1, size - 1)]))
        above.append(lax.ppermute(above[-1], "head", [(i, i - 1) for i in range(1, size - hop + 1)]))
    return below, above


def params(mib=56):
    return pltpu.CompilerParams(vmem_limit_bytes=mib * MIB)


def cost(flops, moved, raised=0):
    return pl.CostEstimate(flops=int(flops), bytes_accessed=int(moved), transcendentals=int(raised))


def modulate_kernel(place, states, rows, mine, other):
    current = states[...]
    centre = jnp.mean(current, axis=-1, keepdims=True)
    centred = current - centre
    spread_of = jnp.mean(centred * centred, axis=-1, keepdims=True)
    shift, scale = rows[0:1, :], rows[1:2, :]
    modulated = (centred * lax.rsqrt(spread_of + 1e-06) * (1.0 + scale) + shift).astype(jnp.bfloat16)
    steps, _, width = mine.shape
    step, core = place[0], place[1]
    for block in range(2 * steps):
        piece = modulated[:, block * width : (block + 1) * width]
        at = jnp.bitwise_xor(step, block // 2)

        @pl.when(core == block % 2)
        def _(piece=piece, at=at):
            mine[at] = piece

        @pl.when(core != block % 2)
        def _(piece=piece, at=at):
            other[at] = piece


def modulate(place, states, rows, steps):
    tokens, width = states.shape
    block = width // (2 * steps)
    tile = 32
    out = jax.ShapeDtypeStruct((steps, tokens, block), jnp.bfloat16)
    spec = pl.BlockSpec((steps, tile, block), lambda i: (0, i, 0))
    return pl.pallas_call(
        modulate_kernel,
        grid=(tokens // tile,),
        in_specs=[SMEM, pl.BlockSpec((tile, width), lambda i: (i, 0)), pl.BlockSpec(rows.shape, lambda i: (0, 0))],
        out_specs=[spec, spec],
        out_shape=[out, out],
        compiler_params=params(),
        cost_estimate=cost(10 * tokens * width, 6 * tokens * width),
        name="modulate",
    )(place, states, rows)


def project_kernel(size, steps, chunks, place, *refs):
    at = 0
    slots = []
    for _ in range(2):
        own = refs[at]
        below = refs[at + 1 : at + size]
        above = refs[at + size : at + 2 * size - 1]
        slots.append((own, below, above))
        at += 2 * size - 1
    weights = refs[at : at + steps * chunks]
    at += steps * chunks
    here, there, x_held, w_held, x_sems, w_sems = refs[at:]
    tokens = slots[0][0].shape[1]
    position = place[2]
    piece_rows = w_held.shape[1] // chunks

    def x_copy(ref, clip, away, step):
        block = pl.ds((clip * size + away) * tokens, tokens)
        return pltpu.make_async_copy(ref.at[step], x_held.at[step, block], x_sems.at[step, clip * size + away])

    def w_copy(step, part):
        block = pl.ds(part * piece_rows, piece_rows)
        return pltpu.make_async_copy(weights[step * chunks + part], w_held.at[step, block], w_sems.at[step, part])

    for step in range(steps):
        for part in range(chunks):
            w_copy(step, part).start()
        for clip, (own, below, above) in enumerate(slots):
            x_copy(own, clip, 0, step).start()
            for away in range(1, size):

                @pl.when(position + away < size)
                def _(clip=clip, away=away, step=step, above=above):
                    x_copy(above[away - 1], clip, away, step).start()

                @pl.when(position + away >= size)
                def _(clip=clip, away=away, step=step, below=below):
                    x_copy(below[size - away - 1], clip, away, step).start()

    for step in range(steps):
        for part in range(chunks):
            w_copy(step, part).wait()
        for clip, (own, _, _) in enumerate(slots):
            for away in range(size):
                x_copy(own, clip, away, step).wait()
        rows = size * tokens
        tile = min(rows, 256)
        for clip, out in enumerate((here, there)):

            @pl.loop(0, rows // tile)
            def _(i, clip=clip, out=out, step=step):
                block = pl.ds(pl.multiple_of(i * tile, tile), tile)
                source = pl.ds(pl.multiple_of(clip * rows + i * tile, tile), tile)
                product = jnp.dot(x_held[step, source], w_held[step], preferred_element_type=jnp.float32)
                if step == 0:
                    out[block] = product
                else:
                    out[block] += product


def project(place, lines, weights, chunks, name):
    size = lax.axis_size("head")
    steps = lax.axis_size("step")
    operands = []
    for below, above in lines:
        operands += [below[0]] + below[1:] + above[1:]
    tokens, block = operands[0].shape[1:]
    columns = weights[0].shape[1]
    out = jax.ShapeDtypeStruct((size * tokens, columns), jnp.float32)
    rows = 2 * size * tokens
    return pl.pallas_call(
        functools.partial(project_kernel, size, steps, chunks),
        in_specs=[SMEM] + [ANY] * (len(operands) + len(weights)),
        out_specs=[VMEM, VMEM],
        out_shape=[out, out],
        scratch_shapes=[
            pltpu.VMEM((steps, rows, block), jnp.bfloat16),
            pltpu.VMEM((steps, block, columns), jnp.bfloat16),
            pltpu.SemaphoreType.DMA((steps, 2 * size)),
            pltpu.SemaphoreType.DMA((steps, chunks)),
        ],
        compiler_params=params(),
        cost_estimate=cost(2 * rows * steps * block * columns, 2 * steps * block * (rows + columns) + 4 * rows * columns),
        name=name,
    )(place, *operands, *weights)


def probs_kernel(tokens, size, place, q_a, q_b, k_a, k_b, q_scale, k_scale, q_gain, k_gain, out):
    queries = ((q_a[...] + q_b[...]) * q_scale[...] * q_gain[...]).astype(jnp.bfloat16)
    keys = ((k_a[...] + k_b[...]) * k_scale[...] * k_gain[...]).astype(jnp.bfloat16)
    scores = lax.dot_general(queries, keys, (((1,), (1,)), ((), ())), preferred_element_type=jnp.float32)
    scores = scores * (1.0 / math.sqrt(HD))
    rows = keys.shape[0]
    column = lax.broadcasted_iota(jnp.int32, (1, rows), 1)
    turned = column + place[2] * tokens
    absolute = jnp.where(turned >= rows, turned - rows, turned)
    scores = jnp.where(absolute < place[3], scores, -jnp.inf)
    highest = jnp.max(scores, axis=-1, keepdims=True)
    raised = jnp.exp(scores - highest)
    out[0] = (raised / jnp.sum(raised, axis=-1, keepdims=True)).astype(jnp.bfloat16)


def probabilities(place, q_parts, k_parts, q_scale, k_scale, q_gain, k_gain, size):
    rows, columns = q_parts[0].shape
    heads = columns // HD
    by_head = pl.BlockSpec((rows, HD), lambda i: (0, i))
    gain = pl.BlockSpec((1, HD), lambda i: (0, i))
    per_row = pl.BlockSpec((rows, 1), lambda i: (0, 0))
    return pl.pallas_call(
        functools.partial(probs_kernel, rows // size, size),
        grid=(heads,),
        in_specs=[SMEM] + [by_head] * 4 + [per_row] * 2 + [gain] * 2,
        out_specs=pl.BlockSpec((1, rows, rows), lambda i: (i, 0, 0)),
        out_shape=jax.ShapeDtypeStruct((heads, rows, rows), jnp.bfloat16),
        compiler_params=params(),
        cost_estimate=cost(2 * heads * rows * rows * HD, 16 * rows * columns + 2 * heads * rows * rows, heads * rows * rows),
        name="probs",
    )(place, *q_parts, *k_parts, q_scale, k_scale, q_gain[None], k_gain[None])


def attend_kernel(probs, v_a, v_b, *outs):
    values = (v_a[...] + v_b[...]).astype(jnp.bfloat16)
    attended = jnp.dot(probs[0], values, preferred_element_type=jnp.float32).astype(jnp.bfloat16)
    tokens = outs[0].shape[0]
    for away, out in enumerate(outs):
        out[...] = attended[away * tokens : (away + 1) * tokens]


def attend(probs, v_parts, size):
    heads, rows, _ = probs.shape
    tokens = rows // size
    by_head = pl.BlockSpec((rows, HD), lambda i: (0, i))
    return pl.pallas_call(
        attend_kernel,
        grid=(heads,),
        in_specs=[pl.BlockSpec((1, rows, rows), lambda i: (i, 0, 0)), by_head, by_head],
        out_specs=[pl.BlockSpec((tokens, HD), lambda i: (0, i))] * size,
        out_shape=[jax.ShapeDtypeStruct((tokens, heads * HD), jnp.bfloat16)] * size,
        compiler_params=params(),
        cost_estimate=cost(2 * heads * rows * rows * HD, 2 * heads * rows * rows + 10 * rows * heads * HD),
        name="attend",
    )(probs, *v_parts)


def out_kernel(size, steps, place, coefs, *refs):
    rows_in = refs[: steps * size]
    weights = refs[steps * size : steps * size + 2 * size]
    gates = refs[steps * size + 2 * size]
    at = steps * size + 2 * size + 1
    updates, sums = refs[at : at + steps], refs[at + steps : at + 2 * steps]
    a_held, w_held, total, a_sems, w_sems = refs[at + 2 * steps :]
    tokens = rows_in[0].shape[0]
    width = weights[0].shape[1]
    core = place[1]

    def a_copy(step, away):
        return pltpu.make_async_copy(
            rows_in[step * size + away], a_held.at[away, pl.ds(step * tokens, tokens)], a_sems.at[step, away]
        )

    def w_copy(half, away):
        return pltpu.make_async_copy(
            weights[half * size + away], w_held.at[jnp.bitwise_xor(core, half), away], w_sems.at[half, away]
        )

    for away in range(size):
        for half in range(2):
            w_copy(half, (size - away) % size).start()
        for step in range(steps):
            a_copy(step, away).start()
    for away in range(size):
        for half in range(2):
            w_copy(half, (size - away) % size).wait()
        for step in range(steps):
            a_copy(step, away).wait()
        for half in range(2):
            part = jnp.dot(a_held[away], w_held[half, (size - away) % size], preferred_element_type=jnp.float32)
            part = part.astype(jnp.bfloat16).astype(jnp.float32)
            if away == 0:
                total[half] = part
            else:
                total[half] += part
    for half in range(2):
        columns = slice(half * width, (half + 1) * width)
        branches = []
        for step in range(steps):
            branch = total[half, step * tokens : (step + 1) * tokens] * gates[step : step + 1, columns]
            updates[step][:, columns] = branch.astype(jnp.bfloat16)
            branches.append(branch)
        for step in range(steps):
            reached = branches[0] * coefs[step, 0]
            for other in range(1, steps):
                reached += branches[other] * coefs[step, other]
            sums[step][:, columns] = reached.astype(jnp.bfloat16)


def project_out(place, coefs, gathered, weights, gates):
    steps, size = len(gathered), len(gathered[0])
    tokens, inner = gathered[0][0].shape
    width = weights[0][0].shape[1]
    out = jax.ShapeDtypeStruct((tokens, 2 * width), jnp.bfloat16)
    rows = steps * tokens
    operands = [x for step in gathered for x in step] + [w for half in weights for w in half]
    outs = pl.pallas_call(
        functools.partial(out_kernel, size, steps),
        in_specs=[SMEM, SMEM] + [ANY] * len(operands) + [VMEM],
        out_specs=[VMEM] * (2 * steps),
        out_shape=[out] * (2 * steps),
        scratch_shapes=[
            pltpu.VMEM((size, rows, inner), jnp.bfloat16),
            pltpu.VMEM((2, size, inner, width), jnp.bfloat16),
            pltpu.VMEM((2, rows, width), jnp.float32),
            pltpu.SemaphoreType.DMA((steps, size)),
            pltpu.SemaphoreType.DMA((2, size)),
        ],
        compiler_params=params(),
        cost_estimate=cost(4 * rows * size * inner * width, 2 * size * inner * (rows + 2 * width) + 8 * rows * width),
        name="project_out",
    )(place, coefs, *operands, gates)
    return outs[:steps], outs[steps:]


def finish_kernel(steps, place, base, *refs):
    updates, sums = refs[:steps], refs[steps : 2 * steps]
    reached, update = refs[2 * steps :]
    width = updates[0].shape[1]
    for offset in range(steps):
        at = jnp.bitwise_xor(place[0], offset)
        columns = pl.ds(pl.multiple_of(at * width, width), width)
        reached[:, columns] = base[:, columns] + sums[offset][...].astype(jnp.float32)
        update[:, columns] = updates[offset][...]


def finish(place, base, updates, sums):
    steps = len(updates)
    return pl.pallas_call(
        functools.partial(finish_kernel, steps),
        in_specs=[SMEM] + [VMEM] * (1 + 2 * steps),
        out_specs=[VMEM, VMEM],
        out_shape=[jax.ShapeDtypeStruct(base.shape, jnp.float32), jax.ShapeDtypeStruct(base.shape, jnp.bfloat16)],
        compiler_params=params(),
        cost_estimate=cost(base.size, 14 * base.size),
        name="finish",
    )(place, base, *updates, *sums)


def body(states, timesteps, lengths, modulation, w_query, w_key, w_value, w_out, q_gain, k_gain):
    steps, size = lax.axis_size("step"), lax.axis_size("head")
    step, core, position = (lax.axis_index(axis) for axis in ("step", "fsdp", "head"))
    current = states[0, 0]
    place = jnp.stack([step, core, position, lengths[0]]).astype(jnp.int32)

    q_shards = spread(w_query, 0)
    k_shards = spread(w_key, 1)
    half_rows = w_value.shape[0] // 2
    v_top = spread(w_value[:half_rows], 0)
    v_bottom = spread(w_value[half_rows:], 1)
    v_shards = [piece for pair in zip(v_top, v_bottom) for piece in pair]

    mine, other = modulate(place, current, modulation[0], steps)
    lines = [along_line(mine), along_line(swap(other, "fsdp", 1))]

    def projected(shards, chunks, name):
        here, there = project(place, lines, shards, chunks, name)
        return here, swap(there, "fsdp", 1)

    q_parts = projected(q_shards, 1, "query")
    k_parts = projected(k_shards, 1, "key")
    squares = jnp.stack([jnp.sum(jnp.square(a + b), axis=1) for a, b in (q_parts, k_parts)])
    square_sum = squares
    for away in range(1, size):
        arrived = lax.ppermute(squares, "head", [(i, (i + away) % size) for i in range(size)])
        square_sum = square_sum + jnp.roll(arrived, -away * current.shape[0], axis=1)
    full_width = float(w_query.shape[1] * size)
    scales = lax.rsqrt(square_sum / full_width + 1e-06)[..., None]
    probs = probabilities(place, q_parts, k_parts, scales[0], scales[1], q_gain, k_gain, size)
    v_parts = projected(v_shards, 2, "value")
    attended = attend(probs, v_parts, size)

    pieces = [attended[0]]
    for away in range(1, size):
        pieces.append(lax.ppermute(attended[away], "head", [(i, (i + away) % size) for i in range(size)]))
    gathered = list(zip(*[spread(piece, turn) for turn, piece in enumerate(pieces)]))

    below, above = along_line(w_out)
    own_columns = [w_out] + [
        jnp.where(position + away < size, above[away], below[size - away]) for away in range(1, size)
    ]
    out_weights = (own_columns, [swap(w, "fsdp", 1) for w in own_columns])

    step_width = (timesteps[0, 1] - timesteps[0, 0]).astype(jnp.float32) / 1000.0
    told = jnp.concatenate([modulation[0, 2], jnp.full((HD,), step_width)])[None]
    heard = jnp.concatenate(
        [told] + [lax.ppermute(told, "step", [(i, i ^ o) for i in range(steps)]) for o in range(1, steps)]
    )
    columns = current.shape[1] // steps
    gates = lax.dynamic_slice(heard, (0, step * columns), (steps, columns))
    offsets = jnp.arange(steps, dtype=jnp.int32)
    order = jnp.bitwise_xor(offsets, step)
    coefs = jnp.where(order[None, :] <= order[:, None], heard[:, -1][None, :], 0.0)

    updates, sums = project_out(place, coefs, gathered, out_weights, gates)
    updates = [updates[0]] + [swap(updates[o], "step", o) for o in range(1, steps)]
    sums = [sums[0]] + [swap(sums[o], "step", o) for o in range(1, steps)]

    carried = step_width * current + jnp.where(step == 0, current, jnp.zeros_like(current))
    base, total = carried, carried
    bit = 1
    while bit < steps:
        arrived = swap(total.astype(jnp.bfloat16), "step", bit).astype(jnp.float32)
        base = base + jnp.where(jnp.bitwise_and(step, bit) != 0, arrived, jnp.zeros_like(arrived))
        total = total + arrived
        bit *= 2
    reached, update = finish(place, base, updates, sums)
    return reached[None, None], update[None, None]


def solution(mesh):
    in_specs = (
        P("step", "fsdp", "head", None),
        P("step", None),
        P("fsdp"),
        P("step", None, None),
        P(("step", "fsdp"), "head"),
        P(("step", "fsdp"), "head"),
        P(("step", "fsdp"), "head"),
        P("head", ("step", "fsdp")),
        P("head"),
        P("head"),
    )
    out_specs = (P("step", "fsdp", "head", None), P("step", "fsdp", "head", None))
    return jax.shard_map(body, mesh=mesh, in_specs=in_specs, out_specs=out_specs, check_vma=False)
```

time: 520 us -> 344 us (0.66)
  waiting for transfers between devices: 409 us -> 153 us
  starting transfers between devices: 0.27 us -> 85.1 us
  Pallas kernels: 0 us -> 72.6 us
  matrix products: 50.5 us -> 0 us
  between operations: 16.2 us -> 3.36 us
  blocking collectives: 12 us -> 0 us
  other arithmetic: 26.8 us -> 18.7 us
  local copies, waits for them, and re-layouts: 4.66 us -> 10.2 us
    all_gather x6 -> x0, waiting for transfers between devices: 315 us -> none  [the longest x1 97.6 us: body(): gathered = lax.all_gather(modulated, 'head', axis=0, tiled=True)]
    ppermute x0 -> x67, waiting for transfers between devices: none -> 153 us  [the longest x40 73.7 us: swap(): lax.ppermute(x, axis, [(i, i ^ offset) for i in range(lax.axis_size(axis))])]
    reduce_scatter x1 -> x0, waiting for transfers between devices: 91.4 us -> none  [body(): lax.psum_scatter(jnp.dot(attended, out_full, preferred_element_type=jnp.f...]
    ppermute x0 -> x67, starting transfers between devices: none -> 85.1 us  [the longest x40 40.1 us: swap(): lax.ppermute(x, axis, [(i, i ^ offset) for i in range(lax.axis_size(axis))])]
    pallas_call x0 -> x8, Pallas kernels: none -> 72.6 us  [the longest x3 38.6 us: project(): pl.pallas_call(functools.partial(project_kernel, size, steps, chunks), in...]
    dot_general x5 -> x0, matrix products: 43.8 us -> none  [the longest x3 29.3 us: body(): jnp.dot(gathered, piece_rows, preferred_element_type=jnp.float32)]
    psum x1 -> x0, blocking collectives: 12 us -> none  [body(): lax.psum((jnp.sum(query_raw * query_raw, axis=1), jnp.sum(key_raw * key_r...]
    sub x1 -> x0, matrix products: 6.7 us -> none  [body(): raised = jnp.exp(scores - highest)]
  transfers between devices with their start and end apart: 7 -> 67, of which waited for: 7 -> 25; matrix products, arithmetic and copies ran while one was open for 9% -> 7% of each run, Pallas kernels for 0% -> 20%
where the time goes in v1:
time: 344 us; the launch traced here: 343 us
  waiting for transfers between devices  153 us (44%)
  starting transfers between devices  85.1 us (25%)
  Pallas kernels  72.6 us (21%)
  other arithmetic  18.7 us (5%)
  local copies, waits for them, and re-layouts  10.2 us (3%)
    ppermute x40, waiting for transfers between devices, swap(): lax.ppermute(x, axis, [(i, i ^ offset) for i in range(lax.axis_size(axis))])  73.7 us
    ppermute x9, waiting for transfers between devices, along_line(): lax.ppermute(above[-1], 'head', [(i, i - 1) for i in range(1, size - hop...  69.3 us
    ppermute x40, starting transfers between devices, swap(): lax.ppermute(x, axis, [(i, i ^ offset) for i in range(lax.axis_size(axis))])  40.1 us
    pallas_call x3, Pallas kernels, project(): pl.pallas_call(functools.partial(project_kernel, size, steps, chunks), in...  38.6 us
    ppermute x9, starting transfers between devices, along_line(): lax.ppermute(below[-1], 'head', [(i, i + 1) for i in range(hop - 1, size...  20.7 us
    ppermute x9, starting transfers between devices, along_line(): lax.ppermute(above[-1], 'head', [(i, i - 1) for i in range(1, size - hop...  11.7 us
    pallas_call x1, Pallas kernels, project_out(): pl.pallas_call(functools.partial(out_kernel, size, steps), in_specs=[SMEM...  10.7 us
    pallas_call x1, Pallas kernels, probabilities(): pl.pallas_call(functools.partial(probs_kernel, rows // size, size), grid=...  7.97 us
  transfers between devices with their start and end apart: 67, of which 25 were waited for; matrix products, arithmetic and copies ran while one was open for 7% of the time, Pallas kernels for 20%

profile of v1, /device:TPU:0, one launch (start us, length us, event | category | flops | bytes accessed | tf_op | source)
XLA Modules:
  0.0 342.8 jit_solution(11410163420378443135)
XLA Ops:
  10.0 4.6 %modulate.1 = (bf16[4,128,640]{2,1,0:T(8,128)(2,1)}, bf16[4,128,640]{2,1,0:T(8,128)(2,1)}) custom-call(s32[4]{0:T(128)} %pad_add_fusion.place, f32[128,5120]{1,0:T(8,128)} %bitcast.20, f32[3,5120]{1,0:T(4,128)} %bitcast.21), custom_call_target="tpu_custom_call" | custom-call | flops 6553600 | bytes 3932160 | tf_op jit(solution)/shard_map/modulate/pallas_call | solution.py:76
  19.0 4.2 %collective-permute-start.5 = (bf16[4,128,640]{2,1,0:T(8,128)(2,1)}, bf16[4,128,640]{2,1,0:T(8,128)(2,1)S(1)}, u32[]{:S(2)}, u32[]{:S(2)}) collective-permute-start(bf16[4,128,640]{2,1,0:T(8,128)(2,1)} %get-tuple-element.24.refs_0_), channel_id=1, source_target_pairs={{0,2},{2,4},{4,6},{1,3},{3,5},{5,7},{8,10},{10,12},{12,14},{9,11},... | collective-permute-start | bytes 1966088 | tf_op jit(solution)/shard_map/ppermute | solution.py:35
  25.8 9.5 %collective-permute-done.8.refs_4_ = bf16[4,128,640]{2,1,0:T(8,128)(2,1)S(1)} collective-permute-done((bf16[4,128,640]{2,1,0:T(8,128)(2,1)}, bf16[4,128,640]{2,1,0:T(8,128)(2,1)S(1)}, u32[]{:S(2)}, u32[]{:S(2)}) %collective-permute-start.8) | collective-permute-done | bytes 655392 | tf_op jit(solution)/shard_map/ppermute | solution.py:36
  35.3 3.4 %collective-permute-start.12 = (bf16[4,128,640]{2,1,0:T(8,128)(2,1)S(1)}, bf16[4,128,640]{2,1,0:T(8,128)(2,1)S(1)}, u32[]{:S(2)}, u32[]{:S(2)}) collective-permute-start(bf16[4,128,640]{2,1,0:T(8,128)(2,1)S(1)} %collective-permute-done.11.refs_7_), channel_id=1, source_target_pairs={{0,2},{2,4},{4,6},{1,3},{3,5},{5,7},{8,10},{10,12},{12,14},{9,11},... | collective-permute-start | bytes 1966088 | tf_op jit(solution)/shard_map/ppermute | solution.py:35
  43.0 17.7 %collective-permute-done.23.refs_16_ = bf16[640,768]{1,0:T(8,128)(2,1)} collective-permute-done((bf16[640,768]{1,0:T(8,128)(2,1)S(1)}, bf16[640,768]{1,0:T(8,128)(2,1)}, u32[]{:S(2)}, u32[]{:S(2)}) %collective-permute-start.23) | collective-permute-done | bytes 983072 | tf_op jit(solution)/shard_map/ppermute | solution.py:19
  64.2 6.7 %collective-permute-done.9.refs_5_ = bf16[4,128,640]{2,1,0:T(8,128)(2,1)S(1)} collective-permute-done((bf16[4,128,640]{2,1,0:T(8,128)(2,1)S(1)}, bf16[4,128,640]{2,1,0:T(8,128)(2,1)S(1)}, u32[]{:S(2)}, u32[]{:S(2)}) %collective-permute-start.9) | collective-permute-done | bytes 655392 | tf_op jit(solution)/shard_map/ppermute | solution.py:36
  75.2 12.6 %collective-permute-done.16.refs_12_ = bf16[4,128,640]{2,1,0:T(8,128)(2,1)} collective-permute-done((bf16[4,128,640]{2,1,0:T(8,128)(2,1)S(1)}, bf16[4,128,640]{2,1,0:T(8,128)(2,1)}, u32[]{:S(2)}, u32[]{:S(2)}) %collective-permute-start.16) | collective-permute-done | bytes 655392 | tf_op jit(solution)/shard_map/ppermute | solution.py:36
  89.3 10.8 %collective-permute-done.10.refs_6_ = bf16[4,128,640]{2,1,0:T(8,128)(2,1)S(1)} collective-permute-done((bf16[4,128,640]{2,1,0:T(8,128)(2,1)S(1)}, bf16[4,128,640]{2,1,0:T(8,128)(2,1)S(1)}, u32[]{:S(2)}, u32[]{:S(2)}) %collective-permute-start.10) | collective-permute-done | bytes 655392 | tf_op jit(solution)/shard_map/ppermute | solution.py:36
  101.4 6.3 %collective-permute-start.52 = (bf16[768,640]{1,0:T(8,128)(2,1)}, bf16[768,640]{1,0:T(8,128)(2,1)}, u32[]{:S(2)}, u32[]{:S(2)}) collective-permute-start(bf16[768,640]{1,0:T(8,128)(2,1)} %refs_16_.1), channel_id=1, source_target_pairs={{0,2},{2,4},{4,6},{1,3},{3,5},{5,7},{8,10},{10,12},{12,14},{9,11},... | collective-permute-start | bytes 2949128 | tf_op jit(solution)/shard_map/ppermute | solution.py:35
  113.0 6.4 %collective-permute-done.17.refs_13_ = bf16[4,128,640]{2,1,0:T(8,128)(2,1)} collective-permute-done((bf16[4,128,640]{2,1,0:T(8,128)(2,1)}, bf16[4,128,640]{2,1,0:T(8,128)(2,1)}, u32[]{:S(2)}, u32[]{:S(2)}) %collective-permute-start.17) | collective-permute-done | bytes 655392 | tf_op jit(solution)/shard_map/ppermute | solution.py:36
  119.9 12.9 %query.1 = (f32[512,768]{1,0:T(8,128)}, f32[512,768]{1,0:T(8,128)}) custom-call(s32[4]{0:T(128)} %pad_add_fusion.place, bf16[4,128,640]{2,1,0:T(8,128)(2,1)} %get-tuple-element.24.refs_0_, bf16[4,128,640]{2,1,0:T(8,128)(2,1)} %copy-done.26, bf16[4,128,640]{2,1,0:T(8,128)(2,1)} %copy-done.30, bf16[4,128,640]{2,1,0:T(8,128)(2,1)} %copy-done.32, ...), custom_call_target="tpu_custom_call" | custom-call | flops 4026531840 | bytes 12320768 | tf_op jit(solution)/shard_map/query/pallas_call | solution.py:158
  132.8 13.0 %key.1 = (f32[512,768]{1,0:T(8,128)}, f32[512,768]{1,0:T(8,128)}) custom-call(s32[4]{0:T(128)} %pad_add_fusion.place, bf16[4,128,640]{2,1,0:T(8,128)(2,1)} %get-tuple-element.24.refs_0_, bf16[4,128,640]{2,1,0:T(8,128)(2,1)} %copy-done.26, bf16[4,128,640]{2,1,0:T(8,128)(2,1)} %copy-done.30, bf16[4,128,640]{2,1,0:T(8,128)(2,1)} %copy-done.32, ...), custom_call_target="tpu_custom_call" | custom-call | flops 4026531840 | bytes 12320768 | tf_op jit(solution)/shard_map/key/pallas_call | solution.py:158
  157.2 23.3 %collective-permute-done.55 = bf16[768,640]{1,0:T(8,128)(2,1)} collective-permute-done((bf16[768,640]{1,0:T(8,128)(2,1)}, bf16[768,640]{1,0:T(8,128)(2,1)}, u32[]{:S(2)}, u32[]{:S(2)}) %collective-permute-start.55) | collective-permute-done | bytes 983072 | tf_op jit(solution)/shard_map/ppermute | solution.py:36
  181.9 12.8 %value.1 = (f32[512,768]{1,0:T(8,128)}, f32[512,768]{1,0:T(8,128)}) custom-call(s32[4]{0:T(128)} %pad_add_fusion.place, bf16[4,128,640]{2,1,0:T(8,128)(2,1)} %get-tuple-element.24.refs_0_, bf16[4,128,640]{2,1,0:T(8,128)(2,1)} %copy-done.26, bf16[4,128,640]{2,1,0:T(8,128)(2,1)} %copy-done.30, bf16[4,128,640]{2,1,0:T(8,128)(2,1)} %copy-done.32, ...), custom_call_target="tpu_custom_call" | custom-call | flops 4026531840 | bytes 12320768 | tf_op jit(solution)/shard_map/value/pallas_call | solution.py:158
  215.1 8.0 %probs.1 = bf16[6,512,512]{2,1,0:T(8,128)(2,1)} custom-call(s32[4]{0:T(128)} %pad_add_fusion.place, f32[512,768]{1,0:T(8,128)} %get-tuple-element.26.q_a, f32[512,768]{1,0:T(8,128)} %collective-permute-done.21.q_b, f32[512,768]{1,0:T(8,128)} %get-tuple-element.28.k_a, f32[512,768]{1,0:T(8,128)} %collective-permute-done.25.k_b, f32[512,1]{1,0:T(8,128)} %copy.12.q_scale, ...), custom_call_target="tpu_custom_call" | custom-call | flops 402653184 | bytes 9437184 | tf_op jit(solution)/shard_map/probs/pallas_call | solution.py:196
  225.3 6.1 %attend.1 = (bf16[128,768]{1,0:T(8,128)(2,1)}, bf16[128,768]{1,0:T(8,128)(2,1)}, bf16[128,768]{1,0:T(8,128)(2,1)}, bf16[128,768]{1,0:T(8,128)(2,1)}) custom-call(bf16[6,512,512]{2,1,0:T(8,128)(2,1)} %probs.1, f32[512,768]{1,0:T(8,128)} %get-tuple-element.30.v_a, f32[512,768]{1,0:T(8,128)} %collective-permute-done.35.v_b), custom_call_target="tpu_custom_call" | custom-call | flops 402653184 | bytes 7077888 | tf_op jit(solution)/shard_map/attend/pallas_call | solution.py:220
  243.2 6.2 %collective-permute-done.37.refs_2_ = bf16[128,768]{1,0:T(8,128)(2,1)S(1)} collective-permute-done((bf16[128,768]{1,0:T(8,128)(2,1)}, bf16[128,768]{1,0:T(8,128)(2,1)S(1)}, u32[]{:S(2)}, u32[]{:S(2)}) %collective-permute-start.37) | collective-permute-done | bytes 196640 | tf_op jit(solution)/shard_map/ppermute | solution.py:369
  253.2 21.9 %collective-permute-done.43.refs_8_ = bf16[128,768]{1,0:T(8,128)(2,1)S(1)} collective-permute-done((bf16[128,768]{1,0:T(8,128)(2,1)S(1)}, bf16[128,768]{1,0:T(8,128)(2,1)S(1)}, u32[]{:S(2)}, u32[]{:S(2)}) %collective-permute-start.43) | collective-permute-done | bytes 196640 | tf_op jit(solution)/shard_map/ppermute | solution.py:19
  296.0 10.7 %project_out.1 = (bf16[128,1280]{1,0:T(8,128)(2,1)}, bf16[128,1280]{1,0:T(8,128)(2,1)}, bf16[128,1280]{1,0:T(8,128)(2,1)}, bf16[128,1280]{1,0:T(8,128)(2,1)}, bf...) custom-call(s32[4]{0:T(128)} %pad_add_fusion.place, ...), custom_call_target="tpu_custom_call" | custom-call | flops 4026531840 | bytes 13631488 | tf_op jit(solution)/shard_map/project_out/pallas_call | solution.py:291
  312.1 5.5 %collective-permute-done.61.refs_1_ = bf16[128,1280]{1,0:T(8,128)(2,1)S(1)} collective-permute-done((bf16[128,1280]{1,0:T(8,128)(2,1)}, bf16[128,1280]{1,0:T(8,128)(2,1)S(1)}, u32[]{:S(2)}, u32[]{:S(2)}) %collective-permute-start.61) | collective-permute-done | bytes 327712 | tf_op jit(solution)/shard_map/ppermute | solution.py:19
  318.9 4.0 %fusion.1.base = f32[128,5120]{1,0:T(8,128)} fusion(bf16[128,5120]{1,0:T(8,128)(2,1)} %collective-permute-done, bf16[128,5120]{1,0:T(8,128)(2,1)} %collective-permute-done.1, f32[]{:T(128)} %bitcast.3, pred[]{:T(512)S(6)} %ne.7, pred[]{:T(512)S(6)} %ne.6, pred[]{:T(512)S(6)} %eq.3, f32[1,1,128,5120]{3,2,1,0:T(8,128)S(1)} %copy-done), kind=kLoop, calls=%fused_computation.3 | loop fusion | flops 5898240 | bytes 7864327 | tf_op jit(solution)/shard_map/add | solution.py:398
  326.0 5.7 %collective-permute-done.64.refs_5_ = bf16[128,1280]{1,0:T(8,128)(2,1)S(1)} collective-permute-done((bf16[128,1280]{1,0:T(8,128)(2,1)}, bf16[128,1280]{1,0:T(8,128)(2,1)S(1)}, u32[]{:S(2)}, u32[]{:S(2)}) %collective-permute-start.64) | collective-permute-done | bytes 327712 | tf_op jit(solution)/shard_map/ppermute | solution.py:19
  331.7 5.6 %collective-permute-done.65.refs_6_ = bf16[128,1280]{1,0:T(8,128)(2,1)S(1)} collective-permute-done((bf16[128,1280]{1,0:T(8,128)(2,1)}, bf16[128,1280]{1,0:T(8,128)(2,1)S(1)}, u32[]{:S(2)}, u32[]{:S(2)}) %collective-permute-start.65) | collective-permute-done | bytes 327712 | tf_op jit(solution)/shard_map/ppermute | solution.py:19
  338.1 4.7 %finish.1 = (f32[128,5120]{1,0:T(8,128)}, bf16[128,5120]{1,0:T(8,128)(2,1)}) custom-call(s32[4]{0:T(128)} %pad_add_fusion.place, f32[128,5120]{1,0:T(8,128)} %fusion.1.base, bf16[128,1280]{1,0:T(8,128)(2,1)} %get-tuple-element.36.refs_0_, bf16[128,1280]{1,0:T(8,128)(2,1)} %copy-done.6, bf16[128,1280]{1,0:T(8,128)(2,1)} %copy-done.7, ...), custom_call_target="tpu_custom_call" | custom-call | flops 655360 | bytes 9175040 | tf_op jit(solution)/shard_map/finish/pallas_call | solution.py:323
  (257 shorter events, 116.9 us)
Async XLA Ops:
  23.2 37.5 %collective-permute-start.23 = (bf16[640,768]{1,0:T(8,128)(2,1)S(1)}, bf16[640,768]{1,0:T(8,128)(2,1)}, u32[]{:S(2)}, u32[]{:S(2)}) collective-permute-start(bf16[640,768]{1,0:T(8,128)(2,1)S(1)} %copy-done.16), channel_id=1, source_target_pairs={{0,16},{8,24},{16,0},{24,8},{1,17},{9,25},{17,1},{25,9},{2,18},{10... | collective-permute-start | bytes 2949128 | tf_op jit(solution)/shard_map/ppermute | solution.py:19
  38.8 33.5 %collective-permute-start.22 = (bf16[640,768]{1,0:T(8,128)(2,1)S(1)}, bf16[640,768]{1,0:T(8,128)(2,1)S(1)}, u32[]{:S(2)}, u32[]{:S(2)}) collective-permute-start(bf16[640,768]{1,0:T(8,128)(2,1)S(1)} %copy-done.16), channel_id=1, source_target_pairs={{0,8},{8,0},{16,24},{24,16},{1,9},{9,1},{17,25},{25,17},{2,10},{10... | collective-permute-start | bytes 2949128 | tf_op jit(solution)/shard_map/ppermute | solution.py:19
  41.7 29.3 %collective-permute-start.9 = (bf16[4,128,640]{2,1,0:T(8,128)(2,1)S(1)}, bf16[4,128,640]{2,1,0:T(8,128)(2,1)S(1)}, u32[]{:S(2)}, u32[]{:S(2)}) collective-permute-start(bf16[4,128,640]{2,1,0:T(8,128)(2,1)S(1)} %collective-permute-done.8.refs_4_), channel_id=1, source_target_pairs={{2,0},{4,2},{3,1},{5,3},{10,8},{12,10},{11,9},{13,11},{18,16},{20,... | collective-permute-start | bytes 1966088 | tf_op jit(solution)/shard_map/ppermute | solution.py:36
  71.0 29.1 %collective-permute-start.10 = (bf16[4,128,640]{2,1,0:T(8,128)(2,1)S(1)}, bf16[4,128,640]{2,1,0:T(8,128)(2,1)S(1)}, u32[]{:S(2)}, u32[]{:S(2)}) collective-permute-start(bf16[4,128,640]{2,1,0:T(8,128)(2,1)S(1)} %collective-permute-done.9.refs_5_), channel_id=1, source_target_pairs={{2,0},{3,1},{10,8},{11,9},{18,16},{19,17},{26,24},{27,25}} | collective-permute-start | bytes 1966088 | tf_op jit(solution)/shard_map/ppermute | solution.py:36
  72.3 35.4 %collective-permute-start.20 = (bf16[640,768]{1,0:T(8,128)(2,1)S(1)}, bf16[640,768]{1,0:T(8,128)(2,1)S(1)}, u32[]{:S(2)}, u32[]{:S(2)}) collective-permute-start(bf16[640,768]{1,0:T(8,128)(2,1)S(1)} %collective-permute-done.18.refs_15_), channel_id=1, source_target_pairs={{0,16},{8,24},{16,0},{24,8},{1,17},{9,25},{17,1},{25,9},{2,18},{10... | collective-permute-start | bytes 2949128 | tf_op jit(solution)/shard_map/ppermute | solution.py:19
  73.4 37.5 %collective-permute-start.24 = (bf16[640,768]{1,0:T(8,128)(2,1)}, bf16[640,768]{1,0:T(8,128)(2,1)S(1)}, u32[]{:S(2)}, u32[]{:S(2)}) collective-permute-start(bf16[640,768]{1,0:T(8,128)(2,1)} %collective-permute-done.23.refs_16_), channel_id=1, source_target_pairs={{0,8},{8,0},{16,24},{24,16},{1,9},{9,1},{17,25},{25,17},{2,10},{10... | collective-permute-start | bytes 2949128 | tf_op jit(solution)/shard_map/ppermute | solution.py:19
  101.4 46.0 %collective-permute-start.52 = (bf16[768,640]{1,0:T(8,128)(2,1)}, bf16[768,640]{1,0:T(8,128)(2,1)}, u32[]{:S(2)}, u32[]{:S(2)}) collective-permute-start(bf16[768,640]{1,0:T(8,128)(2,1)} %refs_16_.1), channel_id=1, source_target_pairs={{0,2},{2,4},{4,6},{1,3},{3,5},{5,7},{8,10},{10,12},{12,14},{9,11},... | collective-permute-start | bytes 2949128 | tf_op jit(solution)/shard_map/ppermute | solution.py:35
  107.8 41.2 %collective-permute-start.51 = (bf16[768,640]{1,0:T(8,128)(2,1)}, bf16[768,640]{1,0:T(8,128)(2,1)}, u32[]{:S(2)}, u32[]{:S(2)}) collective-permute-start(bf16[768,640]{1,0:T(8,128)(2,1)} %refs_16_.1), channel_id=1, source_target_pairs={{2,0},{4,2},{6,4},{3,1},{5,3},{7,5},{10,8},{12,10},{14,12},{11,9},... | collective-permute-start | bytes 2949128 | tf_op jit(solution)/shard_map/ppermute | solution.py:36
  110.9 34.9 %collective-permute-start.30 = (bf16[320,768]{1,0:T(8,128)(2,1)S(1)}, bf16[320,768]{1,0:T(8,128)(2,1)S(1)}, u32[]{:S(2)}, u32[]{:S(2)}) collective-permute-start(bf16[320,768]{1,0:T(8,128)(2,1)S(1)} %get-tuple-element.46.refs_15_), channel_id=1, source_target_pairs={{0,8},{8,0},{16,24},{24,16},{1,9},{9,1},{17,25},{25,17},{2,10},{10... | collective-permute-start | bytes 1474568 | tf_op jit(solution)/shard_map/ppermute | solution.py:19
  111.7 38.7 %collective-permute-start.31 = (bf16[320,768]{1,0:T(8,128)(2,1)}, bf16[320,768]{1,0:T(8,128)(2,1)S(1)}, u32[]{:S(2)}, u32[]{:S(2)}) collective-permute-start(bf16[320,768]{1,0:T(8,128)(2,1)} %get-tuple-element.47.refs_14_), channel_id=1, source_target_pairs={{0,16},{8,24},{16,0},{24,8},{1,17},{9,25},{17,1},{25,9},{2,18},{10... | collective-permute-start | bytes 1474568 | tf_op jit(solution)/shard_map/ppermute | solution.py:19
  119.4 31.0 %collective-permute-start.33 = (bf16[320,768]{1,0:T(8,128)(2,1)}, bf16[320,768]{1,0:T(8,128)(2,1)S(1)}, u32[]{:S(2)}, u32[]{:S(2)}) collective-permute-start(bf16[320,768]{1,0:T(8,128)(2,1)} %collective-permute-done.29.refs_16_), channel_id=1, source_target_pairs={{0,16},{8,24},{16,0},{24,8},{1,17},{9,25},{17,1},{25,9},{2,18},{10... | collective-permute-start | bytes 1474568 | tf_op jit(solution)/shard_map/ppermute | solution.py:19
  149.0 31.4 %collective-permute-start.55 = (bf16[768,640]{1,0:T(8,128)(2,1)}, bf16[768,640]{1,0:T(8,128)(2,1)}, u32[]{:S(2)}, u32[]{:S(2)}) collective-permute-start(bf16[768,640]{1,0:T(8,128)(2,1)} %collective-permute-done.51), channel_id=1, source_target_pairs={{2,0},{4,2},{3,1},{5,3},{10,8},{12,10},{11,9},{13,11},{18,16},{20,... | collective-permute-start | bytes 2949128 | tf_op jit(solution)/shard_map/ppermute | solution.py:36
  150.3 44.4 %collective-permute-start.21 = (f32[512,768]{1,0:T(8,128)}, f32[512,768]{1,0:T(8,128)}, u32[]{:S(2)}, u32[]{:S(2)}) collective-permute-start(f32[512,768]{1,0:T(8,128)} %get-tuple-element.27), channel_id=1, source_target_pairs={{0,1},{1,0},{2,3},{3,2},{4,5},{5,4},{6,7},{7,6},{8,9},{9,8},{10,11... | collective-permute-start | bytes 4718600 | tf_op jit(solution)/shard_map/ppermute | solution.py:19
  150.4 46.1 %collective-permute-start.25 = (f32[512,768]{1,0:T(8,128)}, f32[512,768]{1,0:T(8,128)}, u32[]{:S(2)}, u32[]{:S(2)}) collective-permute-start(f32[512,768]{1,0:T(8,128)} %get-tuple-element.29), channel_id=1, source_target_pairs={{0,1},{1,0},{2,3},{3,2},{4,5},{5,4},{6,7},{7,6},{8,9},{9,8},{10,11... | collective-permute-start | bytes 4718600 | tf_op jit(solution)/shard_map/ppermute | solution.py:19
  155.0 78.3 %collective-permute-start = (bf16[128,5120]{1,0:T(8,128)(2,1)}, bf16[128,5120]{1,0:T(8,128)(2,1)}, u32[]{:S(2)}, u32[]{:S(2)}) collective-permute-start(bf16[128,5120]{1,0:T(8,128)(2,1)} %fusion.3), channel_id=1, source_target_pairs={{0,8},{8,0},{16,24},{24,16},{1,9},{9,1},{17,25},{25,17},{2,10},{10... | collective-permute-start | bytes 3932168 | tf_op jit(solution)/shard_map/ppermute | solution.py:19
  156.5 46.9 %collective-permute-start.54 = (bf16[768,640]{1,0:T(8,128)(2,1)}, bf16[768,640]{1,0:T(8,128)(2,1)S(1)}, u32[]{:S(2)}, u32[]{:S(2)}) collective-permute-start(bf16[768,640]{1,0:T(8,128)(2,1)} %collective-permute-done.53), channel_id=1, source_target_pairs={{4,6},{5,7},{12,14},{13,15},{20,22},{21,23},{28,30},{29,31}} | collective-permute-start | bytes 2949128 | tf_op jit(solution)/shard_map/ppermute | solution.py:35
  194.7 28.9 %collective-permute-start.35 = (f32[512,768]{1,0:T(8,128)}, f32[512,768]{1,0:T(8,128)}, u32[]{:S(2)}, u32[]{:S(2)}) collective-permute-start(f32[512,768]{1,0:T(8,128)} %get-tuple-element.31), channel_id=1, source_target_pairs={{0,1},{1,0},{2,3},{3,2},{4,5},{5,4},{6,7},{7,6},{8,9},{9,8},{10,11... | collective-permute-start | bytes 4718600 | tf_op jit(solution)/shard_map/ppermute | solution.py:19
  203.4 28.6 %collective-permute-start.57 = (bf16[768,640]{1,0:T(8,128)(2,1)}, bf16[768,640]{1,0:T(8,128)(2,1)}, u32[]{:S(2)}, u32[]{:S(2)}) collective-permute-start(bf16[768,640]{1,0:T(8,128)(2,1)} %refs_16_.1), channel_id=1, source_target_pairs={{0,1},{1,0},{2,3},{3,2},{4,5},{5,4},{6,7},{7,6},{8,9},{9,8},{10,11... | collective-permute-start | bytes 2949128 | tf_op jit(solution)/shard_map/ppermute | solution.py:19
  203.4 32.0 %collective-permute-start.59 = (bf16[768,640]{1,0:T(8,128)(2,1)}, bf16[768,640]{1,0:T(8,128)(2,1)}, u32[]{:S(2)}, u32[]{:S(2)}) collective-permute-start(bf16[768,640]{1,0:T(8,128)(2,1)} %broadcast_select_fusion.1.refs_18_), channel_id=1, source_target_pairs={{0,1},{1,0},{2,3},{3,2},{4,5},{5,4},{6,7},{7,6},{8,9},{9,8},{10,11... | collective-permute-start | bytes 2949128 | tf_op jit(solution)/shard_map/ppermute | solution.py:19
  238.9 72.7 %collective-permute-start.1 = (bf16[128,5120]{1,0:T(8,128)(2,1)}, bf16[128,5120]{1,0:T(8,128)(2,1)}, u32[]{:S(2)}, u32[]{:S(2)}) collective-permute-start(bf16[128,5120]{1,0:T(8,128)(2,1)} %fusion.2), channel_id=1, source_target_pairs={{0,16},{8,24},{16,0},{24,8},{1,17},{9,25},{17,1},{25,9},{2,18},{10... | collective-permute-start | bytes 3932168 | tf_op jit(solution)/shard_map/ppermute | solution.py:19
  241.9 33.2 %collective-permute-start.43 = (bf16[128,768]{1,0:T(8,128)(2,1)S(1)}, bf16[128,768]{1,0:T(8,128)(2,1)S(1)}, u32[]{:S(2)}, u32[]{:S(2)}) collective-permute-start(bf16[128,768]{1,0:T(8,128)(2,1)S(1)} %copy-done.37), channel_id=1, source_target_pairs={{0,16},{8,24},{16,0},{24,8},{1,17},{9,25},{17,1},{25,9},{2,18},{10... | collective-permute-start | bytes 589832 | tf_op jit(solution)/shard_map/ppermute | solution.py:19
  249.4 29.8 %collective-permute-start.44 = (bf16[128,768]{1,0:T(8,128)(2,1)S(1)}, bf16[128,768]{1,0:T(8,128)(2,1)S(1)}, u32[]{:S(2)}, u32[]{:S(2)}) collective-permute-start(bf16[128,768]{1,0:T(8,128)(2,1)S(1)} %collective-permute-done.36.refs_1_), channel_id=1, source_target_pairs={{0,16},{8,24},{16,0},{24,8},{1,17},{9,25},{17,1},{25,9},{2,18},{10... | collective-permute-start | bytes 589832 | tf_op jit(solution)/shard_map/ppermute | solution.py:19
  250.8 29.9 %collective-permute-start.41 = (bf16[128,768]{1,0:T(8,128)(2,1)S(1)}, bf16[128,768]{1,0:T(8,128)(2,1)S(1)}, u32[]{:S(2)}, u32[]{:S(2)}) collective-permute-start(bf16[128,768]{1,0:T(8,128)(2,1)S(1)} %collective-permute-done.37.refs_2_), channel_id=1, source_target_pairs={{0,8},{8,0},{16,24},{24,16},{1,9},{9,1},{17,25},{25,17},{2,10},{10... | collective-permute-start | bytes 589832 | tf_op jit(solution)/shard_map/ppermute | solution.py:19
  251.6 33.3 %collective-permute-start.40 = (bf16[128,768]{1,0:T(8,128)(2,1)S(1)}, bf16[128,768]{1,0:T(8,128)(2,1)S(1)}, u32[]{:S(2)}, u32[]{:S(2)}) collective-permute-start(bf16[128,768]{1,0:T(8,128)(2,1)S(1)} %collective-permute-done.36.refs_1_), channel_id=1, source_target_pairs={{0,8},{8,0},{16,24},{24,16},{1,9},{9,1},{17,25},{25,17},{2,10},{10... | collective-permute-start | bytes 589832 | tf_op jit(solution)/shard_map/ppermute | solution.py:19
  (97 other events, 2007.9 us)

commit v2 on v1

v2 whole, which is shorter than its diff:
```python
import functools
import math

import jax
import jax.numpy as jnp
from jax import lax
from jax.experimental import pallas as pl
from jax.experimental.pallas import tpu as pltpu
from jax.sharding import PartitionSpec as P

HD = 128
MIB = 1 << 20
SMEM = pl.BlockSpec(memory_space=pltpu.SMEM)
VMEM = pl.BlockSpec(memory_space=pltpu.VMEM)
ANY = pl.BlockSpec(memory_space=pl.ANY)


def swap(x, axis, offset):
    return lax.ppermute(x, axis, [(i, i ^ offset) for i in range(lax.axis_size(axis))])


def spread(x):
    held = [[x]]
    half = x.shape[0] // 2
    for offset in range(1, lax.axis_size("step")):
        low, high = offset & -offset, 1 << (offset.bit_length() - 1)
        if low == high:
            held.append([swap(x, "step", offset)])
            continue
        top, bottom = held[offset ^ low], held[offset ^ high]
        top = top[0][:half] if len(top) == 1 else top[0]
        bottom = bottom[0][half:] if len(bottom) == 1 else bottom[1]
        held.append([swap(top, "step", low), swap(bottom, "step", high)])
    return held


def after(x, *others):
    return lax.optimization_barrier((x,) + others)[0]


def along_line(x):
    size = lax.axis_size("head")
    below, above = [x], [x]
    for hop in range(1, size):
        below.append(lax.ppermute(below[-1], "head", [(i, i + 1) for i in range(hop - 1, size - 1)]))
        above.append(lax.ppermute(above[-1], "head", [(i, i - 1) for i in range(1, size - hop + 1)]))
    return below, above


def params(mib=56):
    return pltpu.CompilerParams(vmem_limit_bytes=mib * MIB)


def cost(flops, moved, raised=0):
    return pl.CostEstimate(flops=int(flops), bytes_accessed=int(moved), transcendentals=int(raised))


def modulate_kernel(place, states, rows, mine, other):
    current = states[...]
    centre = jnp.mean(current, axis=-1, keepdims=True)
    centred = current - centre
    spread_of = jnp.mean(centred * centred, axis=-1, keepdims=True)
    shift, scale = rows[0:1, :], rows[1:2, :]
    modulated = (centred * lax.rsqrt(spread_of + 1e-06) * (1.0 + scale) + shift).astype(jnp.bfloat16)
    steps, _, width = mine.shape
    core = place[1]
    for block in range(2 * steps):
        piece = modulated[:, block * width : (block + 1) * width]

        @pl.when(core == block % 2)
        def _(piece=piece, at=block // 2):
            mine[at] = piece

        @pl.when(core != block % 2)
        def _(piece=piece, at=block // 2):
            other[at] = piece


def modulate(place, states, rows, steps):
    tokens, width = states.shape
    block = width // (2 * steps)
    tile = 32
    out = jax.ShapeDtypeStruct((steps, tokens, block), jnp.bfloat16)
    spec = pl.BlockSpec((steps, tile, block), lambda i: (0, i, 0))
    return pl.pallas_call(
        modulate_kernel,
        grid=(tokens // tile,),
        in_specs=[SMEM, pl.BlockSpec((tile, width), lambda i: (i, 0)), pl.BlockSpec(rows.shape, lambda i: (0, 0))],
        out_specs=[spec, spec],
        out_shape=[out, out],
        compiler_params=params(),
        cost_estimate=cost(10 * tokens * width, 6 * tokens * width),
        name="modulate",
    )(place, states, rows)


def project_kernel(size, parts, layout, place, *refs):
    count = 2 * size - 1
    own, below, above = refs[0], refs[1:size], refs[size:count]
    weights = refs[count : count + len(layout)]
    here, there, x_held, w_held, x_sems, w_sems = refs[count + len(layout) :]
    steps, tokens = own.shape[1:3]
    step_at, position = place[0], place[2]
    low = position < size // 2
    shift = jnp.where(low, 0, 1)
    early = size - 1

    def x_copy(ref, clip, step, block):
        if parts == "first":
            row = (clip * early + block) * tokens
        elif parts == "last":
            row = clip * tokens
        else:
            row = (clip * size + block) * tokens
        return pltpu.make_async_copy(
            ref.at[clip, step], x_held.at[step, pl.ds(pl.multiple_of(row, tokens), tokens)], x_sems.at[step, clip, block]
        )

    def start_weights():
        for index, (ref, (kind, offset, start, rows)) in enumerate(zip(weights, layout)):
            if kind == "whole":
                for step in range(steps):
                    pltpu.make_async_copy(ref.at[pl.ds(step * rows, rows)], w_held.at[step], w_sems.at[step, 0]).start()
            else:
                at = jnp.bitwise_xor(step_at, offset)
                pltpu.make_async_copy(ref, w_held.at[at, pl.ds(start, rows)], w_sems.at[0, index]).start()

    def wait_weights(step):
        for index, (ref, (kind, offset, start, rows)) in enumerate(zip(weights, layout)):
            if kind == "whole":
                pltpu.make_async_copy(ref.at[pl.ds(step * rows, rows)], w_held.at[step], w_sems.at[step, 0]).wait()
            elif step == 0:
                pltpu.make_async_copy(ref, w_held.at[0, pl.ds(start, rows)], w_sems.at[0, index]).wait()

    def start_rows(step):
        for clip in range(2):
            for away in range(size):
                for sign, held in ((1, above), (-1, below)):
                    if away == 0 and sign < 0:
                        continue
                    source = own if away == 0 else held[away - 1]
                    block_at = position + sign * away
                    block = lax.rem(block_at - shift + size, size)
                    inside = jnp.logical_and(block_at >= 0, block_at < size)
                    if parts == "first":
                        inside = jnp.logical_and(inside, block < early)
                    elif parts == "last":
                        inside = jnp.logical_and(inside, block == early)

                    @pl.when(inside)
                    def _(source=source, block=block, clip=clip):
                        x_copy(source, clip, step, block).start()

    blocks = {"first": range(early), "last": range(early, size), "all": range(size)}[parts]
    for step in range(steps):
        start_rows(step)
        if step == 0:
            start_weights()
    half = here.shape[0]
    for step in range(steps):
        wait_weights(step)
        for clip in range(2):
            for block in blocks:
                x_copy(own, clip, step, block).wait()
        product = jnp.dot(x_held[step], w_held[step], preferred_element_type=jnp.float32)
        if step == 0:
            here[...] = product[:half]
            there[...] = product[half:]
        else:
            here[...] += product[:half]
            there[...] += product[half:]


def project(place, line, shards, parts, name):
    size = lax.axis_size("head")
    below, above = line
    operands = [below[0]] + below[1:] + above[1:]
    _, steps, tokens, block = operands[0].shape
    layout, weights = [], []
    for offset, pieces in enumerate(shards):
        start = 0
        for piece in pieces:
            kind = "whole" if len(shards) == 1 else "piece"
            rows = block if kind == "whole" else piece.shape[0]
            layout.append((kind, offset, start, rows))
            weights.append(piece)
            start += rows
    columns = weights[0].shape[1]
    rows = {"first": size - 1, "last": 1, "all": size}[parts] * tokens
    out = jax.ShapeDtypeStruct((rows, columns), jnp.float32)
    return pl.pallas_call(
        functools.partial(project_kernel, size, parts, tuple(layout)),
        in_specs=[SMEM] + [ANY] * (len(operands) + len(weights)),
        out_specs=[VMEM, VMEM],
        out_shape=[out, out],
        scratch_shapes=[
            pltpu.VMEM((steps, 2 * rows, block), jnp.bfloat16),
            pltpu.VMEM((steps, block, columns), jnp.bfloat16),
            pltpu.SemaphoreType.DMA((steps, 2, size)),
            pltpu.SemaphoreType.DMA((steps, len(layout))),
        ],
        compiler_params=params(),
        cost_estimate=cost(4 * rows * steps * block * columns, 2 * steps * block * (2 * rows + columns) + 8 * rows * columns),
        name=name,
    )(place, *operands, *weights)


def probs_kernel(tokens, place, *refs):
    parts, (q_scale, k_scale, q_gain, k_gain, out) = refs[:8], refs[8:]
    joined = [jnp.concatenate([parts[i][...] + parts[i + 1][...], parts[i + 2][...] + parts[i + 3][...]]) for i in (0, 4)]
    queries = (joined[0] * q_scale[...] * q_gain[...]).astype(jnp.bfloat16)
    keys = (joined[1] * k_scale[...] * k_gain[...]).astype(jnp.bfloat16)
    scores = lax.dot_general(queries, keys, (((1,), (1,)), ((), ())), preferred_element_type=jnp.float32)
    scores = scores * (1.0 / math.sqrt(HD))
    rows = keys.shape[0]
    turned = lax.broadcasted_iota(jnp.int32, (1, rows), 1) + place[4] * tokens
    absolute = jnp.where(turned >= rows, turned - rows, turned)
    scores = jnp.where(absolute < place[3], scores, -jnp.inf)
    highest = jnp.max(scores, axis=-1, keepdims=True)
    raised = jnp.exp(scores - highest)
    out[0] = (raised / jnp.sum(raised, axis=-1, keepdims=True)).astype(jnp.bfloat16)


def probabilities(place, q_parts, k_parts, q_scale, k_scale, q_gain, k_gain):
    columns = q_parts[0].shape[1]
    rows = q_parts[0].shape[0] + q_parts[2].shape[0]
    heads = columns // HD
    by_head = [pl.BlockSpec((part.shape[0], HD), lambda i: (0, i)) for part in q_parts + k_parts]
    gain = pl.BlockSpec((1, HD), lambda i: (0, i))
    per_row = pl.BlockSpec((rows, 1), lambda i: (0, 0))
    return pl.pallas_call(
        functools.partial(probs_kernel, q_parts[2].shape[0]),
        grid=(heads,),
        in_specs=[SMEM] + by_head + [per_row] * 2 + [gain] * 2,
        out_specs=pl.BlockSpec((1, rows, rows), lambda i: (i, 0, 0)),
        out_shape=jax.ShapeDtypeStruct((heads, rows, rows), jnp.bfloat16),
        compiler_params=params(),
        cost_estimate=cost(2 * heads * rows * rows * HD, 16 * rows * columns + 2 * heads * rows * rows, heads * rows * rows),
        name="probs",
    )(place, *q_parts, *k_parts, q_scale, k_scale, q_gain[None], k_gain[None])


def attend_kernel(place, probs, v_a, v_b, out, held):
    values = (v_a[...] + v_b[...]).astype(jnp.bfloat16)
    held[...] = jnp.dot(probs[0], values, preferred_element_type=jnp.float32)
    size, tokens, _ = out.shape
    for block in range(size):
        at = lax.rem(block - place[4] + size, size) * tokens
        out[block] = held[pl.ds(pl.multiple_of(at, tokens), tokens)].astype(jnp.bfloat16)


def attend(place, probs, v_parts, size):
    heads, rows, _ = probs.shape
    tokens = rows // size
    by_head = pl.BlockSpec((rows, HD), lambda i: (0, i))
    return pl.pallas_call(
        attend_kernel,
        grid=(heads,),
        in_specs=[SMEM, pl.BlockSpec((1, rows, rows), lambda i: (i, 0, 0)), by_head, by_head],
        out_specs=pl.BlockSpec((size, tokens, HD), lambda i: (0, 0, i)),
        out_shape=jax.ShapeDtypeStruct((size, tokens, heads * HD), jnp.bfloat16),
        scratch_shapes=[pltpu.VMEM((rows, HD), jnp.float32)],
        compiler_params=params(),
        cost_estimate=cost(2 * heads * rows * rows * HD, 2 * heads * rows * rows + 10 * rows * heads * HD),
        name="attend",
    )(place, probs, *v_parts)


def out_kernel(size, layout, place, widths, *refs):
    pieces, weights = refs[: len(layout)], refs[len(layout) : len(layout) + 2 * size]
    gates, out, a_held, w_held, total, a_sems, w_sems = refs[len(layout) + 2 * size :]
    steps, _, tokens, columns = out.shape
    width = columns // 2
    step_at, core, position = place[0], place[1], place[2]

    def a_copies():
        for index, (offset, start, count) in enumerate(layout):
            row = pl.multiple_of(jnp.bitwise_xor(step_at, offset) * tokens, tokens)
            for group in range(count):
                yield pltpu.make_async_copy(
                    pieces[index].at[group], a_held.at[start + group, pl.ds(row, tokens)], a_sems.at[index, group]
                )

    def w_copy(half, away):
        group = lax.rem(position + away, size)
        return pltpu.make_async_copy(
            weights[half * size + away], w_held.at[jnp.bitwise_xor(core, half), group], w_sems.at[half, away]
        )

    for copy in a_copies():
        copy.start()
    for away in range(size):
        for half in range(2):
            w_copy(half, away).start()
    for copy in a_copies():
        copy.wait()
    for away in range(size):
        group = lax.rem(position + away, size)
        for half in range(2):
            w_copy(half, away).wait()
        for half in range(2):
            part = jnp.dot(a_held[group], w_held[half, group], preferred_element_type=jnp.float32)
            part = part.astype(jnp.bfloat16).astype(jnp.float32)
            if away == 0:
                total[half] = part
            else:
                total[half] += part
    for half in range(2):
        span = slice(half * width, (half + 1) * width)
        reached = None
        for step in range(steps):
            told = jnp.bitwise_xor(step_at, step)
            branch = total[half, step * tokens : (step + 1) * tokens] * gates[pl.ds(told, 1), span]
            out[step, 0, :, span] = branch.astype(jnp.bfloat16)
            drift = branch * widths[told]
            reached = drift if step == 0 else reached + drift
            out[step, 1, :, span] = reached.astype(jnp.bfloat16)


def project_out(place, widths, gathered, weights, gates):
    size = lax.axis_size("head")
    steps = len(gathered)
    _, tokens, inner = gathered[0][0].shape
    width = weights[0][0].shape[1]
    layout, pieces = [], []
    for offset, held in enumerate(gathered):
        start = 0
        for piece in held:
            layout.append((offset, start, piece.shape[0]))
            pieces.append(piece)
            start += piece.shape[0]
    rows = steps * tokens
    operands = pieces + [w for half in weights for w in half]
    return pl.pallas_call(
        functools.partial(out_kernel, size, tuple(layout)),
        in_specs=[SMEM, SMEM] + [ANY] * len(operands) + [VMEM],
        out_specs=VMEM,
        out_shape=jax.ShapeDtypeStruct((steps, 2, tokens, 2 * width), jnp.bfloat16),
        scratch_shapes=[
            pltpu.VMEM((size, rows, inner), jnp.bfloat16),
            pltpu.VMEM((2, size, inner, width), jnp.bfloat16),
            pltpu.VMEM((2, rows, width), jnp.float32),
            pltpu.SemaphoreType.DMA((len(layout), size)),
            pltpu.SemaphoreType.DMA((2, size)),
        ],
        compiler_params=params(),
        cost_estimate=cost(4 * rows * size * inner * width, 2 * size * inner * (rows + 2 * width) + 8 * rows * width),
        name="project_out",
    )(place, widths, *operands, gates)


def finish_kernel(base, arrived, reached, update):
    reached[...] = base[...] + arrived[0, 1].astype(jnp.float32)
    update[...] = arrived[0, 0]


def finish(base, arrived):
    steps, _, tokens, width = arrived.shape
    by_columns = pl.BlockSpec((tokens, width), lambda i: (0, i))
    return pl.pallas_call(
        finish_kernel,
        grid=(steps,),
        in_specs=[by_columns, pl.BlockSpec((1, 2, tokens, width), lambda i: (i, 0, 0, 0))],
        out_specs=[by_columns, by_columns],
        out_shape=[jax.ShapeDtypeStruct(base.shape, jnp.float32), jax.ShapeDtypeStruct(base.shape, jnp.bfloat16)],
        compiler_params=params(),
        cost_estimate=cost(base.size, 14 * base.size),
        name="finish",
    )(base, arrived)


def body(states, timesteps, lengths, modulation, w_query, w_key, w_value, w_out, q_gain, k_gain):
    steps, size = lax.axis_size("step"), lax.axis_size("head")
    step, core, position = (lax.axis_index(axis) for axis in ("step", "fsdp", "head"))
    current = states[0, 0]
    tokens = current.shape[0]
    shift = (position >= size // 2).astype(jnp.int32)
    place = jnp.stack([step, core, position, lengths[0], shift]).astype(jnp.int32)

    mine, other = modulate(place, current, modulation[0], steps)
    line = along_line(jnp.stack([mine, swap(other, "fsdp", 1)]))

    q_shards = [[lax.all_gather(w_query, "step", axis=0, tiled=True)]]
    k_shards = spread(w_key)
    v_shards = [[lax.all_gather(w_value, "step", axis=0, tiled=True)]]

    def projected(shards, parts, name):
        here, there = project(place, line, shards, parts, name)
        return [here, swap(there, "fsdp", 1)]

    def early(held):
        return held[: size - 1]

    whole_line, line = line, tuple(early(held) + [held[0]] for held in line)
    q_parts = projected(q_shards, "first", "query")
    k_parts = projected(k_shards, "first", "key")
    line = whole_line
    q_parts = q_parts + projected(q_shards, "last", "query_last")
    k_parts = k_parts + projected(k_shards, "last", "key_last")

    def squares_of(parts):
        return jnp.concatenate([jnp.sum(jnp.square(parts[i] + parts[i + 1]), axis=1) for i in (0, 2)])

    squares = jnp.stack([squares_of(q_parts), squares_of(k_parts)])
    squares = jnp.where(shift == 0, squares, jnp.roll(squares, tokens, axis=1))
    square_sum = squares
    for away in range(1, size):
        square_sum = square_sum + lax.ppermute(squares, "head", [(i, (i + away) % size) for i in range(size)])
    square_sum = jnp.where(shift == 0, square_sum, jnp.roll(square_sum, -tokens, axis=1))
    full_width = float(w_query.shape[1] * size)
    scales = lax.rsqrt(square_sum / full_width + 1e-06)[..., None]
    probs = probabilities(place, q_parts, k_parts, scales[0], scales[1], q_gain, k_gain)
    v_parts = projected(v_shards, "all", "value")
    attended = attend(place, probs, v_parts, size)

    gathered = spread(lax.all_to_all(attended, "head", 0, 0))

    below, above = along_line(after(w_out, line[0][-1], line[1][-1]))
    own_columns = [w_out] + [
        jnp.where(position + away < size, above[away], below[size - away]) for away in range(1, size)
    ]
    out_weights = (own_columns, [swap(w, "fsdp", 1) for w in own_columns])

    step_width = (timesteps[0, 1] - timesteps[0, 0]).astype(jnp.float32) / 1000.0
    told = jnp.concatenate([modulation[0, 2], jnp.full((HD,), step_width)])[None]
    heard = jnp.concatenate([told] + [swap(told, "step", offset) for offset in range(1, steps)])
    columns = current.shape[1] // steps
    gates = lax.dynamic_slice(heard, (0, step * columns), (steps, columns))

    sent = project_out(place, heard[:, -1], gathered, out_weights, gates)
    arrived = lax.all_to_all(sent, "step", 0, 0)

    carried = step_width * current + jnp.where(step == 0, current, jnp.zeros_like(current))
    base, total = carried, carried
    bit = 1
    while bit < steps:
        brought = swap(total.astype(jnp.bfloat16), "step", bit).astype(jnp.float32)
        base = base + jnp.where(jnp.bitwise_and(step, bit) != 0, brought, jnp.zeros_like(brought))
        total = total + brought
        bit *= 2
    reached, update = finish(base, arrived)
    return reached[None, None], update[None, None]


def solution(mesh):
    in_specs = (
        P("step", "fsdp", "head", None),
        P("step", None),
        P("fsdp"),
        P("step", None, None),
        P(("step", "fsdp"), "head"),
        P(("step", "fsdp"), "head"),
        P(("step", "fsdp"), "head"),
        P("head", ("step", "fsdp")),
        P("head"),
        P("head"),
    )
    out_specs = (P("step", "fsdp", "head", None), P("step", "fsdp", "head", None))
    return jax.shard_map(body, mesh=mesh, in_specs=in_specs, out_specs=out_specs, check_vma=False)
```

time: 344 us -> 344 us (level)
  starting transfers between devices: 85.1 us -> 62.8 us
  between operations: 3.36 us -> 16.6 us
  Pallas kernels: 72.6 us -> 83.8 us
    ppermute x9 -> x6, waiting for transfers between devices: 69.3 us -> 36.2 us  [along_line(): lax.ppermute(above[-1], 'head', [(i, i - 1) for i in range(1, size - hop...]
    ppermute x9 -> x6, waiting for transfers between devices: 0.02 us -> 26.9 us  [along_line(): lax.ppermute(below[-1], 'head', [(i, i + 1) for i in range(hop - 1, size...]
    ppermute x40 -> x23, starting transfers between devices: 40.1 us -> 18 us  [swap(): lax.ppermute(x, axis, [(i, i ^ offset) for i in range(lax.axis_size(axis))])]
    all_to_all x0 -> x2, waiting for transfers between devices: none -> 14.9 us  [the longest x1 9.38 us: body(): arrived = lax.all_to_all(sent, 'step', 0, 0)]
    pallas_call x7 -> x9, Pallas kernels: 68 us -> 79.2 us  [the longest x5 48 us: project(): pl.pallas_call(functools.partial(project_kernel, size, parts, tuple(layou...]
    ppermute x3, starting transfers between devices: 4.89 us -> 14.9 us  [body(): lax.ppermute(squares, 'head', [(i, (i + away) % size) for i in range(size)])]
    all_to_all x0 -> x2, starting transfers between devices: none -> 8.5 us  [the longest x1 4.59 us: body(): arrived = lax.all_to_all(sent, 'step', 0, 0)]
    ppermute x6 -> x0, starting transfers between devices: 7.67 us -> none  [the longest x3 4.11 us: body(): lax.ppermute(attended[away], 'head', [(i, (i + away) % size) for i in ran...]
  transfers between devices with their start and end apart: 67 -> 42, of which waited for: 25 -> 15; matrix products, arithmetic and copies ran while one was open for 7% -> 7% of each run, Pallas kernels for 20% -> 23%
where the time goes in v2:
time: 344 us; the launch traced here: 343 us
  waiting for transfers between devices  154 us (45%)
  Pallas kernels  83.8 us (24%)
  starting transfers between devices  62.8 us (18%)
  between operations  16.6 us (5%)
  other arithmetic  16.3 us (5%)
  local copies, waits for them, and re-layouts  9.73 us (3%)
    ppermute x23, waiting for transfers between devices, swap(): lax.ppermute(x, axis, [(i, i ^ offset) for i in range(lax.axis_size(axis))])  74 us
    pallas_call x5, Pallas kernels, project(): pl.pallas_call(functools.partial(project_kernel, size, parts, tuple(layou...  48 us
    ppermute x6, waiting for transfers between devices, along_line(): lax.ppermute(above[-1], 'head', [(i, i - 1) for i in range(1, size - hop...  36.2 us
    ppermute x6, waiting for transfers between devices, along_line(): lax.ppermute(below[-1], 'head', [(i, i + 1) for i in range(hop - 1, size...  26.9 us
    ppermute x23, starting transfers between devices, swap(): lax.ppermute(x, axis, [(i, i ^ offset) for i in range(lax.axis_size(axis))])  18 us
    ppermute x3, starting transfers between devices, body(): lax.ppermute(squares, 'head', [(i, (i + away) % size) for i in range(size)])  14.9 us
    ppermute x6, starting transfers between devices, along_line(): lax.ppermute(below[-1], 'head', [(i, i + 1) for i in range(hop - 1, size...  13.1 us
    pallas_call x1, Pallas kernels, project_out(): pl.pallas_call(functools.partial(out_kernel, size, tuple(layout)), in_spe...  11.9 us
  transfers between devices with their start and end apart: 42, of which 15 were waited for; matrix products, arithmetic and copies ran while one was open for 7% of the time, Pallas kernels for 23%

profile of v2, /device:TPU:0, one launch (start us, length us, event | category | flops | bytes accessed | tf_op | source)
XLA Modules:
  0.0 343.1 jit_solution(17678008558224793888)
XLA Ops:
  10.7 4.6 %modulate.1 = (bf16[4,128,640]{2,1,0:T(8,128)(2,1)}, bf16[4,128,640]{2,1,0:T(8,128)(2,1)}) custom-call(s32[5]{0:T(128)} %stack.37.place, f32[128,5120]{1,0:T(8,128)} %bitcast.23, f32[3,5120]{1,0:T(4,128)} %bitcast.26), custom_call_target="tpu_custom_call" | custom-call | flops 6553600 | bytes 3932160 | tf_op jit(solution)/shard_map/modulate/pallas_call | solution.py:85
  18.8 5.0 %collective-permute-start.6 = (bf16[2,4,128,640]{3,2,1,0:T(8,128)(2,1)S(1)}, bf16[2,4,128,640]{3,2,1,0:T(8,128)(2,1)S(1)}, u32[]{:S(2)}, u32[]{:S(2)}) collective-permute-start(bf16[2,4,128,640]{3,2,1,0:T(8,128)(2,1)S(1)} %pad_maximum_fusion.refs_0_.refs_3_.refs_6_), channel_id=1, source_target_pairs={{0,2},{2,4},{4,6},{1,3},{3,5},{5,7},{8,10},{10,12},{12,14},{9,11},... | collective-permute-start | bytes 3932168 | tf_op jit(solution)/shard_map/ppermute | solution.py:45
  25.2 26.9 %collective-permute-done.6.refs_1_ = bf16[2,4,128,640]{3,2,1,0:T(8,128)(2,1)S(1)} collective-permute-done((bf16[2,4,128,640]{3,2,1,0:T(8,128)(2,1)S(1)}, bf16[2,4,128,640]{3,2,1,0:T(8,128)(2,1)S(1)}, u32[]{:S(2)}, u32[]{:S(2)}) %collective-permute-start.6) | collective-permute-done | bytes 1310752 | tf_op jit(solution)/shard_map/ppermute | solution.py:45
  60.7 26.5 %collective-permute-done.15.refs_9_ = bf16[640,768]{1,0:T(8,128)(2,1)S(1)} collective-permute-done((bf16[640,768]{1,0:T(8,128)(2,1)S(1)}, bf16[640,768]{1,0:T(8,128)(2,1)S(1)}, u32[]{:S(2)}, u32[]{:S(2)}) %collective-permute-start.15) | collective-permute-done | bytes 983072 | tf_op jit(solution)/shard_map/ppermute | solution.py:19
  92.7 12.2 %collective-permute-done.16.refs_10_ = bf16[320,768]{1,0:T(8,128)(2,1)S(1)} collective-permute-done((bf16[320,768]{1,0:T(8,128)(2,1)S(1)}, bf16[320,768]{1,0:T(8,128)(2,1)S(1)}, u32[]{:S(2)}, u32[]{:S(2)}) %collective-permute-start.16) | collective-permute-done | bytes 491552 | tf_op jit(solution)/shard_map/ppermute | solution.py:19
  106.5 11.7 %key.1 = (f32[384,768]{1,0:T(8,128)}, f32[384,768]{1,0:T(8,128)}) custom-call(s32[5]{0:T(128)} %stack.37.place, bf16[2,4,128,640]{3,2,1,0:T(8,128)(2,1)} %copy-done, bf16[2,4,128,640]{3,2,1,0:T(8,128)(2,1)} %copy-done.2, bf16[2,4,128,640]{3,2,1,0:T(8,128)(2,1)} %copy-done.4, bf16[2,4,128,640]{3,2,1,0:T(8,128)(2,1)} %copy-done, ...), custom_call_target="tpu_custom_call" | custom-call | flops 3019898880 | bytes 10223616 | tf_op jit(solution)/shard_map/key/pallas_call | solution.py:191
  123.9 6.7 %key_last.1 = (f32[128,768]{1,0:T(8,128)}, f32[128,768]{1,0:T(8,128)}) custom-call(s32[5]{0:T(128)} %stack.37.place, bf16[2,4,128,640]{3,2,1,0:T(8,128)(2,1)} %copy-done, bf16[2,4,128,640]{3,2,1,0:T(8,128)(2,1)} %copy-done.2, bf16[2,4,128,640]{3,2,1,0:T(8,128)(2,1)} %copy-done.4, bf16[2,4,128,640]{3,2,1,0:T(8,128)(2,1)} %collective-permute-done.11.refs_3_, ...), custom_call_target="tpu_custom_call" | custom-call | flops 1006632960 | bytes 6029312 | tf_op jit(solution)/shard_map/key_last/pallas_call | solution.py:191
  130.8 10.8 %query.1 = (f32[384,768]{1,0:T(8,128)}, f32[384,768]{1,0:T(8,128)}) custom-call(s32[5]{0:T(128)} %stack.37.place, bf16[2,4,128,640]{3,2,1,0:T(8,128)(2,1)} %copy-done, bf16[2,4,128,640]{3,2,1,0:T(8,128)(2,1)} %copy-done.2, bf16[2,4,128,640]{3,2,1,0:T(8,128)(2,1)} %copy-done.4, bf16[2,4,128,640]{3,2,1,0:T(8,128)(2,1)} %copy-done, ...), custom_call_target="tpu_custom_call" | custom-call | flops 3019898880 | bytes 10223616 | tf_op jit(solution)/shard_map/query/pallas_call | solution.py:191
  145.0 5.8 %query_last.1 = (f32[128,768]{1,0:T(8,128)}, f32[128,768]{1,0:T(8,128)}) custom-call(s32[5]{0:T(128)} %stack.37.place, bf16[2,4,128,640]{3,2,1,0:T(8,128)(2,1)} %copy-done, bf16[2,4,128,640]{3,2,1,0:T(8,128)(2,1)} %copy-done.2, bf16[2,4,128,640]{3,2,1,0:T(8,128)(2,1)} %copy-done.4, bf16[2,4,128,640]{3,2,1,0:T(8,128)(2,1)} %collective-permute-done.11.refs_3_, ...), custom_call_target="tpu_custom_call" | custom-call | flops 1006632960 | bytes 6029312 | tf_op jit(solution)/shard_map/query_last/pallas_call | solution.py:191
  152.7 13.1 %value.1 = (f32[512,768]{1,0:T(8,128)}, f32[512,768]{1,0:T(8,128)}) custom-call(s32[5]{0:T(128)} %stack.37.place, bf16[2,4,128,640]{3,2,1,0:T(8,128)(2,1)} %copy-done, bf16[2,4,128,640]{3,2,1,0:T(8,128)(2,1)} %copy-done.2, bf16[2,4,128,640]{3,2,1,0:T(8,128)(2,1)} %copy-done.4, bf16[2,4,128,640]{3,2,1,0:T(8,128)(2,1)} %collective-permute-done.11.refs_3_, ...), custom_call_target="tpu_custom_call" | custom-call | flops 4026531840 | bytes 12320768 | tf_op jit(solution)/shard_map/value/pallas_call | solution.py:191
  167.1 4.3 %collective-permute-start.20 = (f32[2,512]{1,0:T(2,128)S(1)}, f32[2,512]{1,0:T(2,128)S(1)}, u32[]{:S(2)}, u32[]{:S(2)}) collective-permute-start(f32[2,512]{1,0:T(2,128)S(1)} %fusion.4), channel_id=1, source_target_pairs={{0,2},{2,4},{4,6},{6,0},{1,3},{3,5},{5,7},{7,1},{8,10},{10,12},{12... | collective-permute-start | bytes 12296 | tf_op jit(solution)/shard_map/ppermute | solution.py:408
  173.5 9.0 %collective-permute-start.22 = (f32[2,512]{1,0:T(2,128)S(1)}, f32[2,512]{1,0:T(2,128)S(1)}, u32[]{:S(2)}, u32[]{:S(2)}) collective-permute-start(f32[2,512]{1,0:T(2,128)S(1)} %fusion.4), channel_id=1, source_target_pairs={{0,6},{2,0},{4,2},{6,4},{1,7},{3,1},{5,3},{7,5},{8,14},{10,8},{12,... | collective-permute-start | bytes 12296 | tf_op jit(solution)/shard_map/ppermute | solution.py:408
  190.1 8.2 %probs.1 = bf16[6,512,512]{2,1,0:T(8,128)(2,1)} custom-call(s32[5]{0:T(128)} %stack.37.place, f32[384,768]{1,0:T(8,128)} %get-tuple-element.19.refs_0_, f32[384,768]{1,0:T(8,128)} %copy-done.11, f32[128,768]{1,0:T(8,128)} %get-tuple-element.21.refs_2_, f32[128,768]{1,0:T(8,128)} %copy-done.17, f32[384,768]{1,0:T(8,128)} %get-tuple-element.23.refs_4_, ...), custom_call_target="tpu_custom_call" | custom-call | flops 402653184 | bytes 9437184 | tf_op jit(solution)/shard_map/probs/pallas_call | solution.py:231
  202.7 6.3 %attend.1 = bf16[4,128,768]{2,1,0:T(8,128)(2,1)} custom-call(s32[5]{0:T(128)} %stack.37.place, bf16[6,512,512]{2,1,0:T(8,128)(2,1)} %probs.1, f32[512,768]{1,0:T(8,128)} %get-tuple-element.27.v_a, f32[512,768]{1,0:T(8,128)} %collective-permute-done.23.v_b), custom_call_target="tpu_custom_call" | custom-call | flops 402653184 | bytes 7077888 | tf_op jit(solution)/shard_map/attend/pallas_call | solution.py:256
  215.6 15.0 %collective-permute-done.32 = bf16[768,640]{1,0:T(8,128)(2,1)} collective-permute-done((bf16[768,640]{1,0:T(8,128)(2,1)}, bf16[768,640]{1,0:T(8,128)(2,1)}, u32[]{:S(2)}, u32[]{:S(2)}) %collective-permute-start.32) | collective-permute-done | bytes 983072 | tf_op jit(solution)/shard_map/ppermute | solution.py:46
  233.0 5.5 %all-to-all-done.refs_0_ = bf16[4,128,768]{2,1,0:T(8,128)(2,1)S(1)} async-done(((bf16[4,128,768]{2,1,0:T(8,128)(2,1)}), bf16[4,128,768]{2,1,0:T(8,128)(2,1)S(1)}, u32[]{:S(2)}, u32[]{:S(2)}) %all-to-all-start) | async-done | bytes 786464 | tf_op jit(solution)/shard_map/all_to_all | solution.py:416
  243.5 14.4 %collective-permute-done.33 = bf16[768,640]{1,0:T(8,128)(2,1)} collective-permute-done((bf16[768,640]{1,0:T(8,128)(2,1)}, bf16[768,640]{1,0:T(8,128)(2,1)}, u32[]{:S(2)}, u32[]{:S(2)}) %collective-permute-start.33) | collective-permute-done | bytes 983072 | tf_op jit(solution)/shard_map/ppermute | solution.py:46
  270.2 4.0 %collective-permute-done.26.refs_3_ = bf16[2,128,768]{2,1,0:T(8,128)(2,1)S(1)} collective-permute-done((bf16[2,128,768]{2,1,0:T(8,128)(2,1)S(1)}, bf16[2,128,768]{2,1,0:T(8,128)(2,1)S(1)}, u32[]{:S(2)}, u32[]{:S(2)}) %collective-permute-start.26) | collective-permute-done | bytes 393248 | tf_op jit(solution)/shard_map/ppermute | solution.py:19
  276.6 11.9 %project_out.1 = bf16[4,2,128,1280]{3,2,1,0:T(8,128)(2,1)} custom-call(s32[5]{0:T(128)} %stack.37.place, f32[4]{0:T(128)} %slice_reduce_fusion.widths, bf16[4,128,768]{2,1,0:T(8,128)(2,1)} %copy-done.21, bf16[4,128,768]{2,1,0:T(8,128)(2,1)} %copy-done.23, bf16[4,128,768]{2,1,0:T(8,128)(2,1)} %copy-done.22, bf16[2,128,768]{2,1,0:T(8,128)(2,1)} %copy-done.31, ...), custom_call_target="tpu_custom_call" | custom-call | flops 4026531840 | bytes 13631488 | tf_op jit(solution)/shard_map/project_out/pallas_call | solution.py:334
  288.5 4.6 %all-to-all-start.1 = ((bf16[4,2,128,1280]{3,2,1,0:T(8,128)(2,1)}), bf16[4,2,128,1280]{3,2,1,0:T(8,128)(2,1)}, u32[]{:S(2)}, u32[]{:S(2)}) async-start(bf16[4,2,128,1280]{3,2,1,0:T(8,128)(2,1)} %project_out.1), calls=%async_computation.1 | async-start | bytes 5242880 | tf_op jit(solution)/shard_map/all_to_all | solution.py:431
  293.1 25.0 %collective-permute-done.1 = bf16[128,5120]{1,0:T(8,128)(2,1)} collective-permute-done((bf16[128,5120]{1,0:T(8,128)(2,1)}, bf16[128,5120]{1,0:T(8,128)(2,1)}, u32[]{:S(2)}, u32[]{:S(2)}) %collective-permute-start.1) | collective-permute-done | bytes 1310752 | tf_op jit(solution)/shard_map/ppermute | solution.py:19
  318.1 4.0 %fusion.1.base = f32[128,5120]{1,0:T(8,128)} fusion(bf16[128,5120]{1,0:T(8,128)(2,1)} %collective-permute-done, bf16[128,5120]{1,0:T(8,128)(2,1)} %collective-permute-done.1, f32[]{:T(128)} %bitcast, pred[]{:T(512)S(6)} %ne.7, pred[]{:T(512)S(6)} %ne.6, pred[]{:T(512)S(6)} %eq.7, f32[1,1,128,5120]{3,2,1,0:T(8,128)S(1)} %copy-done.1), kind=kLoop, calls=%fused_computation.3 | loop fusion | flops 5898240 | bytes 7864327 | tf_op jit(solution)/shard_map/add | solution.py:438
  322.1 9.4 %all-to-all-done.1.arrived = bf16[4,2,128,1280]{3,2,1,0:T(8,128)(2,1)} async-done(((bf16[4,2,128,1280]{3,2,1,0:T(8,128)(2,1)}), bf16[4,2,128,1280]{3,2,1,0:T(8,128)(2,1)}, u32[]{:S(2)}, u32[]{:S(2)}) %all-to-all-start.1) | async-done | bytes 2621472 | tf_op jit(solution)/shard_map/all_to_all | solution.py:431
  331.4 4.8 %finish.1 = (f32[128,5120]{1,0:T(8,128)}, bf16[128,5120]{1,0:T(8,128)(2,1)}) custom-call(f32[128,5120]{1,0:T(8,128)} %fusion.1.base, bf16[4,2,128,1280]{3,2,1,0:T(8,128)(2,1)} %all-to-all-done.1.arrived), custom_call_target="tpu_custom_call" | custom-call | flops 655360 | bytes 9175040 | tf_op jit(solution)/shard_map/finish/pallas_call | solution.py:360
  (177 shorter events, 76.9 us)
Async XLA Ops:
  7.2 123.6 %all-gather.3.cloned.1.call-start = ((), (), s32[]{:S(2)}) async-start(), calls=%async_computation.2 | async-start | bytes 4915200 | tf_op jit(solution)/shard_map/all_gather | solution.py:383
  7.9 144.8 %all-gather.5.cloned.1.call-start = ((), (), s32[]{:S(2)}) async-start(), calls=%async_computation.3 | async-start | bytes 4915200 | tf_op jit(solution)/shard_map/all_gather | solution.py:385
  18.8 33.2 %collective-permute-start.6 = (bf16[2,4,128,640]{3,2,1,0:T(8,128)(2,1)S(1)}, bf16[2,4,128,640]{3,2,1,0:T(8,128)(2,1)S(1)}, u32[]{:S(2)}, u32[]{:S(2)}) collective-permute-start(bf16[2,4,128,640]{3,2,1,0:T(8,128)(2,1)S(1)} %pad_maximum_fusion.refs_0_.refs_3_.refs_6_), channel_id=1, source_target_pairs={{0,2},{2,4},{4,6},{1,3},{3,5},{5,7},{8,10},{10,12},{12,14},{9,11},... | collective-permute-start | bytes 3932168 | tf_op jit(solution)/shard_map/ppermute | solution.py:45
  23.9 32.4 %collective-permute-start.8 = (bf16[2,4,128,640]{3,2,1,0:T(8,128)(2,1)S(1)}, bf16[2,4,128,640]{3,2,1,0:T(8,128)(2,1)S(1)}, u32[]{:S(2)}, u32[]{:S(2)}) collective-permute-start(bf16[2,4,128,640]{3,2,1,0:T(8,128)(2,1)S(1)} %pad_maximum_fusion.refs_0_.refs_3_.refs_6_), channel_id=1, source_target_pairs={{2,0},{4,2},{6,4},{3,1},{5,3},{7,5},{10,8},{12,10},{14,12},{11,9},... | collective-permute-start | bytes 3932168 | tf_op jit(solution)/shard_map/ppermute | solution.py:46
  52.1 37.6 %collective-permute-start.7 = (bf16[2,4,128,640]{3,2,1,0:T(8,128)(2,1)S(1)}, bf16[2,4,128,640]{3,2,1,0:T(8,128)(2,1)S(1)}, u32[]{:S(2)}, u32[]{:S(2)}) collective-permute-start(bf16[2,4,128,640]{3,2,1,0:T(8,128)(2,1)S(1)} %collective-permute-done.6.refs_1_), channel_id=1, source_target_pairs={{2,4},{4,6},{3,5},{5,7},{10,12},{12,14},{11,13},{13,15},{18,20},{2... | collective-permute-start | bytes 3932168 | tf_op jit(solution)/shard_map/ppermute | solution.py:45
  56.3 35.1 %collective-permute-start.9 = (bf16[2,4,128,640]{3,2,1,0:T(8,128)(2,1)S(1)}, bf16[2,4,128,640]{3,2,1,0:T(8,128)(2,1)S(1)}, u32[]{:S(2)}, u32[]{:S(2)}) collective-permute-start(bf16[2,4,128,640]{3,2,1,0:T(8,128)(2,1)S(1)} %collective-permute-done.8.refs_4_), channel_id=1, source_target_pairs={{2,0},{4,2},{3,1},{5,3},{10,8},{12,10},{11,9},{13,11},{18,16},{20,... | collective-permute-start | bytes 3932168 | tf_op jit(solution)/shard_map/ppermute | solution.py:46
  57.6 29.6 %collective-permute-start.15 = (bf16[640,768]{1,0:T(8,128)(2,1)S(1)}, bf16[640,768]{1,0:T(8,128)(2,1)S(1)}, u32[]{:S(2)}, u32[]{:S(2)}) collective-permute-start(bf16[640,768]{1,0:T(8,128)(2,1)S(1)} %copy-done.12), channel_id=1, source_target_pairs={{0,16},{8,24},{16,0},{24,8},{1,17},{9,25},{17,1},{25,9},{2,18},{10... | collective-permute-start | bytes 2949128 | tf_op jit(solution)/shard_map/ppermute | solution.py:19
  59.2 29.6 %collective-permute-start.14 = (bf16[640,768]{1,0:T(8,128)(2,1)S(1)}, bf16[640,768]{1,0:T(8,128)(2,1)S(1)}, u32[]{:S(2)}, u32[]{:S(2)}) collective-permute-start(bf16[640,768]{1,0:T(8,128)(2,1)S(1)} %copy-done.12), channel_id=1, source_target_pairs={{0,8},{8,0},{16,24},{24,16},{1,9},{9,1},{17,25},{25,17},{2,10},{10... | collective-permute-start | bytes 2949128 | tf_op jit(solution)/shard_map/ppermute | solution.py:19
  89.7 28.6 %collective-permute-start.11 = (bf16[2,4,128,640]{3,2,1,0:T(8,128)(2,1)S(1)}, bf16[2,4,128,640]{3,2,1,0:T(8,128)(2,1)}, u32[]{:S(2)}, u32[]{:S(2)}) collective-permute-start(bf16[2,4,128,640]{3,2,1,0:T(8,128)(2,1)S(1)} %collective-permute-done.7.refs_2_), channel_id=1, source_target_pairs={{4,6},{5,7},{12,14},{13,15},{20,22},{21,23},{28,30},{29,31}} | collective-permute-start | bytes 3932168 | tf_op jit(solution)/shard_map/ppermute | solution.py:45
  91.4 30.2 %collective-permute-start.12 = (bf16[2,4,128,640]{3,2,1,0:T(8,128)(2,1)S(1)}, bf16[2,4,128,640]{3,2,1,0:T(8,128)(2,1)}, u32[]{:S(2)}, u32[]{:S(2)}) collective-permute-start(bf16[2,4,128,640]{3,2,1,0:T(8,128)(2,1)S(1)} %collective-permute-done.9.refs_5_), channel_id=1, source_target_pairs={{2,0},{3,1},{10,8},{11,9},{18,16},{19,17},{26,24},{27,25}} | collective-permute-start | bytes 3932168 | tf_op jit(solution)/shard_map/ppermute | solution.py:46
  121.6 29.4 %collective-permute-start.29 = (bf16[768,640]{1,0:T(8,128)(2,1)}, bf16[768,640]{1,0:T(8,128)(2,1)}, u32[]{:S(2)}, u32[]{:S(2)}) collective-permute-start(bf16[768,640]{1,0:T(8,128)(2,1)} %refs_5_.1), channel_id=1, source_target_pairs={{0,2},{2,4},{4,6},{1,3},{3,5},{5,7},{8,10},{10,12},{12,14},{9,11},... | collective-permute-start | bytes 2949128 | tf_op jit(solution)/shard_map/ppermute | solution.py:45
  142.2 56.0 %collective-permute-start.28 = (bf16[768,640]{1,0:T(8,128)(2,1)}, bf16[768,640]{1,0:T(8,128)(2,1)}, u32[]{:S(2)}, u32[]{:S(2)}) collective-permute-start(bf16[768,640]{1,0:T(8,128)(2,1)} %refs_5_.1), channel_id=1, source_target_pairs={{2,0},{4,2},{6,4},{3,1},{5,3},{7,5},{10,8},{12,10},{14,12},{11,9},... | collective-permute-start | bytes 2949128 | tf_op jit(solution)/shard_map/ppermute | solution.py:46
  151.0 48.8 %collective-permute-start.30 = (bf16[768,640]{1,0:T(8,128)(2,1)}, bf16[768,640]{1,0:T(8,128)(2,1)}, u32[]{:S(2)}, u32[]{:S(2)}) collective-permute-start(bf16[768,640]{1,0:T(8,128)(2,1)} %collective-permute-done.29), channel_id=1, source_target_pairs={{2,4},{4,6},{3,5},{5,7},{10,12},{12,14},{11,13},{13,15},{18,20},{2... | collective-permute-start | bytes 2949128 | tf_op jit(solution)/shard_map/ppermute | solution.py:45
  165.8 35.2 %collective-permute-start.23 = (f32[512,768]{1,0:T(8,128)}, f32[512,768]{1,0:T(8,128)}, u32[]{:S(2)}, u32[]{:S(2)}) collective-permute-start(f32[512,768]{1,0:T(8,128)} %get-tuple-element.28), channel_id=1, source_target_pairs={{0,1},{1,0},{2,3},{3,2},{4,5},{5,4},{6,7},{7,6},{8,9},{9,8},{10,11... | collective-permute-start | bytes 4718600 | tf_op jit(solution)/shard_map/ppermute | solution.py:19
  186.3 28.0 %collective-permute-start.2 = (f32[1,5248]{1,0:T(1,128)}, f32[1,5248]{1,0:T(1,128)}, u32[]{:S(2)}, u32[]{:S(2)}) collective-permute-start(f32[1,5248]{1,0:T(1,128)} %broadcast_in_dim.17), channel_id=1, source_target_pairs={{0,8},{8,0},{16,24},{24,16},{1,9},{9,1},{17,25},{25,17},{2,10},{10... | collective-permute-start | bytes 62984 | tf_op jit(solution)/shard_map/ppermute | solution.py:19
  186.8 27.5 %collective-permute-start.3 = (f32[1,5248]{1,0:T(1,128)}, f32[1,5248]{1,0:T(1,128)}, u32[]{:S(2)}, u32[]{:S(2)}) collective-permute-start(f32[1,5248]{1,0:T(1,128)} %broadcast_in_dim.17), channel_id=1, source_target_pairs={{0,16},{8,24},{16,0},{24,8},{1,17},{9,25},{17,1},{25,9},{2,18},{10... | collective-permute-start | bytes 62984 | tf_op jit(solution)/shard_map/ppermute | solution.py:19
  198.2 33.9 %collective-permute-start.4 = (f32[1,5248]{1,0:T(1,128)}, f32[1,5248]{1,0:T(1,128)S(1)}, u32[]{:S(2)}, u32[]{:S(2)}) collective-permute-start(f32[1,5248]{1,0:T(1,128)} %broadcast_in_dim.17), channel_id=1, source_target_pairs={{0,24},{8,16},{16,8},{24,0},{1,25},{9,17},{17,9},{25,1},{2,26},{10... | collective-permute-start | bytes 62984 | tf_op jit(solution)/shard_map/ppermute | solution.py:19
  199.8 30.8 %collective-permute-start.32 = (bf16[768,640]{1,0:T(8,128)(2,1)}, bf16[768,640]{1,0:T(8,128)(2,1)}, u32[]{:S(2)}, u32[]{:S(2)}) collective-permute-start(bf16[768,640]{1,0:T(8,128)(2,1)} %collective-permute-done.28), channel_id=1, source_target_pairs={{2,0},{4,2},{3,1},{5,3},{10,8},{12,10},{11,9},{13,11},{18,16},{20,... | collective-permute-start | bytes 2949128 | tf_op jit(solution)/shard_map/ppermute | solution.py:46
  201.1 38.9 %collective-permute-start.31 = (bf16[768,640]{1,0:T(8,128)(2,1)}, bf16[768,640]{1,0:T(8,128)(2,1)}, u32[]{:S(2)}, u32[]{:S(2)}) collective-permute-start(bf16[768,640]{1,0:T(8,128)(2,1)} %collective-permute-done.30), channel_id=1, source_target_pairs={{4,6},{5,7},{12,14},{13,15},{20,22},{21,23},{28,30},{29,31}} | collective-permute-start | bytes 2949128 | tf_op jit(solution)/shard_map/ppermute | solution.py:45
  209.0 29.5 %all-to-all-start = ((bf16[4,128,768]{2,1,0:T(8,128)(2,1)}), bf16[4,128,768]{2,1,0:T(8,128)(2,1)S(1)}, u32[]{:S(2)}, u32[]{:S(2)}) async-start(bf16[4,128,768]{2,1,0:T(8,128)(2,1)} %attend.1), calls=%async_computation | async-start | bytes 1572864 | tf_op jit(solution)/shard_map/all_to_all | solution.py:416
  214.3 48.3 %collective-permute-start.34 = (bf16[768,640]{1,0:T(8,128)(2,1)}, bf16[768,640]{1,0:T(8,128)(2,1)}, u32[]{:S(2)}, u32[]{:S(2)}) collective-permute-start(bf16[768,640]{1,0:T(8,128)(2,1)} %refs_5_.1), channel_id=1, source_target_pairs={{0,1},{1,0},{2,3},{3,2},{4,5},{5,4},{6,7},{7,6},{8,9},{9,8},{10,11... | collective-permute-start | bytes 2949128 | tf_op jit(solution)/shard_map/ppermute | solution.py:19
  214.3 49.6 %collective-permute-start = (bf16[128,5120]{1,0:T(8,128)(2,1)}, bf16[128,5120]{1,0:T(8,128)(2,1)}, u32[]{:S(2)}, u32[]{:S(2)}) collective-permute-start(bf16[128,5120]{1,0:T(8,128)(2,1)} %fusion.3), channel_id=1, source_target_pairs={{0,8},{8,0},{16,24},{24,16},{1,9},{9,1},{17,25},{25,17},{2,10},{10... | collective-permute-start | bytes 3932168 | tf_op jit(solution)/shard_map/ppermute | solution.py:19
  268.2 49.9 %collective-permute-start.1 = (bf16[128,5120]{1,0:T(8,128)(2,1)}, bf16[128,5120]{1,0:T(8,128)(2,1)}, u32[]{:S(2)}, u32[]{:S(2)}) collective-permute-start(bf16[128,5120]{1,0:T(8,128)(2,1)} %fusion.2), channel_id=1, source_target_pairs={{0,16},{8,24},{16,0},{24,8},{1,17},{9,25},{17,1},{25,9},{2,18},{10... | collective-permute-start | bytes 3932168 | tf_op jit(solution)/shard_map/ppermute | solution.py:19
  288.5 43.0 %all-to-all-start.1 = ((bf16[4,2,128,1280]{3,2,1,0:T(8,128)(2,1)}), bf16[4,2,128,1280]{3,2,1,0:T(8,128)(2,1)}, u32[]{:S(2)}, u32[]{:S(2)}) async-start(bf16[4,2,128,1280]{3,2,1,0:T(8,128)(2,1)} %project_out.1), calls=%async_computation.1 | async-start | bytes 5242880 | tf_op jit(solution)/shard_map/all_to_all | solution.py:431
  (52 other events, 766.3 us)
Sparse Core Ops, SparseCore 0:
  9.9 56.2 all-gather.2
  68.0 61.4 all-gather.4

commit v3 on v2

--- a/solution.py
+++ b/solution.py
@@ -38,12 +38,15 @@
     return lax.optimization_barrier((x,) + others)[0]
 
 
-def along_line(x):
+def along_line(x, awaited=()):
     size = lax.axis_size("head")
     below, above = [x], [x]
     for hop in range(1, size):
-        below.append(lax.ppermute(below[-1], "head", [(i, i + 1) for i in range(hop - 1, size - 1)]))
-        above.append(lax.ppermute(above[-1], "head", [(i, i - 1) for i in range(1, size - hop + 1)]))
+        up, down = below[-1], above[-1]
+        if 0 <= hop - 2 < len(awaited):
+            up, down = after((up, down), *awaited[hop - 2])
+        below.append(lax.ppermute(up, "head", [(i, i + 1) for i in range(hop - 1, size - 1)]))
+        above.append(lax.ppermute(down, "head", [(i, i - 1) for i in range(1, size - hop + 1)]))
     return below, above
 
 
@@ -55,35 +58,35 @@
     return pl.CostEstimate(flops=int(flops), bytes_accessed=int(moved), transcendentals=int(raised))
 
 
-def modulate_kernel(place, states, rows, mine, other):
+def modulate_kernel(steps, place, states, rows, mine, other):
     current = states[...]
     centre = jnp.mean(current, axis=-1, keepdims=True)
     centred = current - centre
     spread_of = jnp.mean(centred * centred, axis=-1, keepdims=True)
     shift, scale = rows[0:1, :], rows[1:2, :]
     modulated = (centred * lax.rsqrt(spread_of + 1e-06) * (1.0 + scale) + shift).astype(jnp.bfloat16)
-    steps, _, width = mine.shape
     core = place[1]
     for block in range(2 * steps):
+        width = modulated.shape[1] // (2 * steps)
         piece = modulated[:, block * width : (block + 1) * width]
+        at = slice(block // 2 * width, (block // 2 + 1) * width)
 
         @pl.when(core == block % 2)
-        def _(piece=piece, at=block // 2):
-            mine[at] = piece
+        def _(piece=piece, at=at):
+            mine[:, at] = piece
 
         @pl.when(core != block % 2)
-        def _(piece=piece, at=block // 2):
-            other[at] = piece
+        def _(piece=piece, at=at):
+            other[:, at] = piece
 
 
 def modulate(place, states, rows, steps):
     tokens, width = states.shape
-    block = width // (2 * steps)
     tile = 32
-    out = jax.ShapeDtypeStruct((steps, tokens, block), jnp.bfloat16)
-    spec = pl.BlockSpec((steps, tile, block), lambda i: (0, i, 0))
-    return pl.pallas_call(
-        modulate_kernel,
+    out = jax.ShapeDtypeStruct((tokens, width // 2), jnp.bfloat16)
+    spec = pl.BlockSpec((tile, width // 2), lambda i: (i, 0))
+    return pl.pallas_call(
+        functools.partial(modulate_kernel, steps),
         grid=(tokens // tile,),
         in_specs=[SMEM, pl.BlockSpec((tile, width), lambda i: (i, 0)), pl.BlockSpec(rows.shape, lambda i: (0, 0))],
         out_specs=[spec, spec],
@@ -99,40 +102,31 @@
     own, below, above = refs[0], refs[1:size], refs[size:count]
     weights = refs[count : count + len(layout)]
     here, there, x_held, w_held, x_sems, w_sems = refs[count + len(layout) :]
-    steps, tokens = own.shape[1:3]
+    tokens, depth = own.shape[1:]
+    half = depth // 2
     step_at, position = place[0], place[2]
-    low = position < size // 2
-    shift = jnp.where(low, 0, 1)
+    shift = place[4]
     early = size - 1
-
-    def x_copy(ref, clip, step, block):
-        if parts == "first":
-            row = (clip * early + block) * tokens
-        elif parts == "last":
-            row = clip * tokens
-        else:
-            row = (clip * size + block) * tokens
-        return pltpu.make_async_copy(
-            ref.at[clip, step], x_held.at[step, pl.ds(pl.multiple_of(row, tokens), tokens)], x_sems.at[step, clip, block]
-        )
-
-    def start_weights():
-        for index, (ref, (kind, offset, start, rows)) in enumerate(zip(weights, layout)):
-            if kind == "whole":
-                for step in range(steps):
-                    pltpu.make_async_copy(ref.at[pl.ds(step * rows, rows)], w_held.at[step], w_sems.at[step, 0]).start()
-            else:
-                at = jnp.bitwise_xor(step_at, offset)
-                pltpu.make_async_copy(ref, w_held.at[at, pl.ds(start, rows)], w_sems.at[0, index]).start()
-
-    def wait_weights(step):
-        for index, (ref, (kind, offset, start, rows)) in enumerate(zip(weights, layout)):
-            if kind == "whole":
-                pltpu.make_async_copy(ref.at[pl.ds(step * rows, rows)], w_held.at[step], w_sems.at[step, 0]).wait()
-            elif step == 0:
-                pltpu.make_async_copy(ref, w_held.at[0, pl.ds(start, rows)], w_sems.at[0, index]).wait()
-
-    def start_rows(step):
+    blocks = {"first": range(early), "last": range(early, size), "all": range(size)}[parts]
+
+    def x_copy(ref, clip, part, block):
+        row = (clip * len(blocks) + block - blocks[0]) * tokens
+        rows, columns = pl.ds(pl.multiple_of(row, tokens), tokens), pl.ds(part * half, half)
+        return pltpu.make_async_copy(ref.at[clip, :, columns], x_held.at[rows, columns], x_sems.at[part, clip, block])
+
+    def w_copies(part):
+        if len(layout) == 1:
+            rows = pl.ds(part * half, half)
+            yield pltpu.make_async_copy(weights[0].at[rows], w_held.at[rows], w_sems.at[0, part])
+        elif part == 0:
+            for index, (ref, (offset, whole, start, rows)) in enumerate(zip(weights, layout)):
+                at = jnp.bitwise_xor(step_at, offset) * whole + start
+                target = w_held.at[pl.ds(pl.multiple_of(at, rows), rows)]
+                yield pltpu.make_async_copy(ref, target, w_sems.at[1, index])
+
+    for part in range(2):
+        for copy in w_copies(part):
+            copy.start()
         for clip in range(2):
             for away in range(size):
                 for sign, held in ((1, above), (-1, below)):
@@ -142,49 +136,41 @@
                     block_at = position + sign * away
                     block = lax.rem(block_at - shift + size, size)
                     inside = jnp.logical_and(block_at >= 0, block_at < size)
-                    if parts == "first":
-                        inside = jnp.logical_and(inside, block < early)
-                    elif parts == "last":
-                        inside = jnp.logical_and(inside, block == early)
+                    inside = jnp.logical_and(inside, jnp.logical_and(block >= blocks[0], block <= blocks[-1]))
 
                     @pl.when(inside)
-                    def _(source=source, block=block, clip=clip):
-                        x_copy(source, clip, step, block).start()
-
-    blocks = {"first": range(early), "last": range(early, size), "all": range(size)}[parts]
-    for step in range(steps):
-        start_rows(step)
-        if step == 0:
-            start_weights()
-    half = here.shape[0]
-    for step in range(steps):
-        wait_weights(step)
+                    def _(source=source, block=block, clip=clip, part=part):
+                        x_copy(source, clip, part, block).start()
+
+    rows = here.shape[0]
+    for part in range(2):
+        for copy in w_copies(part):
+            copy.wait()
         for clip in range(2):
             for block in blocks:
-                x_copy(own, clip, step, block).wait()
-        product = jnp.dot(x_held[step], w_held[step], preferred_element_type=jnp.float32)
-        if step == 0:
-            here[...] = product[:half]
-            there[...] = product[half:]
+                x_copy(own, clip, part, block).wait()
+        span = slice(part * half, (part + 1) * half)
+        product = jnp.dot(x_held[:, span], w_held[span], preferred_element_type=jnp.float32)
+        if part == 0:
+            here[...] = product[:rows]
+            there[...] = product[rows:]
         else:
-            here[...] += product[:half]
-            there[...] += product[half:]
+            here[...] += product[:rows]
+            there[...] += product[rows:]
 
 
 def project(place, line, shards, parts, name):
     size = lax.axis_size("head")
     below, above = line
     operands = [below[0]] + below[1:] + above[1:]
-    _, steps, tokens, block = operands[0].shape
+    _, tokens, depth = operands[0].shape
     layout, weights = [], []
     for offset, pieces in enumerate(shards):
         start = 0
         for piece in pieces:
-            kind = "whole" if len(shards) == 1 else "piece"
-            rows = block if kind == "whole" else piece.shape[0]
-            layout.append((kind, offset, start, rows))
+            layout.append((offset, depth // len(shards), start, piece.shape[0]))
             weights.append(piece)
-            start += rows
+            start += piece.shape[0]
     columns = weights[0].shape[1]
     rows = {"first": size - 1, "last": 1, "all": size}[parts] * tokens
     out = jax.ShapeDtypeStruct((rows, columns), jnp.float32)
@@ -194,13 +180,13 @@
         out_specs=[VMEM, VMEM],
         out_shape=[out, out],
         scratch_shapes=[
-            pltpu.VMEM((steps, 2 * rows, block), jnp.bfloat16),
-            pltpu.VMEM((steps, block, columns), jnp.bfloat16),
-            pltpu.SemaphoreType.DMA((steps, 2, size)),
-            pltpu.SemaphoreType.DMA((steps, len(layout))),
+            pltpu.VMEM((2 * rows, depth), jnp.bfloat16),
+            pltpu.VMEM((depth, columns), jnp.bfloat16),
+            pltpu.SemaphoreType.DMA((2, 2, size)),
+            pltpu.SemaphoreType.DMA((2, max(2, len(layout)))),
         ],
         compiler_params=params(),
-        cost_estimate=cost(4 * rows * steps * block * columns, 2 * steps * block * (2 * rows + columns) + 8 * rows * columns),
+        cost_estimate=cost(4 * rows * depth * columns, 2 * depth * (2 * rows + columns) + 8 * rows * columns),
         name=name,
     )(place, *operands, *weights)
 
@@ -271,6 +257,8 @@
     gates, out, a_held, w_held, total, a_sems, w_sems = refs[len(layout) + 2 * size :]
     steps, _, tokens, columns = out.shape
     width = columns // 2
+    halves, _, _, span_width = w_held.shape
+    joined = halves == 1
     step_at, core, position = place[0], place[1], place[2]
 
     def a_copies():
@@ -283,9 +271,13 @@
 
     def w_copy(half, away):
         group = lax.rem(position + away, size)
-        return pltpu.make_async_copy(
-            weights[half * size + away], w_held.at[jnp.bitwise_xor(core, half), group], w_sems.at[half, away]
-        )
+        at = jnp.bitwise_xor(core, half)
+        if joined:
+            span = pl.ds(pl.multiple_of(at * width, 128), width)
+            target = w_held.at[0, group, :, span]
+        else:
+            target = w_held.at[at, group]
+        return pltpu.make_async_copy(weights[half * size + away], target, w_sems.at[half, away])
 
     for copy in a_copies():
         copy.start()
@@ -298,21 +290,20 @@
         group = lax.rem(position + away, size)
         for half in range(2):
             w_copy(half, away).wait()
-        for half in range(2):
+        for half in range(halves):
             part = jnp.dot(a_held[group], w_held[half, group], preferred_element_type=jnp.float32)
             part = part.astype(jnp.bfloat16).astype(jnp.float32)
             if away == 0:
                 total[half] = part
             else:
                 total[half] += part
-    for half in range(2):
-        span = slice(half * width, (half + 1) * width)
+    for half in range(halves):
+        span = slice(half * span_width, (half + 1) * span_width)
         reached = None
         for step in range(steps):
-            told = jnp.bitwise_xor(step_at, step)
-            branch = total[half, step * tokens : (step + 1) * tokens] * gates[pl.ds(told, 1), span]
+            branch = total[half, step * tokens : (step + 1) * tokens] * gates[step : step + 1, span]
             out[step, 0, :, span] = branch.astype(jnp.bfloat16)
-            drift = branch * widths[told]
+            drift = branch * widths[step]
             reached = drift if step == 0 else reached + drift
             out[step, 1, :, span] = reached.astype(jnp.bfloat16)
 
@@ -330,6 +321,7 @@
             pieces.append(piece)
             start += piece.shape[0]
     rows = steps * tokens
+    halves = 1 if width % 128 == 0 else 2
     operands = pieces + [w for half in weights for w in half]
     return pl.pallas_call(
         functools.partial(out_kernel, size, tuple(layout)),
@@ -338,8 +330,8 @@
         out_shape=jax.ShapeDtypeStruct((steps, 2, tokens, 2 * width), jnp.bfloat16),
         scratch_shapes=[
             pltpu.VMEM((size, rows, inner), jnp.bfloat16),
-            pltpu.VMEM((2, size, inner, width), jnp.bfloat16),
-            pltpu.VMEM((2, rows, width), jnp.float32),
+            pltpu.VMEM((halves, size, inner, 2 * width // halves), jnp.bfloat16),
+            pltpu.VMEM((halves, rows, 2 * width // halves), jnp.float32),
             pltpu.SemaphoreType.DMA((len(layout), size)),
             pltpu.SemaphoreType.DMA((2, size)),
         ],
@@ -377,11 +369,19 @@
     shift = (position >= size // 2).astype(jnp.int32)
     place = jnp.stack([step, core, position, lengths[0], shift]).astype(jnp.int32)
 
-    mine, other = modulate(place, current, modulation[0], steps)
-    line = along_line(jnp.stack([mine, swap(other, "fsdp", 1)]))
+    columns = current.shape[1] // steps
+    step_width = (timesteps[0, 1] - timesteps[0, 0]).astype(jnp.float32) / 1000.0
+    told = jnp.concatenate([modulation[0, 2].reshape(steps, columns), jnp.full((steps, HD), step_width)], axis=1)
+    heard = lax.all_to_all(told, "step", 0, 0)
+    gates, widths = heard[:, :columns], heard[:, columns]
 
     q_shards = [[lax.all_gather(w_query, "step", axis=0, tiled=True)]]
     k_shards = spread(w_key)
+
+    mine, other = modulate(place, current, modulation[0], steps)
+    direct = [piece for held in k_shards for piece in held if piece.shape == w_key.shape]
+    forwarded = [piece for held in k_shards for piece in held if piece.shape != w_key.shape]
+    line = along_line(jnp.stack([mine, swap(other, "fsdp", 1)]), (direct + [heard], forwarded))
     v_shards = [[lax.all_gather(w_value, "step", axis=0, tiled=True)]]
 
     def projected(shards, parts, name):
@@ -403,9 +403,7 @@
 
     squares = jnp.stack([squares_of(q_parts), squares_of(k_parts)])
     squares = jnp.where(shift == 0, squares, jnp.roll(squares, tokens, axis=1))
-    square_sum = squares
-    for away in range(1, size):
-        square_sum = square_sum + lax.ppermute(squares, "head", [(i, (i + away) % size) for i in range(size)])
+    square_sum = jnp.sum(lax.all_to_all(jnp.broadcast_to(squares[None], (size,) + squares.shape), "head", 0, 0), axis=0)
     square_sum = jnp.where(shift == 0, square_sum, jnp.roll(square_sum, -tokens, axis=1))
     full_width = float(w_query.shape[1] * size)
     scales = lax.rsqrt(square_sum / full_width + 1e-06)[..., None]
@@ -415,26 +413,20 @@
 
     gathered = spread(lax.all_to_all(attended, "head", 0, 0))
 
-    below, above = along_line(after(w_out, line[0][-1], line[1][-1]))
+    below, above = along_line(after(w_out, line[0][-1], line[1][-1], q_parts[0], k_parts[0]))
     own_columns = [w_out] + [
         jnp.where(position + away < size, above[away], below[size - away]) for away in range(1, size)
     ]
     out_weights = (own_columns, [swap(w, "fsdp", 1) for w in own_columns])
 
-    step_width = (timesteps[0, 1] - timesteps[0, 0]).astype(jnp.float32) / 1000.0
-    told = jnp.concatenate([modulation[0, 2], jnp.full((HD,), step_width)])[None]
-    heard = jnp.concatenate([told] + [swap(told, "step", offset) for offset in range(1, steps)])
-    columns = current.shape[1] // steps
-    gates = lax.dynamic_slice(heard, (0, step * columns), (steps, columns))
-
-    sent = project_out(place, heard[:, -1], gathered, out_weights, gates)
+    sent = project_out(place, widths, gathered, out_weights, gates)
     arrived = lax.all_to_all(sent, "step", 0, 0)
 
     carried = step_width * current + jnp.where(step == 0, current, jnp.zeros_like(current))
     base, total = carried, carried
     bit = 1
     while bit < steps:
-        brought = swap(total.astype(jnp.bfloat16), "step", bit).astype(jnp.float32)
+        brought = swap(after(total.astype(jnp.bfloat16), v_shards[0][0]), "step", bit).astype(jnp.float32)
         base = base + jnp.where(jnp.bitwise_and(step, bit) != 0, brought, jnp.zeros_like(brought))
         total = total + brought
         bit *= 2

time: 344 us -> 342 us (level)
  blocking collectives: 0 us -> 35.2 us
  waiting for transfers between devices: 154 us -> 130 us
  starting transfers between devices: 62.8 us -> 52.7 us
  Pallas kernels: 83.8 us -> 76.8 us
    all_to_all x0 -> x1, blocking collectives: none -> 35.2 us  [body(): heard = lax.all_to_all(told, 'step', 0, 0)]
    ppermute x15 -> x12, waiting for transfers between devices: 63.7 us -> 47.4 us  [the longest x6 47.4 us: along_line(): lax.ppermute(down, 'head', [(i, i - 1) for i in range(1, size - hop + 1)])]
    ppermute x23 -> x20, waiting for transfers between devices: 74 us -> 59.1 us  [swap(): lax.ppermute(x, axis, [(i, i ^ offset) for i in range(lax.axis_size(axis))])]
    ppermute x15 -> x12, starting transfers between devices: 36.3 us -> 22.3 us  [the longest x6 14.2 us: along_line(): lax.ppermute(up, 'head', [(i, i + 1) for i in range(hop - 1, size - 1)])]
    all_to_all x1, waiting for transfers between devices: 5.52 us -> 13 us  [body(): gathered = spread(lax.all_to_all(attended, 'head', 0, 0))]
    pallas_call x5, Pallas kernels: 48 us -> 41.2 us  [project(): pl.pallas_call(functools.partial(project_kernel, size, parts, tuple(layou...]
    all_to_all x0 -> x1, starting transfers between devices: none -> 5.14 us  [body(): lax.all_to_all(jnp.broadcast_to(squares[None], (size,) + squares.shape),...]
    ppermute x23 -> x20, starting transfers between devices: 18 us -> 14.3 us  [swap(): lax.ppermute(x, axis, [(i, i ^ offset) for i in range(lax.axis_size(axis))])]
  transfers between devices with their start and end apart: 42 -> 37, of which waited for: 15 -> 14; matrix products, arithmetic and copies ran while one was open for 7% -> 8% of each run, Pallas kernels for 23% -> 21%
where the time goes in v3:
time: 342 us; the launch traced here: 340 us
  waiting for transfers between devices  130 us (38%)
  Pallas kernels  76.8 us (22%)
  starting transfers between devices  52.7 us (15%)
  blocking collectives  35.2 us (10%)
  other arithmetic  17.7 us (5%)
  between operations  16.6 us (5%)
  local copies, waits for them, and re-layouts  10.4 us (3%)
    ppermute x20, waiting for transfers between devices, swap(): lax.ppermute(x, axis, [(i, i ^ offset) for i in range(lax.axis_size(axis))])  59.1 us
    ppermute x6, waiting for transfers between devices, along_line(): lax.ppermute(down, 'head', [(i, i - 1) for i in range(1, size - hop + 1)])  47.4 us
    pallas_call x5, Pallas kernels, project(): pl.pallas_call(functools.partial(project_kernel, size, parts, tuple(layou...  41.2 us
    all_to_all x1, blocking collectives, body(): heard = lax.all_to_all(told, 'step', 0, 0)  35.2 us
    ppermute x20, starting transfers between devices, swap(): lax.ppermute(x, axis, [(i, i ^ offset) for i in range(lax.axis_size(axis))])  14.3 us
    ppermute x6, starting transfers between devices, along_line(): lax.ppermute(up, 'head', [(i, i + 1) for i in range(hop - 1, size - 1)])  14.2 us
    all_to_all x1, waiting for transfers between devices, body(): gathered = spread(lax.all_to_all(attended, 'head', 0, 0))  13 us
    pallas_call x1, Pallas kernels, project_out(): pl.pallas_call(functools.partial(out_kernel, size, tuple(layout)), in_spe...  11.8 us
  transfers between devices with their start and end apart: 37, of which 14 were waited for; matrix products, arithmetic and copies ran while one was open for 8% of the time, Pallas kernels for 21%

profile of v3, /device:TPU:0, one launch (start us, length us, event | category | flops | bytes accessed | tf_op | source)
XLA Modules:
  0.0 339.7 jit_solution(17399386451882144051)
XLA Ops:
  10.6 4.6 %modulate.1 = (bf16[128,2560]{1,0:T(8,128)(2,1)}, bf16[128,2560]{1,0:T(8,128)(2,1)}) custom-call(s32[5]{0:T(128)} %stack.37.place, f32[128,5120]{1,0:T(8,128)} %bitcast.25, f32[3,5120]{1,0:T(4,128)} %bitcast.28), custom_call_target="tpu_custom_call" | custom-call | flops 6553600 | bytes 3932160 | tf_op jit(solution)/shard_map/modulate/pallas_call | solution.py:88
  18.8 5.0 %collective-permute-start.3 = (bf16[2,128,2560]{2,1,0:T(8,128)(2,1)S(1)}, bf16[2,128,2560]{2,1,0:T(8,128)(2,1)S(1)}, u32[]{:S(2)}, u32[]{:S(2)}) collective-permute-start(bf16[2,128,2560]{2,1,0:T(8,128)(2,1)S(1)} %pad_maximum_fusion.refs_0_.refs_3_.refs_6_), channel_id=1, source_target_pairs={{0,2},{2,4},{4,6},{1,3},{3,5},{5,7},{8,10},{10,12},{12,14},{9,11},... | collective-permute-start | bytes 3932168 | tf_op jit(solution)/shard_map/ppermute | solution.py:48
  30.2 35.2 %all_to_all.27 = f32[4,1,1408]{2,1,0:T(1,128)S(1)} all-to-all(f32[4,1,1408]{2,1,0:T(1,128)S(1)} %all_to_all.17), channel_id=1, replica_groups=mesh['step'=4,'head'=4,'fsdp'=2] {'step'}, dimensions={0} | all-to-all | bytes 45056 | tf_op jit(solution)/shard_map/all_to_all | solution.py:375
  73.4 13.1 %collective-permute-done.10.refs_10_ = bf16[320,768]{1,0:T(8,128)(2,1)S(1)} collective-permute-done((bf16[320,768]{1,0:T(8,128)(2,1)S(1)}, bf16[320,768]{1,0:T(8,128)(2,1)S(1)}, u32[]{:S(2)}, u32[]{:S(2)}) %collective-permute-start.10) | collective-permute-done | bytes 491552 | tf_op jit(solution)/shard_map/ppermute | solution.py:19
  87.0 14.5 %collective-permute-done.8.refs_5_ = bf16[2,128,2560]{2,1,0:T(8,128)(2,1)} collective-permute-done((bf16[2,128,2560]{2,1,0:T(8,128)(2,1)}, bf16[2,128,2560]{2,1,0:T(8,128)(2,1)}, u32[]{:S(2)}, u32[]{:S(2)}) %collective-permute-start.8) | collective-permute-done | bytes 1310752 | tf_op jit(solution)/shard_map/ppermute | solution.py:49
  104.5 9.8 %key.1 = (f32[384,768]{1,0:T(8,128)}, f32[384,768]{1,0:T(8,128)}) custom-call(s32[5]{0:T(128)} %stack.37.place, bf16[2,128,2560]{2,1,0:T(8,128)(2,1)} %copy-done, bf16[2,128,2560]{2,1,0:T(8,128)(2,1)} %copy-done.2, bf16[2,128,2560]{2,1,0:T(8,128)(2,1)} %collective-permute-done.7.refs_2_, bf16[2,128,2560]{2,1,0:T(8,128)(2,1)} %copy-done, ...), custom_call_target="tpu_custom_call" | custom-call | flops 3019898880 | bytes 10223616 | tf_op jit(solution)/shard_map/key/pallas_call | solution.py:177
  114.4 9.2 %query.1 = (f32[384,768]{1,0:T(8,128)}, f32[384,768]{1,0:T(8,128)}) custom-call(s32[5]{0:T(128)} %stack.37.place, bf16[2,128,2560]{2,1,0:T(8,128)(2,1)} %copy-done, bf16[2,128,2560]{2,1,0:T(8,128)(2,1)} %copy-done.2, bf16[2,128,2560]{2,1,0:T(8,128)(2,1)} %collective-permute-done.7.refs_2_, bf16[2,128,2560]{2,1,0:T(8,128)(2,1)} %copy-done, ...), custom_call_target="tpu_custom_call" | custom-call | flops 3019898880 | bytes 10223616 | tf_op jit(solution)/shard_map/query/pallas_call | solution.py:177
  124.1 9.5 %collective-permute-done.13.refs_6_ = bf16[2,128,2560]{2,1,0:T(8,128)(2,1)} collective-permute-done((bf16[2,128,2560]{2,1,0:T(8,128)(2,1)}, bf16[2,128,2560]{2,1,0:T(8,128)(2,1)}, u32[]{:S(2)}, u32[]{:S(2)}) %collective-permute-start.13) | collective-permute-done | bytes 1310752 | tf_op jit(solution)/shard_map/ppermute | solution.py:49
  133.6 5.9 %key_last.1 = (f32[128,768]{1,0:T(8,128)}, f32[128,768]{1,0:T(8,128)}) custom-call(s32[5]{0:T(128)} %stack.37.place, bf16[2,128,2560]{2,1,0:T(8,128)(2,1)} %copy-done, bf16[2,128,2560]{2,1,0:T(8,128)(2,1)} %copy-done.2, bf16[2,128,2560]{2,1,0:T(8,128)(2,1)} %collective-permute-done.7.refs_2_, bf16[2,128,2560]{2,1,0:T(8,128)(2,1)} %collective-permute-done.12.refs_3_, ...), custom_call_target="tpu_custom_call" | custom-call | flops 1006632960 | bytes 6029312 | tf_op jit(solution)/shard_map/key_last/pallas_call | solution.py:177
  142.0 5.2 %query_last.1 = (f32[128,768]{1,0:T(8,128)}, f32[128,768]{1,0:T(8,128)}) custom-call(s32[5]{0:T(128)} %stack.37.place, bf16[2,128,2560]{2,1,0:T(8,128)(2,1)} %copy-done, bf16[2,128,2560]{2,1,0:T(8,128)(2,1)} %copy-done.2, bf16[2,128,2560]{2,1,0:T(8,128)(2,1)} %collective-permute-done.7.refs_2_, bf16[2,128,2560]{2,1,0:T(8,128)(2,1)} %collective-permute-done.12.refs_3_, ...), custom_call_target="tpu_custom_call" | custom-call | flops 1006632960 | bytes 6029312 | tf_op jit(solution)/shard_map/query_last/pallas_call | solution.py:177
  147.7 11.1 %value.1 = (f32[512,768]{1,0:T(8,128)}, f32[512,768]{1,0:T(8,128)}) custom-call(s32[5]{0:T(128)} %stack.37.place, bf16[2,128,2560]{2,1,0:T(8,128)(2,1)} %copy-done, bf16[2,128,2560]{2,1,0:T(8,128)(2,1)} %copy-done.2, bf16[2,128,2560]{2,1,0:T(8,128)(2,1)} %collective-permute-done.7.refs_2_, bf16[2,128,2560]{2,1,0:T(8,128)(2,1)} %collective-permute-done.12.refs_3_, ...), custom_call_target="tpu_custom_call" | custom-call | flops 4026531840 | bytes 12320768 | tf_op jit(solution)/shard_map/value/pallas_call | solution.py:177
  167.0 5.1 %all-to-all-start.1 = ((f32[4,2,512]{2,1,0:T(2,128)}), f32[4,2,512]{2,1,0:T(2,128)S(1)}, u32[]{:S(2)}, u32[]{:S(2)}) async-start(f32[4,2,512]{2,1,0:T(2,128)} %broadcast_in_dim.20), calls=%async_computation.1 | async-start | bytes 32768 | tf_op jit(solution)/shard_map/all_to_all | solution.py:406
  173.3 12.5 %collective-permute-done.22 = bf16[768,640]{1,0:T(8,128)(2,1)} collective-permute-done((bf16[768,640]{1,0:T(8,128)(2,1)}, bf16[768,640]{1,0:T(8,128)(2,1)}, u32[]{:S(2)}, u32[]{:S(2)}) %collective-permute-start.22) | collective-permute-done | bytes 983072 | tf_op jit(solution)/shard_map/ppermute | solution.py:49
  188.9 8.2 %probs.1 = bf16[6,512,512]{2,1,0:T(8,128)(2,1)} custom-call(s32[5]{0:T(128)} %stack.37.place, f32[384,768]{1,0:T(8,128)} %get-tuple-element.29.refs_0_, f32[384,768]{1,0:T(8,128)} %collective-permute-done.9.refs_1_, f32[128,768]{1,0:T(8,128)} %get-tuple-element.33.refs_2_, f32[128,768]{1,0:T(8,128)} %collective-permute-done.14.refs_3_, ...), custom_call_target="tpu_custom_call" | custom-call | flops 402653184 | bytes 9437184 | tf_op jit(solution)/shard_map/probs/pallas_call | solution.py:217
  197.1 6.3 %attend.1 = bf16[4,128,768]{2,1,0:T(8,128)(2,1)} custom-call(s32[5]{0:T(128)} %stack.37.place, bf16[6,512,512]{2,1,0:T(8,128)(2,1)} %probs.1, f32[512,768]{1,0:T(8,128)} %get-tuple-element.39.v_a, f32[512,768]{1,0:T(8,128)} %collective-permute-done.17.v_b), custom_call_target="tpu_custom_call" | custom-call | flops 402653184 | bytes 7077888 | tf_op jit(solution)/shard_map/attend/pallas_call | solution.py:242
  203.4 6.3 %all-to-all-start.2 = ((bf16[4,128,768]{2,1,0:T(8,128)(2,1)}), bf16[4,128,768]{2,1,0:T(8,128)(2,1)S(1)}, u32[]{:S(2)}, u32[]{:S(2)}) async-start(bf16[4,128,768]{2,1,0:T(8,128)(2,1)} %attend.1), calls=%async_computation.2 | async-start | bytes 1572864 | tf_op jit(solution)/shard_map/all_to_all | solution.py:414
  215.8 13.0 %all-to-all-done.2.refs_0_ = bf16[4,128,768]{2,1,0:T(8,128)(2,1)S(1)} async-done(((bf16[4,128,768]{2,1,0:T(8,128)(2,1)}), bf16[4,128,768]{2,1,0:T(8,128)(2,1)S(1)}, u32[]{:S(2)}, u32[]{:S(2)}) %all-to-all-start.2) | async-done | bytes 786464 | tf_op jit(solution)/shard_map/all_to_all | solution.py:414
  233.9 10.9 %collective-permute-done.27 = bf16[768,640]{1,0:T(8,128)(2,1)} collective-permute-done((bf16[768,640]{1,0:T(8,128)(2,1)}, bf16[768,640]{1,0:T(8,128)(2,1)}, u32[]{:S(2)}, u32[]{:S(2)}) %collective-permute-start.27) | collective-permute-done | bytes 983072 | tf_op jit(solution)/shard_map/ppermute | solution.py:49
  248.5 10.4 %collective-permute-done.18.refs_1_ = bf16[4,128,768]{2,1,0:T(8,128)(2,1)S(1)} collective-permute-done((bf16[4,128,768]{2,1,0:T(8,128)(2,1)S(1)}, bf16[4,128,768]{2,1,0:T(8,128)(2,1)S(1)}, u32[]{:S(2)}, u32[]{:S(2)}) %collective-permute-start.18) | collective-permute-done | bytes 786464 | tf_op jit(solution)/shard_map/ppermute | solution.py:19
  273.3 11.8 %project_out.1 = bf16[4,2,128,1280]{3,2,1,0:T(8,128)(2,1)} custom-call(s32[5]{0:T(128)} %stack.37.place, f32[4]{0:T(128)} %slice_reduce_fusion.1.widths, bf16[4,128,768]{2,1,0:T(8,128)(2,1)} %copy-done.13, bf16[4,128,768]{2,1,0:T(8,128)(2,1)} %copy-done.14, bf16[4,128,768]{2,1,0:T(8,128)(2,1)} %copy-done.15, bf16[2,128,768]{2,1,0:T(8,128)(2,1)} %copy-done.24, ...), custom_call_target="tpu_custom_call" | custom-call | flops 4026531840 | bytes 13631488 | tf_op jit(solution)/shard_map/project_out/pallas_call | solution.py:326
  285.1 4.6 %all-to-all-start.3 = ((bf16[4,2,128,1280]{3,2,1,0:T(8,128)(2,1)}), bf16[4,2,128,1280]{3,2,1,0:T(8,128)(2,1)}, u32[]{:S(2)}, u32[]{:S(2)}) async-start(bf16[4,2,128,1280]{3,2,1,0:T(8,128)(2,1)} %project_out.1), calls=%async_computation.3 | async-start | bytes 5242880 | tf_op jit(solution)/shard_map/all_to_all | solution.py:423
  289.6 25.1 %collective-permute-done.1 = bf16[128,5120]{1,0:T(8,128)(2,1)} collective-permute-done((bf16[128,5120]{1,0:T(8,128)(2,1)}, bf16[128,5120]{1,0:T(8,128)(2,1)}, u32[]{:S(2)}, u32[]{:S(2)}) %collective-permute-start.1) | collective-permute-done | bytes 1310752 | tf_op jit(solution)/shard_map/ppermute | solution.py:19
  318.7 9.4 %all-to-all-done.3.arrived = bf16[4,2,128,1280]{3,2,1,0:T(8,128)(2,1)} async-done(((bf16[4,2,128,1280]{3,2,1,0:T(8,128)(2,1)}), bf16[4,2,128,1280]{3,2,1,0:T(8,128)(2,1)}, u32[]{:S(2)}, u32[]{:S(2)}) %all-to-all-start.3) | async-done | bytes 2621472 | tf_op jit(solution)/shard_map/all_to_all | solution.py:423
  328.1 4.8 %finish.1 = (f32[128,5120]{1,0:T(8,128)}, bf16[128,5120]{1,0:T(8,128)(2,1)}) custom-call(f32[128,5120]{1,0:T(8,128)} %fusion.1.base, bf16[4,2,128,1280]{3,2,1,0:T(8,128)(2,1)} %all-to-all-done.3.arrived), custom_call_target="tpu_custom_call" | custom-call | flops 655360 | bytes 9175040 | tf_op jit(solution)/shard_map/finish/pallas_call | solution.py:352
  (155 shorter events, 71.8 us)
Async XLA Ops:
  7.2 107.2 %all-gather.5.cloned.1.call-start = ((), (), s32[]{:S(2)}) async-start(), calls=%async_computation.5 | async-start | bytes 4915200 | tf_op jit(solution)/shard_map/all_gather | solution.py:378
  7.9 139.8 %all-gather.3.cloned.1.call-start = ((), (), s32[]{:S(2)}) async-start(), calls=%async_computation.4 | async-start | bytes 4915200 | tf_op jit(solution)/shard_map/all_gather | solution.py:385
  18.8 47.2 %collective-permute-start.3 = (bf16[2,128,2560]{2,1,0:T(8,128)(2,1)S(1)}, bf16[2,128,2560]{2,1,0:T(8,128)(2,1)S(1)}, u32[]{:S(2)}, u32[]{:S(2)}) collective-permute-start(bf16[2,128,2560]{2,1,0:T(8,128)(2,1)S(1)} %pad_maximum_fusion.refs_0_.refs_3_.refs_6_), channel_id=1, source_target_pairs={{0,2},{2,4},{4,6},{1,3},{3,5},{5,7},{8,10},{10,12},{12,14},{9,11},... | collective-permute-start | bytes 3932168 | tf_op jit(solution)/shard_map/ppermute | solution.py:48
  23.8 42.2 %collective-permute-start.4 = (bf16[2,128,2560]{2,1,0:T(8,128)(2,1)S(1)}, bf16[2,128,2560]{2,1,0:T(8,128)(2,1)}, u32[]{:S(2)}, u32[]{:S(2)}) collective-permute-start(bf16[2,128,2560]{2,1,0:T(8,128)(2,1)S(1)} %pad_maximum_fusion.refs_0_.refs_3_.refs_6_), channel_id=1, source_target_pairs={{2,0},{4,2},{6,4},{3,1},{5,3},{7,5},{10,8},{12,10},{14,12},{11,9},... | collective-permute-start | bytes 3932168 | tf_op jit(solution)/shard_map/ppermute | solution.py:49
  25.1 40.9 %collective-permute-start.5 = (bf16[640,768]{1,0:T(8,128)(2,1)}, bf16[640,768]{1,0:T(8,128)(2,1)}, u32[]{:S(2)}, u32[]{:S(2)}) collective-permute-start(bf16[640,768]{1,0:T(8,128)(2,1)} %refs_7_.3), channel_id=1, source_target_pairs={{0,8},{8,0},{16,24},{24,16},{1,9},{9,1},{17,25},{25,17},{2,10},{10... | collective-permute-start | bytes 2949128 | tf_op jit(solution)/shard_map/ppermute | solution.py:19
  26.6 39.4 %collective-permute-start.6 = (bf16[640,768]{1,0:T(8,128)(2,1)}, bf16[640,768]{1,0:T(8,128)(2,1)}, u32[]{:S(2)}, u32[]{:S(2)}) collective-permute-start(bf16[640,768]{1,0:T(8,128)(2,1)} %refs_7_.3), channel_id=1, source_target_pairs={{0,16},{8,24},{16,0},{24,8},{1,17},{9,25},{17,1},{25,9},{2,18},{10... | collective-permute-start | bytes 2949128 | tf_op jit(solution)/shard_map/ppermute | solution.py:19
  66.0 20.9 %collective-permute-start.7 = (bf16[2,128,2560]{2,1,0:T(8,128)(2,1)S(1)}, bf16[2,128,2560]{2,1,0:T(8,128)(2,1)}, u32[]{:S(2)}, u32[]{:S(2)}) collective-permute-start(bf16[2,128,2560]{2,1,0:T(8,128)(2,1)S(1)} %collective-permute-done.3.refs_1_), channel_id=1, source_target_pairs={{2,4},{4,6},{3,5},{5,7},{10,12},{12,14},{11,13},{13,15},{18,20},{2... | collective-permute-start | bytes 3932168 | tf_op jit(solution)/shard_map/ppermute | solution.py:48
  67.8 33.7 %collective-permute-start.8 = (bf16[2,128,2560]{2,1,0:T(8,128)(2,1)}, bf16[2,128,2560]{2,1,0:T(8,128)(2,1)}, u32[]{:S(2)}, u32[]{:S(2)}) collective-permute-start(bf16[2,128,2560]{2,1,0:T(8,128)(2,1)} %collective-permute-done.4.refs_4_), channel_id=1, source_target_pairs={{2,0},{4,2},{3,1},{5,3},{10,8},{12,10},{11,9},{13,11},{18,16},{20,... | collective-permute-start | bytes 3932168 | tf_op jit(solution)/shard_map/ppermute | solution.py:49
  101.4 22.7 %collective-permute-start.12 = (bf16[2,128,2560]{2,1,0:T(8,128)(2,1)}, bf16[2,128,2560]{2,1,0:T(8,128)(2,1)}, u32[]{:S(2)}, u32[]{:S(2)}) collective-permute-start(bf16[2,128,2560]{2,1,0:T(8,128)(2,1)} %collective-permute-done.7.refs_2_), channel_id=1, source_target_pairs={{4,6},{5,7},{12,14},{13,15},{20,22},{21,23},{28,30},{29,31}} | collective-permute-start | bytes 3932168 | tf_op jit(solution)/shard_map/ppermute | solution.py:48
  103.2 30.4 %collective-permute-start.13 = (bf16[2,128,2560]{2,1,0:T(8,128)(2,1)}, bf16[2,128,2560]{2,1,0:T(8,128)(2,1)}, u32[]{:S(2)}, u32[]{:S(2)}) collective-permute-start(bf16[2,128,2560]{2,1,0:T(8,128)(2,1)} %collective-permute-done.8.refs_5_), channel_id=1, source_target_pairs={{2,0},{3,1},{10,8},{11,9},{18,16},{19,17},{26,24},{27,25}} | collective-permute-start | bytes 3932168 | tf_op jit(solution)/shard_map/ppermute | solution.py:49
  114.3 44.5 %collective-permute-start.15 = (f32[384,768]{1,0:T(8,128)}, f32[384,768]{1,0:T(8,128)S(1)}, u32[]{:S(2)}, u32[]{:S(2)}) collective-permute-start(f32[384,768]{1,0:T(8,128)} %get-tuple-element.36), channel_id=1, source_target_pairs={{0,1},{1,0},{2,3},{3,2},{4,5},{5,4},{6,7},{7,6},{8,9},{9,8},{10,11... | collective-permute-start | bytes 3538952 | tf_op jit(solution)/shard_map/ppermute | solution.py:19
  123.6 41.3 %collective-permute-start.9 = (f32[384,768]{1,0:T(8,128)}, f32[384,768]{1,0:T(8,128)}, u32[]{:S(2)}, u32[]{:S(2)}) collective-permute-start(f32[384,768]{1,0:T(8,128)} %get-tuple-element.30), channel_id=1, source_target_pairs={{0,1},{1,0},{2,3},{3,2},{4,5},{5,4},{6,7},{7,6},{8,9},{9,8},{10,11... | collective-permute-start | bytes 3538952 | tf_op jit(solution)/shard_map/ppermute | solution.py:19
  139.6 23.5 %collective-permute-start.23 = (bf16[768,640]{1,0:T(8,128)(2,1)}, bf16[768,640]{1,0:T(8,128)(2,1)}, u32[]{:S(2)}, u32[]{:S(2)}) collective-permute-start(bf16[768,640]{1,0:T(8,128)(2,1)} %refs_5_.1), channel_id=1, source_target_pairs={{0,2},{2,4},{4,6},{1,3},{3,5},{5,7},{8,10},{10,12},{12,14},{9,11},... | collective-permute-start | bytes 2949128 | tf_op jit(solution)/shard_map/ppermute | solution.py:48
  158.8 38.2 %collective-permute-start.17 = (f32[512,768]{1,0:T(8,128)}, f32[512,768]{1,0:T(8,128)}, u32[]{:S(2)}, u32[]{:S(2)}) collective-permute-start(f32[512,768]{1,0:T(8,128)} %get-tuple-element.40), channel_id=1, source_target_pairs={{0,1},{1,0},{2,3},{3,2},{4,5},{5,4},{6,7},{7,6},{8,9},{9,8},{10,11... | collective-permute-start | bytes 4718600 | tf_op jit(solution)/shard_map/ppermute | solution.py:19
  159.4 26.4 %collective-permute-start.22 = (bf16[768,640]{1,0:T(8,128)(2,1)}, bf16[768,640]{1,0:T(8,128)(2,1)}, u32[]{:S(2)}, u32[]{:S(2)}) collective-permute-start(bf16[768,640]{1,0:T(8,128)(2,1)} %refs_5_.1), channel_id=1, source_target_pairs={{2,0},{4,2},{6,4},{3,1},{5,3},{7,5},{10,8},{12,10},{14,12},{11,9},... | collective-permute-start | bytes 2949128 | tf_op jit(solution)/shard_map/ppermute | solution.py:49
  163.2 46.6 %collective-permute-start.24 = (bf16[768,640]{1,0:T(8,128)(2,1)}, bf16[768,640]{1,0:T(8,128)(2,1)}, u32[]{:S(2)}, u32[]{:S(2)}) collective-permute-start(bf16[768,640]{1,0:T(8,128)(2,1)} %collective-permute-done.23), channel_id=1, source_target_pairs={{2,4},{4,6},{3,5},{5,7},{10,12},{12,14},{11,13},{13,15},{18,20},{2... | collective-permute-start | bytes 2949128 | tf_op jit(solution)/shard_map/ppermute | solution.py:48
  185.8 28.4 %collective-permute-start.26 = (bf16[768,640]{1,0:T(8,128)(2,1)}, bf16[768,640]{1,0:T(8,128)(2,1)}, u32[]{:S(2)}, u32[]{:S(2)}) collective-permute-start(bf16[768,640]{1,0:T(8,128)(2,1)} %collective-permute-done.22), channel_id=1, source_target_pairs={{2,0},{4,2},{3,1},{5,3},{10,8},{12,10},{11,9},{13,11},{18,16},{20,... | collective-permute-start | bytes 2949128 | tf_op jit(solution)/shard_map/ppermute | solution.py:49
  203.4 25.4 %all-to-all-start.2 = ((bf16[4,128,768]{2,1,0:T(8,128)(2,1)}), bf16[4,128,768]{2,1,0:T(8,128)(2,1)S(1)}, u32[]{:S(2)}, u32[]{:S(2)}) async-start(bf16[4,128,768]{2,1,0:T(8,128)(2,1)} %attend.1), calls=%async_computation.2 | async-start | bytes 1572864 | tf_op jit(solution)/shard_map/all_to_all | solution.py:414
  212.7 47.8 %collective-permute-start = (bf16[128,5120]{1,0:T(8,128)(2,1)}, bf16[128,5120]{1,0:T(8,128)(2,1)}, u32[]{:S(2)}, u32[]{:S(2)}) collective-permute-start(bf16[128,5120]{1,0:T(8,128)(2,1)} %fusion.3), channel_id=1, source_target_pairs={{0,8},{8,0},{16,24},{24,16},{1,9},{9,1},{17,25},{25,17},{2,10},{10... | collective-permute-start | bytes 3932168 | tf_op jit(solution)/shard_map/ppermute | solution.py:19
  214.2 30.6 %collective-permute-start.27 = (bf16[768,640]{1,0:T(8,128)(2,1)}, bf16[768,640]{1,0:T(8,128)(2,1)}, u32[]{:S(2)}, u32[]{:S(2)}) collective-permute-start(bf16[768,640]{1,0:T(8,128)(2,1)} %collective-permute-done.26), channel_id=1, source_target_pairs={{2,0},{3,1},{10,8},{11,9},{18,16},{19,17},{26,24},{27,25}} | collective-permute-start | bytes 2949128 | tf_op jit(solution)/shard_map/ppermute | solution.py:49
  215.7 43.3 %collective-permute-start.28 = (bf16[768,640]{1,0:T(8,128)(2,1)}, bf16[768,640]{1,0:T(8,128)(2,1)}, u32[]{:S(2)}, u32[]{:S(2)}) collective-permute-start(bf16[768,640]{1,0:T(8,128)(2,1)} %refs_5_.1), channel_id=1, source_target_pairs={{0,1},{1,0},{2,3},{3,2},{4,5},{5,4},{6,7},{7,6},{8,9},{9,8},{10,11... | collective-permute-start | bytes 2949128 | tf_op jit(solution)/shard_map/ppermute | solution.py:19
  228.8 30.1 %collective-permute-start.18 = (bf16[4,128,768]{2,1,0:T(8,128)(2,1)S(1)}, bf16[4,128,768]{2,1,0:T(8,128)(2,1)S(1)}, u32[]{:S(2)}, u32[]{:S(2)}) collective-permute-start(bf16[4,128,768]{2,1,0:T(8,128)(2,1)S(1)} %all-to-all-done.2.refs_0_), channel_id=1, source_target_pairs={{0,8},{8,0},{16,24},{24,16},{1,9},{9,1},{17,25},{25,17},{2,10},{10... | collective-permute-start | bytes 2359304 | tf_op jit(solution)/shard_map/ppermute | solution.py:19
  264.0 50.8 %collective-permute-start.1 = (bf16[128,5120]{1,0:T(8,128)(2,1)}, bf16[128,5120]{1,0:T(8,128)(2,1)}, u32[]{:S(2)}, u32[]{:S(2)}) collective-permute-start(bf16[128,5120]{1,0:T(8,128)(2,1)} %fusion.2), channel_id=1, source_target_pairs={{0,16},{8,24},{16,0},{24,8},{1,17},{9,25},{17,1},{25,9},{2,18},{10... | collective-permute-start | bytes 3932168 | tf_op jit(solution)/shard_map/ppermute | solution.py:19
  285.1 43.0 %all-to-all-start.3 = ((bf16[4,2,128,1280]{3,2,1,0:T(8,128)(2,1)}), bf16[4,2,128,1280]{3,2,1,0:T(8,128)(2,1)}, u32[]{:S(2)}, u32[]{:S(2)}) async-start(bf16[4,2,128,1280]{3,2,1,0:T(8,128)(2,1)} %project_out.1), calls=%async_computation.3 | async-start | bytes 5242880 | tf_op jit(solution)/shard_map/all_to_all | solution.py:423
  (39 other events, 523.6 us)
Sparse Core Ops, SparseCore 0:
  9.9 69.9 all-gather.4
  81.7 51.3 all-gather.2

commit v4 on v3

v4 whole, which is shorter than its diff:
```python
import functools
import math

import jax
import jax.numpy as jnp
from jax import lax
from jax.experimental import pallas as pl
from jax.experimental.pallas import tpu as pltpu
from jax.sharding import PartitionSpec as P

HD = 128
MIB = 1 << 20
SMEM = pl.BlockSpec(memory_space=pltpu.SMEM)
VMEM = pl.BlockSpec(memory_space=pltpu.VMEM)
ANY = pl.BlockSpec(memory_space=pl.ANY)


def swap(x, axis, offset):
    return lax.ppermute(x, axis, [(i, i ^ offset) for i in range(lax.axis_size(axis))])


def bits_of(axis):
    return [1 << bit for bit in range(lax.axis_size(axis).bit_length() - 1)]


def direct(x):
    return {bit: [swap(x, "step", bit)] for bit in bits_of("step")}


def forwarded(x, near, turn=None):
    held = {0: [x], **near}
    half = x.shape[0] // 2
    for offset in range(1, lax.axis_size("step")):
        low, high = offset & -offset, 1 << (offset.bit_length() - 1)
        if offset in held:
            continue
        if turn is not None:
            last = (low, high)[turn]
            held[offset] = [swap(held[offset ^ last][0], "step", last)]
            continue
        top, bottom = held[offset ^ low], held[offset ^ high]
        top = top[0][:half] if len(top) == 1 else top[0]
        bottom = bottom[0][half:] if len(bottom) == 1 else bottom[1]
        held[offset] = [swap(top, "step", low), swap(bottom, "step", high)]
    return [held[offset] for offset in range(lax.axis_size("step"))]


def listed(held):
    return [piece for pieces in (held.values() if isinstance(held, dict) else held) for piece in pieces]


def after(x, *others):
    return lax.optimization_barrier((x,) + others)[0]


def along_line(x, awaited=()):
    size = lax.axis_size("head")
    below, above = [x], [x]
    for hop in range(1, size):
        up, down = below[-1], above[-1]
        if 0 <= hop - 2 < len(awaited):
            up, down = after((up, down), *awaited[hop - 2])
        below.append(lax.ppermute(up, "head", [(i, i + 1) for i in range(hop - 1, size - 1)]))
        above.append(lax.ppermute(down, "head", [(i, i - 1) for i in range(1, size - hop + 1)]))
    return below, above


def params(mib=56):
    return pltpu.CompilerParams(vmem_limit_bytes=mib * MIB)


def cost(flops, moved, raised=0):
    return pl.CostEstimate(flops=int(flops) // 4, bytes_accessed=int(moved) // 4, transcendentals=int(raised) // 4)


def modulate_kernel(steps, place, states, rows, mine, other):
    current = states[...]
    centre = jnp.mean(current, axis=-1, keepdims=True)
    centred = current - centre
    spread_of = jnp.mean(centred * centred, axis=-1, keepdims=True)
    shift, scale = rows[0:1, :], rows[1:2, :]
    modulated = (centred * lax.rsqrt(spread_of + 1e-06) * (1.0 + scale) + shift).astype(jnp.bfloat16)
    core = place[1]
    for block in range(2 * steps):
        width = modulated.shape[1] // (2 * steps)
        piece = modulated[:, block * width : (block + 1) * width]
        at = slice(block // 2 * width, (block // 2 + 1) * width)

        @pl.when(core == block % 2)
        def _(piece=piece, at=at):
            mine[:, at] = piece

        @pl.when(core != block % 2)
        def _(piece=piece, at=at):
            other[:, at] = piece


def modulate(place, states, rows, steps):
    tokens, width = states.shape
    tile = 32
    out = jax.ShapeDtypeStruct((tokens, width // 2), jnp.bfloat16)
    spec = pl.BlockSpec((tile, width // 2), lambda i: (i, 0))
    return pl.pallas_call(
        functools.partial(modulate_kernel, steps),
        grid=(tokens // tile,),
        in_specs=[SMEM, pl.BlockSpec((tile, width), lambda i: (i, 0)), pl.BlockSpec(rows.shape, lambda i: (0, 0))],
        out_specs=[spec, spec],
        out_shape=[out, out],
        compiler_params=params(),
        cost_estimate=cost(10 * tokens * width, 6 * tokens * width),
        name="modulate",
    )(place, states, rows)


def project_kernel(size, parts, layouts, place, *refs):
    count = 2 * size - 1
    own, below, above = refs[0], refs[1:size], refs[size:count]
    weights = []
    for layout in layouts:
        weights.append(refs[count : count + len(layout)])
        count += len(layout)
    outs = refs[count : count + 2 * len(layouts)]
    x_held, w_held, x_sems, w_sems = refs[count + 2 * len(layouts) :]
    tokens, depth = own.shape[1:]
    step_at, position, shift = place[0], place[2], place[4]
    early = size - 1
    blocks = {"first": range(early), "last": range(early, size), "all": range(size)}[parts]

    def x_copy(ref, clip, block):
        row = (clip * len(blocks) + block - blocks[0]) * tokens
        return pltpu.make_async_copy(
            ref.at[clip], x_held.at[pl.ds(pl.multiple_of(row, tokens), tokens)], x_sems.at[clip, block]
        )

    def w_copies(which):
        for index, (ref, (offset, whole, start, rows)) in enumerate(zip(weights[which], layouts[which])):
            at = jnp.bitwise_xor(step_at, offset) * whole + start
            target = w_held.at[which, pl.ds(pl.multiple_of(at, rows), rows)]
            yield pltpu.make_async_copy(ref, target, w_sems.at[which, index])

    for which in range(len(layouts)):
        for copy in w_copies(which):
            copy.start()
        if which:
            continue
        for clip in range(2):
            for away in range(size):
                for sign, held in ((1, above), (-1, below)):
                    if away == 0 and sign < 0:
                        continue
                    source = own if away == 0 else held[away - 1]
                    block_at = position + sign * away
                    block = lax.rem(block_at - shift + size, size)
                    inside = jnp.logical_and(block_at >= 0, block_at < size)
                    inside = jnp.logical_and(inside, jnp.logical_and(block >= blocks[0], block <= blocks[-1]))

                    @pl.when(inside)
                    def _(source=source, block=block, clip=clip):
                        x_copy(source, clip, block).start()

    rows = outs[0].shape[0]
    for clip in range(2):
        for block in blocks:
            x_copy(own, clip, block).wait()
    for which in range(len(layouts)):
        for copy in w_copies(which):
            copy.wait()
        for clip in range(2):
            span = slice(clip * rows, (clip + 1) * rows)
            outs[2 * which + clip][...] = jnp.dot(x_held[span], w_held[which], preferred_element_type=jnp.float32)


def project(place, line, all_shards, parts, name):
    size = lax.axis_size("head")
    below, above = line
    operands = [below[0]] + below[1:] + above[1:]
    _, tokens, depth = operands[0].shape
    layouts, weights = [], []
    for shards in all_shards:
        layout = []
        for offset, pieces in enumerate(shards):
            start = 0
            for piece in pieces:
                layout.append((offset, depth // len(shards), start, piece.shape[0]))
                weights.append(piece)
                start += piece.shape[0]
        layouts.append(tuple(layout))
    sets = len(layouts)
    columns = weights[0].shape[1]
    rows = {"first": size - 1, "last": 1, "all": size}[parts] * tokens
    out = jax.ShapeDtypeStruct((rows, columns), jnp.float32)
    moved = 2 * depth * (2 * rows + sets * columns) + 8 * sets * rows * columns
    outs = pl.pallas_call(
        functools.partial(project_kernel, size, parts, tuple(layouts)),
        in_specs=[SMEM] + [ANY] * (len(operands) + len(weights)),
        out_specs=[VMEM] * (2 * sets),
        out_shape=[out] * (2 * sets),
        scratch_shapes=[
            pltpu.VMEM((2 * rows, depth), jnp.bfloat16),
            pltpu.VMEM((sets, depth, columns), jnp.bfloat16),
            pltpu.SemaphoreType.DMA((2, size)),
            pltpu.SemaphoreType.DMA((sets, max(len(layout) for layout in layouts))),
        ],
        compiler_params=params(),
        cost_estimate=cost(4 * rows * sets * depth * columns, moved),
        name=name,
    )(place, *operands, *weights)
    return [[outs[2 * which], swap(outs[2 * which + 1], "fsdp", 1)] for which in range(sets)]


def norms_kernel(place, *refs):
    parts, out = refs[:8], refs[8]
    tokens = parts[2].shape[0]
    rows = []
    for at in (0, 4):
        found = []
        for part in (at + 2, at, at + 2):
            total = parts[part][...] + parts[part + 1][...]
            total = total * total
            lanes = total[:, :HD]
            for group in range(1, total.shape[1] // HD):
                lanes = lanes + total[:, group * HD : (group + 1) * HD]
            found.append(jnp.sum(lanes.T, axis=0, keepdims=True))
        wrapped = jnp.concatenate(found[:2], axis=1)
        straight = jnp.concatenate(found[1:], axis=1)
        rows.append(jnp.where(place[4] == 0, straight, wrapped))
    both = jnp.concatenate(rows, axis=0)
    for peer in range(out.shape[0]):
        out[peer] = both


def norms(place, q_parts, k_parts, size):
    rows = q_parts[0].shape[0] + q_parts[2].shape[0]
    operands = q_parts + k_parts
    return pl.pallas_call(
        norms_kernel,
        in_specs=[SMEM] + [VMEM] * 8,
        out_specs=VMEM,
        out_shape=jax.ShapeDtypeStruct((size, 2, rows), jnp.float32),
        compiler_params=params(),
        cost_estimate=cost(8 * rows * q_parts[0].shape[1], 16 * rows * q_parts[0].shape[1]),
        name="norms",
    )(place, *operands)


def probs_kernel(tokens, full_width, place, squares, *refs):
    parts, (q_gain, k_gain, out, scales) = refs[:8], refs[8:]
    rows = scales.shape[1]

    @pl.when(pl.program_id(0) == 0)
    def _():
        total = squares[0]
        for peer in range(1, squares.shape[0]):
            total = total + squares[peer]
        turned = jnp.concatenate([total[:, tokens:], total[:, :tokens]], axis=1)
        total = jnp.where(place[4] == 0, total, turned)
        scale = lax.rsqrt(total / full_width + 1e-06)
        for which in range(2):
            scales[which] = jnp.broadcast_to(scale[which : which + 1], (HD, rows)).T

    column = lax.broadcasted_iota(jnp.int32, (1, rows), 1) + place[4] * tokens
    valid = jnp.where(column >= rows, column - rows, column) < place[3]
    for head in range(out.shape[0]):
        span = slice(head * HD, (head + 1) * HD)

        def normed(at, gain, which):
            joined = [parts[at + i][:, span] + parts[at + i + 1][:, span] for i in (0, 2)]
            return (jnp.concatenate(joined) * scales[which] * gain[:, span]).astype(jnp.bfloat16)

        queries, keys = normed(0, q_gain, 0), normed(4, k_gain, 1)
        scores = lax.dot_general(queries, keys, (((1,), (1,)), ((), ())), preferred_element_type=jnp.float32)
        scores = jnp.where(valid, scores * (1.0 / math.sqrt(HD)), -jnp.inf)
        raised = jnp.exp(scores - jnp.max(scores, axis=-1, keepdims=True))
        out[head] = (raised * (1.0 / jnp.sum(raised, axis=-1, keepdims=True))).astype(jnp.bfloat16)


def at_once(heads):
    return 2 if heads % 2 == 0 else 1


def probabilities(place, squares, q_parts, k_parts, q_gain, k_gain):
    columns = q_parts[0].shape[1]
    rows = q_parts[0].shape[0] + q_parts[2].shape[0]
    heads = columns // HD
    group = at_once(heads)
    by_head = [pl.BlockSpec((part.shape[0], group * HD), lambda i: (0, i)) for part in q_parts + k_parts]
    gain = pl.BlockSpec((1, group * HD), lambda i: (0, i))
    return pl.pallas_call(
        functools.partial(probs_kernel, q_parts[2].shape[0], float(columns * squares.shape[0])),
        grid=(heads // group,),
        in_specs=[SMEM, pl.BlockSpec(squares.shape, lambda i: (0, 0, 0))] + by_head + [gain] * 2,
        out_specs=pl.BlockSpec((group, rows, rows), lambda i: (i, 0, 0)),
        out_shape=jax.ShapeDtypeStruct((heads, rows, rows), jnp.bfloat16),
        scratch_shapes=[pltpu.VMEM((2, rows, HD), jnp.float32)],
        compiler_params=params(),
        cost_estimate=cost(2 * heads * rows * rows * HD, 16 * rows * columns + 2 * heads * rows * rows, heads * rows * rows),
        name="probs",
    )(place, squares, *q_parts, *k_parts, q_gain[None], k_gain[None])


def attend_kernel(place, probs, v_a, v_b, out, held):
    size, tokens, _ = out.shape
    for head in range(probs.shape[0]):
        span = slice(head * HD, (head + 1) * HD)
        values = (v_a[:, span] + v_b[:, span]).astype(jnp.bfloat16)
        held[:, span] = jnp.dot(probs[head], values, preferred_element_type=jnp.float32)
    for block in range(size):
        at = lax.rem(block - place[4] + size, size) * tokens
        out[block] = held[pl.ds(pl.multiple_of(at, tokens), tokens)].astype(jnp.bfloat16)


def attend(place, probs, v_parts, size):
    heads, rows, _ = probs.shape
    tokens = rows // size
    group = at_once(heads)
    by_head = pl.BlockSpec((rows, group * HD), lambda i: (0, i))
    return pl.pallas_call(
        attend_kernel,
        grid=(heads // group,),
        in_specs=[SMEM, pl.BlockSpec((group, rows, rows), lambda i: (i, 0, 0)), by_head, by_head],
        out_specs=pl.BlockSpec((size, tokens, group * HD), lambda i: (0, 0, i)),
        out_shape=jax.ShapeDtypeStruct((size, tokens, heads * HD), jnp.bfloat16),
        scratch_shapes=[pltpu.VMEM((rows, group * HD), jnp.float32)],
        compiler_params=params(),
        cost_estimate=cost(2 * heads * rows * rows * HD, 2 * heads * rows * rows + 10 * rows * heads * HD),
        name="attend",
    )(place, probs, *v_parts)


def out_kernel(size, layout, place, widths, *refs):
    pieces, weights = refs[: len(layout)], refs[len(layout) : len(layout) + 2 * size]
    gates, out, a_held, w_held, total, a_sems, w_sems = refs[len(layout) + 2 * size :]
    steps, _, tokens, columns = out.shape
    width = columns // 2
    halves, _, _, span_width = w_held.shape
    joined = halves == 1
    step_at, core, position = place[0], place[1], place[2]

    def a_copies():
        for index, (offset, start, count) in enumerate(layout):
            row = pl.multiple_of(jnp.bitwise_xor(step_at, offset) * tokens, tokens)
            for group in range(count):
                yield pltpu.make_async_copy(
                    pieces[index].at[group], a_held.at[start + group, pl.ds(row, tokens)], a_sems.at[index, group]
                )

    def w_copy(half, away):
        group = lax.rem(position + away, size)
        at = jnp.bitwise_xor(core, half)
        if joined:
            span = pl.ds(pl.multiple_of(at * width, 128), width)
            target = w_held.at[0, group, :, span]
        else:
            target = w_held.at[at, group]
        return pltpu.make_async_copy(weights[half * size + away], target, w_sems.at[half, away])

    for copy in a_copies():
        copy.start()
    for away in range(size):
        for half in range(2):
            w_copy(half, away).start()
    for copy in a_copies():
        copy.wait()
    for away in range(size):
        group = lax.rem(position + away, size)
        for half in range(2):
            w_copy(half, away).wait()
        for half in range(halves):
            part = jnp.dot(a_held[group], w_held[half, group], preferred_element_type=jnp.float32)
            part = part.astype(jnp.bfloat16).astype(jnp.float32)
            if away == 0:
                total[half] = part
            else:
                total[half] += part
    for half in range(halves):
        span = slice(half * span_width, (half + 1) * span_width)
        reached = None
        for step in range(steps):
            told = jnp.bitwise_xor(step_at, step)
            branch = total[half, step * tokens : (step + 1) * tokens] * gates[pl.ds(told, 1), span]
            out[step, 0, :, span] = branch.astype(jnp.bfloat16)
            drift = branch * widths[told]
            reached = drift if step == 0 else reached + drift
            out[step, 1, :, span] = reached.astype(jnp.bfloat16)


def project_out(place, widths, gathered, weights, gates):
    size = lax.axis_size("head")
    steps = len(gathered)
    _, tokens, inner = gathered[0][0].shape
    width = weights[0][0].shape[1]
    layout, pieces = [], []
    for offset, held in enumerate(gathered):
        start = 0
        for piece in held:
            layout.append((offset, start, piece.shape[0]))
            pieces.append(piece)
            start += piece.shape[0]
    rows = steps * tokens
    halves = 1 if width % 128 == 0 else 2
    operands = pieces + [w for half in weights for w in half]
    return pl.pallas_call(
        functools.partial(out_kernel, size, tuple(layout)),
        in_specs=[SMEM, SMEM] + [ANY] * len(operands) + [VMEM],
        out_specs=VMEM,
        out_shape=jax.ShapeDtypeStruct((steps, 2, tokens, 2 * width), jnp.bfloat16),
        scratch_shapes=[
            pltpu.VMEM((size, rows, inner), jnp.bfloat16),
            pltpu.VMEM((halves, size, inner, 2 * width // halves), jnp.bfloat16),
            pltpu.VMEM((halves, rows, 2 * width // halves), jnp.float32),
            pltpu.SemaphoreType.DMA((len(layout), size)),
            pltpu.SemaphoreType.DMA((2, size)),
        ],
        compiler_params=params(),
        cost_estimate=cost(4 * rows * size * inner * width, 2 * size * inner * (rows + 2 * width) + 8 * rows * width),
        name="project_out",
    )(place, widths, *operands, gates)


def finish_kernel(base, arrived, reached, update):
    reached[...] = base[...] + arrived[0, 1].astype(jnp.float32)
    update[...] = arrived[0, 0]


def finish(base, arrived):
    steps, _, tokens, width = arrived.shape
    by_columns = pl.BlockSpec((tokens, width), lambda i: (0, i))
    return pl.pallas_call(
        finish_kernel,
        grid=(steps,),
        in_specs=[by_columns, pl.BlockSpec((1, 2, tokens, width), lambda i: (i, 0, 0, 0))],
        out_specs=[by_columns, by_columns],
        out_shape=[jax.ShapeDtypeStruct(base.shape, jnp.float32), jax.ShapeDtypeStruct(base.shape, jnp.bfloat16)],
        compiler_params=params(),
        cost_estimate=cost(base.size, 14 * base.size),
        name="finish",
    )(base, arrived)


def body(states, timesteps, lengths, modulation, w_query, w_key, w_value, w_out, q_gain, k_gain):
    steps, size = lax.axis_size("step"), lax.axis_size("head")
    step, core, position = (lax.axis_index(axis) for axis in ("step", "fsdp", "head"))
    current = states[0, 0]
    shift = (position >= size // 2).astype(jnp.int32)
    place = jnp.stack([step, core, position, lengths[0], shift]).astype(jnp.int32)

    q_near = direct(w_query)
    k_near = direct(after(w_key, *listed(q_near)))
    q_near = dict(zip(q_near, [[piece] for piece in after(tuple(listed(q_near)), *listed(k_near))]))
    q_shards = forwarded(w_query, q_near, 0)
    k_shards = forwarded(w_key, k_near, 1)
    v_near = direct(after(w_value, *listed(q_shards), *listed(k_shards)))
    v_shards = forwarded(w_value, v_near)

    mine, other = modulate(place, current, modulation[0], steps)
    line = along_line(jnp.stack([mine, swap(other, "fsdp", 1)]), (listed(q_near), listed(k_near)))
    early = tuple(held[: size - 1] + [held[0]] for held in line)

    q_parts, k_parts = project(place, early, (q_shards, k_shards), "first", "first")
    below, above = along_line(after(w_out, line[0][-1], line[1][-1], q_parts[0], k_parts[0]))
    q_last, k_last = project(place, line, (q_shards, k_shards), "last", "last")
    q_parts, k_parts = q_parts + q_last, k_parts + k_last
    own_squares = norms(place, q_parts, k_parts, size)
    squares = lax.all_to_all(own_squares, "head", 0, 0)
    (v_parts,) = project(after(place, own_squares), line, (v_shards,), "all", "value")
    squares = after(squares, v_parts[0], below[1], above[1])
    probs = probabilities(place, squares, q_parts, k_parts, q_gain, k_gain)

    step_width = (timesteps[0, 1] - timesteps[0, 0]).astype(jnp.float32) / 1000.0
    carried = step_width * current + jnp.where(step == 0, current, jnp.zeros_like(current))
    base, total = carried, carried
    swapped = []
    for bit in bits_of("step"):
        swapped.append(swap(after(total.astype(jnp.bfloat16), *listed(v_shards)), "step", bit))
        brought = swapped[-1].astype(jnp.float32)
        base = base + jnp.where(jnp.bitwise_and(step, bit) != 0, brought, jnp.zeros_like(brought))
        total = total + brought

    columns = current.shape[1] // steps
    told = jnp.concatenate([modulation[0, 2], jnp.full((HD,), step_width)])[None]
    sent_told = after(told, probs)
    heard = jnp.concatenate([told] + [swap(sent_told, "step", offset) for offset in range(1, steps)])
    gates = lax.dynamic_slice(heard, (0, step * columns), (steps, columns))

    attended = attend(place, after(probs, swapped[0]), v_parts, size)
    quarter = after(lax.all_to_all(attended, "head", 0, 0), swapped[-1], below[2], above[2])
    gathered = forwarded(quarter, direct(quarter))

    own_columns = [w_out] + [
        jnp.where(position + away < size, above[away], below[size - away]) for away in range(1, size)
    ]
    out_weights = (own_columns, [swap(w, "fsdp", 1) for w in own_columns])

    sent = project_out(place, heard[:, -1], gathered, out_weights, gates)
    arrived = lax.all_to_all(sent, "step", 0, 0)
    reached, update = finish(base, arrived)
    return reached[None, None], update[None, None]


def solution(mesh):
    in_specs = (
        P("step", "fsdp", "head", None),
        P("step", None),
        P("fsdp"),
        P("step", None, None),
        P(("step", "fsdp"), "head"),
        P(("step", "fsdp"), "head"),
        P(("step", "fsdp"), "head"),
        P("head", ("step", "fsdp")),
        P("head"),
        P("head"),
    )
    out_specs = (P("step", "fsdp", "head", None), P("step", "fsdp", "head", None))
    return jax.shard_map(body, mesh=mesh, in_specs=in_specs, out_specs=out_specs, check_vma=False)
```

time: 342 us -> 358 us (1.047)
  waiting for transfers between devices: 130 us -> 206 us
  blocking collectives: 35.2 us -> 0 us
  between operations: 16.6 us -> 3.16 us
  Pallas kernels: 76.8 us -> 65.6 us
  starting transfers between devices: 52.7 us -> 58.5 us
  other arithmetic: 17.7 us -> 12.3 us
    all_to_all x1 -> x0, blocking collectives: 35.2 us -> none  [body(): heard = lax.all_to_all(told, 'step', 0, 0)]
    ppermute x6, waiting for transfers between devices: 47.4 us -> 77.9 us  [along_line(): lax.ppermute(down, 'head', [(i, i - 1) for i in range(1, size - hop + 1)])]
    ppermute x20 -> x29, waiting for transfers between devices: 59.1 us -> 86.1 us  [swap(): lax.ppermute(x, axis, [(i, i ^ offset) for i in range(lax.axis_size(axis))])]
    all_to_all x1, waiting for transfers between devices: 9.36 us -> 26.3 us  [body(): arrived = lax.all_to_all(sent, 'step', 0, 0)]
    pallas_call x5 -> x3, Pallas kernels: 41.2 us -> 28.5 us  [project(): pl.pallas_call(functools.partial(project_kernel, size, parts, tuple(layou...]
    ppermute x20 -> x29, starting transfers between devices: 14.3 us -> 24.5 us  [swap(): lax.ppermute(x, axis, [(i, i ^ offset) for i in range(lax.axis_size(axis))])]
    reduce_sum x5 -> x0, other arithmetic: 3.92 us -> none  [the longest x4 3.91 us: squares_of(): jnp.sum(jnp.square(parts[i] + parts[i + 1]), axis=1)]
    unnamed x54 -> x77, local copies, waits for them, and re-layouts: 2.14 us -> 5.8 us
  transfers between devices with their start and end apart: 37 -> 44, of which waited for: 14 -> 20; matrix products, arithmetic and copies ran while one was open for 8% -> 5% of each run, Pallas kernels for 21% -> 14%
where the time goes in v4:
time: 358 us; the launch traced here: 357 us
  waiting for transfers between devices  206 us (58%)
  Pallas kernels  65.6 us (18%)
  starting transfers between devices  58.5 us (16%)
  other arithmetic  12.3 us (3%)
  local copies, waits for them, and re-layouts  11.5 us (3%)
    ppermute x29, waiting for transfers between devices, swap(): lax.ppermute(x, axis, [(i, i ^ offset) for i in range(lax.axis_size(axis))])  86.1 us
    ppermute x6, waiting for transfers between devices, along_line(): lax.ppermute(down, 'head', [(i, i - 1) for i in range(1, size - hop + 1)])  77.9 us
    pallas_call x3, Pallas kernels, project(): pl.pallas_call(functools.partial(project_kernel, size, parts, tuple(layou...  28.5 us
    all_to_all x1, waiting for transfers between devices, body(): arrived = lax.all_to_all(sent, 'step', 0, 0)  26.3 us
    ppermute x29, starting transfers between devices, swap(): lax.ppermute(x, axis, [(i, i ^ offset) for i in range(lax.axis_size(axis))])  24.5 us
    all_to_all x1, waiting for transfers between devices, body(): squares = lax.all_to_all(own_squares, 'head', 0, 0)  15.7 us
    ppermute x6, starting transfers between devices, along_line(): lax.ppermute(up, 'head', [(i, i + 1) for i in range(hop - 1, size - 1)])  11.8 us
    pallas_call x1, Pallas kernels, project_out(): pl.pallas_call(functools.partial(out_kernel, size, tuple(layout)), in_spe...  11.8 us
  transfers between devices with their start and end apart: 44, of which 20 were waited for; matrix products, arithmetic and copies ran while one was open for 5% of the time, Pallas kernels for 14%

profile of v4, /device:TPU:0, one launch (start us, length us, event | category | flops | bytes accessed | tf_op | source)
XLA Modules:
  0.0 357.1 jit_solution(1956989961260263334)
XLA Ops:
  7.9 4.6 %modulate.1 = (bf16[128,2560]{1,0:T(8,128)(2,1)}, bf16[128,2560]{1,0:T(8,128)(2,1)}) custom-call(s32[5]{0:T(128)} %stack.32.place, f32[128,5120]{1,0:T(8,128)} %bitcast.17, f32[3,5120]{1,0:T(4,128)} %bitcast.20), custom_call_target="tpu_custom_call" | custom-call | flops 1638400 | bytes 983040 | tf_op jit(solution)/shard_map/modulate/pallas_call | solution.py:103
  12.5 13.1 %collective-permute-done.refs_8_ = bf16[640,768]{1,0:T(8,128)(2,1)S(1)} collective-permute-done((bf16[640,768]{1,0:T(8,128)(2,1)}, bf16[640,768]{1,0:T(8,128)(2,1)S(1)}, u32[]{:S(2)}, u32[]{:S(2)}) %collective-permute-start) | collective-permute-done | bytes 983072 | tf_op jit(solution)/shard_map/ppermute | solution.py:19
  35.3 14.3 %collective-permute-done.2.refs_12_ = bf16[640,768]{1,0:T(8,128)(2,1)S(1)} collective-permute-done((bf16[640,768]{1,0:T(8,128)(2,1)}, bf16[640,768]{1,0:T(8,128)(2,1)S(1)}, u32[]{:S(2)}, u32[]{:S(2)}) %collective-permute-start.2) | collective-permute-done | bytes 983072 | tf_op jit(solution)/shard_map/ppermute | solution.py:19
  52.8 18.7 %collective-permute-done.4.refs_10_ = bf16[640,768]{1,0:T(8,128)(2,1)S(1)} collective-permute-done((bf16[640,768]{1,0:T(8,128)(2,1)S(1)}, bf16[640,768]{1,0:T(8,128)(2,1)S(1)}, u32[]{:S(2)}, u32[]{:S(2)}) %collective-permute-start.4) | collective-permute-done | bytes 983072 | tf_op jit(solution)/shard_map/ppermute | solution.py:19
  78.3 15.0 %collective-permute-done.7.refs_9_ = bf16[640,768]{1,0:T(8,128)(2,1)S(1)} collective-permute-done((bf16[640,768]{1,0:T(8,128)(2,1)}, bf16[640,768]{1,0:T(8,128)(2,1)S(1)}, u32[]{:S(2)}, u32[]{:S(2)}) %collective-permute-start.7) | collective-permute-done | bytes 983072 | tf_op jit(solution)/shard_map/ppermute | solution.py:19
  98.0 8.8 %collective-permute-done.16.refs_5_ = bf16[2,128,2560]{2,1,0:T(8,128)(2,1)} collective-permute-done((bf16[2,128,2560]{2,1,0:T(8,128)(2,1)}, bf16[2,128,2560]{2,1,0:T(8,128)(2,1)}, u32[]{:S(2)}, u32[]{:S(2)}) %collective-permute-start.16) | collective-permute-done | bytes 1310752 | tf_op jit(solution)/shard_map/ppermute | solution.py:64
  106.9 11.7 %first.1 = (f32[384,768]{1,0:T(8,128)}, f32[384,768]{1,0:T(8,128)}, f32[384,768]{1,0:T(8,128)}, f32[384,768]{1,0:T(8,128)}) custom-call(s32[5]{0:T(128)} %stack.32.place, bf16[2,128,2560]{2,1,0:T(8,128)(2,1)} %copy-done, bf16[2,128,2560]{2,1,0:T(8,128)(2,1)} %copy-done.3, bf16[2,128,2560]{2,1,0:T(8,128)(2,1)} %collective-permute-done.15.refs_2_, ...), custom_call_target="tpu_custom_call" | custom-call | flops 1509949440 | bytes 4128768 | tf_op jit(solution)/shard_map/first/pallas_call | solution.py:193
  124.3 11.4 %collective-permute-done.9.refs_11_ = bf16[320,768]{1,0:T(8,128)(2,1)} collective-permute-done((bf16[320,768]{1,0:T(8,128)(2,1)S(1)}, bf16[320,768]{1,0:T(8,128)(2,1)}, u32[]{:S(2)}, u32[]{:S(2)}) %collective-permute-start.9) | collective-permute-done | bytes 491552 | tf_op jit(solution)/shard_map/ppermute | solution.py:19
  136.6 16.1 %collective-permute-done.19.refs_6_ = bf16[2,128,2560]{2,1,0:T(8,128)(2,1)S(1)} collective-permute-done((bf16[2,128,2560]{2,1,0:T(8,128)(2,1)}, bf16[2,128,2560]{2,1,0:T(8,128)(2,1)S(1)}, u32[]{:S(2)}, u32[]{:S(2)}) %collective-permute-start.19) | collective-permute-done | bytes 1310752 | tf_op jit(solution)/shard_map/ppermute | solution.py:64
  155.2 7.0 %last.1 = (f32[128,768]{1,0:T(8,128)}, f32[128,768]{1,0:T(8,128)}, f32[128,768]{1,0:T(8,128)}, f32[128,768]{1,0:T(8,128)}) custom-call(s32[5]{0:T(128)} %stack.32.place, bf16[2,128,2560]{2,1,0:T(8,128)(2,1)} %copy-done, bf16[2,128,2560]{2,1,0:T(8,128)(2,1)} %copy-done.3, bf16[2,128,2560]{2,1,0:T(8,128)(2,1)} %collective-permute-done.15.refs_2_, ...), custom_call_target="tpu_custom_call" | custom-call | flops 503316480 | bytes 2686976 | tf_op jit(solution)/shard_map/last/pallas_call | solution.py:193
  169.5 9.7 %value.1 = (f32[512,768]{1,0:T(8,128)}, f32[512,768]{1,0:T(8,128)}) custom-call(s32[5]{0:T(128)} %stack.32.place, bf16[2,128,2560]{2,1,0:T(8,128)(2,1)} %copy-done, bf16[2,128,2560]{2,1,0:T(8,128)(2,1)} %copy-done.3, bf16[2,128,2560]{2,1,0:T(8,128)(2,1)} %collective-permute-done.15.refs_2_, bf16[2,128,2560]{2,1,0:T(8,128)(2,1)} %copy-done.4, ...), custom_call_target="tpu_custom_call" | custom-call | flops 1006632960 | bytes 3080192 | tf_op jit(solution)/shard_map/value/pallas_call | solution.py:193
  184.5 4.5 %all-to-all-start = ((f32[4,2,512]{2,1,0:T(2,128)}), f32[4,2,512]{2,1,0:T(2,128)S(1)}, u32[]{:S(2)}, u32[]{:S(2)}) async-start(f32[4,2,512]{2,1,0:T(2,128)} %norms.1), calls=%async_computation | async-start | bytes 32768 | tf_op jit(solution)/shard_map/all_to_all | solution.py:464
  190.2 15.7 %all-to-all-done.squares = f32[4,2,512]{2,1,0:T(2,128)S(1)} async-done(((f32[4,2,512]{2,1,0:T(2,128)}), f32[4,2,512]{2,1,0:T(2,128)S(1)}, u32[]{:S(2)}, u32[]{:S(2)}) %all-to-all-start) | async-done | bytes 16416 | tf_op jit(solution)/shard_map/all_to_all | solution.py:464
  206.5 7.0 %probs.1 = bf16[6,512,512]{2,1,0:T(8,128)(2,1)} custom-call(s32[5]{0:T(128)} %stack.32.place, f32[4,2,512]{2,1,0:T(2,128)} %copy-done.34, f32[384,768]{1,0:T(8,128)} %get-tuple-element.42.refs_0_, f32[384,768]{1,0:T(8,128)} %copy-done.7, f32[128,768]{1,0:T(8,128)} %get-tuple-element.46.refs_2_, f32[128,768]{1,0:T(8,128)} %copy-done.22, ...), custom_call_target="tpu_custom_call" | custom-call | flops 100663296 | bytes 2359296 | tf_op jit(solution)/shard_map/probs/pallas_call | solution.py:288
  214.7 5.0 %attend.1 = bf16[4,128,768]{2,1,0:T(8,128)(2,1)} custom-call(s32[5]{0:T(128)} %stack.32.place, bf16[6,512,512]{2,1,0:T(8,128)(2,1)} %probs.1, f32[512,768]{1,0:T(8,128)} %get-tuple-element.53.v_a, f32[512,768]{1,0:T(8,128)} %copy-done.24), custom_call_target="tpu_custom_call" | custom-call | flops 100663296 | bytes 1769472 | tf_op jit(solution)/shard_map/attend/pallas_call | solution.py:317
  219.7 5.0 %all-to-all-start.1 = ((bf16[4,128,768]{2,1,0:T(8,128)(2,1)}), bf16[4,128,768]{2,1,0:T(8,128)(2,1)S(1)}, u32[]{:S(2)}, u32[]{:S(2)}) async-start(bf16[4,128,768]{2,1,0:T(8,128)(2,1)} %attend.1), calls=%async_computation.1 | async-start | bytes 1572864 | tf_op jit(solution)/shard_map/all_to_all | solution.py:486
  227.6 32.7 %collective-permute-done.30 = bf16[768,640]{1,0:T(8,128)(2,1)} collective-permute-done((bf16[768,640]{1,0:T(8,128)(2,1)}, bf16[768,640]{1,0:T(8,128)(2,1)}, u32[]{:S(2)}, u32[]{:S(2)}) %collective-permute-start.30) | collective-permute-done | bytes 983072 | tf_op jit(solution)/shard_map/ppermute | solution.py:64
  268.3 20.3 %collective-permute-done.36 = bf16[768,640]{1,0:T(8,128)(2,1)} collective-permute-done((bf16[768,640]{1,0:T(8,128)(2,1)}, bf16[768,640]{1,0:T(8,128)(2,1)}, u32[]{:S(2)}, u32[]{:S(2)}) %collective-permute-start.36) | collective-permute-done | bytes 983072 | tf_op jit(solution)/shard_map/ppermute | solution.py:64
  296.9 6.8 %collective-permute-done.33.refs_3_ = bf16[2,128,768]{2,1,0:T(8,128)(2,1)S(1)} collective-permute-done((bf16[2,128,768]{2,1,0:T(8,128)(2,1)S(1)}, bf16[2,128,768]{2,1,0:T(8,128)(2,1)S(1)}, u32[]{:S(2)}, u32[]{:S(2)}) %collective-permute-start.33) | collective-permute-done | bytes 393248 | tf_op jit(solution)/shard_map/ppermute | solution.py:19
  305.4 11.8 %project_out.1 = bf16[4,2,128,1280]{3,2,1,0:T(8,128)(2,1)} custom-call(s32[5]{0:T(128)} %stack.32.place, f32[4]{0:T(128)} %slice_reduce_fusion.widths, bf16[4,128,768]{2,1,0:T(8,128)(2,1)} %copy-done.18, bf16[4,128,768]{2,1,0:T(8,128)(2,1)} %copy-done.21, bf16[4,128,768]{2,1,0:T(8,128)(2,1)} %copy-done.20, bf16[2,128,768]{2,1,0:T(8,128)(2,1)} %copy-done.30, ...), custom_call_target="tpu_custom_call" | custom-call | flops 1006632960 | bytes 3407872 | tf_op jit(solution)/shard_map/project_out/pallas_call | solution.py:402
  317.1 4.8 %all-to-all-start.2 = ((bf16[4,2,128,1280]{3,2,1,0:T(8,128)(2,1)}), bf16[4,2,128,1280]{3,2,1,0:T(8,128)(2,1)}, u32[]{:S(2)}, u32[]{:S(2)}) async-start(bf16[4,2,128,1280]{3,2,1,0:T(8,128)(2,1)} %project_out.1), calls=%async_computation.2 | async-start | bytes 5242880 | tf_op jit(solution)/shard_map/all_to_all | solution.py:495
  322.0 4.0 %fusion.1.base = f32[128,5120]{1,0:T(8,128)} fusion(bf16[128,5120]{1,0:T(8,128)(2,1)} %copy-done.6, bf16[128,5120]{1,0:T(8,128)(2,1)} %copy-done.25, f32[]{:T(128)} %bitcast, pred[]{:T(512)S(6)} %ne.7, pred[]{:T(512)S(6)} %ne.6, pred[]{:T(512)S(6)} %eq.3, f32[1,1,128,5120]{3,2,1,0:T(8,128)S(1)} %copy-done.2), kind=kLoop, calls=%fused_computation.3 | loop fusion | flops 5898240 | bytes 7864327 | tf_op jit(solution)/shard_map/add | solution.py:476
  326.0 26.3 %all-to-all-done.2.arrived = bf16[4,2,128,1280]{3,2,1,0:T(8,128)(2,1)} async-done(((bf16[4,2,128,1280]{3,2,1,0:T(8,128)(2,1)}), bf16[4,2,128,1280]{3,2,1,0:T(8,128)(2,1)}, u32[]{:S(2)}, u32[]{:S(2)}) %all-to-all-start.2) | async-done | bytes 2621472 | tf_op jit(solution)/shard_map/all_to_all | solution.py:495
  352.3 4.8 %finish.1 = (f32[128,5120]{1,0:T(8,128)}, bf16[128,5120]{1,0:T(8,128)(2,1)}) custom-call(f32[128,5120]{1,0:T(8,128)} %fusion.1.base, bf16[4,2,128,1280]{3,2,1,0:T(8,128)(2,1)} %all-to-all-done.2.arrived), custom_call_target="tpu_custom_call" | custom-call | flops 163840 | bytes 2293760 | tf_op jit(solution)/shard_map/finish/pallas_call | solution.py:428
  (172 shorter events, 74.9 us)
Async XLA Ops:
  0.6 25.0 %collective-permute-start = (bf16[640,768]{1,0:T(8,128)(2,1)}, bf16[640,768]{1,0:T(8,128)(2,1)S(1)}, u32[]{:S(2)}, u32[]{:S(2)}) collective-permute-start(bf16[640,768]{1,0:T(8,128)(2,1)} %refs_7_.4), channel_id=1, source_target_pairs={{0,8},{8,0},{16,24},{24,16},{1,9},{9,1},{17,25},{25,17},{2,10},{10... | collective-permute-start | bytes 2949128 | tf_op jit(solution)/shard_map/ppermute | solution.py:19
  30.4 44.1 %collective-permute-start.13 = (bf16[2,128,2560]{2,1,0:T(8,128)(2,1)S(1)}, bf16[2,128,2560]{2,1,0:T(8,128)(2,1)S(1)}, u32[]{:S(2)}, u32[]{:S(2)}) collective-permute-start(bf16[2,128,2560]{2,1,0:T(8,128)(2,1)S(1)} %pad_maximum_fusion.refs_0_.refs_3_.refs_6_), channel_id=1, source_target_pairs={{0,2},{2,4},{4,6},{1,3},{3,5},{5,7},{8,10},{10,12},{12,14},{9,11},... | collective-permute-start | bytes 3932168 | tf_op jit(solution)/shard_map/ppermute | solution.py:63
  34.0 40.5 %collective-permute-start.14 = (bf16[2,128,2560]{2,1,0:T(8,128)(2,1)S(1)}, bf16[2,128,2560]{2,1,0:T(8,128)(2,1)}, u32[]{:S(2)}, u32[]{:S(2)}) collective-permute-start(bf16[2,128,2560]{2,1,0:T(8,128)(2,1)S(1)} %pad_maximum_fusion.refs_0_.refs_3_.refs_6_), channel_id=1, source_target_pairs={{2,0},{4,2},{6,4},{3,1},{5,3},{7,5},{10,8},{12,10},{14,12},{11,9},... | collective-permute-start | bytes 3932168 | tf_op jit(solution)/shard_map/ppermute | solution.py:64
  76.3 30.6 %collective-permute-start.16 = (bf16[2,128,2560]{2,1,0:T(8,128)(2,1)}, bf16[2,128,2560]{2,1,0:T(8,128)(2,1)}, u32[]{:S(2)}, u32[]{:S(2)}) collective-permute-start(bf16[2,128,2560]{2,1,0:T(8,128)(2,1)} %collective-permute-done.14.refs_4_), channel_id=1, source_target_pairs={{2,0},{4,2},{3,1},{5,3},{10,8},{12,10},{11,9},{13,11},{18,16},{20,... | collective-permute-start | bytes 3932168 | tf_op jit(solution)/shard_map/ppermute | solution.py:64
  77.6 43.1 %collective-permute-start.6 = (bf16[640,768]{1,0:T(8,128)(2,1)}, bf16[640,768]{1,0:T(8,128)(2,1)}, u32[]{:S(2)}, u32[]{:S(2)}) collective-permute-start(bf16[640,768]{1,0:T(8,128)(2,1)} %refs_7_.5), channel_id=1, source_target_pairs={{0,8},{8,0},{16,24},{24,16},{1,9},{9,1},{17,25},{25,17},{2,10},{10... | collective-permute-start | bytes 2949128 | tf_op jit(solution)/shard_map/ppermute | solution.py:19
  95.1 27.3 %collective-permute-start.8 = (bf16[320,768]{1,0:T(8,128)(2,1)}, bf16[320,768]{1,0:T(8,128)(2,1)S(1)}, u32[]{:S(2)}, u32[]{:S(2)}) collective-permute-start(bf16[320,768]{1,0:T(8,128)(2,1)} %slice.32), channel_id=1, source_target_pairs={{0,8},{8,0},{16,24},{24,16},{1,9},{9,1},{17,25},{25,17},{2,10},{10... | collective-permute-start | bytes 1474568 | tf_op jit(solution)/shard_map/ppermute | solution.py:19
  118.6 43.7 %collective-permute-start.17 = (f32[384,768]{1,0:T(8,128)}, f32[384,768]{1,0:T(8,128)S(1)}, u32[]{:S(2)}, u32[]{:S(2)}) collective-permute-start(f32[384,768]{1,0:T(8,128)} %get-tuple-element.43), channel_id=1, source_target_pairs={{0,1},{1,0},{2,3},{3,2},{4,5},{5,4},{6,7},{7,6},{8,9},{9,8},{10,11... | collective-permute-start | bytes 3538952 | tf_op jit(solution)/shard_map/ppermute | solution.py:19
  119.4 33.3 %collective-permute-start.19 = (bf16[2,128,2560]{2,1,0:T(8,128)(2,1)}, bf16[2,128,2560]{2,1,0:T(8,128)(2,1)S(1)}, u32[]{:S(2)}, u32[]{:S(2)}) collective-permute-start(bf16[2,128,2560]{2,1,0:T(8,128)(2,1)} %collective-permute-done.16.refs_5_), channel_id=1, source_target_pairs={{2,0},{3,1},{10,8},{11,9},{18,16},{19,17},{26,24},{27,25}} | collective-permute-start | bytes 3932168 | tf_op jit(solution)/shard_map/ppermute | solution.py:64
  120.7 42.1 %collective-permute-start.21 = (f32[384,768]{1,0:T(8,128)}, f32[384,768]{1,0:T(8,128)}, u32[]{:S(2)}, u32[]{:S(2)}) collective-permute-start(f32[384,768]{1,0:T(8,128)} %get-tuple-element.49), channel_id=1, source_target_pairs={{0,1},{1,0},{2,3},{3,2},{4,5},{5,4},{6,7},{7,6},{8,9},{9,8},{10,11... | collective-permute-start | bytes 3538952 | tf_op jit(solution)/shard_map/ppermute | solution.py:19
  135.7 46.7 %collective-permute-start.10 = (bf16[128,5120]{1,0:T(8,128)(2,1)}, bf16[128,5120]{1,0:T(8,128)(2,1)S(1)}, u32[]{:S(2)}, u32[]{:S(2)}) collective-permute-start(bf16[128,5120]{1,0:T(8,128)(2,1)} %fusion.3), channel_id=1, source_target_pairs={{0,8},{8,0},{16,24},{24,16},{1,9},{9,1},{17,25},{25,17},{2,10},{10... | collective-permute-start | bytes 3932168 | tf_op jit(solution)/shard_map/ppermute | solution.py:19
  152.7 28.1 %collective-permute-start.23 = (bf16[768,640]{1,0:T(8,128)(2,1)}, bf16[768,640]{1,0:T(8,128)(2,1)}, u32[]{:S(2)}, u32[]{:S(2)}) collective-permute-start(bf16[768,640]{1,0:T(8,128)(2,1)} %refs_5_.1), channel_id=1, source_target_pairs={{0,2},{2,4},{4,6},{1,3},{3,5},{5,7},{8,10},{10,12},{12,14},{9,11},... | collective-permute-start | bytes 2949128 | tf_op jit(solution)/shard_map/ppermute | solution.py:63
  179.3 34.3 %collective-permute-start.28 = (f32[512,768]{1,0:T(8,128)}, f32[512,768]{1,0:T(8,128)S(1)}, u32[]{:S(2)}, u32[]{:S(2)}) collective-permute-start(f32[512,768]{1,0:T(8,128)} %get-tuple-element.58), channel_id=1, source_target_pairs={{0,1},{1,0},{2,3},{3,2},{4,5},{5,4},{6,7},{7,6},{8,9},{9,8},{10,11... | collective-permute-start | bytes 4718600 | tf_op jit(solution)/shard_map/ppermute | solution.py:19
  179.5 26.5 %collective-permute-start.24 = (bf16[768,640]{1,0:T(8,128)(2,1)}, bf16[768,640]{1,0:T(8,128)(2,1)}, u32[]{:S(2)}, u32[]{:S(2)}) collective-permute-start(bf16[768,640]{1,0:T(8,128)(2,1)} %refs_5_.1), channel_id=1, source_target_pairs={{2,0},{4,2},{6,4},{3,1},{5,3},{7,5},{10,8},{12,10},{14,12},{11,9},... | collective-permute-start | bytes 2949128 | tf_op jit(solution)/shard_map/ppermute | solution.py:64
  180.8 45.2 %collective-permute-start.29 = (bf16[768,640]{1,0:T(8,128)(2,1)}, bf16[768,640]{1,0:T(8,128)(2,1)}, u32[]{:S(2)}, u32[]{:S(2)}) collective-permute-start(bf16[768,640]{1,0:T(8,128)(2,1)} %collective-permute-done.23), channel_id=1, source_target_pairs={{2,4},{4,6},{3,5},{5,7},{10,12},{12,14},{11,13},{13,15},{18,20},{2... | collective-permute-start | bytes 2949128 | tf_op jit(solution)/shard_map/ppermute | solution.py:63
  184.0 77.8 %collective-permute-start.11 = (bf16[128,5120]{1,0:T(8,128)(2,1)}, bf16[128,5120]{1,0:T(8,128)(2,1)S(1)}, u32[]{:S(2)}, u32[]{:S(2)}) collective-permute-start(bf16[128,5120]{1,0:T(8,128)(2,1)} %fusion.2), channel_id=1, source_target_pairs={{0,16},{8,24},{16,0},{24,8},{1,17},{9,25},{17,1},{25,9},{2,18},{10... | collective-permute-start | bytes 3932168 | tf_op jit(solution)/shard_map/ppermute | solution.py:19
  219.7 42.1 %all-to-all-start.1 = ((bf16[4,128,768]{2,1,0:T(8,128)(2,1)}), bf16[4,128,768]{2,1,0:T(8,128)(2,1)S(1)}, u32[]{:S(2)}, u32[]{:S(2)}) async-start(bf16[4,128,768]{2,1,0:T(8,128)(2,1)} %attend.1), calls=%async_computation.1 | async-start | bytes 1572864 | tf_op jit(solution)/shard_map/all_to_all | solution.py:486
  224.7 35.6 %collective-permute-start.30 = (bf16[768,640]{1,0:T(8,128)(2,1)}, bf16[768,640]{1,0:T(8,128)(2,1)}, u32[]{:S(2)}, u32[]{:S(2)}) collective-permute-start(bf16[768,640]{1,0:T(8,128)(2,1)} %collective-permute-done.24), channel_id=1, source_target_pairs={{2,0},{4,2},{3,1},{5,3},{10,8},{12,10},{11,9},{13,11},{18,16},{20,... | collective-permute-start | bytes 2949128 | tf_op jit(solution)/shard_map/ppermute | solution.py:64
  226.0 38.8 %collective-permute-start.35 = (bf16[768,640]{1,0:T(8,128)(2,1)}, bf16[768,640]{1,0:T(8,128)(2,1)}, u32[]{:S(2)}, u32[]{:S(2)}) collective-permute-start(bf16[768,640]{1,0:T(8,128)(2,1)} %collective-permute-done.29), channel_id=1, source_target_pairs={{4,6},{5,7},{12,14},{13,15},{20,22},{21,23},{28,30},{29,31}} | collective-permute-start | bytes 2949128 | tf_op jit(solution)/shard_map/ppermute | solution.py:63
  260.3 28.3 %collective-permute-start.36 = (bf16[768,640]{1,0:T(8,128)(2,1)}, bf16[768,640]{1,0:T(8,128)(2,1)}, u32[]{:S(2)}, u32[]{:S(2)}) collective-permute-start(bf16[768,640]{1,0:T(8,128)(2,1)} %collective-permute-done.30), channel_id=1, source_target_pairs={{2,0},{3,1},{10,8},{11,9},{18,16},{19,17},{26,24},{27,25}} | collective-permute-start | bytes 2949128 | tf_op jit(solution)/shard_map/ppermute | solution.py:64
  261.9 27.2 %collective-permute-start.32 = (bf16[4,128,768]{2,1,0:T(8,128)(2,1)S(1)}, bf16[4,128,768]{2,1,0:T(8,128)(2,1)S(1)}, u32[]{:S(2)}, u32[]{:S(2)}) collective-permute-start(bf16[4,128,768]{2,1,0:T(8,128)(2,1)S(1)} %all-to-all-done.1.refs_0_), channel_id=1, source_target_pairs={{0,16},{8,24},{16,0},{24,8},{1,17},{9,25},{17,1},{25,9},{2,18},{10... | collective-permute-start | bytes 2359304 | tf_op jit(solution)/shard_map/ppermute | solution.py:19
  262.4 29.2 %collective-permute-start.37 = (bf16[768,640]{1,0:T(8,128)(2,1)}, bf16[768,640]{1,0:T(8,128)(2,1)}, u32[]{:S(2)}, u32[]{:S(2)}) collective-permute-start(bf16[768,640]{1,0:T(8,128)(2,1)} %refs_5_.1), channel_id=1, source_target_pairs={{0,1},{1,0},{2,3},{3,2},{4,5},{5,4},{6,7},{7,6},{8,9},{9,8},{10,11... | collective-permute-start | bytes 2949128 | tf_op jit(solution)/shard_map/ppermute | solution.py:19
  262.5 29.0 %collective-permute-start.31 = (bf16[4,128,768]{2,1,0:T(8,128)(2,1)S(1)}, bf16[4,128,768]{2,1,0:T(8,128)(2,1)S(1)}, u32[]{:S(2)}, u32[]{:S(2)}) collective-permute-start(bf16[4,128,768]{2,1,0:T(8,128)(2,1)S(1)} %all-to-all-done.1.refs_0_), channel_id=1, source_target_pairs={{0,8},{8,0},{16,24},{24,16},{1,9},{9,1},{17,25},{25,17},{2,10},{10... | collective-permute-start | bytes 2359304 | tf_op jit(solution)/shard_map/ppermute | solution.py:19
  264.8 27.4 %collective-permute-start.27 = (f32[1,5248]{1,0:T(1,128)S(1)}, f32[1,5248]{1,0:T(1,128)S(1)}, u32[]{:S(2)}, u32[]{:S(2)}) collective-permute-start(f32[1,5248]{1,0:T(1,128)S(1)} %broadcast_in_dim.16), channel_id=1, source_target_pairs={{0,24},{8,16},{16,8},{24,0},{1,25},{9,17},{17,9},{25,1},{2,26},{10... | collective-permute-start | bytes 62984 | tf_op jit(solution)/shard_map/ppermute | solution.py:19
  317.1 35.2 %all-to-all-start.2 = ((bf16[4,2,128,1280]{3,2,1,0:T(8,128)(2,1)}), bf16[4,2,128,1280]{3,2,1,0:T(8,128)(2,1)}, u32[]{:S(2)}, u32[]{:S(2)}) async-start(bf16[4,2,128,1280]{3,2,1,0:T(8,128)(2,1)} %project_out.1), calls=%async_computation.2 | async-start | bytes 5242880 | tf_op jit(solution)/shard_map/all_to_all | solution.py:495
  (59 other events, 894.1 us)

commit v5 on v4

--- a/solution.py
+++ b/solution.py
@@ -27,20 +27,18 @@
     return {bit: [swap(x, "step", bit)] for bit in bits_of("step")}
 
 
-def forwarded(x, near, turn=None):
+def forwarded(x, near, *awaited):
     held = {0: [x], **near}
     half = x.shape[0] // 2
     for offset in range(1, lax.axis_size("step")):
         low, high = offset & -offset, 1 << (offset.bit_length() - 1)
         if offset in held:
             continue
-        if turn is not None:
-            last = (low, high)[turn]
-            held[offset] = [swap(held[offset ^ last][0], "step", last)]
-            continue
         top, bottom = held[offset ^ low], held[offset ^ high]
         top = top[0][:half] if len(top) == 1 else top[0]
         bottom = bottom[0][half:] if len(bottom) == 1 else bottom[1]
+        if awaited:
+            top, bottom = after((top, bottom), *awaited)
         held[offset] = [swap(top, "step", low), swap(bottom, "step", high)]
     return [held[offset] for offset in range(lax.axis_size("step"))]
 
@@ -53,15 +51,12 @@
     return lax.optimization_barrier((x,) + others)[0]
 
 
-def along_line(x, awaited=()):
+def along_line(x):
     size = lax.axis_size("head")
     below, above = [x], [x]
     for hop in range(1, size):
-        up, down = below[-1], above[-1]
-        if 0 <= hop - 2 < len(awaited):
-            up, down = after((up, down), *awaited[hop - 2])
-        below.append(lax.ppermute(up, "head", [(i, i + 1) for i in range(hop - 1, size - 1)]))
-        above.append(lax.ppermute(down, "head", [(i, i - 1) for i in range(1, size - hop + 1)]))
+        below.append(lax.ppermute(below[-1], "head", [(i, i + 1) for i in range(hop - 1, size - 1)]))
+        above.append(lax.ppermute(above[-1], "head", [(i, i - 1) for i in range(1, size - hop + 1)]))
     return below, above
 
 
@@ -78,7 +73,7 @@
     centre = jnp.mean(current, axis=-1, keepdims=True)
     centred = current - centre
     spread_of = jnp.mean(centred * centred, axis=-1, keepdims=True)
-    shift, scale = rows[0:1, :], rows[1:2, :]
+    shift, scale = rows[0, 0:1, :], rows[0, 1:2, :]
     modulated = (centred * lax.rsqrt(spread_of + 1e-06) * (1.0 + scale) + shift).astype(jnp.bfloat16)
     core = place[1]
     for block in range(2 * steps):
@@ -103,7 +98,7 @@
     return pl.pallas_call(
         functools.partial(modulate_kernel, steps),
         grid=(tokens // tile,),
-        in_specs=[SMEM, pl.BlockSpec((tile, width), lambda i: (i, 0)), pl.BlockSpec(rows.shape, lambda i: (0, 0))],
+        in_specs=[SMEM, pl.BlockSpec((tile, width), lambda i: (i, 0)), pl.BlockSpec(rows.shape, lambda i: (0, 0, 0))],
         out_specs=[spec, spec],
         out_shape=[out, out],
         compiler_params=params(),
@@ -112,15 +107,11 @@
     )(place, states, rows)
 
 
-def project_kernel(size, parts, layouts, place, *refs):
+def project_kernel(size, parts, layout, place, *refs):
     count = 2 * size - 1
     own, below, above = refs[0], refs[1:size], refs[size:count]
-    weights = []
-    for layout in layouts:
-        weights.append(refs[count : count + len(layout)])
-        count += len(layout)
-    outs = refs[count : count + 2 * len(layouts)]
-    x_held, w_held, x_sems, w_sems = refs[count + 2 * len(layouts) :]
+    weights = refs[count : count + len(layout)]
+    here, there, x_held, w_held, x_sems, w_sems = refs[count + len(layout) :]
     tokens, depth = own.shape[1:]
     step_at, position, shift = place[0], place[2], place[4]
     early = size - 1
@@ -132,115 +123,105 @@
             ref.at[clip], x_held.at[pl.ds(pl.multiple_of(row, tokens), tokens)], x_sems.at[clip, block]
         )
 
-    def w_copies(which):
-        for index, (ref, (offset, whole, start, rows)) in enumerate(zip(weights[which], layouts[which])):
+    def w_copies():
+        for index, (ref, (offset, whole, start, rows)) in enumerate(zip(weights, layout)):
             at = jnp.bitwise_xor(step_at, offset) * whole + start
-            target = w_held.at[which, pl.ds(pl.multiple_of(at, rows), rows)]
-            yield pltpu.make_async_copy(ref, target, w_sems.at[which, index])
-
-    for which in range(len(layouts)):
-        for copy in w_copies(which):
-            copy.start()
-        if which:
-            continue
-        for clip in range(2):
-            for away in range(size):
-                for sign, held in ((1, above), (-1, below)):
-                    if away == 0 and sign < 0:
-                        continue
-                    source = own if away == 0 else held[away - 1]
-                    block_at = position + sign * away
-                    block = lax.rem(block_at - shift + size, size)
-                    inside = jnp.logical_and(block_at >= 0, block_at < size)
-                    inside = jnp.logical_and(inside, jnp.logical_and(block >= blocks[0], block <= blocks[-1]))
-
-                    @pl.when(inside)
-                    def _(source=source, block=block, clip=clip):
-                        x_copy(source, clip, block).start()
-
-    rows = outs[0].shape[0]
+            yield pltpu.make_async_copy(ref, w_held.at[pl.ds(pl.multiple_of(at, rows), rows)], w_sems.at[index])
+
+    for copy in w_copies():
+        copy.start()
+    for clip in range(2):
+        for away in range(size):
+            for sign, held in ((1, above), (-1, below)):
+                if away == 0 and sign < 0:
+                    continue
+                source = own if away == 0 else held[away - 1]
+                block_at = position + sign * away
+                block = lax.rem(block_at - shift + size, size)
+                inside = jnp.logical_and(block_at >= 0, block_at < size)
+                inside = jnp.logical_and(inside, jnp.logical_and(block >= blocks[0], block <= blocks[-1]))
+
+                @pl.when(inside)
+                def _(source=source, block=block, clip=clip):
+                    x_copy(source, clip, block).start()
+
+    for copy in w_copies():
+        copy.wait()
     for clip in range(2):
         for block in blocks:
             x_copy(own, clip, block).wait()
-    for which in range(len(layouts)):
-        for copy in w_copies(which):
-            copy.wait()
-        for clip in range(2):
-            span = slice(clip * rows, (clip + 1) * rows)
-            outs[2 * which + clip][...] = jnp.dot(x_held[span], w_held[which], preferred_element_type=jnp.float32)
-
-
-def project(place, line, all_shards, parts, name):
+    rows, columns = here.shape
+    width = columns if columns % 512 else columns // 2
+    for start in range(0, columns, width):
+        span = slice(start, start + width)
+        product = jnp.dot(x_held[...], w_held[:, span], preferred_element_type=jnp.float32)
+        here[:, span] = product[:rows]
+        there[:, span] = product[rows:]
+
+
+def project(place, line, shards, parts, name):
     size = lax.axis_size("head")
     below, above = line
     operands = [below[0]] + below[1:] + above[1:]
     _, tokens, depth = operands[0].shape
-    layouts, weights = [], []
-    for shards in all_shards:
-        layout = []
-        for offset, pieces in enumerate(shards):
-            start = 0
-            for piece in pieces:
-                layout.append((offset, depth // len(shards), start, piece.shape[0]))
-                weights.append(piece)
-                start += piece.shape[0]
-        layouts.append(tuple(layout))
-    sets = len(layouts)
+    layout, weights = [], []
+    for offset, pieces in enumerate(shards):
+        start = 0
+        for piece in pieces:
+            layout.append((offset, depth // len(shards), start, piece.shape[0]))
+            weights.append(piece)
+            start += piece.shape[0]
     columns = weights[0].shape[1]
     rows = {"first": size - 1, "last": 1, "all": size}[parts] * tokens
     out = jax.ShapeDtypeStruct((rows, columns), jnp.float32)
-    moved = 2 * depth * (2 * rows + sets * columns) + 8 * sets * rows * columns
-    outs = pl.pallas_call(
-        functools.partial(project_kernel, size, parts, tuple(layouts)),
+    moved = 2 * depth * (2 * rows + columns) + 8 * rows * columns
+    return pl.pallas_call(
+        functools.partial(project_kernel, size, parts, tuple(layout)),
         in_specs=[SMEM] + [ANY] * (len(operands) + len(weights)),
-        out_specs=[VMEM] * (2 * sets),
-        out_shape=[out] * (2 * sets),
+        out_specs=[VMEM, VMEM],
+        out_shape=[out, out],
         scratch_shapes=[
             pltpu.VMEM((2 * rows, depth), jnp.bfloat16),
-            pltpu.VMEM((sets, depth, columns), jnp.bfloat16),
+            pltpu.VMEM((depth, columns), jnp.bfloat16),
             pltpu.SemaphoreType.DMA((2, size)),
-            pltpu.SemaphoreType.DMA((sets, max(len(layout) for layout in layouts))),
+            pltpu.SemaphoreType.DMA((len(layout),)),
         ],
         compiler_params=params(),
-        cost_estimate=cost(4 * rows * sets * depth * columns, moved),
+        cost_estimate=cost(4 * rows * depth * columns, moved),
         name=name,
     )(place, *operands, *weights)
-    return [[outs[2 * which], swap(outs[2 * which + 1], "fsdp", 1)] for which in range(sets)]
-
-
-def norms_kernel(place, *refs):
-    parts, out = refs[:8], refs[8]
-    tokens = parts[2].shape[0]
+
+
+def norms_kernel(place, first_a, first_b, last_a, last_b, out):
+    width = first_a.shape[1] // 2
     rows = []
-    for at in (0, 4):
+    for which in range(2):
         found = []
-        for part in (at + 2, at, at + 2):
-            total = parts[part][...] + parts[part + 1][...]
-            total = total * total
-            lanes = total[:, :HD]
-            for group in range(1, total.shape[1] // HD):
-                lanes = lanes + total[:, group * HD : (group + 1) * HD]
+        for one, other in ((first_a, first_b), (last_a, last_b)):
+            lanes = None
+            for start in range(which * width, (which + 1) * width, HD):
+                total = one[:, start : start + HD] + other[:, start : start + HD]
+                lanes = total * total if lanes is None else lanes + total * total
             found.append(jnp.sum(lanes.T, axis=0, keepdims=True))
-        wrapped = jnp.concatenate(found[:2], axis=1)
-        straight = jnp.concatenate(found[1:], axis=1)
+        straight = jnp.concatenate(found, axis=1)
+        wrapped = jnp.concatenate(found[::-1], axis=1)
         rows.append(jnp.where(place[4] == 0, straight, wrapped))
     both = jnp.concatenate(rows, axis=0)
     for peer in range(out.shape[0]):
         out[peer] = both
 
 
-def norms(place, q_parts, k_parts, size):
-    rows = q_parts[0].shape[0] + q_parts[2].shape[0]
-    operands = q_parts + k_parts
+def norms(place, parts, size):
+    rows = parts[0].shape[0] + parts[2].shape[0]
     return pl.pallas_call(
         norms_kernel,
-        in_specs=[SMEM] + [VMEM] * 8,
+        in_specs=[SMEM] + [VMEM] * 4,
         out_specs=VMEM,
         out_shape=jax.ShapeDtypeStruct((size, 2, rows), jnp.float32),
         compiler_params=params(),
-        cost_estimate=cost(8 * rows * q_parts[0].shape[1], 16 * rows * q_parts[0].shape[1]),
+        cost_estimate=cost(4 * rows * parts[0].shape[1], 8 * rows * parts[0].shape[1]),
         name="norms",
-    )(place, *operands)
+    )(place, *parts)
 
 
 def probs_kernel(tokens, full_width, place, squares, *refs):
@@ -278,24 +259,25 @@
     return 2 if heads % 2 == 0 else 1
 
 
-def probabilities(place, squares, q_parts, k_parts, q_gain, k_gain):
-    columns = q_parts[0].shape[1]
-    rows = q_parts[0].shape[0] + q_parts[2].shape[0]
+def probabilities(place, squares, parts, q_gain, k_gain):
+    columns = parts[0].shape[1] // 2
+    rows = parts[0].shape[0] + parts[2].shape[0]
     heads = columns // HD
     group = at_once(heads)
-    by_head = [pl.BlockSpec((part.shape[0], group * HD), lambda i: (0, i)) for part in q_parts + k_parts]
+    q_blocks = [pl.BlockSpec((part.shape[0], group * HD), lambda i: (0, i)) for part in parts]
+    k_blocks = [pl.BlockSpec((part.shape[0], group * HD), lambda i: (0, i + heads // group)) for part in parts]
     gain = pl.BlockSpec((1, group * HD), lambda i: (0, i))
     return pl.pallas_call(
-        functools.partial(probs_kernel, q_parts[2].shape[0], float(columns * squares.shape[0])),
+        functools.partial(probs_kernel, parts[2].shape[0], float(columns * squares.shape[0])),
         grid=(heads // group,),
-        in_specs=[SMEM, pl.BlockSpec(squares.shape, lambda i: (0, 0, 0))] + by_head + [gain] * 2,
+        in_specs=[SMEM, pl.BlockSpec(squares.shape, lambda i: (0, 0, 0))] + q_blocks + k_blocks + [gain] * 2,
         out_specs=pl.BlockSpec((group, rows, rows), lambda i: (i, 0, 0)),
         out_shape=jax.ShapeDtypeStruct((heads, rows, rows), jnp.bfloat16),
         scratch_shapes=[pltpu.VMEM((2, rows, HD), jnp.float32)],
         compiler_params=params(),
         cost_estimate=cost(2 * heads * rows * rows * HD, 16 * rows * columns + 2 * heads * rows * rows, heads * rows * rows),
         name="probs",
-    )(place, squares, *q_parts, *k_parts, q_gain[None], k_gain[None])
+    )(place, squares, *parts, *parts, q_gain[None], k_gain[None])
 
 
 def attend_kernel(place, probs, v_a, v_b, out, held):
@@ -444,34 +426,45 @@
     shift = (position >= size // 2).astype(jnp.int32)
     place = jnp.stack([step, core, position, lengths[0], shift]).astype(jnp.int32)
 
-    q_near = direct(w_query)
-    k_near = direct(after(w_key, *listed(q_near)))
-    q_near = dict(zip(q_near, [[piece] for piece in after(tuple(listed(q_near)), *listed(k_near))]))
-    q_shards = forwarded(w_query, q_near, 0)
-    k_shards = forwarded(w_key, k_near, 1)
-    v_near = direct(after(w_value, *listed(q_shards), *listed(k_shards)))
-    v_shards = forwarded(w_value, v_near)
-
-    mine, other = modulate(place, current, modulation[0], steps)
-    line = along_line(jnp.stack([mine, swap(other, "fsdp", 1)]), (listed(q_near), listed(k_near)))
+    mine, other = modulate(place, current, modulation, steps)
+    tokens = jnp.stack([mine, swap(other, "fsdp", 1)])
+    line = along_line(tokens)
     early = tuple(held[: size - 1] + [held[0]] for held in line)
 
-    q_parts, k_parts = project(place, early, (q_shards, k_shards), "first", "first")
-    below, above = along_line(after(w_out, line[0][-1], line[1][-1], q_parts[0], k_parts[0]))
-    q_last, k_last = project(place, line, (q_shards, k_shards), "last", "last")
-    q_parts, k_parts = q_parts + q_last, k_parts + k_last
-    own_squares = norms(place, q_parts, k_parts, size)
+    w_both = after(jnp.concatenate([w_query, w_key], axis=1), tokens)
+    both_shards = forwarded(w_both, direct(w_both), line[0][1], line[1][1])
+    first_here, first_there = project(place, early, both_shards, "first", "first")
+    v_near = direct(after(w_value, *listed(both_shards)))
+    v_shards = forwarded(w_value, v_near, first_here)
+
+    first_there = after(first_there, line[0][-1], line[1][-1])
+    parts = [first_here, swap(first_there, "fsdp", 1)]
+    last_here, last_there = project(place, line, both_shards, "last", "last")
+    parts += [last_here, swap(last_there, "fsdp", 1)]
+    own_squares = norms(place, parts, size)
     squares = lax.all_to_all(own_squares, "head", 0, 0)
-    (v_parts,) = project(after(place, own_squares), line, (v_shards,), "all", "value")
-    squares = after(squares, v_parts[0], below[1], above[1])
-    probs = probabilities(place, squares, q_parts, k_parts, q_gain, k_gain)
+    v_here, v_there = project(after(place, own_squares), line, v_shards, "all", "value")
+    v_parts = [v_here, swap(v_there, "fsdp", 1)]
+
+    below, above = [w_out], [w_out]
+    for hop in range(1, size):
+        up, down = below[-1], above[-1]
+        if hop == 1:
+            up, down = after((up, down), line[0][-1], line[1][-1], first_here)
+        if hop == size - 1:
+            probs = probabilities(place, after(squares, v_here, below[1], above[1]), parts, q_gain, k_gain)
+            attended = attend(place, probs, v_parts, size)
+            quarter = lax.all_to_all(attended, "head", 0, 0)
+            up, down = after((up, down), quarter)
+        below.append(lax.ppermute(up, "head", [(i, i + 1) for i in range(hop - 1, size - 1)]))
+        above.append(lax.ppermute(down, "head", [(i, i - 1) for i in range(1, size - hop + 1)]))
 
     step_width = (timesteps[0, 1] - timesteps[0, 0]).astype(jnp.float32) / 1000.0
     carried = step_width * current + jnp.where(step == 0, current, jnp.zeros_like(current))
     base, total = carried, carried
     swapped = []
     for bit in bits_of("step"):
-        swapped.append(swap(after(total.astype(jnp.bfloat16), *listed(v_shards)), "step", bit))
+        swapped.append(swap(after(total.astype(jnp.bfloat16), own_squares, *listed(v_shards)), "step", bit))
         brought = swapped[-1].astype(jnp.float32)
         base = base + jnp.where(jnp.bitwise_and(step, bit) != 0, brought, jnp.zeros_like(brought))
         total = total + brought
@@ -482,8 +475,7 @@
     heard = jnp.concatenate([told] + [swap(sent_told, "step", offset) for offset in range(1, steps)])
     gates = lax.dynamic_slice(heard, (0, step * columns), (steps, columns))
 
-    attended = attend(place, after(probs, swapped[0]), v_parts, size)
-    quarter = after(lax.all_to_all(attended, "head", 0, 0), swapped[-1], below[2], above[2])
+    quarter = after(quarter, swapped[-1], heard)
     gathered = forwarded(quarter, direct(quarter))
 
     own_columns = [w_out] + [

time: 358 us -> 353 us (0.986)
  waiting for transfers between devices: 206 us -> 188 us
  other arithmetic: 12.3 us -> 16.1 us
    ppermute x29 -> x25, waiting for transfers between devices: 86.1 us -> 57.2 us  [swap(): lax.ppermute(x, axis, [(i, i ^ offset) for i in range(lax.axis_size(axis))])]
    ppermute x12, waiting for transfers between devices: 77.9 us -> 93.9 us  [the longest x3 33.2 us: along_line(): lax.ppermute(above[-1], 'head', [(i, i - 1) for i in range(1, size - hop...]
    all_to_all x1, waiting for transfers between devices: 15.7 us -> 0.01 us  [body(): squares = lax.all_to_all(own_squares, 'head', 0, 0)]
    all_to_all x1, waiting for transfers between devices: 0.01 us -> 10.7 us  [body(): quarter = lax.all_to_all(attended, 'head', 0, 0)]
    ppermute x12, starting transfers between devices: 19.7 us -> 24.8 us  [the longest x3 9.53 us: body(): lax.ppermute(up, 'head', [(i, i + 1) for i in range(hop - 1, size - 1)])]
    unnamed x77 -> x51, local copies, waits for them, and re-layouts: 5.8 us -> 7.57 us
    ppermute x29 -> x25, starting transfers between devices: 24.5 us -> 24 us  [swap(): lax.ppermute(x, axis, [(i, i ^ offset) for i in range(lax.axis_size(axis))])]
  transfers between devices with their start and end apart: 44 -> 40, of which waited for: 20 -> 18; matrix products, arithmetic and copies ran while one was open for 5% -> 6% of each run, Pallas kernels for 14% -> 11%
where the time goes in v5:
time: 353 us; the launch traced here: 352 us
  waiting for transfers between devices  188 us (53%)
  Pallas kernels  68.4 us (19%)
  starting transfers between devices  61.8 us (18%)
  other arithmetic  16.1 us (5%)
  local copies, waits for them, and re-layouts  14.7 us (4%)
    ppermute x25, waiting for transfers between devices, swap(): lax.ppermute(x, axis, [(i, i ^ offset) for i in range(lax.axis_size(axis))])  57.2 us
    ppermute x3, waiting for transfers between devices, along_line(): lax.ppermute(above[-1], 'head', [(i, i - 1) for i in range(1, size - hop...  33.2 us
    pallas_call x3, Pallas kernels, project(): pl.pallas_call(functools.partial(project_kernel, size, parts, tuple(layou...  31.4 us
    all_to_all x1, waiting for transfers between devices, body(): arrived = lax.all_to_all(sent, 'step', 0, 0)  26 us
    ppermute x25, starting transfers between devices, swap(): lax.ppermute(x, axis, [(i, i ^ offset) for i in range(lax.axis_size(axis))])  24 us
    ppermute x3, waiting for transfers between devices, along_line(): lax.ppermute(below[-1], 'head', [(i, i + 1) for i in range(hop - 1, size...  23.7 us
    ppermute x3, waiting for transfers between devices, body(): lax.ppermute(down, 'head', [(i, i - 1) for i in range(1, size - hop + 1)])  22.5 us
    ppermute x3, waiting for transfers between devices, body(): lax.ppermute(up, 'head', [(i, i + 1) for i in range(hop - 1, size - 1)])  14.5 us
  transfers between devices with their start and end apart: 40, of which 18 were waited for; matrix products, arithmetic and copies ran while one was open for 6% of the time, Pallas kernels for 11%

profile of v5, /device:TPU:0, one launch (start us, length us, event | category | flops | bytes accessed | tf_op | source)
XLA Modules:
  0.0 351.8 jit_solution(13292653865067546330)
XLA Ops:
  3.4 4.7 %modulate.1 = (bf16[128,2560]{1,0:T(8,128)(2,1)}, bf16[128,2560]{1,0:T(8,128)(2,1)}) custom-call(s32[5]{0:T(128)} %stack.32.place, f32[128,5120]{1,0:T(8,128)} %bitcast.14, f32[1,3,5120]{2,1,0:T(4,128)} %copy.13.rows), custom_call_target="tpu_custom_call" | custom-call | flops 1638400 | bytes 983040 | tf_op jit(solution)/shard_map/modulate/pallas_call | solution.py:98
  11.7 4.9 %collective-permute-start.1 = (bf16[2,128,2560]{2,1,0:T(8,128)(2,1)S(1)}, bf16[2,128,2560]{2,1,0:T(8,128)(2,1)S(1)}, u32[]{:S(2)}, u32[]{:S(2)}) collective-permute-start(bf16[2,128,2560]{2,1,0:T(8,128)(2,1)S(1)} %pad_maximum_fusion.1.refs_0_.refs_3_.refs_6_), channel_id=1, source_target_pairs={{0,2},{2,4},{4,6},{1,3},{3,5},{5,7},{8,10},{10,12},{12,14},{9,11},... | collective-permute-start | bytes 3932168 | tf_op jit(solution)/shard_map/ppermute | solution.py:58
  21.2 23.7 %collective-permute-done.1.refs_1_ = bf16[2,128,2560]{2,1,0:T(8,128)(2,1)S(1)} collective-permute-done((bf16[2,128,2560]{2,1,0:T(8,128)(2,1)S(1)}, bf16[2,128,2560]{2,1,0:T(8,128)(2,1)S(1)}, u32[]{:S(2)}, u32[]{:S(2)}) %collective-permute-start.1) | collective-permute-done | bytes 1310752 | tf_op jit(solution)/shard_map/ppermute | solution.py:58
  51.1 30.8 %collective-permute-done.4.refs_5_ = bf16[2,128,2560]{2,1,0:T(8,128)(2,1)} collective-permute-done((bf16[2,128,2560]{2,1,0:T(8,128)(2,1)S(1)}, bf16[2,128,2560]{2,1,0:T(8,128)(2,1)}, u32[]{:S(2)}, u32[]{:S(2)}) %collective-permute-start.4) | collective-permute-done | bytes 1310752 | tf_op jit(solution)/shard_map/ppermute | solution.py:59
  86.5 19.0 %collective-permute-done.7.refs_10_ = bf16[320,1536]{1,0:T(8,128)(2,1)S(1)} collective-permute-done((bf16[320,1536]{1,0:T(8,128)(2,1)S(1)}, bf16[320,1536]{1,0:T(8,128)(2,1)S(1)}, u32[]{:S(2)}, u32[]{:S(2)}) %collective-permute-start.7) | collective-permute-done | bytes 983072 | tf_op jit(solution)/shard_map/ppermute | solution.py:19
  106.9 13.5 %first.1 = (f32[384,1536]{1,0:T(8,128)}, f32[384,1536]{1,0:T(8,128)}) custom-call(s32[5]{0:T(128)} %stack.32.place, bf16[2,128,2560]{2,1,0:T(8,128)(2,1)} %copy-done, bf16[2,128,2560]{2,1,0:T(8,128)(2,1)} %copy-done.6, bf16[2,128,2560]{2,1,0:T(8,128)(2,1)} %collective-permute-done.2.refs_2_, bf16[2,128,2560]{2,1,0:T(8,128)(2,1)} %copy-done, ...), custom_call_target="tpu_custom_call" | custom-call | flops 1509949440 | bytes 4128768 | tf_op jit(solution)/shard_map/first/pallas_call | solution.py:178
  124.2 7.7 %last.1 = (f32[128,1536]{1,0:T(8,128)}, f32[128,1536]{1,0:T(8,128)}) custom-call(s32[5]{0:T(128)} %stack.32.place, bf16[2,128,2560]{2,1,0:T(8,128)(2,1)} %copy-done, bf16[2,128,2560]{2,1,0:T(8,128)(2,1)} %copy-done.6, bf16[2,128,2560]{2,1,0:T(8,128)(2,1)} %collective-permute-done.2.refs_2_, bf16[2,128,2560]{2,1,0:T(8,128)(2,1)} %copy-done.9, ...), custom_call_target="tpu_custom_call" | custom-call | flops 503316480 | bytes 2686976 | tf_op jit(solution)/shard_map/last/pallas_call | solution.py:178
  132.0 13.9 %collective-permute-done.14.refs_9_ = bf16[640,768]{1,0:T(8,128)(2,1)S(1)} collective-permute-done((bf16[640,768]{1,0:T(8,128)(2,1)}, bf16[640,768]{1,0:T(8,128)(2,1)S(1)}, u32[]{:S(2)}, u32[]{:S(2)}) %collective-permute-start.14) | collective-permute-done | bytes 983072 | tf_op jit(solution)/shard_map/ppermute | solution.py:19
  163.5 10.1 %value.1 = (f32[512,768]{1,0:T(8,128)}, f32[512,768]{1,0:T(8,128)}) custom-call(s32[5]{0:T(128)} %stack.32.place, bf16[2,128,2560]{2,1,0:T(8,128)(2,1)} %copy-done, bf16[2,128,2560]{2,1,0:T(8,128)(2,1)} %copy-done.6, bf16[2,128,2560]{2,1,0:T(8,128)(2,1)} %collective-permute-done.2.refs_2_, bf16[2,128,2560]{2,1,0:T(8,128)(2,1)} %copy-done.9, ...), custom_call_target="tpu_custom_call" | custom-call | flops 1006632960 | bytes 3080192 | tf_op jit(solution)/shard_map/value/pallas_call | solution.py:178
  176.1 6.3 %collective-permute-start.19 = (bf16[768,640]{1,0:T(8,128)(2,1)}, bf16[768,640]{1,0:T(8,128)(2,1)}, u32[]{:S(2)}, u32[]{:S(2)}) collective-permute-start(bf16[768,640]{1,0:T(8,128)(2,1)} %refs_5_.1), channel_id=1, source_target_pairs={{0,2},{2,4},{4,6},{1,3},{3,5},{5,7},{8,10},{10,12},{12,14},{9,11},... | collective-permute-start | bytes 2949128 | tf_op jit(solution)/shard_map/ppermute | solution.py:459
  188.8 14.4 %collective-permute-done.19 = bf16[768,640]{1,0:T(8,128)(2,1)} collective-permute-done((bf16[768,640]{1,0:T(8,128)(2,1)}, bf16[768,640]{1,0:T(8,128)(2,1)}, u32[]{:S(2)}, u32[]{:S(2)}) %collective-permute-start.19) | collective-permute-done | bytes 983072 | tf_op jit(solution)/shard_map/ppermute | solution.py:459
  210.5 7.0 %probs.1 = bf16[6,512,512]{2,1,0:T(8,128)(2,1)} custom-call(s32[5]{0:T(128)} %stack.32.place, f32[4,2,512]{2,1,0:T(2,128)} %copy-done.20, f32[384,1536]{1,0:T(8,128)} %get-tuple-element.34.first_a.refs_0_.refs_4_, f32[384,1536]{1,0:T(8,128)} %copy-done.2, f32[128,1536]{1,0:T(8,128)} %get-tuple-element.37.last_a.refs_2_.refs_6_, f32[128,1536]{1,0:T(8,128)} %copy-done.8, ...), custom_call_target="tpu_custom_call" | custom-call | flops 100663296 | bytes 2359296 | tf_op jit(solution)/shard_map/probs/pallas_call | solution.py:270
  217.4 5.0 %attend.1 = bf16[4,128,768]{2,1,0:T(8,128)(2,1)} custom-call(s32[5]{0:T(128)} %stack.32.place, bf16[6,512,512]{2,1,0:T(8,128)(2,1)} %probs.1, f32[512,768]{1,0:T(8,128)} %get-tuple-element.45.v_a, f32[512,768]{1,0:T(8,128)} %collective-permute-done.24.v_b), custom_call_target="tpu_custom_call" | custom-call | flops 100663296 | bytes 1769472 | tf_op jit(solution)/shard_map/attend/pallas_call | solution.py:299
  222.4 4.5 %all-to-all-start.1 = ((bf16[4,128,768]{2,1,0:T(8,128)(2,1)}), bf16[4,128,768]{2,1,0:T(8,128)(2,1)S(1)}, u32[]{:S(2)}, u32[]{:S(2)}) async-start(bf16[4,128,768]{2,1,0:T(8,128)(2,1)} %attend.1), calls=%async_computation.1 | async-start | bytes 1572864 | tf_op jit(solution)/shard_map/all_to_all | solution.py:457
  234.9 4.5 %collective-permute-done.30 = bf16[768,640]{1,0:T(8,128)(2,1)} collective-permute-done((bf16[768,640]{1,0:T(8,128)(2,1)}, bf16[768,640]{1,0:T(8,128)(2,1)}, u32[]{:S(2)}, u32[]{:S(2)}) %collective-permute-start.30) | collective-permute-done | bytes 983072 | tf_op jit(solution)/shard_map/ppermute | solution.py:460
  239.5 10.7 %all-to-all-done.1.refs_0_ = bf16[4,128,768]{2,1,0:T(8,128)(2,1)S(1)} async-done(((bf16[4,128,768]{2,1,0:T(8,128)(2,1)}), bf16[4,128,768]{2,1,0:T(8,128)(2,1)S(1)}, u32[]{:S(2)}, u32[]{:S(2)}) %all-to-all-start.1) | async-done | bytes 786464 | tf_op jit(solution)/shard_map/all_to_all | solution.py:457
  251.8 8.6 %collective-permute-done.22 = f32[1,5248]{1,0:T(1,128)S(1)} collective-permute-done((f32[1,5248]{1,0:T(1,128)S(1)}, f32[1,5248]{1,0:T(1,128)S(1)}, u32[]{:S(2)}, u32[]{:S(2)}) %collective-permute-start.22) | collective-permute-done | bytes 21024 | tf_op jit(solution)/shard_map/ppermute | solution.py:19
  269.8 14.4 %collective-permute-done.32 = bf16[768,640]{1,0:T(8,128)(2,1)S(1)} collective-permute-done((bf16[768,640]{1,0:T(8,128)(2,1)}, bf16[768,640]{1,0:T(8,128)(2,1)S(1)}, u32[]{:S(2)}, u32[]{:S(2)}) %collective-permute-start.32) | collective-permute-done | bytes 983072 | tf_op jit(solution)/shard_map/ppermute | solution.py:460
  291.6 6.5 %collective-permute-done.27.refs_3_ = bf16[2,128,768]{2,1,0:T(8,128)(2,1)S(1)} collective-permute-done((bf16[2,128,768]{2,1,0:T(8,128)(2,1)}, bf16[2,128,768]{2,1,0:T(8,128)(2,1)S(1)}, u32[]{:S(2)}, u32[]{:S(2)}) %collective-permute-start.27) | collective-permute-done | bytes 393248 | tf_op jit(solution)/shard_map/ppermute | solution.py:19
  300.6 11.8 %project_out.1 = bf16[4,2,128,1280]{3,2,1,0:T(8,128)(2,1)} custom-call(s32[5]{0:T(128)} %stack.32.place, f32[4]{0:T(128)} %slice_reduce_fusion.widths, bf16[4,128,768]{2,1,0:T(8,128)(2,1)} %copy-done.11, bf16[4,128,768]{2,1,0:T(8,128)(2,1)} %copy-done.15, bf16[4,128,768]{2,1,0:T(8,128)(2,1)} %copy-done.14, bf16[2,128,768]{2,1,0:T(8,128)(2,1)} %copy-done.18, ...), custom_call_target="tpu_custom_call" | custom-call | flops 1006632960 | bytes 3407872 | tf_op jit(solution)/shard_map/project_out/pallas_call | solution.py:384
  312.3 4.6 %all-to-all-start.2 = ((bf16[4,2,128,1280]{3,2,1,0:T(8,128)(2,1)}), bf16[4,2,128,1280]{3,2,1,0:T(8,128)(2,1)}, u32[]{:S(2)}, u32[]{:S(2)}) async-start(bf16[4,2,128,1280]{3,2,1,0:T(8,128)(2,1)} %project_out.1), calls=%async_computation.2 | async-start | bytes 5242880 | tf_op jit(solution)/shard_map/all_to_all | solution.py:487
  316.9 4.0 %fusion.1.base = f32[128,5120]{1,0:T(8,128)} fusion(bf16[128,5120]{1,0:T(8,128)(2,1)} %collective-permute-done.17, bf16[128,5120]{1,0:T(8,128)(2,1)} %collective-permute-done.18, f32[]{:T(128)} %bitcast, pred[]{:T(512)S(6)} %ne.7, pred[]{:T(512)S(6)} %ne.6, pred[]{:T(512)S(6)} %eq.3, f32[1,1,128,5120]{3,2,1,0:T(8,128)S(1)} %copy-done.1), kind=kLoop, calls=%fused_computation.3 | loop fusion | flops 5898240 | bytes 7864327 | tf_op jit(solution)/shard_map/add | solution.py:469
  320.9 26.0 %all-to-all-done.2.arrived = bf16[4,2,128,1280]{3,2,1,0:T(8,128)(2,1)} async-done(((bf16[4,2,128,1280]{3,2,1,0:T(8,128)(2,1)}), bf16[4,2,128,1280]{3,2,1,0:T(8,128)(2,1)}, u32[]{:S(2)}, u32[]{:S(2)}) %all-to-all-start.2) | async-done | bytes 2621472 | tf_op jit(solution)/shard_map/all_to_all | solution.py:487
  347.0 4.8 %finish.1 = (f32[128,5120]{1,0:T(8,128)}, bf16[128,5120]{1,0:T(8,128)(2,1)}) custom-call(f32[128,5120]{1,0:T(8,128)} %fusion.1.base, bf16[4,2,128,1280]{3,2,1,0:T(8,128)(2,1)} %all-to-all-done.2.arrived), custom_call_target="tpu_custom_call" | custom-call | flops 163840 | bytes 2293760 | tf_op jit(solution)/shard_map/finish/pallas_call | solution.py:410
  (141 shorter events, 87.2 us)
Async XLA Ops:
  11.7 33.2 %collective-permute-start.1 = (bf16[2,128,2560]{2,1,0:T(8,128)(2,1)S(1)}, bf16[2,128,2560]{2,1,0:T(8,128)(2,1)S(1)}, u32[]{:S(2)}, u32[]{:S(2)}) collective-permute-start(bf16[2,128,2560]{2,1,0:T(8,128)(2,1)S(1)} %pad_maximum_fusion.1.refs_0_.refs_3_.refs_6_), channel_id=1, source_target_pairs={{0,2},{2,4},{4,6},{1,3},{3,5},{5,7},{8,10},{10,12},{12,14},{9,11},... | collective-permute-start | bytes 3932168 | tf_op jit(solution)/shard_map/ppermute | solution.py:58
  16.7 32.4 %collective-permute-start.3 = (bf16[2,128,2560]{2,1,0:T(8,128)(2,1)S(1)}, bf16[2,128,2560]{2,1,0:T(8,128)(2,1)S(1)}, u32[]{:S(2)}, u32[]{:S(2)}) collective-permute-start(bf16[2,128,2560]{2,1,0:T(8,128)(2,1)S(1)} %pad_maximum_fusion.1.refs_0_.refs_3_.refs_6_), channel_id=1, source_target_pairs={{2,0},{4,2},{6,4},{3,1},{5,3},{7,5},{10,8},{12,10},{14,12},{11,9},... | collective-permute-start | bytes 3932168 | tf_op jit(solution)/shard_map/ppermute | solution.py:59
  18.1 65.0 %collective-permute-start.6 = (bf16[640,1536]{1,0:T(8,128)(2,1)S(1)}, bf16[640,1536]{1,0:T(8,128)(2,1)S(1)}, u32[]{:S(2)}, u32[]{:S(2)}) collective-permute-start(bf16[640,1536]{1,0:T(8,128)(2,1)S(1)} %pad_maximum_fusion.refs_7_), channel_id=1, source_target_pairs={{0,16},{8,24},{16,0},{24,8},{1,17},{9,25},{17,1},{25,9},{2,18},{10... | collective-permute-start | bytes 5898248 | tf_op jit(solution)/shard_map/ppermute | solution.py:19
  19.7 63.6 %collective-permute-start.5 = (bf16[640,1536]{1,0:T(8,128)(2,1)S(1)}, bf16[640,1536]{1,0:T(8,128)(2,1)S(1)}, u32[]{:S(2)}, u32[]{:S(2)}) collective-permute-start(bf16[640,1536]{1,0:T(8,128)(2,1)S(1)} %pad_maximum_fusion.refs_7_), channel_id=1, source_target_pairs={{0,8},{8,0},{16,24},{24,16},{1,9},{9,1},{17,25},{25,17},{2,10},{10... | collective-permute-start | bytes 5898248 | tf_op jit(solution)/shard_map/ppermute | solution.py:19
  49.1 32.8 %collective-permute-start.4 = (bf16[2,128,2560]{2,1,0:T(8,128)(2,1)S(1)}, bf16[2,128,2560]{2,1,0:T(8,128)(2,1)}, u32[]{:S(2)}, u32[]{:S(2)}) collective-permute-start(bf16[2,128,2560]{2,1,0:T(8,128)(2,1)S(1)} %collective-permute-done.3.refs_4_), channel_id=1, source_target_pairs={{2,0},{4,2},{3,1},{5,3},{10,8},{12,10},{11,9},{13,11},{18,16},{20,... | collective-permute-start | bytes 3932168 | tf_op jit(solution)/shard_map/ppermute | solution.py:59
  50.4 70.0 %collective-permute-start.9 = (bf16[2,128,2560]{2,1,0:T(8,128)(2,1)}, bf16[2,128,2560]{2,1,0:T(8,128)(2,1)S(1)}, u32[]{:S(2)}, u32[]{:S(2)}) collective-permute-start(bf16[2,128,2560]{2,1,0:T(8,128)(2,1)} %collective-permute-done.2.refs_2_), channel_id=1, source_target_pairs={{4,6},{5,7},{12,14},{13,15},{20,22},{21,23},{28,30},{29,31}} | collective-permute-start | bytes 3932168 | tf_op jit(solution)/shard_map/ppermute | solution.py:58
  81.9 38.5 %collective-permute-start.10 = (bf16[2,128,2560]{2,1,0:T(8,128)(2,1)}, bf16[2,128,2560]{2,1,0:T(8,128)(2,1)}, u32[]{:S(2)}, u32[]{:S(2)}) collective-permute-start(bf16[2,128,2560]{2,1,0:T(8,128)(2,1)} %collective-permute-done.4.refs_5_), channel_id=1, source_target_pairs={{2,0},{3,1},{10,8},{11,9},{18,16},{19,17},{26,24},{27,25}} | collective-permute-start | bytes 3932168 | tf_op jit(solution)/shard_map/ppermute | solution.py:59
  121.5 32.4 %collective-permute-start.11 = (f32[384,1536]{1,0:T(8,128)}, f32[384,1536]{1,0:T(8,128)S(1)}, u32[]{:S(2)}, u32[]{:S(2)}) collective-permute-start(f32[384,1536]{1,0:T(8,128)} %get-tuple-element.36), channel_id=1, source_target_pairs={{0,1},{1,0},{2,3},{3,2},{4,5},{5,4},{6,7},{7,6},{8,9},{9,8},{10,11... | collective-permute-start | bytes 7077896 | tf_op jit(solution)/shard_map/ppermute | solution.py:19
  121.5 24.4 %collective-permute-start.14 = (bf16[640,768]{1,0:T(8,128)(2,1)}, bf16[640,768]{1,0:T(8,128)(2,1)S(1)}, u32[]{:S(2)}, u32[]{:S(2)}) collective-permute-start(bf16[640,768]{1,0:T(8,128)(2,1)} %refs_7_.1), channel_id=1, source_target_pairs={{0,16},{8,24},{16,0},{24,8},{1,17},{9,25},{17,1},{25,9},{2,18},{10... | collective-permute-start | bytes 2949128 | tf_op jit(solution)/shard_map/ppermute | solution.py:19
  123.1 24.7 %collective-permute-start.13 = (bf16[640,768]{1,0:T(8,128)(2,1)}, bf16[640,768]{1,0:T(8,128)(2,1)S(1)}, u32[]{:S(2)}, u32[]{:S(2)}) collective-permute-start(bf16[640,768]{1,0:T(8,128)(2,1)} %refs_7_.1), channel_id=1, source_target_pairs={{0,8},{8,0},{16,24},{24,16},{1,9},{9,1},{17,25},{25,17},{2,10},{10... | collective-permute-start | bytes 2949128 | tf_op jit(solution)/shard_map/ppermute | solution.py:19
  173.7 43.8 %collective-permute-start.24 = (f32[512,768]{1,0:T(8,128)}, f32[512,768]{1,0:T(8,128)}, u32[]{:S(2)}, u32[]{:S(2)}) collective-permute-start(f32[512,768]{1,0:T(8,128)} %get-tuple-element.50), channel_id=1, source_target_pairs={{0,1},{1,0},{2,3},{3,2},{4,5},{5,4},{6,7},{7,6},{8,9},{9,8},{10,11... | collective-permute-start | bytes 4718600 | tf_op jit(solution)/shard_map/ppermute | solution.py:19
  175.1 51.8 %collective-permute-start.17 = (bf16[128,5120]{1,0:T(8,128)(2,1)}, bf16[128,5120]{1,0:T(8,128)(2,1)}, u32[]{:S(2)}, u32[]{:S(2)}) collective-permute-start(bf16[128,5120]{1,0:T(8,128)(2,1)} %fusion.3), channel_id=1, source_target_pairs={{0,8},{8,0},{16,24},{24,16},{1,9},{9,1},{17,25},{25,17},{2,10},{10... | collective-permute-start | bytes 3932168 | tf_op jit(solution)/shard_map/ppermute | solution.py:19
  176.1 27.2 %collective-permute-start.19 = (bf16[768,640]{1,0:T(8,128)(2,1)}, bf16[768,640]{1,0:T(8,128)(2,1)}, u32[]{:S(2)}, u32[]{:S(2)}) collective-permute-start(bf16[768,640]{1,0:T(8,128)(2,1)} %refs_5_.1), channel_id=1, source_target_pairs={{0,2},{2,4},{4,6},{1,3},{3,5},{5,7},{8,10},{10,12},{12,14},{9,11},... | collective-permute-start | bytes 2949128 | tf_op jit(solution)/shard_map/ppermute | solution.py:459
  182.4 26.0 %collective-permute-start.20 = (bf16[768,640]{1,0:T(8,128)(2,1)}, bf16[768,640]{1,0:T(8,128)(2,1)}, u32[]{:S(2)}, u32[]{:S(2)}) collective-permute-start(bf16[768,640]{1,0:T(8,128)(2,1)} %refs_5_.1), channel_id=1, source_target_pairs={{2,0},{4,2},{6,4},{3,1},{5,3},{7,5},{10,8},{12,10},{14,12},{11,9},... | collective-permute-start | bytes 2949128 | tf_op jit(solution)/shard_map/ppermute | solution.py:460
  183.7 26.2 %all-to-all-start = ((f32[4,2,512]{2,1,0:T(2,128)}), f32[4,2,512]{2,1,0:T(2,128)S(1)}, u32[]{:S(2)}, u32[]{:S(2)}) async-start(f32[4,2,512]{2,1,0:T(2,128)} %norms.1), calls=%async_computation | async-start | bytes 32768 | tf_op jit(solution)/shard_map/all_to_all | solution.py:445
  203.2 30.8 %collective-permute-start.29 = (bf16[768,640]{1,0:T(8,128)(2,1)}, bf16[768,640]{1,0:T(8,128)(2,1)}, u32[]{:S(2)}, u32[]{:S(2)}) collective-permute-start(bf16[768,640]{1,0:T(8,128)(2,1)} %collective-permute-done.19), channel_id=1, source_target_pairs={{2,4},{4,6},{3,5},{5,7},{10,12},{12,14},{11,13},{13,15},{18,20},{2... | collective-permute-start | bytes 2949128 | tf_op jit(solution)/shard_map/ppermute | solution.py:459
  208.4 31.1 %collective-permute-start.30 = (bf16[768,640]{1,0:T(8,128)(2,1)}, bf16[768,640]{1,0:T(8,128)(2,1)}, u32[]{:S(2)}, u32[]{:S(2)}) collective-permute-start(bf16[768,640]{1,0:T(8,128)(2,1)} %collective-permute-done.20), channel_id=1, source_target_pairs={{2,0},{4,2},{3,1},{5,3},{10,8},{12,10},{11,9},{13,11},{18,16},{20,... | collective-permute-start | bytes 2949128 | tf_op jit(solution)/shard_map/ppermute | solution.py:460
  222.4 27.7 %all-to-all-start.1 = ((bf16[4,128,768]{2,1,0:T(8,128)(2,1)}), bf16[4,128,768]{2,1,0:T(8,128)(2,1)S(1)}, u32[]{:S(2)}, u32[]{:S(2)}) async-start(bf16[4,128,768]{2,1,0:T(8,128)(2,1)} %attend.1), calls=%async_computation.1 | async-start | bytes 1572864 | tf_op jit(solution)/shard_map/all_to_all | solution.py:457
  229.8 32.7 %collective-permute-start.18 = (bf16[128,5120]{1,0:T(8,128)(2,1)}, bf16[128,5120]{1,0:T(8,128)(2,1)}, u32[]{:S(2)}, u32[]{:S(2)}) collective-permute-start(bf16[128,5120]{1,0:T(8,128)(2,1)} %fusion.2), channel_id=1, source_target_pairs={{0,16},{8,24},{16,0},{24,8},{1,17},{9,25},{17,1},{25,9},{2,18},{10... | collective-permute-start | bytes 3932168 | tf_op jit(solution)/shard_map/ppermute | solution.py:19
  232.5 27.9 %collective-permute-start.22 = (f32[1,5248]{1,0:T(1,128)S(1)}, f32[1,5248]{1,0:T(1,128)S(1)}, u32[]{:S(2)}, u32[]{:S(2)}) collective-permute-start(f32[1,5248]{1,0:T(1,128)S(1)} %broadcast_in_dim.16), channel_id=1, source_target_pairs={{0,16},{8,24},{16,0},{24,8},{1,17},{9,25},{17,1},{25,9},{2,18},{10... | collective-permute-start | bytes 62984 | tf_op jit(solution)/shard_map/ppermute | solution.py:19
  234.0 27.7 %collective-permute-start.21 = (f32[1,5248]{1,0:T(1,128)S(1)}, f32[1,5248]{1,0:T(1,128)}, u32[]{:S(2)}, u32[]{:S(2)}) collective-permute-start(f32[1,5248]{1,0:T(1,128)S(1)} %broadcast_in_dim.16), channel_id=1, source_target_pairs={{0,8},{8,0},{16,24},{24,16},{1,9},{9,1},{17,25},{25,17},{2,10},{10... | collective-permute-start | bytes 62984 | tf_op jit(solution)/shard_map/ppermute | solution.py:19
  251.8 36.9 %collective-permute-start.33 = (bf16[768,640]{1,0:T(8,128)(2,1)}, bf16[768,640]{1,0:T(8,128)(2,1)}, u32[]{:S(2)}, u32[]{:S(2)}) collective-permute-start(bf16[768,640]{1,0:T(8,128)(2,1)} %refs_5_.1), channel_id=1, source_target_pairs={{0,1},{1,0},{2,3},{3,2},{4,5},{5,4},{6,7},{7,6},{8,9},{9,8},{10,11... | collective-permute-start | bytes 2949128 | tf_op jit(solution)/shard_map/ppermute | solution.py:19
  266.4 25.2 %collective-permute-start.35 = (bf16[768,640]{1,0:T(8,128)(2,1)}, bf16[768,640]{1,0:T(8,128)(2,1)}, u32[]{:S(2)}, u32[]{:S(2)}) collective-permute-start(bf16[768,640]{1,0:T(8,128)(2,1)} %broadcast_select_fusion.1.refs_7_), channel_id=1, source_target_pairs={{0,1},{1,0},{2,3},{3,2},{4,5},{5,4},{6,7},{7,6},{8,9},{9,8},{10,11... | collective-permute-start | bytes 2949128 | tf_op jit(solution)/shard_map/ppermute | solution.py:19
  312.3 34.6 %all-to-all-start.2 = ((bf16[4,2,128,1280]{3,2,1,0:T(8,128)(2,1)}), bf16[4,2,128,1280]{3,2,1,0:T(8,128)(2,1)}, u32[]{:S(2)}, u32[]{:S(2)}) async-start(bf16[4,2,128,1280]{3,2,1,0:T(8,128)(2,1)} %project_out.1), calls=%async_computation.2 | async-start | bytes 5242880 | tf_op jit(solution)/shard_map/all_to_all | solution.py:487
  (42 other events, 676.5 us)

commit v6 on v5

--- a/solution.py
+++ b/solution.py
@@ -43,21 +43,59 @@
     return [held[offset] for offset in range(lax.axis_size("step"))]
 
 
-def listed(held):
-    return [piece for pieces in (held.values() if isinstance(held, dict) else held) for piece in pieces]
+def placed(held, column=0):
+    found = []
+    for offset, pieces in enumerate(held):
+        row = 0
+        for piece in pieces:
+            found.append((piece, offset, row, 0, column, piece.shape[1]))
+            row += piece.shape[0]
+    return found
+
+
+def in_rounds(w_both, w_value, line_hops):
+    width = w_value.shape[1]
+    part = width // 768 * 256
+    rest = width - part
+    a1, a2 = swap(w_both, "step", 1), swap(w_both, "step", 2)
+    hop = line_hops((a1, a2))
+    a1, a2 = after((a1, a2), *hop)
+    b1 = swap(jnp.concatenate([a2[:, :width], w_value[:, :part]], axis=1), "step", 1)
+    b2 = swap(jnp.concatenate([a1[:, width:], w_value[:, :part]], axis=1), "step", 2)
+    hop = line_hops((b1, b2))
+    e1, e2 = after((b1, b2), *hop)
+    middle = width + part // 2
+    c1 = swap(jnp.concatenate([w_value[:, part:], e2[:, width:middle]], axis=1), "step", 1)
+    c2 = swap(jnp.concatenate([w_value[:, part:], e1[:, middle:]], axis=1), "step", 2)
+    both = [
+        (w_both, 0, 0, 0, 0, 2 * width),
+        (a1, 1, 0, 0, 0, 2 * width),
+        (a2, 2, 0, 0, 0, 2 * width),
+        (b1, 3, 0, 0, 0, width),
+        (b2, 3, 0, 0, width, width),
+    ]
+
+    def finished(*awaited):
+        f1, f2 = after((c1, c2), *awaited)
+        d1 = swap(f2[:, : rest // 2], "step", 1)
+        d2 = swap(f1[:, rest // 2 : rest], "step", 2)
+        return [
+            (w_value, 0, 0, 0, 0, width),
+            (b1, 1, 0, width, 0, part),
+            (c1, 1, 0, 0, part, rest),
+            (b2, 2, 0, width, 0, part),
+            (c2, 2, 0, 0, part, rest),
+            (c1, 3, 0, rest, 0, part // 2),
+            (c2, 3, 0, rest, part // 2, part // 2),
+            (d1, 3, 0, 0, part, rest // 2),
+            (d2, 3, 0, 0, part + rest // 2, rest // 2),
+        ]
+
+    return both, (c1, c2), finished
 
 
 def after(x, *others):
     return lax.optimization_barrier((x,) + others)[0]
-
-
-def along_line(x):
-    size = lax.axis_size("head")
-    below, above = [x], [x]
-    for hop in range(1, size):
-        below.append(lax.ppermute(below[-1], "head", [(i, i + 1) for i in range(hop - 1, size - 1)]))
-        above.append(lax.ppermute(above[-1], "head", [(i, i - 1) for i in range(1, size - hop + 1)]))
-    return below, above
 
 
 def params(mib=56):
@@ -107,7 +145,7 @@
     )(place, states, rows)
 
 
-def project_kernel(size, parts, layout, place, *refs):
+def project_kernel(size, parts, shard, layout, place, *refs):
     count = 2 * size - 1
     own, below, above = refs[0], refs[1:size], refs[size:count]
     weights = refs[count : count + len(layout)]
@@ -124,9 +162,11 @@
         )
 
     def w_copies():
-        for index, (ref, (offset, whole, start, rows)) in enumerate(zip(weights, layout)):
-            at = jnp.bitwise_xor(step_at, offset) * whole + start
-            yield pltpu.make_async_copy(ref, w_held.at[pl.ds(pl.multiple_of(at, rows), rows)], w_sems.at[index])
+        for index, (ref, (offset, row, source, target, count)) in enumerate(zip(weights, layout)):
+            at = jnp.bitwise_xor(step_at, offset) * shard + row
+            rows = ref.shape[0]
+            part = w_held.at[pl.ds(pl.multiple_of(at, rows), rows), pl.ds(target, count)]
+            yield pltpu.make_async_copy(ref.at[:, pl.ds(source, count)], part, w_sems.at[index])
 
     for copy in w_copies():
         copy.start()
@@ -164,19 +204,14 @@
     below, above = line
     operands = [below[0]] + below[1:] + above[1:]
     _, tokens, depth = operands[0].shape
-    layout, weights = [], []
-    for offset, pieces in enumerate(shards):
-        start = 0
-        for piece in pieces:
-            layout.append((offset, depth // len(shards), start, piece.shape[0]))
-            weights.append(piece)
-            start += piece.shape[0]
-    columns = weights[0].shape[1]
+    weights = [piece[0] for piece in shards]
+    layout = [piece[1:] for piece in shards]
+    shard, columns = weights[0].shape
     rows = {"first": size - 1, "last": 1, "all": size}[parts] * tokens
     out = jax.ShapeDtypeStruct((rows, columns), jnp.float32)
     moved = 2 * depth * (2 * rows + columns) + 8 * rows * columns
     return pl.pallas_call(
-        functools.partial(project_kernel, size, parts, tuple(layout)),
+        functools.partial(project_kernel, size, parts, shard, tuple(layout)),
         in_specs=[SMEM] + [ANY] * (len(operands) + len(weights)),
         out_specs=[VMEM, VMEM],
         out_shape=[out, out],
@@ -428,43 +463,73 @@
 
     mine, other = modulate(place, current, modulation, steps)
     tokens = jnp.stack([mine, swap(other, "fsdp", 1)])
-    line = along_line(tokens)
+    below, above = [tokens], [tokens]
+
+    def hop(awaited=()):
+        count = len(below)
+        up, down = below[-1], above[-1]
+        if awaited:
+            up, down = after((up, down), *awaited)
+        below.append(lax.ppermute(up, "head", [(i, i + 1) for i in range(count - 1, size - 1)]))
+        above.append(lax.ppermute(down, "head", [(i, i - 1) for i in range(1, size - count + 1)]))
+        return below[-1], above[-1]
+
+    w_both = jnp.concatenate([w_query, w_key], axis=1)
+    hop()
+    if steps == 4 and size > 3 and w_value.shape[1] % 768 == 0:
+
+        def line_hops(awaited):
+            arrived = (below[-1], above[-1])
+            hop(awaited)
+            return arrived
+
+        both_shards, last_round, finished = in_rounds(w_both, w_value, line_hops)
+    else:
+        both = forwarded(w_both, direct(w_both))
+        both_shards = placed(both)
+        last_round = tuple(both[-1])
+
+        def finished(*awaited):
+            return placed(forwarded(w_value, direct(after(w_value, *awaited))))
+
+    while len(below) < size:
+        hop()
+    line = below, above
     early = tuple(held[: size - 1] + [held[0]] for held in line)
-
-    w_both = after(jnp.concatenate([w_query, w_key], axis=1), tokens)
-    both_shards = forwarded(w_both, direct(w_both), line[0][1], line[1][1])
     first_here, first_there = project(place, early, both_shards, "first", "first")
-    v_near = direct(after(w_value, *listed(both_shards)))
-    v_shards = forwarded(w_value, v_near, first_here)
-
-    first_there = after(first_there, line[0][-1], line[1][-1])
+    ended = (below[-1], above[-1]) + last_round
+    first_there = after(first_there, *ended)
+    v_shards = finished(*ended, first_here)
     parts = [first_here, swap(first_there, "fsdp", 1)]
     last_here, last_there = project(place, line, both_shards, "last", "last")
-    parts += [last_here, swap(last_there, "fsdp", 1)]
+    parts += [last_here, swap(after(last_there, v_shards[-1][0], v_shards[-2][0]), "fsdp", 1)]
     own_squares = norms(place, parts, size)
     squares = lax.all_to_all(own_squares, "head", 0, 0)
-    v_here, v_there = project(after(place, own_squares), line, v_shards, "all", "value")
-    v_parts = [v_here, swap(v_there, "fsdp", 1)]
 
     below, above = [w_out], [w_out]
-    for hop in range(1, size):
+    for count in range(1, size):
         up, down = below[-1], above[-1]
-        if hop == 1:
-            up, down = after((up, down), line[0][-1], line[1][-1], first_here)
-        if hop == size - 1:
-            probs = probabilities(place, after(squares, v_here, below[1], above[1]), parts, q_gain, k_gain)
-            attended = attend(place, probs, v_parts, size)
+        if count == 1:
+            up, down = after((up, down), *ended, first_here)
+        if count == size - 1:
+            up, down = after((up, down), quarter)
+        below.append(lax.ppermute(up, "head", [(i, i + 1) for i in range(count - 1, size - 1)]))
+        above.append(lax.ppermute(down, "head", [(i, i - 1) for i in range(1, size - count + 1)]))
+        if count == 1:
+            v_place = after(place, own_squares, below[-1], above[-1])
+            v_here, v_there = project(v_place, line, v_shards, "all", "value")
+            v_parts = [v_here, swap(v_there, "fsdp", 1)]
+            probs = probabilities(place, after(squares, v_here), parts, q_gain, k_gain)
+        if count == size - 2:
+            attended = attend(place, after(probs, below[-1], above[-1]), v_parts, size)
             quarter = lax.all_to_all(attended, "head", 0, 0)
-            up, down = after((up, down), quarter)
-        below.append(lax.ppermute(up, "head", [(i, i + 1) for i in range(hop - 1, size - 1)]))
-        above.append(lax.ppermute(down, "head", [(i, i - 1) for i in range(1, size - hop + 1)]))
 
     step_width = (timesteps[0, 1] - timesteps[0, 0]).astype(jnp.float32) / 1000.0
     carried = step_width * current + jnp.where(step == 0, current, jnp.zeros_like(current))
     base, total = carried, carried
     swapped = []
     for bit in bits_of("step"):
-        swapped.append(swap(after(total.astype(jnp.bfloat16), own_squares, *listed(v_shards)), "step", bit))
+        swapped.append(swap(after(total.astype(jnp.bfloat16), own_squares, v_shards[-1][0], v_shards[-2][0]), "step", bit))
         brought = swapped[-1].astype(jnp.float32)
         base = base + jnp.where(jnp.bitwise_and(step, bit) != 0, brought, jnp.zeros_like(brought))
         total = total + brought

time: 353 us -> 341 us (0.966)
  starting transfers between devices: 61.8 us -> 53.3 us
  waiting for transfers between devices: 188 us -> 180 us
    ppermute x12, waiting for transfers between devices: 93.9 us -> 59.1 us  [the longest x3 26.7 us: hop(): lax.ppermute(up, 'head', [(i, i + 1) for i in range(count - 1, size - 1)])]
    all_to_all x1, waiting for transfers between devices: 0.01 us -> 18.7 us  [body(): squares = lax.all_to_all(own_squares, 'head', 0, 0)]
    ppermute x25, waiting for transfers between devices: 57.2 us -> 68.2 us  [swap(): lax.ppermute(x, axis, [(i, i ^ offset) for i in range(lax.axis_size(axis))])]
    ppermute x12, starting transfers between devices: 24.8 us -> 17.5 us  [the longest x3 5.04 us: hop(): lax.ppermute(up, 'head', [(i, i + 1) for i in range(count - 1, size - 1)])]
    unnamed x51 -> x66, local copies, waits for them, and re-layouts: 7.57 us -> 7.72 us
  transfers between devices with their start and end apart: 40 -> 40, of which waited for: 18 -> 22; matrix products, arithmetic and copies ran while one was open for 6% -> 7% of each run, Pallas kernels for 11% -> 11%
where the time goes in v6:
time: 341 us; the launch traced here: 337 us
  waiting for transfers between devices  180 us (53%)
  Pallas kernels  68.6 us (20%)
  starting transfers between devices  53.3 us (16%)
  other arithmetic  17.4 us (5%)
  local copies, waits for them, and re-layouts  13.5 us (4%)
    ppermute x25, waiting for transfers between devices, swap(): lax.ppermute(x, axis, [(i, i ^ offset) for i in range(lax.axis_size(axis))])  68.2 us
    pallas_call x3, Pallas kernels, project(): pl.pallas_call(functools.partial(project_kernel, size, parts, shard, tupl...  31.5 us
    ppermute x3, waiting for transfers between devices, hop(): lax.ppermute(up, 'head', [(i, i + 1) for i in range(count - 1, size - 1)])  26.7 us
    all_to_all x1, waiting for transfers between devices, body(): arrived = lax.all_to_all(sent, 'step', 0, 0)  23.2 us
    ppermute x25, starting transfers between devices, swap(): lax.ppermute(x, axis, [(i, i ^ offset) for i in range(lax.axis_size(axis))])  20.5 us
    ppermute x3, waiting for transfers between devices, hop(): lax.ppermute(down, 'head', [(i, i - 1) for i in range(1, size - count + 1)])  19.3 us
    all_to_all x1, waiting for transfers between devices, body(): squares = lax.all_to_all(own_squares, 'head', 0, 0)  18.7 us
    pallas_call x1, Pallas kernels, project_out(): pl.pallas_call(functools.partial(out_kernel, size, tuple(layout)), in_spe...  11.8 us
  transfers between devices with their start and end apart: 40, of which 22 were waited for; matrix products, arithmetic and copies ran while one was open for 7% of the time, Pallas kernels for 11%

profile of v6, /device:TPU:0, one launch (start us, length us, event | category | flops | bytes accessed | tf_op | source)
XLA Modules:
  0.0 336.6 jit_solution(7778834180094308217)
XLA Ops:
  3.5 4.6 %modulate.1 = (bf16[128,2560]{1,0:T(8,128)(2,1)}, bf16[128,2560]{1,0:T(8,128)(2,1)}) custom-call(s32[5]{0:T(128)} %stack.32.place, f32[128,5120]{1,0:T(8,128)} %bitcast.14, f32[1,3,5120]{2,1,0:T(4,128)} %copy.13.rows), custom_call_target="tpu_custom_call" | custom-call | flops 1638400 | bytes 983040 | tf_op jit(solution)/shard_map/modulate/pallas_call | solution.py:136
  17.9 26.7 %collective-permute-done.1.refs_1_ = bf16[2,128,2560]{2,1,0:T(8,128)(2,1)S(1)} collective-permute-done((bf16[2,128,2560]{2,1,0:T(8,128)(2,1)S(1)}, bf16[2,128,2560]{2,1,0:T(8,128)(2,1)S(1)}, u32[]{:S(2)}, u32[]{:S(2)}) %collective-permute-start.1) | collective-permute-done | bytes 1310752 | tf_op jit(solution)/shard_map/ppermute | solution.py:473
  44.6 4.2 %collective-permute-done.2.refs_4_ = bf16[2,128,2560]{2,1,0:T(8,128)(2,1)S(1)} collective-permute-done((bf16[2,128,2560]{2,1,0:T(8,128)(2,1)S(1)}, bf16[2,128,2560]{2,1,0:T(8,128)(2,1)S(1)}, u32[]{:S(2)}, u32[]{:S(2)}) %collective-permute-start.2) | collective-permute-done | bytes 1310752 | tf_op jit(solution)/shard_map/ppermute | solution.py:474
  48.8 6.0 %collective-permute-done.3.refs_8_ = bf16[640,1536]{1,0:T(8,128)(2,1)S(1)} collective-permute-done((bf16[640,1536]{1,0:T(8,128)(2,1)S(1)}, bf16[640,1536]{1,0:T(8,128)(2,1)S(1)}, u32[]{:S(2)}, u32[]{:S(2)}) %collective-permute-start.3) | collective-permute-done | bytes 1966112 | tf_op jit(solution)/shard_map/ppermute | solution.py:19
  62.0 25.7 %collective-permute-done.7.refs_10_.refs_8_ = bf16[640,1024]{1,0:T(8,128)(2,1)S(1)} collective-permute-done((bf16[640,1024]{1,0:T(8,128)(2,1)S(1)}, bf16[640,1024]{1,0:T(8,128)(2,1)S(1)}, u32[]{:S(2)}, u32[]{:S(2)}) %collective-permute-start.7) | collective-permute-done | bytes 1310752 | tf_op jit(solution)/shard_map/ppermute | solution.py:19
  88.6 6.3 %collective-permute-done.6.refs_5_ = bf16[2,128,2560]{2,1,0:T(8,128)(2,1)S(1)} collective-permute-done((bf16[2,128,2560]{2,1,0:T(8,128)(2,1)S(1)}, bf16[2,128,2560]{2,1,0:T(8,128)(2,1)S(1)}, u32[]{:S(2)}, u32[]{:S(2)}) %collective-permute-start.6) | collective-permute-done | bytes 1310752 | tf_op jit(solution)/shard_map/ppermute | solution.py:474
  99.5 13.5 %first.1 = (f32[384,1536]{1,0:T(8,128)}, f32[384,1536]{1,0:T(8,128)}) custom-call(s32[5]{0:T(128)} %stack.32.place, bf16[2,128,2560]{2,1,0:T(8,128)(2,1)} %copy-done, bf16[2,128,2560]{2,1,0:T(8,128)(2,1)} %copy-done.8, bf16[2,128,2560]{2,1,0:T(8,128)(2,1)} %copy-done.10, bf16[2,128,2560]{2,1,0:T(8,128)(2,1)} %copy-done, bf16[2,128,2560]{2,1,0:T(8,128)(2,1)} %copy-done.9, ...), custom_call_target="tpu_custom_call" | custom-call | flops 1509949440 | bytes 4128768 | tf_op jit(solution)/shard_map/first/pallas_call | solution.py:213
  116.8 8.9 %collective-permute-done.10.refs_6_ = bf16[2,128,2560]{2,1,0:T(8,128)(2,1)S(1)} collective-permute-done((bf16[2,128,2560]{2,1,0:T(8,128)(2,1)S(1)}, bf16[2,128,2560]{2,1,0:T(8,128)(2,1)S(1)}, u32[]{:S(2)}, u32[]{:S(2)}) %collective-permute-start.10) | collective-permute-done | bytes 1310752 | tf_op jit(solution)/shard_map/ppermute | solution.py:474
  131.7 7.8 %last.1 = (f32[128,1536]{1,0:T(8,128)}, f32[128,1536]{1,0:T(8,128)}) custom-call(s32[5]{0:T(128)} %stack.32.place, bf16[2,128,2560]{2,1,0:T(8,128)(2,1)} %copy-done, bf16[2,128,2560]{2,1,0:T(8,128)(2,1)} %copy-done.8, bf16[2,128,2560]{2,1,0:T(8,128)(2,1)} %copy-done.10, bf16[2,128,2560]{2,1,0:T(8,128)(2,1)} %copy-done.14, bf16[2,128,2560]{2,1,0:T(8,128)(2,1)} %copy-done.9, ...), custom_call_target="tpu_custom_call" | custom-call | flops 503316480 | bytes 2686976 | tf_op jit(solution)/shard_map/last/pallas_call | solution.py:213
  151.0 5.1 %collective-permute-done.20 = bf16[768,640]{1,0:T(8,128)(2,1)} collective-permute-done((bf16[768,640]{1,0:T(8,128)(2,1)}, bf16[768,640]{1,0:T(8,128)(2,1)}, u32[]{:S(2)}, u32[]{:S(2)}) %collective-permute-start.20) | collective-permute-done | bytes 983072 | tf_op jit(solution)/shard_map/ppermute | solution.py:517
  156.1 10.2 %value.1 = (f32[512,768]{1,0:T(8,128)}, f32[512,768]{1,0:T(8,128)}) custom-call(s32[5]{0:T(128)} %stack.32.place, bf16[2,128,2560]{2,1,0:T(8,128)(2,1)} %copy-done, bf16[2,128,2560]{2,1,0:T(8,128)(2,1)} %copy-done.8, bf16[2,128,2560]{2,1,0:T(8,128)(2,1)} %copy-done.10, bf16[2,128,2560]{2,1,0:T(8,128)(2,1)} %copy-done.14, bf16[2,128,2560]{2,1,0:T(8,128)(2,1)} %copy-done.9, ...), custom_call_target="tpu_custom_call" | custom-call | flops 1006632960 | bytes 3080192 | tf_op jit(solution)/shard_map/value/pallas_call | solution.py:213
  172.2 7.3 %all-to-all-start = ((f32[4,2,512]{2,1,0:T(2,128)}), f32[4,2,512]{2,1,0:T(2,128)S(1)}, u32[]{:S(2)}, u32[]{:S(2)}) async-start(f32[4,2,512]{2,1,0:T(2,128)} %norms.1), calls=%async_computation | async-start | bytes 32768 | tf_op jit(solution)/shard_map/all_to_all | solution.py:507
  180.6 18.7 %all-to-all-done.squares = f32[4,2,512]{2,1,0:T(2,128)S(1)} async-done(((f32[4,2,512]{2,1,0:T(2,128)}), f32[4,2,512]{2,1,0:T(2,128)S(1)}, u32[]{:S(2)}, u32[]{:S(2)}) %all-to-all-start) | async-done | bytes 16416 | tf_op jit(solution)/shard_map/all_to_all | solution.py:507
  199.9 7.0 %probs.1 = bf16[6,512,512]{2,1,0:T(8,128)(2,1)} custom-call(s32[5]{0:T(128)} %stack.32.place, f32[4,2,512]{2,1,0:T(2,128)} %copy-done.27, f32[384,1536]{1,0:T(8,128)} %get-tuple-element.41.first_a.refs_0_.refs_4_, f32[384,1536]{1,0:T(8,128)} %copy-done.2, f32[128,1536]{1,0:T(8,128)} %get-tuple-element.48.last_a.refs_2_.refs_6_, f32[128,1536]{1,0:T(8,128)} %copy-done.12, ...), custom_call_target="tpu_custom_call" | custom-call | flops 100663296 | bytes 2359296 | tf_op jit(solution)/shard_map/probs/pallas_call | solution.py:305
  207.0 5.0 %attend.1 = bf16[4,128,768]{2,1,0:T(8,128)(2,1)} custom-call(s32[5]{0:T(128)} %stack.32.place, bf16[6,512,512]{2,1,0:T(8,128)(2,1)} %probs.1, f32[512,768]{1,0:T(8,128)} %get-tuple-element.58.v_a, f32[512,768]{1,0:T(8,128)} %collective-permute-done.26.v_b), custom_call_target="tpu_custom_call" | custom-call | flops 100663296 | bytes 1769472 | tf_op jit(solution)/shard_map/attend/pallas_call | solution.py:334
  223.4 11.3 %all-to-all-done.1.refs_0_ = bf16[4,128,768]{2,1,0:T(8,128)(2,1)S(1)} async-done(((bf16[4,128,768]{2,1,0:T(8,128)(2,1)}), bf16[4,128,768]{2,1,0:T(8,128)(2,1)S(1)}, u32[]{:S(2)}, u32[]{:S(2)}) %all-to-all-start.1) | async-done | bytes 786464 | tf_op jit(solution)/shard_map/all_to_all | solution.py:525
  236.1 12.8 %collective-permute-done.22 = f32[1,5248]{1,0:T(1,128)S(1)} collective-permute-done((f32[1,5248]{1,0:T(1,128)S(1)}, f32[1,5248]{1,0:T(1,128)S(1)}, u32[]{:S(2)}, u32[]{:S(2)}) %collective-permute-start.22) | collective-permute-done | bytes 21024 | tf_op jit(solution)/shard_map/ppermute | solution.py:19
  254.3 5.3 %collective-permute-done.32 = bf16[768,640]{1,0:T(8,128)(2,1)} collective-permute-done((bf16[768,640]{1,0:T(8,128)(2,1)}, bf16[768,640]{1,0:T(8,128)(2,1)}, u32[]{:S(2)}, u32[]{:S(2)}) %collective-permute-start.32) | collective-permute-done | bytes 983072 | tf_op jit(solution)/shard_map/ppermute | solution.py:517
  268.7 8.5 %collective-permute-done.27.refs_1_ = bf16[4,128,768]{2,1,0:T(8,128)(2,1)S(1)} collective-permute-done((bf16[4,128,768]{2,1,0:T(8,128)(2,1)S(1)}, bf16[4,128,768]{2,1,0:T(8,128)(2,1)S(1)}, u32[]{:S(2)}, u32[]{:S(2)}) %collective-permute-start.27) | collective-permute-done | bytes 786464 | tf_op jit(solution)/shard_map/ppermute | solution.py:19
  288.1 11.8 %project_out.1 = bf16[4,2,128,1280]{3,2,1,0:T(8,128)(2,1)} custom-call(s32[5]{0:T(128)} %stack.32.place, f32[4]{0:T(128)} %slice_reduce_fusion.widths, bf16[4,128,768]{2,1,0:T(8,128)(2,1)} %copy-done.17, bf16[4,128,768]{2,1,0:T(8,128)(2,1)} %copy-done.19, bf16[4,128,768]{2,1,0:T(8,128)(2,1)} %copy-done.18, bf16[2,128,768]{2,1,0:T(8,128)(2,1)} %copy-done.23, ...), custom_call_target="tpu_custom_call" | custom-call | flops 1006632960 | bytes 3407872 | tf_op jit(solution)/shard_map/project_out/pallas_call | solution.py:419
  299.9 4.6 %all-to-all-start.2 = ((bf16[4,2,128,1280]{3,2,1,0:T(8,128)(2,1)}), bf16[4,2,128,1280]{3,2,1,0:T(8,128)(2,1)}, u32[]{:S(2)}, u32[]{:S(2)}) async-start(bf16[4,2,128,1280]{3,2,1,0:T(8,128)(2,1)} %project_out.1), calls=%async_computation.2 | async-start | bytes 5242880 | tf_op jit(solution)/shard_map/all_to_all | solution.py:552
  304.5 4.1 %fusion.1.base = f32[128,5120]{1,0:T(8,128)} fusion(bf16[128,5120]{1,0:T(8,128)(2,1)} %collective-permute-done.17, bf16[128,5120]{1,0:T(8,128)(2,1)} %collective-permute-done.18, f32[]{:T(128)} %bitcast, pred[]{:T(512)S(6)} %ne.7, pred[]{:T(512)S(6)} %ne.6, pred[]{:T(512)S(6)} %eq.3, f32[1,1,128,5120]{3,2,1,0:T(8,128)S(1)} %copy-done.1), kind=kLoop, calls=%fused_computation.3 | loop fusion | flops 5898240 | bytes 7864327 | tf_op jit(solution)/shard_map/add | solution.py:534
  308.5 23.2 %all-to-all-done.2.arrived = bf16[4,2,128,1280]{3,2,1,0:T(8,128)(2,1)} async-done(((bf16[4,2,128,1280]{3,2,1,0:T(8,128)(2,1)}), bf16[4,2,128,1280]{3,2,1,0:T(8,128)(2,1)}, u32[]{:S(2)}, u32[]{:S(2)}) %all-to-all-start.2) | async-done | bytes 2621472 | tf_op jit(solution)/shard_map/all_to_all | solution.py:552
  331.7 4.8 %finish.1 = (f32[128,5120]{1,0:T(8,128)}, bf16[128,5120]{1,0:T(8,128)(2,1)}) custom-call(f32[128,5120]{1,0:T(8,128)} %fusion.1.base, bf16[4,2,128,1280]{3,2,1,0:T(8,128)(2,1)} %all-to-all-done.2.arrived), custom_call_target="tpu_custom_call" | custom-call | flops 163840 | bytes 2293760 | tf_op jit(solution)/shard_map/finish/pallas_call | solution.py:445
  (164 shorter events, 90.1 us)
Async XLA Ops:
  8.8 46.1 %collective-permute-start.3 = (bf16[640,1536]{1,0:T(8,128)(2,1)S(1)}, bf16[640,1536]{1,0:T(8,128)(2,1)S(1)}, u32[]{:S(2)}, u32[]{:S(2)}) collective-permute-start(bf16[640,1536]{1,0:T(8,128)(2,1)S(1)} %constant_dynamic-update-slice_fusion.refs_7_), channel_id=1, source_target_pairs={{0,8},{8,0},{16,24},{24,16},{1,9},{9,1},{17,25},{25,17},{2,10},{10... | collective-permute-start | bytes 5898248 | tf_op jit(solution)/shard_map/ppermute | solution.py:19
  11.3 44.9 %collective-permute-start.4 = (bf16[640,1536]{1,0:T(8,128)(2,1)S(1)}, bf16[640,1536]{1,0:T(8,128)(2,1)S(1)}, u32[]{:S(2)}, u32[]{:S(2)}) collective-permute-start(bf16[640,1536]{1,0:T(8,128)(2,1)S(1)} %constant_dynamic-update-slice_fusion.refs_7_), channel_id=1, source_target_pairs={{0,16},{8,24},{16,0},{24,8},{1,17},{9,25},{17,1},{25,9},{2,18},{10... | collective-permute-start | bytes 5898248 | tf_op jit(solution)/shard_map/ppermute | solution.py:19
  13.0 31.6 %collective-permute-start.1 = (bf16[2,128,2560]{2,1,0:T(8,128)(2,1)S(1)}, bf16[2,128,2560]{2,1,0:T(8,128)(2,1)S(1)}, u32[]{:S(2)}, u32[]{:S(2)}) collective-permute-start(bf16[2,128,2560]{2,1,0:T(8,128)(2,1)S(1)} %pad_maximum_fusion.2.refs_0_.refs_3_.refs_6_), channel_id=1, source_target_pairs={{0,2},{2,4},{4,6},{1,3},{3,5},{5,7},{8,10},{10,12},{12,14},{9,11},... | collective-permute-start | bytes 3932168 | tf_op jit(solution)/shard_map/ppermute | solution.py:473
  16.6 32.2 %collective-permute-start.2 = (bf16[2,128,2560]{2,1,0:T(8,128)(2,1)S(1)}, bf16[2,128,2560]{2,1,0:T(8,128)(2,1)S(1)}, u32[]{:S(2)}, u32[]{:S(2)}) collective-permute-start(bf16[2,128,2560]{2,1,0:T(8,128)(2,1)S(1)} %pad_maximum_fusion.2.refs_0_.refs_3_.refs_6_), channel_id=1, source_target_pairs={{2,0},{4,2},{6,4},{3,1},{5,3},{7,5},{10,8},{12,10},{14,12},{11,9},... | collective-permute-start | bytes 3932168 | tf_op jit(solution)/shard_map/ppermute | solution.py:474
  57.6 30.1 %collective-permute-start.7 = (bf16[640,1024]{1,0:T(8,128)(2,1)S(1)}, bf16[640,1024]{1,0:T(8,128)(2,1)S(1)}, u32[]{:S(2)}, u32[]{:S(2)}) collective-permute-start(bf16[640,1024]{1,0:T(8,128)(2,1)S(1)} %get-tuple-element.71), channel_id=1, source_target_pairs={{0,8},{8,0},{16,24},{24,16},{1,9},{9,1},{17,25},{25,17},{2,10},{10... | collective-permute-start | bytes 3932168 | tf_op jit(solution)/shard_map/ppermute | solution.py:19
  58.4 30.1 %collective-permute-start.8 = (bf16[640,1024]{1,0:T(8,128)(2,1)S(1)}, bf16[640,1024]{1,0:T(8,128)(2,1)S(1)}, u32[]{:S(2)}, u32[]{:S(2)}) collective-permute-start(bf16[640,1024]{1,0:T(8,128)(2,1)S(1)} %get-tuple-element.70), channel_id=1, source_target_pairs={{0,16},{8,24},{16,0},{24,8},{1,17},{9,25},{17,1},{25,9},{2,18},{10... | collective-permute-start | bytes 3932168 | tf_op jit(solution)/shard_map/ppermute | solution.py:19
  59.9 28.6 %collective-permute-start.5 = (bf16[2,128,2560]{2,1,0:T(8,128)(2,1)S(1)}, bf16[2,128,2560]{2,1,0:T(8,128)(2,1)S(1)}, u32[]{:S(2)}, u32[]{:S(2)}) collective-permute-start(bf16[2,128,2560]{2,1,0:T(8,128)(2,1)S(1)} %collective-permute-done.1.refs_1_), channel_id=1, source_target_pairs={{2,4},{4,6},{3,5},{5,7},{10,12},{12,14},{11,13},{13,15},{18,20},{2... | collective-permute-start | bytes 3932168 | tf_op jit(solution)/shard_map/ppermute | solution.py:473
  60.7 34.1 %collective-permute-start.6 = (bf16[2,128,2560]{2,1,0:T(8,128)(2,1)S(1)}, bf16[2,128,2560]{2,1,0:T(8,128)(2,1)S(1)}, u32[]{:S(2)}, u32[]{:S(2)}) collective-permute-start(bf16[2,128,2560]{2,1,0:T(8,128)(2,1)S(1)} %collective-permute-done.2.refs_4_), channel_id=1, source_target_pairs={{2,0},{4,2},{3,1},{5,3},{10,8},{12,10},{11,9},{13,11},{18,16},{20,... | collective-permute-start | bytes 3932168 | tf_op jit(solution)/shard_map/ppermute | solution.py:474
  94.8 30.8 %collective-permute-start.10 = (bf16[2,128,2560]{2,1,0:T(8,128)(2,1)S(1)}, bf16[2,128,2560]{2,1,0:T(8,128)(2,1)S(1)}, u32[]{:S(2)}, u32[]{:S(2)}) collective-permute-start(bf16[2,128,2560]{2,1,0:T(8,128)(2,1)S(1)} %collective-permute-done.6.refs_5_), channel_id=1, source_target_pairs={{2,0},{3,1},{10,8},{11,9},{18,16},{19,17},{26,24},{27,25}} | collective-permute-start | bytes 3932168 | tf_op jit(solution)/shard_map/ppermute | solution.py:474
  96.1 29.5 %collective-permute-start.9 = (bf16[2,128,2560]{2,1,0:T(8,128)(2,1)S(1)}, bf16[2,128,2560]{2,1,0:T(8,128)(2,1)S(1)}, u32[]{:S(2)}, u32[]{:S(2)}) collective-permute-start(bf16[2,128,2560]{2,1,0:T(8,128)(2,1)S(1)} %collective-permute-done.5.refs_2_), channel_id=1, source_target_pairs={{4,6},{5,7},{12,14},{13,15},{20,22},{21,23},{28,30},{29,31}} | collective-permute-start | bytes 3932168 | tf_op jit(solution)/shard_map/ppermute | solution.py:473
  130.4 25.6 %collective-permute-start.20 = (bf16[768,640]{1,0:T(8,128)(2,1)}, bf16[768,640]{1,0:T(8,128)(2,1)}, u32[]{:S(2)}, u32[]{:S(2)}) collective-permute-start(bf16[768,640]{1,0:T(8,128)(2,1)} %refs_5_.1), channel_id=1, source_target_pairs={{2,0},{4,2},{6,4},{3,1},{5,3},{7,5},{10,8},{12,10},{14,12},{11,9},... | collective-permute-start | bytes 2949128 | tf_op jit(solution)/shard_map/ppermute | solution.py:517
  166.3 40.6 %collective-permute-start.26 = (f32[512,768]{1,0:T(8,128)}, f32[512,768]{1,0:T(8,128)}, u32[]{:S(2)}, u32[]{:S(2)}) collective-permute-start(f32[512,768]{1,0:T(8,128)} %get-tuple-element.62), channel_id=1, source_target_pairs={{0,1},{1,0},{2,3},{3,2},{4,5},{5,4},{6,7},{7,6},{8,9},{9,8},{10,11... | collective-permute-start | bytes 4718600 | tf_op jit(solution)/shard_map/ppermute | solution.py:19
  167.8 47.7 %collective-permute-start.17 = (bf16[128,5120]{1,0:T(8,128)(2,1)}, bf16[128,5120]{1,0:T(8,128)(2,1)}, u32[]{:S(2)}, u32[]{:S(2)}) collective-permute-start(bf16[128,5120]{1,0:T(8,128)(2,1)} %fusion.3), channel_id=1, source_target_pairs={{0,8},{8,0},{16,24},{24,16},{1,9},{9,1},{17,25},{25,17},{2,10},{10... | collective-permute-start | bytes 3932168 | tf_op jit(solution)/shard_map/ppermute | solution.py:19
  169.3 37.7 %collective-permute-start.24 = (bf16[768,640]{1,0:T(8,128)(2,1)}, bf16[768,640]{1,0:T(8,128)(2,1)}, u32[]{:S(2)}, u32[]{:S(2)}) collective-permute-start(bf16[768,640]{1,0:T(8,128)(2,1)} %collective-permute-done.19), channel_id=1, source_target_pairs={{2,4},{4,6},{3,5},{5,7},{10,12},{12,14},{11,13},{13,15},{18,20},{2... | collective-permute-start | bytes 2949128 | tf_op jit(solution)/shard_map/ppermute | solution.py:516
  170.9 36.0 %collective-permute-start.25 = (bf16[768,640]{1,0:T(8,128)(2,1)}, bf16[768,640]{1,0:T(8,128)(2,1)}, u32[]{:S(2)}, u32[]{:S(2)}) collective-permute-start(bf16[768,640]{1,0:T(8,128)(2,1)} %collective-permute-done.20), channel_id=1, source_target_pairs={{2,0},{4,2},{3,1},{5,3},{10,8},{12,10},{11,9},{13,11},{18,16},{20,... | collective-permute-start | bytes 2949128 | tf_op jit(solution)/shard_map/ppermute | solution.py:517
  172.2 27.1 %all-to-all-start = ((f32[4,2,512]{2,1,0:T(2,128)}), f32[4,2,512]{2,1,0:T(2,128)S(1)}, u32[]{:S(2)}, u32[]{:S(2)}) async-start(f32[4,2,512]{2,1,0:T(2,128)} %norms.1), calls=%async_computation | async-start | bytes 32768 | tf_op jit(solution)/shard_map/all_to_all | solution.py:507
  218.3 32.1 %collective-permute-start.18 = (bf16[128,5120]{1,0:T(8,128)(2,1)}, bf16[128,5120]{1,0:T(8,128)(2,1)}, u32[]{:S(2)}, u32[]{:S(2)}) collective-permute-start(bf16[128,5120]{1,0:T(8,128)(2,1)} %fusion.2), channel_id=1, source_target_pairs={{0,16},{8,24},{16,0},{24,8},{1,17},{9,25},{17,1},{25,9},{2,18},{10... | collective-permute-start | bytes 3932168 | tf_op jit(solution)/shard_map/ppermute | solution.py:19
  220.5 28.4 %collective-permute-start.22 = (f32[1,5248]{1,0:T(1,128)S(1)}, f32[1,5248]{1,0:T(1,128)S(1)}, u32[]{:S(2)}, u32[]{:S(2)}) collective-permute-start(f32[1,5248]{1,0:T(1,128)S(1)} %broadcast_in_dim.16), channel_id=1, source_target_pairs={{0,16},{8,24},{16,0},{24,8},{1,17},{9,25},{17,1},{25,9},{2,18},{10... | collective-permute-start | bytes 62984 | tf_op jit(solution)/shard_map/ppermute | solution.py:19
  221.0 28.6 %collective-permute-start.23 = (f32[1,5248]{1,0:T(1,128)S(1)}, f32[1,5248]{1,0:T(1,128)}, u32[]{:S(2)}, u32[]{:S(2)}) collective-permute-start(f32[1,5248]{1,0:T(1,128)S(1)} %broadcast_in_dim.16), channel_id=1, source_target_pairs={{0,24},{8,16},{16,8},{24,0},{1,25},{9,17},{17,9},{25,1},{2,26},{10... | collective-permute-start | bytes 62984 | tf_op jit(solution)/shard_map/ppermute | solution.py:19
  234.7 24.9 %collective-permute-start.32 = (bf16[768,640]{1,0:T(8,128)(2,1)}, bf16[768,640]{1,0:T(8,128)(2,1)}, u32[]{:S(2)}, u32[]{:S(2)}) collective-permute-start(bf16[768,640]{1,0:T(8,128)(2,1)} %collective-permute-done.25), channel_id=1, source_target_pairs={{2,0},{3,1},{10,8},{11,9},{18,16},{19,17},{26,24},{27,25}} | collective-permute-start | bytes 2949128 | tf_op jit(solution)/shard_map/ppermute | solution.py:517
  236.0 42.9 %collective-permute-start.33 = (bf16[768,640]{1,0:T(8,128)(2,1)}, bf16[768,640]{1,0:T(8,128)(2,1)}, u32[]{:S(2)}, u32[]{:S(2)}) collective-permute-start(bf16[768,640]{1,0:T(8,128)(2,1)} %refs_5_.1), channel_id=1, source_target_pairs={{0,1},{1,0},{2,3},{3,2},{4,5},{5,4},{6,7},{7,6},{8,9},{9,8},{10,11... | collective-permute-start | bytes 2949128 | tf_op jit(solution)/shard_map/ppermute | solution.py:19
  254.3 27.5 %collective-permute-start.35 = (bf16[768,640]{1,0:T(8,128)(2,1)}, bf16[768,640]{1,0:T(8,128)(2,1)}, u32[]{:S(2)}, u32[]{:S(2)}) collective-permute-start(bf16[768,640]{1,0:T(8,128)(2,1)} %broadcast_select_fusion.1.refs_7_), channel_id=1, source_target_pairs={{0,1},{1,0},{2,3},{3,2},{4,5},{5,4},{6,7},{7,6},{8,9},{9,8},{10,11... | collective-permute-start | bytes 2949128 | tf_op jit(solution)/shard_map/ppermute | solution.py:19
  262.5 24.9 %collective-permute-start.36 = (bf16[768,640]{1,0:T(8,128)(2,1)}, bf16[768,640]{1,0:T(8,128)(2,1)}, u32[]{:S(2)}, u32[]{:S(2)}) collective-permute-start(bf16[768,640]{1,0:T(8,128)(2,1)} %broadcast_select_fusion.refs_8_), channel_id=1, source_target_pairs={{0,1},{1,0},{2,3},{3,2},{4,5},{5,4},{6,7},{7,6},{8,9},{9,8},{10,11... | collective-permute-start | bytes 2949128 | tf_op jit(solution)/shard_map/ppermute | solution.py:19
  299.9 31.8 %all-to-all-start.2 = ((bf16[4,2,128,1280]{3,2,1,0:T(8,128)(2,1)}), bf16[4,2,128,1280]{3,2,1,0:T(8,128)(2,1)}, u32[]{:S(2)}, u32[]{:S(2)}) async-start(bf16[4,2,128,1280]{3,2,1,0:T(8,128)(2,1)} %project_out.1), calls=%async_computation.2 | async-start | bytes 5242880 | tf_op jit(solution)/shard_map/all_to_all | solution.py:552
  (51 other events, 659.6 us)

commit v7 on v6

--- a/solution.py
+++ b/solution.py
@@ -345,8 +345,9 @@
 
 
 def out_kernel(size, layout, place, widths, *refs):
-    pieces, weights = refs[: len(layout)], refs[len(layout) : len(layout) + 2 * size]
-    gates, out, a_held, w_held, total, a_sems, w_sems = refs[len(layout) + 2 * size :]
+    count = 2 * size - 1
+    pieces, weights = refs[: len(layout)], refs[len(layout) : len(layout) + 2 * count]
+    gates, out, a_held, w_held, total, a_sems, w_sems = refs[len(layout) + 2 * count :]
     steps, _, tokens, columns = out.shape
     width = columns // 2
     halves, _, _, span_width = w_held.shape
@@ -354,14 +355,14 @@
     step_at, core, position = place[0], place[1], place[2]
 
     def a_copies():
-        for index, (offset, start, count) in enumerate(layout):
+        for index, (offset, start, groups) in enumerate(layout):
             row = pl.multiple_of(jnp.bitwise_xor(step_at, offset) * tokens, tokens)
-            for group in range(count):
+            for group in range(groups):
                 yield pltpu.make_async_copy(
                     pieces[index].at[group], a_held.at[start + group, pl.ds(row, tokens)], a_sems.at[index, group]
                 )
 
-    def w_copy(half, away):
+    def w_copy(half, away, slot):
         group = lax.rem(position + away, size)
         at = jnp.bitwise_xor(core, half)
         if joined:
@@ -369,19 +370,30 @@
             target = w_held.at[0, group, :, span]
         else:
             target = w_held.at[at, group]
-        return pltpu.make_async_copy(weights[half * size + away], target, w_sems.at[half, away])
+        return pltpu.make_async_copy(weights[half * count + slot], target, w_sems.at[half, away])
 
     for copy in a_copies():
         copy.start()
     for away in range(size):
         for half in range(2):
-            w_copy(half, away).start()
+            if away == 0:
+                w_copy(half, 0, 0).start()
+                continue
+
+            @pl.when(position + away < size)
+            def _(half=half, away=away):
+                w_copy(half, away, size - 1 + away).start()
+
+            @pl.when(position + away >= size)
+            def _(half=half, away=away):
+                w_copy(half, away, size - away).start()
+
     for copy in a_copies():
         copy.wait()
     for away in range(size):
         group = lax.rem(position + away, size)
         for half in range(2):
-            w_copy(half, away).wait()
+            w_copy(half, away, 0).wait()
         for half in range(halves):
             part = jnp.dot(a_held[group], w_held[half, group], preferred_element_type=jnp.float32)
             part = part.astype(jnp.bfloat16).astype(jnp.float32)
@@ -461,7 +473,8 @@
     shift = (position >= size // 2).astype(jnp.int32)
     place = jnp.stack([step, core, position, lengths[0], shift]).astype(jnp.int32)
 
-    mine, other = modulate(place, current, modulation, steps)
+    w_both = jnp.concatenate([w_query, w_key], axis=1)
+    mine, other = modulate(place, after(current, w_both), modulation, steps)
     tokens = jnp.stack([mine, swap(other, "fsdp", 1)])
     below, above = [tokens], [tokens]
 
@@ -474,7 +487,6 @@
         above.append(lax.ppermute(down, "head", [(i, i - 1) for i in range(1, size - count + 1)]))
         return below[-1], above[-1]
 
-    w_both = jnp.concatenate([w_query, w_key], axis=1)
     hop()
     if steps == 4 and size > 3 and w_value.shape[1] % 768 == 0:
 
@@ -497,14 +509,35 @@
     line = below, above
     early = tuple(held[: size - 1] + [held[0]] for held in line)
     first_here, first_there = project(place, early, both_shards, "first", "first")
+
+    step_width = (timesteps[0, 1] - timesteps[0, 0]).astype(jnp.float32) / 1000.0
+    carried = step_width * current + jnp.where(step == 0, current, jnp.zeros_like(current))
+    base, total = carried, carried
+    swapped = []
+
+    def add_states(base, total, bit, awaited):
+        swapped.append(swap(after(total.astype(jnp.bfloat16), *awaited), "step", bit))
+        brought = swapped[-1].astype(jnp.float32)
+        return base + jnp.where(jnp.bitwise_and(step, bit) != 0, brought, jnp.zeros_like(brought)), total + brought
+
+    awaited = (early[0][-2], early[1][-2], both_shards[-1][0], both_shards[-2][0])
+    base, total = add_states(base, total, 1, awaited)
     ended = (below[-1], above[-1]) + last_round
     first_there = after(first_there, *ended)
     v_shards = finished(*ended, first_here)
+    for bit in bits_of("step")[1:]:
+        base, total = add_states(base, total, bit, (v_shards[-1][0], v_shards[-2][0]))
     parts = [first_here, swap(first_there, "fsdp", 1)]
     last_here, last_there = project(place, line, both_shards, "last", "last")
     parts += [last_here, swap(after(last_there, v_shards[-1][0], v_shards[-2][0]), "fsdp", 1)]
     own_squares = norms(place, parts, size)
     squares = lax.all_to_all(own_squares, "head", 0, 0)
+
+    columns = current.shape[1] // steps
+    told = jnp.concatenate([modulation[0, 2], jnp.full((HD,), step_width)])[None]
+    sent_told = after(told, own_squares)
+    heard = jnp.concatenate([told] + [swap(sent_told, "step", offset) for offset in range(1, steps)])
+    gates = lax.dynamic_slice(heard, (0, step * columns), (steps, columns))
 
     below, above = [w_out], [w_out]
     for count in range(1, size):
@@ -516,37 +549,18 @@
         below.append(lax.ppermute(up, "head", [(i, i + 1) for i in range(count - 1, size - 1)]))
         above.append(lax.ppermute(down, "head", [(i, i - 1) for i in range(1, size - count + 1)]))
         if count == 1:
-            v_place = after(place, own_squares, below[-1], above[-1])
+            v_place = after(place, squares, below[-1], above[-1], heard, swapped[-1])
             v_here, v_there = project(v_place, line, v_shards, "all", "value")
             v_parts = [v_here, swap(v_there, "fsdp", 1)]
-            probs = probabilities(place, after(squares, v_here), parts, q_gain, k_gain)
+            probs = probabilities(place, squares, parts, q_gain, k_gain)
         if count == size - 2:
-            attended = attend(place, after(probs, below[-1], above[-1]), v_parts, size)
+            attended = attend(place, probs, v_parts, size)
             quarter = lax.all_to_all(attended, "head", 0, 0)
 
-    step_width = (timesteps[0, 1] - timesteps[0, 0]).astype(jnp.float32) / 1000.0
-    carried = step_width * current + jnp.where(step == 0, current, jnp.zeros_like(current))
-    base, total = carried, carried
-    swapped = []
-    for bit in bits_of("step"):
-        swapped.append(swap(after(total.astype(jnp.bfloat16), own_squares, v_shards[-1][0], v_shards[-2][0]), "step", bit))
-        brought = swapped[-1].astype(jnp.float32)
-        base = base + jnp.where(jnp.bitwise_and(step, bit) != 0, brought, jnp.zeros_like(brought))
-        total = total + brought
-
-    columns = current.shape[1] // steps
-    told = jnp.concatenate([modulation[0, 2], jnp.full((HD,), step_width)])[None]
-    sent_told = after(told, probs)
-    heard = jnp.concatenate([told] + [swap(sent_told, "step", offset) for offset in range(1, steps)])
-    gates = lax.dynamic_slice(heard, (0, step * columns), (steps, columns))
-
-    quarter = after(quarter, swapped[-1], heard)
     gathered = forwarded(quarter, direct(quarter))
 
-    own_columns = [w_out] + [
-        jnp.where(position + away < size, above[away], below[size - away]) for away in range(1, size)
-    ]
-    out_weights = (own_columns, [swap(w, "fsdp", 1) for w in own_columns])
+    raw = [w_out] + below[1:] + above[1:]
+    out_weights = (raw, [swap(w, "fsdp", 1) for w in raw])
 
     sent = project_out(place, heard[:, -1], gathered, out_weights, gates)
     arrived = lax.all_to_all(sent, "step", 0, 0)

time: 341 us -> 356 us (1.044)
  waiting for transfers between devices: 180 us -> 199 us
  other arithmetic: 17.4 us -> 12.7 us
    ppermute x25 -> x28, waiting for transfers between devices: 68.2 us -> 88.7 us  [swap(): lax.ppermute(x, axis, [(i, i ^ offset) for i in range(lax.axis_size(axis))])]
    all_to_all x1, waiting for transfers between devices: 18.7 us -> 0.01 us  [body(): squares = lax.all_to_all(own_squares, 'head', 0, 0)]
    ppermute x3, waiting for transfers between devices: 10.4 us -> 22.1 us  [body(): lax.ppermute(down, 'head', [(i, i - 1) for i in range(1, size - count + 1)])]
    select_n x3 -> x0, other arithmetic: 6.82 us -> none  [body(): jnp.where(position + away < size, above[away], below[size - away])]
    all_to_all x1, waiting for transfers between devices: 11.3 us -> 18 us  [body(): quarter = lax.all_to_all(attended, 'head', 0, 0)]
    ppermute x3, starting transfers between devices: 4.73 us -> 8.52 us  [body(): lax.ppermute(up, 'head', [(i, i + 1) for i in range(count - 1, size - 1)])]
    unnamed x66 -> x44, local copies, waits for them, and re-layouts: 7.72 us -> 6.06 us
    ppermute x25 -> x28, starting transfers between devices: 20.5 us -> 20 us  [swap(): lax.ppermute(x, axis, [(i, i ^ offset) for i in range(lax.axis_size(axis))])]
  transfers between devices with their start and end apart: 40 -> 43, of which waited for: 22 -> 20; matrix products, arithmetic and copies ran while one was open for 7% -> 6% of each run, Pallas kernels for 11% -> 9%
where the time goes in v7:
time: 356 us; the launch traced here: 355 us
  waiting for transfers between devices  199 us (56%)
  Pallas kernels  69.1 us (19%)
  starting transfers between devices  55.4 us (16%)
  local copies, waits for them, and re-layouts  15.7 us (4%)
  other arithmetic  12.7 us (4%)
    ppermute x28, waiting for transfers between devices, swap(): lax.ppermute(x, axis, [(i, i ^ offset) for i in range(lax.axis_size(axis))])  88.7 us
    pallas_call x3, Pallas kernels, project(): pl.pallas_call(functools.partial(project_kernel, size, parts, shard, tupl...  31.6 us
    all_to_all x1, waiting for transfers between devices, body(): arrived = lax.all_to_all(sent, 'step', 0, 0)  26.4 us
    ppermute x3, waiting for transfers between devices, hop(): lax.ppermute(up, 'head', [(i, i + 1) for i in range(count - 1, size - 1)])  25.7 us
    ppermute x3, waiting for transfers between devices, body(): lax.ppermute(down, 'head', [(i, i - 1) for i in range(1, size - count + 1)])  22.1 us
    ppermute x28, starting transfers between devices, swap(): lax.ppermute(x, axis, [(i, i ^ offset) for i in range(lax.axis_size(axis))])  20 us
    all_to_all x1, waiting for transfers between devices, body(): quarter = lax.all_to_all(attended, 'head', 0, 0)  18 us
    ppermute x3, waiting for transfers between devices, hop(): lax.ppermute(down, 'head', [(i, i - 1) for i in range(1, size - count + 1)])  17.6 us
  transfers between devices with their start and end apart: 43, of which 20 were waited for; matrix products, arithmetic and copies ran while one was open for 6% of the time, Pallas kernels for 9%

profile of v7, /device:TPU:0, one launch (start us, length us, event | category | flops | bytes accessed | tf_op | source)
XLA Modules:
  0.0 354.8 jit_solution(2629358586548282819)
XLA Ops:
  4.2 4.6 %modulate.1 = (bf16[128,2560]{1,0:T(8,128)(2,1)}, bf16[128,2560]{1,0:T(8,128)(2,1)}) custom-call(s32[5]{0:T(128)} %stack.32.place, f32[128,5120]{1,0:T(8,128)} %bitcast.14, f32[1,3,5120]{2,1,0:T(4,128)} %copy.13.rows), custom_call_target="tpu_custom_call" | custom-call | flops 1638400 | bytes 983040 | tf_op jit(solution)/shard_map/modulate/pallas_call | solution.py:136
  14.5 4.6 %collective-permute-start.1 = (bf16[2,128,2560]{2,1,0:T(8,128)(2,1)S(1)}, bf16[2,128,2560]{2,1,0:T(8,128)(2,1)}, u32[]{:S(2)}, u32[]{:S(2)}) collective-permute-start(bf16[2,128,2560]{2,1,0:T(8,128)(2,1)S(1)} %pad_maximum_fusion.2.refs_0_.refs_3_.refs_6_), channel_id=1, source_target_pairs={{0,2},{2,4},{4,6},{1,3},{3,5},{5,7},{8,10},{10,12},{12,14},{9,11},... | collective-permute-start | bytes 3932168 | tf_op jit(solution)/shard_map/ppermute | solution.py:486
  20.4 25.7 %collective-permute-done.1.refs_1_ = bf16[2,128,2560]{2,1,0:T(8,128)(2,1)} collective-permute-done((bf16[2,128,2560]{2,1,0:T(8,128)(2,1)S(1)}, bf16[2,128,2560]{2,1,0:T(8,128)(2,1)}, u32[]{:S(2)}, u32[]{:S(2)}) %collective-permute-start.1) | collective-permute-done | bytes 1310752 | tf_op jit(solution)/shard_map/ppermute | solution.py:486
  46.1 5.3 %collective-permute-done.2.refs_4_ = bf16[2,128,2560]{2,1,0:T(8,128)(2,1)} collective-permute-done((bf16[2,128,2560]{2,1,0:T(8,128)(2,1)S(1)}, bf16[2,128,2560]{2,1,0:T(8,128)(2,1)}, u32[]{:S(2)}, u32[]{:S(2)}) %collective-permute-start.2) | collective-permute-done | bytes 1310752 | tf_op jit(solution)/shard_map/ppermute | solution.py:487
  68.0 22.5 %collective-permute-done.7.refs_11_.refs_10_ = bf16[640,1024]{1,0:T(8,128)(2,1)} collective-permute-done((bf16[640,1024]{1,0:T(8,128)(2,1)}, bf16[640,1024]{1,0:T(8,128)(2,1)}, u32[]{:S(2)}, u32[]{:S(2)}) %collective-permute-start.7) | collective-permute-done | bytes 1310752 | tf_op jit(solution)/shard_map/ppermute | solution.py:19
  91.9 7.2 %collective-permute-done.6.refs_5_ = bf16[2,128,2560]{2,1,0:T(8,128)(2,1)} collective-permute-done((bf16[2,128,2560]{2,1,0:T(8,128)(2,1)}, bf16[2,128,2560]{2,1,0:T(8,128)(2,1)}, u32[]{:S(2)}, u32[]{:S(2)}) %collective-permute-start.6) | collective-permute-done | bytes 1310752 | tf_op jit(solution)/shard_map/ppermute | solution.py:487
  108.2 13.6 %first.1 = (f32[384,1536]{1,0:T(8,128)}, f32[384,1536]{1,0:T(8,128)}) custom-call(s32[5]{0:T(128)} %stack.32.place, bf16[2,128,2560]{2,1,0:T(8,128)(2,1)} %copy-done, bf16[2,128,2560]{2,1,0:T(8,128)(2,1)} %collective-permute-done.1.refs_1_, bf16[2,128,2560]{2,1,0:T(8,128)(2,1)} %collective-permute-done.5.refs_2_, bf16[2,128,2560]{2,1,0:T(8,128)(2,1)} %copy-done, ...), custom_call_target="tpu_custom_call" | custom-call | flops 1509949440 | bytes 4128768 | tf_op jit(solution)/shard_map/first/pallas_call | solution.py:213
  125.7 5.1 %collective-permute-done.13.refs_6_ = bf16[2,128,2560]{2,1,0:T(8,128)(2,1)S(1)} collective-permute-done((bf16[2,128,2560]{2,1,0:T(8,128)(2,1)}, bf16[2,128,2560]{2,1,0:T(8,128)(2,1)S(1)}, u32[]{:S(2)}, u32[]{:S(2)}) %collective-permute-start.13) | collective-permute-done | bytes 1310752 | tf_op jit(solution)/shard_map/ppermute | solution.py:487
  134.3 7.8 %last.1 = (f32[128,1536]{1,0:T(8,128)}, f32[128,1536]{1,0:T(8,128)}) custom-call(s32[5]{0:T(128)} %stack.32.place, bf16[2,128,2560]{2,1,0:T(8,128)(2,1)} %copy-done, bf16[2,128,2560]{2,1,0:T(8,128)(2,1)} %collective-permute-done.1.refs_1_, bf16[2,128,2560]{2,1,0:T(8,128)(2,1)} %collective-permute-done.5.refs_2_, bf16[2,128,2560]{2,1,0:T(8,128)(2,1)} %copy-done.7, ...), custom_call_target="tpu_custom_call" | custom-call | flops 503316480 | bytes 2686976 | tf_op jit(solution)/shard_map/last/pallas_call | solution.py:213
  142.2 15.9 %collective-permute-done.15.refs_14_ = bf16[640,256]{1,0:T(8,128)(2,1)} collective-permute-done((bf16[640,256]{1,0:T(8,128)(2,1)S(1)}, bf16[640,256]{1,0:T(8,128)(2,1)}, u32[]{:S(2)}, u32[]{:S(2)}) %collective-permute-start.15) | collective-permute-done | bytes 327712 | tf_op jit(solution)/shard_map/ppermute | solution.py:19
  161.5 5.3 %collective-permute-start.22 = (bf16[768,640]{1,0:T(8,128)(2,1)}, bf16[768,640]{1,0:T(8,128)(2,1)}, u32[]{:S(2)}, u32[]{:S(2)}) collective-permute-start(bf16[768,640]{1,0:T(8,128)(2,1)} %refs_5_.1), channel_id=1, source_target_pairs={{0,2},{2,4},{4,6},{1,3},{3,5},{5,7},{8,10},{10,12},{12,14},{9,11},... | collective-permute-start | bytes 2949128 | tf_op jit(solution)/shard_map/ppermute | solution.py:549
  182.7 10.5 %collective-permute-done.20 = f32[1,5248]{1,0:T(1,128)S(1)} collective-permute-done((f32[1,5248]{1,0:T(1,128)S(1)}, f32[1,5248]{1,0:T(1,128)S(1)}, u32[]{:S(2)}, u32[]{:S(2)}) %collective-permute-start.20) | collective-permute-done | bytes 21024 | tf_op jit(solution)/shard_map/ppermute | solution.py:19
  193.4 10.3 %value.1 = (f32[512,768]{1,0:T(8,128)}, f32[512,768]{1,0:T(8,128)}) custom-call(s32[5]{0:T(128)} %stack.32.place, bf16[2,128,2560]{2,1,0:T(8,128)(2,1)} %copy-done, bf16[2,128,2560]{2,1,0:T(8,128)(2,1)} %collective-permute-done.1.refs_1_, bf16[2,128,2560]{2,1,0:T(8,128)(2,1)} %collective-permute-done.5.refs_2_, bf16[2,128,2560]{2,1,0:T(8,128)(2,1)} %copy-done.7, ...), custom_call_target="tpu_custom_call" | custom-call | flops 1006632960 | bytes 3080192 | tf_op jit(solution)/shard_map/value/pallas_call | solution.py:213
  205.0 7.0 %probs.1 = bf16[6,512,512]{2,1,0:T(8,128)(2,1)} custom-call(s32[5]{0:T(128)} %stack.32.place, f32[4,2,512]{2,1,0:T(2,128)} %copy-done.17, f32[384,1536]{1,0:T(8,128)} %get-tuple-element.45.first_a.refs_0_.refs_4_, f32[384,1536]{1,0:T(8,128)} %copy-done.2, f32[128,1536]{1,0:T(8,128)} %get-tuple-element.51.last_a.refs_2_.refs_6_, f32[128,1536]{1,0:T(8,128)} %copy-done.6, ...), custom_call_target="tpu_custom_call" | custom-call | flops 100663296 | bytes 2359296 | tf_op jit(solution)/shard_map/probs/pallas_call | solution.py:305
  213.2 5.0 %attend.1 = bf16[4,128,768]{2,1,0:T(8,128)(2,1)} custom-call(s32[5]{0:T(128)} %stack.32.place, bf16[6,512,512]{2,1,0:T(8,128)(2,1)} %probs.1, f32[512,768]{1,0:T(8,128)} %get-tuple-element.58.v_a, f32[512,768]{1,0:T(8,128)} %copy-done.14), custom_call_target="tpu_custom_call" | custom-call | flops 100663296 | bytes 1769472 | tf_op jit(solution)/shard_map/attend/pallas_call | solution.py:334
  225.4 18.0 %all-to-all-done.1.refs_0_ = bf16[4,128,768]{2,1,0:T(8,128)(2,1)S(1)} async-done(((bf16[4,128,768]{2,1,0:T(8,128)(2,1)}), bf16[4,128,768]{2,1,0:T(8,128)(2,1)S(1)}, u32[]{:S(2)}, u32[]{:S(2)}) %all-to-all-start.1) | async-done | bytes 786464 | tf_op jit(solution)/shard_map/all_to_all | solution.py:558
  244.0 15.4 %collective-permute-done.30.refs_10_ = bf16[768,640]{1,0:T(8,128)(2,1)} collective-permute-done((bf16[768,640]{1,0:T(8,128)(2,1)}, bf16[768,640]{1,0:T(8,128)(2,1)}, u32[]{:S(2)}, u32[]{:S(2)}) %collective-permute-start.30) | collective-permute-done | bytes 983072 | tf_op jit(solution)/shard_map/ppermute | solution.py:550
  263.5 18.3 %collective-permute-done.25.refs_1_ = bf16[4,128,768]{2,1,0:T(8,128)(2,1)S(1)} collective-permute-done((bf16[4,128,768]{2,1,0:T(8,128)(2,1)S(1)}, bf16[4,128,768]{2,1,0:T(8,128)(2,1)S(1)}, u32[]{:S(2)}, u32[]{:S(2)}) %collective-permute-start.25) | collective-permute-done | bytes 786464 | tf_op jit(solution)/shard_map/ppermute | solution.py:19
  282.3 6.7 %collective-permute-done.32.refs_11_ = bf16[768,640]{1,0:T(8,128)(2,1)} collective-permute-done((bf16[768,640]{1,0:T(8,128)(2,1)}, bf16[768,640]{1,0:T(8,128)(2,1)}, u32[]{:S(2)}, u32[]{:S(2)}) %collective-permute-start.32) | collective-permute-done | bytes 983072 | tf_op jit(solution)/shard_map/ppermute | solution.py:550
  293.5 8.8 %collective-permute-done.27.refs_3_ = bf16[2,128,768]{2,1,0:T(8,128)(2,1)} collective-permute-done((bf16[2,128,768]{2,1,0:T(8,128)(2,1)}, bf16[2,128,768]{2,1,0:T(8,128)(2,1)}, u32[]{:S(2)}, u32[]{:S(2)}) %collective-permute-start.27) | collective-permute-done | bytes 393248 | tf_op jit(solution)/shard_map/ppermute | solution.py:19
  302.6 12.4 %project_out.1 = bf16[4,2,128,1280]{3,2,1,0:T(8,128)(2,1)} custom-call(s32[5]{0:T(128)} %stack.32.place, f32[4]{0:T(128)} %slice_reduce_fusion.widths, bf16[4,128,768]{2,1,0:T(8,128)(2,1)} %copy-done.11, bf16[4,128,768]{2,1,0:T(8,128)(2,1)} %copy-done.13, bf16[4,128,768]{2,1,0:T(8,128)(2,1)} %copy-done.12, ...), custom_call_target="tpu_custom_call" | custom-call | flops 1006632960 | bytes 3407872 | tf_op jit(solution)/shard_map/project_out/pallas_call | solution.py:431
  315.0 4.5 %all-to-all-start.2 = ((bf16[4,2,128,1280]{3,2,1,0:T(8,128)(2,1)}), bf16[4,2,128,1280]{3,2,1,0:T(8,128)(2,1)}, u32[]{:S(2)}, u32[]{:S(2)}) async-start(bf16[4,2,128,1280]{3,2,1,0:T(8,128)(2,1)} %project_out.1), calls=%async_computation.2 | async-start | bytes 5242880 | tf_op jit(solution)/shard_map/all_to_all | solution.py:566
  323.6 26.4 %all-to-all-done.2.arrived = bf16[4,2,128,1280]{3,2,1,0:T(8,128)(2,1)} async-done(((bf16[4,2,128,1280]{3,2,1,0:T(8,128)(2,1)}), bf16[4,2,128,1280]{3,2,1,0:T(8,128)(2,1)}, u32[]{:S(2)}, u32[]{:S(2)}) %all-to-all-start.2) | async-done | bytes 2621472 | tf_op jit(solution)/shard_map/all_to_all | solution.py:566
  350.0 4.8 %finish.1 = (f32[128,5120]{1,0:T(8,128)}, bf16[128,5120]{1,0:T(8,128)(2,1)}) custom-call(f32[128,5120]{1,0:T(8,128)} %fusion.1.base, bf16[4,2,128,1280]{3,2,1,0:T(8,128)(2,1)} %all-to-all-done.2.arrived), custom_call_target="tpu_custom_call" | custom-call | flops 163840 | bytes 2293760 | tf_op jit(solution)/shard_map/finish/pallas_call | solution.py:457
  (145 shorter events, 85.8 us)
Async XLA Ops:
  9.2 46.0 %collective-permute-start.3 = (bf16[640,1536]{1,0:T(8,128)(2,1)S(1)}, bf16[640,1536]{1,0:T(8,128)(2,1)S(1)}, u32[]{:S(2)}, u32[]{:S(2)}) collective-permute-start(bf16[640,1536]{1,0:T(8,128)(2,1)S(1)} %constant_dynamic-update-slice_fusion.refs_7_), channel_id=1, source_target_pairs={{0,8},{8,0},{16,24},{24,16},{1,9},{9,1},{17,25},{25,17},{2,10},{10... | collective-permute-start | bytes 5898248 | tf_op jit(solution)/shard_map/ppermute | solution.py:19
  11.7 44.9 %collective-permute-start.4 = (bf16[640,1536]{1,0:T(8,128)(2,1)S(1)}, bf16[640,1536]{1,0:T(8,128)(2,1)S(1)}, u32[]{:S(2)}, u32[]{:S(2)}) collective-permute-start(bf16[640,1536]{1,0:T(8,128)(2,1)S(1)} %constant_dynamic-update-slice_fusion.refs_7_), channel_id=1, source_target_pairs={{0,16},{8,24},{16,0},{24,8},{1,17},{9,25},{17,1},{25,9},{2,18},{10... | collective-permute-start | bytes 5898248 | tf_op jit(solution)/shard_map/ppermute | solution.py:19
  14.5 31.6 %collective-permute-start.1 = (bf16[2,128,2560]{2,1,0:T(8,128)(2,1)S(1)}, bf16[2,128,2560]{2,1,0:T(8,128)(2,1)}, u32[]{:S(2)}, u32[]{:S(2)}) collective-permute-start(bf16[2,128,2560]{2,1,0:T(8,128)(2,1)S(1)} %pad_maximum_fusion.2.refs_0_.refs_3_.refs_6_), channel_id=1, source_target_pairs={{0,2},{2,4},{4,6},{1,3},{3,5},{5,7},{8,10},{10,12},{12,14},{9,11},... | collective-permute-start | bytes 3932168 | tf_op jit(solution)/shard_map/ppermute | solution.py:486
  19.1 32.3 %collective-permute-start.2 = (bf16[2,128,2560]{2,1,0:T(8,128)(2,1)S(1)}, bf16[2,128,2560]{2,1,0:T(8,128)(2,1)}, u32[]{:S(2)}, u32[]{:S(2)}) collective-permute-start(bf16[2,128,2560]{2,1,0:T(8,128)(2,1)S(1)} %pad_maximum_fusion.2.refs_0_.refs_3_.refs_6_), channel_id=1, source_target_pairs={{2,0},{4,2},{6,4},{3,1},{5,3},{7,5},{10,8},{12,10},{14,12},{11,9},... | collective-permute-start | bytes 3932168 | tf_op jit(solution)/shard_map/ppermute | solution.py:487
  59.9 30.7 %collective-permute-start.7 = (bf16[640,1024]{1,0:T(8,128)(2,1)}, bf16[640,1024]{1,0:T(8,128)(2,1)}, u32[]{:S(2)}, u32[]{:S(2)}) collective-permute-start(bf16[640,1024]{1,0:T(8,128)(2,1)} %get-tuple-element.67), channel_id=1, source_target_pairs={{0,16},{8,24},{16,0},{24,8},{1,17},{9,25},{17,1},{25,9},{2,18},{10... | collective-permute-start | bytes 3932168 | tf_op jit(solution)/shard_map/ppermute | solution.py:19
  61.5 30.4 %collective-permute-start.8 = (bf16[640,1024]{1,0:T(8,128)(2,1)}, bf16[640,1024]{1,0:T(8,128)(2,1)}, u32[]{:S(2)}, u32[]{:S(2)}) collective-permute-start(bf16[640,1024]{1,0:T(8,128)(2,1)} %get-tuple-element.66), channel_id=1, source_target_pairs={{0,8},{8,0},{16,24},{24,16},{1,9},{9,1},{17,25},{25,17},{2,10},{10... | collective-permute-start | bytes 3932168 | tf_op jit(solution)/shard_map/ppermute | solution.py:19
  63.0 28.9 %collective-permute-start.5 = (bf16[2,128,2560]{2,1,0:T(8,128)(2,1)}, bf16[2,128,2560]{2,1,0:T(8,128)(2,1)}, u32[]{:S(2)}, u32[]{:S(2)}) collective-permute-start(bf16[2,128,2560]{2,1,0:T(8,128)(2,1)} %collective-permute-done.1.refs_1_), channel_id=1, source_target_pairs={{2,4},{4,6},{3,5},{5,7},{10,12},{12,14},{11,13},{13,15},{18,20},{2... | collective-permute-start | bytes 3932168 | tf_op jit(solution)/shard_map/ppermute | solution.py:486
  64.7 34.4 %collective-permute-start.6 = (bf16[2,128,2560]{2,1,0:T(8,128)(2,1)}, bf16[2,128,2560]{2,1,0:T(8,128)(2,1)}, u32[]{:S(2)}, u32[]{:S(2)}) collective-permute-start(bf16[2,128,2560]{2,1,0:T(8,128)(2,1)} %collective-permute-done.2.refs_4_), channel_id=1, source_target_pairs={{2,0},{4,2},{3,1},{5,3},{10,8},{12,10},{11,9},{13,11},{18,16},{20,... | collective-permute-start | bytes 3932168 | tf_op jit(solution)/shard_map/ppermute | solution.py:487
  99.1 26.7 %collective-permute-start.12 = (bf16[2,128,2560]{2,1,0:T(8,128)(2,1)}, bf16[2,128,2560]{2,1,0:T(8,128)(2,1)S(1)}, u32[]{:S(2)}, u32[]{:S(2)}) collective-permute-start(bf16[2,128,2560]{2,1,0:T(8,128)(2,1)} %collective-permute-done.5.refs_2_), channel_id=1, source_target_pairs={{4,6},{5,7},{12,14},{13,15},{20,22},{21,23},{28,30},{29,31}} | collective-permute-start | bytes 3932168 | tf_op jit(solution)/shard_map/ppermute | solution.py:486
  99.8 31.0 %collective-permute-start.13 = (bf16[2,128,2560]{2,1,0:T(8,128)(2,1)}, bf16[2,128,2560]{2,1,0:T(8,128)(2,1)S(1)}, u32[]{:S(2)}, u32[]{:S(2)}) collective-permute-start(bf16[2,128,2560]{2,1,0:T(8,128)(2,1)} %collective-permute-done.6.refs_5_), channel_id=1, source_target_pairs={{2,0},{3,1},{10,8},{11,9},{18,16},{19,17},{26,24},{27,25}} | collective-permute-start | bytes 3932168 | tf_op jit(solution)/shard_map/ppermute | solution.py:487
  106.8 51.4 %collective-permute-start.9 = (bf16[128,5120]{1,0:T(8,128)(2,1)}, bf16[128,5120]{1,0:T(8,128)(2,1)}, u32[]{:S(2)}, u32[]{:S(2)}) collective-permute-start(bf16[128,5120]{1,0:T(8,128)(2,1)} %fusion.3), channel_id=1, source_target_pairs={{0,8},{8,0},{16,24},{24,16},{1,9},{9,1},{17,25},{25,17},{2,10},{10... | collective-permute-start | bytes 3932168 | tf_op jit(solution)/shard_map/ppermute | solution.py:19
  130.8 37.3 %collective-permute-start.17 = (f32[384,1536]{1,0:T(8,128)}, f32[384,1536]{1,0:T(8,128)S(1)}, u32[]{:S(2)}, u32[]{:S(2)}) collective-permute-start(f32[384,1536]{1,0:T(8,128)} %get-tuple-element.50), channel_id=1, source_target_pairs={{0,1},{1,0},{2,3},{3,2},{4,5},{5,4},{6,7},{7,6},{8,9},{9,8},{10,11... | collective-permute-start | bytes 7077896 | tf_op jit(solution)/shard_map/ppermute | solution.py:19
  133.7 24.4 %collective-permute-start.15 = (bf16[640,256]{1,0:T(8,128)(2,1)S(1)}, bf16[640,256]{1,0:T(8,128)(2,1)}, u32[]{:S(2)}, u32[]{:S(2)}) collective-permute-start(bf16[640,256]{1,0:T(8,128)(2,1)S(1)} %slice.53), channel_id=1, source_target_pairs={{0,8},{8,0},{16,24},{24,16},{1,9},{9,1},{17,25},{25,17},{2,10},{10... | collective-permute-start | bytes 983048 | tf_op jit(solution)/shard_map/ppermute | solution.py:19
  161.0 32.4 %collective-permute-start.16 = (bf16[128,5120]{1,0:T(8,128)(2,1)}, bf16[128,5120]{1,0:T(8,128)(2,1)}, u32[]{:S(2)}, u32[]{:S(2)}) collective-permute-start(bf16[128,5120]{1,0:T(8,128)(2,1)} %fusion.2), channel_id=1, source_target_pairs={{0,16},{8,24},{16,0},{24,8},{1,17},{9,25},{17,1},{25,9},{2,18},{10... | collective-permute-start | bytes 3932168 | tf_op jit(solution)/shard_map/ppermute | solution.py:19
  161.5 31.9 %collective-permute-start.22 = (bf16[768,640]{1,0:T(8,128)(2,1)}, bf16[768,640]{1,0:T(8,128)(2,1)}, u32[]{:S(2)}, u32[]{:S(2)}) collective-permute-start(bf16[768,640]{1,0:T(8,128)(2,1)} %refs_5_.1), channel_id=1, source_target_pairs={{0,2},{2,4},{4,6},{1,3},{3,5},{5,7},{8,10},{10,12},{12,14},{9,11},... | collective-permute-start | bytes 2949128 | tf_op jit(solution)/shard_map/ppermute | solution.py:549
  166.8 26.6 %collective-permute-start.23 = (bf16[768,640]{1,0:T(8,128)(2,1)}, bf16[768,640]{1,0:T(8,128)(2,1)}, u32[]{:S(2)}, u32[]{:S(2)}) collective-permute-start(bf16[768,640]{1,0:T(8,128)(2,1)} %refs_5_.1), channel_id=1, source_target_pairs={{2,0},{4,2},{6,4},{3,1},{5,3},{7,5},{10,8},{12,10},{14,12},{11,9},... | collective-permute-start | bytes 2949128 | tf_op jit(solution)/shard_map/ppermute | solution.py:550
  218.2 25.2 %all-to-all-start.1 = ((bf16[4,128,768]{2,1,0:T(8,128)(2,1)}), bf16[4,128,768]{2,1,0:T(8,128)(2,1)S(1)}, u32[]{:S(2)}, u32[]{:S(2)}) async-start(bf16[4,128,768]{2,1,0:T(8,128)(2,1)} %attend.1), calls=%async_computation.1 | async-start | bytes 1572864 | tf_op jit(solution)/shard_map/all_to_all | solution.py:558
  223.5 35.9 %collective-permute-start.30 = (bf16[768,640]{1,0:T(8,128)(2,1)}, bf16[768,640]{1,0:T(8,128)(2,1)}, u32[]{:S(2)}, u32[]{:S(2)}) collective-permute-start(bf16[768,640]{1,0:T(8,128)(2,1)} %collective-permute-done.23.refs_9_), channel_id=1, source_target_pairs={{2,0},{4,2},{3,1},{5,3},{10,8},{12,10},{11,9},{13,11},{18,16},{20,... | collective-permute-start | bytes 2949128 | tf_op jit(solution)/shard_map/ppermute | solution.py:550
  224.8 37.5 %collective-permute-start.33 = (bf16[768,640]{1,0:T(8,128)(2,1)}, bf16[768,640]{1,0:T(8,128)(2,1)}, u32[]{:S(2)}, u32[]{:S(2)}) collective-permute-start(bf16[768,640]{1,0:T(8,128)(2,1)} %refs_5_.1), channel_id=1, source_target_pairs={{0,1},{1,0},{2,3},{3,2},{4,5},{5,4},{6,7},{7,6},{8,9},{9,8},{10,11... | collective-permute-start | bytes 2949128 | tf_op jit(solution)/shard_map/ppermute | solution.py:19
  225.1 37.8 %collective-permute-start.34 = (bf16[768,640]{1,0:T(8,128)(2,1)}, bf16[768,640]{1,0:T(8,128)(2,1)}, u32[]{:S(2)}, u32[]{:S(2)}) collective-permute-start(bf16[768,640]{1,0:T(8,128)(2,1)} %collective-permute-done.22.refs_6_), channel_id=1, source_target_pairs={{0,1},{1,0},{2,3},{3,2},{4,5},{5,4},{6,7},{7,6},{8,9},{9,8},{10,11... | collective-permute-start | bytes 2949128 | tf_op jit(solution)/shard_map/ppermute | solution.py:19
  261.0 27.9 %collective-permute-start.32 = (bf16[768,640]{1,0:T(8,128)(2,1)}, bf16[768,640]{1,0:T(8,128)(2,1)}, u32[]{:S(2)}, u32[]{:S(2)}) collective-permute-start(bf16[768,640]{1,0:T(8,128)(2,1)} %collective-permute-done.30.refs_10_), channel_id=1, source_target_pairs={{2,0},{3,1},{10,8},{11,9},{18,16},{19,17},{26,24},{27,25}} | collective-permute-start | bytes 2949128 | tf_op jit(solution)/shard_map/ppermute | solution.py:550
  262.9 27.6 %collective-permute-start.37 = (bf16[768,640]{1,0:T(8,128)(2,1)}, bf16[768,640]{1,0:T(8,128)(2,1)}, u32[]{:S(2)}, u32[]{:S(2)}) collective-permute-start(bf16[768,640]{1,0:T(8,128)(2,1)} %collective-permute-done.23.refs_9_), channel_id=1, source_target_pairs={{0,1},{1,0},{2,3},{3,2},{4,5},{5,4},{6,7},{7,6},{8,9},{9,8},{10,11... | collective-permute-start | bytes 2949128 | tf_op jit(solution)/shard_map/ppermute | solution.py:19
  263.0 28.1 %collective-permute-start.35 = (bf16[768,640]{1,0:T(8,128)(2,1)}, bf16[768,640]{1,0:T(8,128)(2,1)}, u32[]{:S(2)}, u32[]{:S(2)}) collective-permute-start(bf16[768,640]{1,0:T(8,128)(2,1)} %collective-permute-done.29.refs_7_), channel_id=1, source_target_pairs={{0,1},{1,0},{2,3},{3,2},{4,5},{5,4},{6,7},{7,6},{8,9},{9,8},{10,11... | collective-permute-start | bytes 2949128 | tf_op jit(solution)/shard_map/ppermute | solution.py:19
  315.0 35.0 %all-to-all-start.2 = ((bf16[4,2,128,1280]{3,2,1,0:T(8,128)(2,1)}), bf16[4,2,128,1280]{3,2,1,0:T(8,128)(2,1)}, u32[]{:S(2)}, u32[]{:S(2)}) async-start(bf16[4,2,128,1280]{3,2,1,0:T(8,128)(2,1)} %project_out.1), calls=%async_computation.2 | async-start | bytes 5242880 | tf_op jit(solution)/shard_map/all_to_all | solution.py:566
  (43 other events, 632.1 us)

commit v8 on v7

--- a/solution.py
+++ b/solution.py
@@ -53,20 +53,13 @@
     return found
 
 
-def in_rounds(w_both, w_value, line_hops):
+def in_rounds(w_both, w_value, hop):
     width = w_value.shape[1]
-    part = width // 768 * 256
-    rest = width - part
     a1, a2 = swap(w_both, "step", 1), swap(w_both, "step", 2)
-    hop = line_hops((a1, a2))
-    a1, a2 = after((a1, a2), *hop)
-    b1 = swap(jnp.concatenate([a2[:, :width], w_value[:, :part]], axis=1), "step", 1)
-    b2 = swap(jnp.concatenate([a1[:, width:], w_value[:, :part]], axis=1), "step", 2)
-    hop = line_hops((b1, b2))
-    e1, e2 = after((b1, b2), *hop)
-    middle = width + part // 2
-    c1 = swap(jnp.concatenate([w_value[:, part:], e2[:, width:middle]], axis=1), "step", 1)
-    c2 = swap(jnp.concatenate([w_value[:, part:], e1[:, middle:]], axis=1), "step", 2)
+    e1, e2 = after((a1, a2), *hop())
+    b1, b2 = swap(e2[:, :width], "step", 1), swap(e1[:, width:], "step", 2)
+    v1, v2 = after((w_value, w_value), b1, b2, *hop(b1, b2))
+    c1, c2 = swap(v1, "step", 1), swap(v2, "step", 2)
     both = [
         (w_both, 0, 0, 0, 0, 2 * width),
         (a1, 1, 0, 0, 0, 2 * width),
@@ -77,19 +70,9 @@
 
     def finished(*awaited):
         f1, f2 = after((c1, c2), *awaited)
-        d1 = swap(f2[:, : rest // 2], "step", 1)
-        d2 = swap(f1[:, rest // 2 : rest], "step", 2)
-        return [
-            (w_value, 0, 0, 0, 0, width),
-            (b1, 1, 0, width, 0, part),
-            (c1, 1, 0, 0, part, rest),
-            (b2, 2, 0, width, 0, part),
-            (c2, 2, 0, 0, part, rest),
-            (c1, 3, 0, rest, 0, part // 2),
-            (c2, 3, 0, rest, part // 2, part // 2),
-            (d1, 3, 0, 0, part, rest // 2),
-            (d2, 3, 0, 0, part + rest // 2, rest // 2),
-        ]
+        d1, d2 = swap(f2[:, : width // 2], "step", 1), swap(f1[:, width // 2 :], "step", 2)
+        whole = [(w_value, 0, 0, 0, 0, width), (c1, 1, 0, 0, 0, width), (c2, 2, 0, 0, 0, width)]
+        return whole + [(d1, 3, 0, 0, 0, width // 2), (d2, 3, 0, 0, width // 2, width // 2)]
 
     return both, (c1, c2), finished
 
@@ -143,6 +126,43 @@
         cost_estimate=cost(10 * tokens * width, 6 * tokens * width),
         name="modulate",
     )(place, states, rows)
+
+
+def terms(x):
+    high = x.astype(jnp.bfloat16).astype(jnp.float32)
+    middle = (x - high).astype(jnp.bfloat16).astype(jnp.float32)
+    return [high, middle, x - high - middle]
+
+
+def tell_kernel(place, step_width, states, rows, out):
+    current = states[...]
+    tokens, columns = current.shape
+    width = step_width[0]
+    anchor = jnp.where(place[0] == 0, 1.0, 0.0)
+    out[0, :tokens] = (width * current + anchor * current).astype(jnp.bfloat16)
+    told = terms(rows[0, 2:3, :]) + terms(jnp.full((1, columns), width, jnp.float32))
+    told.append(jnp.zeros((10, columns), jnp.float32))
+    out[0, tokens:] = jnp.concatenate(told).astype(jnp.bfloat16)
+
+
+def tell(place, step_width, states, rows, steps):
+    tokens, width = states.shape
+    columns = width // steps
+    return pl.pallas_call(
+        tell_kernel,
+        grid=(steps,),
+        in_specs=[
+            SMEM,
+            SMEM,
+            pl.BlockSpec((tokens, columns), lambda i: (0, i)),
+            pl.BlockSpec((1, rows.shape[1], columns), lambda i: (0, 0, i)),
+        ],
+        out_specs=pl.BlockSpec((1, tokens + 16, columns), lambda i: (i, 0, 0)),
+        out_shape=jax.ShapeDtypeStruct((steps, tokens + 16, columns), jnp.bfloat16),
+        compiler_params=params(),
+        cost_estimate=cost(4 * tokens * width, 6 * tokens * width),
+        name="tell",
+    )(place, step_width, states, rows)
 
 
 def project_kernel(size, parts, shard, layout, place, *refs):
@@ -344,10 +364,10 @@
     )(place, probs, *v_parts)
 
 
-def out_kernel(size, layout, place, widths, *refs):
+def out_kernel(size, layout, place, *refs):
     count = 2 * size - 1
     pieces, weights = refs[: len(layout)], refs[len(layout) : len(layout) + 2 * count]
-    gates, out, a_held, w_held, total, a_sems, w_sems = refs[len(layout) + 2 * count :]
+    heard, out, a_held, w_held, total, a_sems, w_sems = refs[len(layout) + 2 * count :]
     steps, _, tokens, columns = out.shape
     width = columns // 2
     halves, _, _, span_width = w_held.shape
@@ -403,17 +423,19 @@
                 total[half] += part
     for half in range(halves):
         span = slice(half * span_width, (half + 1) * span_width)
-        reached = None
+        reached = jnp.zeros((tokens, span_width), jnp.float32)
         for step in range(steps):
-            told = jnp.bitwise_xor(step_at, step)
-            branch = total[half, step * tokens : (step + 1) * tokens] * gates[pl.ds(told, 1), span]
+            told = heard[step, tokens : tokens + 16, span].astype(jnp.float32)
+            gate = told[0:1] + told[1:2] + told[2:3]
+            step_width = told[3:4] + told[4:5] + told[5:6]
+            branch = total[half, step * tokens : (step + 1) * tokens] * gate
             out[step, 0, :, span] = branch.astype(jnp.bfloat16)
-            drift = branch * widths[told]
-            reached = drift if step == 0 else reached + drift
+            reached += branch * step_width
             out[step, 1, :, span] = reached.astype(jnp.bfloat16)
-
-
-def project_out(place, widths, gathered, weights, gates):
+            reached += heard[step, :tokens, span].astype(jnp.float32)
+
+
+def project_out(place, heard, gathered, weights):
     size = lax.axis_size("head")
     steps = len(gathered)
     _, tokens, inner = gathered[0][0].shape
@@ -430,7 +452,7 @@
     operands = pieces + [w for half in weights for w in half]
     return pl.pallas_call(
         functools.partial(out_kernel, size, tuple(layout)),
-        in_specs=[SMEM, SMEM] + [ANY] * len(operands) + [VMEM],
+        in_specs=[SMEM] + [ANY] * len(operands) + [VMEM],
         out_specs=VMEM,
         out_shape=jax.ShapeDtypeStruct((steps, 2, tokens, 2 * width), jnp.bfloat16),
         scratch_shapes=[
@@ -443,7 +465,7 @@
         compiler_params=params(),
         cost_estimate=cost(4 * rows * size * inner * width, 2 * size * inner * (rows + 2 * width) + 8 * rows * width),
         name="project_out",
-    )(place, widths, *operands, gates)
+    )(place, *operands, heard)
 
 
 def finish_kernel(base, arrived, reached, update):
@@ -478,24 +500,17 @@
     tokens = jnp.stack([mine, swap(other, "fsdp", 1)])
     below, above = [tokens], [tokens]
 
-    def hop(awaited=()):
+    def hop(*awaited):
         count = len(below)
-        up, down = below[-1], above[-1]
-        if awaited:
-            up, down = after((up, down), *awaited)
+        arrived = (below[-1], above[-1])
+        up, down = after(arrived, *awaited) if awaited else arrived
         below.append(lax.ppermute(up, "head", [(i, i + 1) for i in range(count - 1, size - 1)]))
         above.append(lax.ppermute(down, "head", [(i, i - 1) for i in range(1, size - count + 1)]))
-        return below[-1], above[-1]
+        return arrived
 
     hop()
-    if steps == 4 and size > 3 and w_value.shape[1] % 768 == 0:
-
-        def line_hops(awaited):
-            arrived = (below[-1], above[-1])
-            hop(awaited)
-            return arrived
-
-        both_shards, last_round, finished = in_rounds(w_both, w_value, line_hops)
+    if steps == 4 and size > 3 and w_value.shape[1] % 256 == 0:
+        both_shards, last_round, finished = in_rounds(w_both, w_value, hop)
     else:
         both = forwarded(w_both, direct(w_both))
         both_shards = placed(both)
@@ -508,63 +523,52 @@
         hop()
     line = below, above
     early = tuple(held[: size - 1] + [held[0]] for held in line)
-    first_here, first_there = project(place, early, both_shards, "first", "first")
-
     step_width = (timesteps[0, 1] - timesteps[0, 0]).astype(jnp.float32) / 1000.0
-    carried = step_width * current + jnp.where(step == 0, current, jnp.zeros_like(current))
-    base, total = carried, carried
-    swapped = []
-
-    def add_states(base, total, bit, awaited):
-        swapped.append(swap(after(total.astype(jnp.bfloat16), *awaited), "step", bit))
-        brought = swapped[-1].astype(jnp.float32)
-        return base + jnp.where(jnp.bitwise_and(step, bit) != 0, brought, jnp.zeros_like(brought)), total + brought
-
-    awaited = (early[0][-2], early[1][-2], both_shards[-1][0], both_shards[-2][0])
-    base, total = add_states(base, total, 1, awaited)
+    told = tell(place, step_width[None], current, modulation, steps)
+    partner_below, partner_above = [swap(after(w_out, below[1], above[1]), "fsdp", 1)], []
+    first_here, first_there = project(after(place, told, *partner_below), early, both_shards, "first", "first")
     ended = (below[-1], above[-1]) + last_round
     first_there = after(first_there, *ended)
     v_shards = finished(*ended, first_here)
-    for bit in bits_of("step")[1:]:
-        base, total = add_states(base, total, bit, (v_shards[-1][0], v_shards[-2][0]))
+    v_last = (v_shards[-1][0], v_shards[-2][0])
     parts = [first_here, swap(first_there, "fsdp", 1)]
     last_here, last_there = project(place, line, both_shards, "last", "last")
-    parts += [last_here, swap(after(last_there, v_shards[-1][0], v_shards[-2][0]), "fsdp", 1)]
-    own_squares = norms(place, parts, size)
-    squares = lax.all_to_all(own_squares, "head", 0, 0)
-
-    columns = current.shape[1] // steps
-    told = jnp.concatenate([modulation[0, 2], jnp.full((HD,), step_width)])[None]
-    sent_told = after(told, own_squares)
-    heard = jnp.concatenate([told] + [swap(sent_told, "step", offset) for offset in range(1, steps)])
-    gates = lax.dynamic_slice(heard, (0, step * columns), (steps, columns))
+    parts += [last_here, swap(after(last_there, *v_last), "fsdp", 1)]
+    v_here, v_there = project(after(place, last_here), line, v_shards, "all", "value")
+    v_parts = [v_here, swap(v_there, "fsdp", 1)]
+    heard = lax.all_to_all(after(told, *v_last), "step", 0, 0)
 
     below, above = [w_out], [w_out]
     for count in range(1, size):
         up, down = below[-1], above[-1]
         if count == 1:
             up, down = after((up, down), *ended, first_here)
+        if count == 2:
+            up, down = after((up, down), squares)
         if count == size - 1:
             up, down = after((up, down), quarter)
         below.append(lax.ppermute(up, "head", [(i, i + 1) for i in range(count - 1, size - 1)]))
         above.append(lax.ppermute(down, "head", [(i, i - 1) for i in range(1, size - count + 1)]))
+        partner_below.append(swap(below[-1], "fsdp", 1))
+        partner_above.append(swap(above[-1], "fsdp", 1))
         if count == 1:
-            v_place = after(place, squares, below[-1], above[-1], heard, swapped[-1])
-            v_here, v_there = project(v_place, line, v_shards, "all", "value")
-            v_parts = [v_here, swap(v_there, "fsdp", 1)]
-            probs = probabilities(place, squares, parts, q_gain, k_gain)
+            own_squares = norms(after(place, below[-1], above[-1], v_here, heard), parts, size)
+            squares = lax.all_to_all(own_squares, "head", 0, 0)
+            ready = after(squares, *partner_below, *partner_above)
+            probs = probabilities(place, ready, parts, q_gain, k_gain)
         if count == size - 2:
-            attended = attend(place, probs, v_parts, size)
-            quarter = lax.all_to_all(attended, "head", 0, 0)
+            attended = after(attend(place, probs, v_parts, size), below[-1], above[-1])
+            quarter = after(lax.all_to_all(attended, "head", 0, 0), partner_below[-1], partner_above[-1])
 
     gathered = forwarded(quarter, direct(quarter))
 
     raw = [w_out] + below[1:] + above[1:]
-    out_weights = (raw, [swap(w, "fsdp", 1) for w in raw])
-
-    sent = project_out(place, heard[:, -1], gathered, out_weights, gates)
+    out_weights = (raw, partner_below + partner_above)
+    carried = step_width * current + jnp.where(step == 0, current, jnp.zeros_like(current))
+
+    sent = project_out(place, heard, gathered, out_weights)
     arrived = lax.all_to_all(sent, "step", 0, 0)
-    reached, update = finish(base, arrived)
+    reached, update = finish(carried, arrived)
     return reached[None, None], update[None, None]
 
 

time: 356 us -> 319 us (0.90)
  waiting for transfers between devices: 199 us -> 166 us
  other arithmetic: 12.7 us -> 3.06 us
  Pallas kernels: 69.1 us -> 74.3 us
    ppermute x28 -> x23, waiting for transfers between devices: 88.7 us -> 56.7 us  [swap(): lax.ppermute(x, axis, [(i, i ^ offset) for i in range(lax.axis_size(axis))])]
    ppermute x3, waiting for transfers between devices: 25.7 us -> 0.01 us  [hop(): lax.ppermute(up, 'head', [(i, i + 1) for i in range(count - 1, size - 1)])]
    ppermute x3, waiting for transfers between devices: 17.6 us -> 30.9 us  [hop(): lax.ppermute(down, 'head', [(i, i - 1) for i in range(1, size - count + 1)])]
    ppermute x3, waiting for transfers between devices: 22.1 us -> 31.8 us  [body(): lax.ppermute(down, 'head', [(i, i - 1) for i in range(1, size - count + 1)])]
    all_to_all x1 -> x2, waiting for transfers between devices: 18 us -> 12.6 us  [the longest x1 12.6 us: body(): lax.all_to_all(attended, 'head', 0, 0)]
    all_to_all x1, waiting for transfers between devices: 0.01 us -> 5.1 us  [body(): squares = lax.all_to_all(own_squares, 'head', 0, 0)]
    convert_element_type x2 -> x0, other arithmetic: 4.22 us -> none  [add_states(): total.astype(jnp.bfloat16)]
    all_to_all x1 -> x2, starting transfers between devices: 3.71 us -> 7.81 us  [the longest x1 4.32 us: body(): heard = lax.all_to_all(after(told, *v_last), 'step', 0, 0)]
  transfers between devices with their start and end apart: 43 -> 39, of which waited for: 20 -> 20; matrix products, arithmetic and copies ran while one was open for 6% -> 2% of each run, Pallas kernels for 9% -> 16%
where the time goes in v8:
time: 319 us; the launch traced here: 317 us
  waiting for transfers between devices  166 us (52%)
  Pallas kernels  74.3 us (23%)
  starting transfers between devices  58 us (18%)
  local copies, waits for them, and re-layouts  13.1 us (4%)
    ppermute x23, waiting for transfers between devices, swap(): lax.ppermute(x, axis, [(i, i ^ offset) for i in range(lax.axis_size(axis))])  56.7 us
    ppermute x3, waiting for transfers between devices, body(): lax.ppermute(down, 'head', [(i, i - 1) for i in range(1, size - count + 1)])  31.8 us
    pallas_call x3, Pallas kernels, project(): pl.pallas_call(functools.partial(project_kernel, size, parts, shard, tupl...  31.5 us
    ppermute x3, waiting for transfers between devices, hop(): lax.ppermute(down, 'head', [(i, i - 1) for i in range(1, size - count + 1)])  30.9 us
    all_to_all x1, waiting for transfers between devices, body(): arrived = lax.all_to_all(sent, 'step', 0, 0)  28.5 us
    ppermute x23, starting transfers between devices, swap(): lax.ppermute(x, axis, [(i, i ^ offset) for i in range(lax.axis_size(axis))])  20.4 us
    pallas_call x1, Pallas kernels, project_out(): pl.pallas_call(functools.partial(out_kernel, size, tuple(layout)), in_spe...  13 us
    all_to_all x1, waiting for transfers between devices, body(): lax.all_to_all(attended, 'head', 0, 0)  12.6 us
  transfers between devices with their start and end apart: 39, of which 20 were waited for; matrix products, arithmetic and copies ran while one was open for 2% of the time, Pallas kernels for 16%

profile of v8, /device:TPU:0, one launch (start us, length us, event | category | flops | bytes accessed | tf_op | source)
XLA Modules:
  0.0 317.3 jit_solution(7592610146507021375)
XLA Ops:
  5.0 4.6 %modulate.1 = (bf16[128,2560]{1,0:T(8,128)(2,1)}, bf16[128,2560]{1,0:T(8,128)(2,1)}) custom-call(s32[5]{0:T(128)} %stack.32.place, f32[128,5120]{1,0:T(8,128)} %bitcast.12, f32[1,3,5120]{2,1,0:T(4,128)} %copy.12.rows), custom_call_target="tpu_custom_call" | custom-call | flops 1638400 | bytes 983040 | tf_op jit(solution)/shard_map/modulate/pallas_call | solution.py:119
  16.7 4.6 %collective-permute-start.1 = (bf16[2,128,2560]{2,1,0:T(8,128)(2,1)S(1)}, bf16[2,128,2560]{2,1,0:T(8,128)(2,1)S(1)}, u32[]{:S(2)}, u32[]{:S(2)}) collective-permute-start(bf16[2,128,2560]{2,1,0:T(8,128)(2,1)S(1)} %pad_maximum_fusion.refs_0_.refs_3_.refs_6_), channel_id=1, source_target_pairs={{0,2},{2,4},{4,6},{1,3},{3,5},{5,7},{8,10},{10,12},{12,14},{9,11},... | collective-permute-start | bytes 3932168 | tf_op jit(solution)/shard_map/ppermute | solution.py:507
  21.3 26.6 %collective-permute-done.3.refs_4_ = bf16[2,128,2560]{2,1,0:T(8,128)(2,1)S(1)} collective-permute-done((bf16[2,128,2560]{2,1,0:T(8,128)(2,1)S(1)}, bf16[2,128,2560]{2,1,0:T(8,128)(2,1)S(1)}, u32[]{:S(2)}, u32[]{:S(2)}) %collective-permute-start.3) | collective-permute-done | bytes 1310752 | tf_op jit(solution)/shard_map/ppermute | solution.py:508
  50.9 5.0 %collective-permute-done.6.refs_9_ = bf16[640,1536]{1,0:T(8,128)(2,1)S(1)} collective-permute-done((bf16[640,1536]{1,0:T(8,128)(2,1)S(1)}, bf16[640,1536]{1,0:T(8,128)(2,1)S(1)}, u32[]{:S(2)}, u32[]{:S(2)}) %collective-permute-start.6) | collective-permute-done | bytes 1966112 | tf_op jit(solution)/shard_map/ppermute | solution.py:19
  59.6 21.1 %collective-permute-done.8.refs_11_ = bf16[640,768]{1,0:T(8,128)(2,1)S(1)} collective-permute-done((bf16[640,768]{1,0:T(8,128)(2,1)S(1)}, bf16[640,768]{1,0:T(8,128)(2,1)S(1)}, u32[]{:S(2)}, u32[]{:S(2)}) %collective-permute-start.8) | collective-permute-done | bytes 983072 | tf_op jit(solution)/shard_map/ppermute | solution.py:19
  93.1 13.5 %first.1 = (f32[384,1536]{1,0:T(8,128)}, f32[384,1536]{1,0:T(8,128)}) custom-call(s32[5]{0:T(128)} %stack.32.place, bf16[2,128,2560]{2,1,0:T(8,128)(2,1)} %copy-done, bf16[2,128,2560]{2,1,0:T(8,128)(2,1)} %copy-done.7, bf16[2,128,2560]{2,1,0:T(8,128)(2,1)} %collective-permute-done.2.refs_2_, bf16[2,128,2560]{2,1,0:T(8,128)(2,1)} %copy-done, ...), custom_call_target="tpu_custom_call" | custom-call | flops 1509949440 | bytes 4128768 | tf_op jit(solution)/shard_map/first/pallas_call | solution.py:233
  109.9 4.4 %collective-permute-done.10.refs_6_ = bf16[2,128,2560]{2,1,0:T(8,128)(2,1)S(1)} collective-permute-done((bf16[2,128,2560]{2,1,0:T(8,128)(2,1)}, bf16[2,128,2560]{2,1,0:T(8,128)(2,1)S(1)}, u32[]{:S(2)}, u32[]{:S(2)}) %collective-permute-start.10) | collective-permute-done | bytes 1310752 | tf_op jit(solution)/shard_map/ppermute | solution.py:508
  120.2 11.2 %collective-permute-done.17.refs_11_ = bf16[640,384]{1,0:T(8,128)(2,1)} collective-permute-done((bf16[640,384]{1,0:T(8,128)(2,1)S(1)}, bf16[640,384]{1,0:T(8,128)(2,1)}, u32[]{:S(2)}, u32[]{:S(2)}) %collective-permute-start.17) | collective-permute-done | bytes 491552 | tf_op jit(solution)/shard_map/ppermute | solution.py:19
  132.2 4.3 %all-to-all-start = ((bf16[4,144,1280]{2,1,0:T(8,128)(2,1)}), bf16[4,144,1280]{2,1,0:T(8,128)(2,1)}, u32[]{:S(2)}, u32[]{:S(2)}) async-start(bf16[4,144,1280]{2,1,0:T(8,128)(2,1)} %tell.1), calls=%async_computation | async-start | bytes 2949120 | tf_op jit(solution)/shard_map/all_to_all | solution.py:539
  140.4 7.8 %last.1 = (f32[128,1536]{1,0:T(8,128)}, f32[128,1536]{1,0:T(8,128)}) custom-call(s32[5]{0:T(128)} %stack.32.place, bf16[2,128,2560]{2,1,0:T(8,128)(2,1)} %copy-done, bf16[2,128,2560]{2,1,0:T(8,128)(2,1)} %copy-done.7, bf16[2,128,2560]{2,1,0:T(8,128)(2,1)} %collective-permute-done.2.refs_2_, bf16[2,128,2560]{2,1,0:T(8,128)(2,1)} %copy-done.9, ...), custom_call_target="tpu_custom_call" | custom-call | flops 503316480 | bytes 2686976 | tf_op jit(solution)/shard_map/last/pallas_call | solution.py:233
  148.3 10.3 %value.1 = (f32[512,768]{1,0:T(8,128)}, f32[512,768]{1,0:T(8,128)}) custom-call(s32[5]{0:T(128)} %stack.32.place, bf16[2,128,2560]{2,1,0:T(8,128)(2,1)} %copy-done, bf16[2,128,2560]{2,1,0:T(8,128)(2,1)} %copy-done.7, bf16[2,128,2560]{2,1,0:T(8,128)(2,1)} %collective-permute-done.2.refs_2_, bf16[2,128,2560]{2,1,0:T(8,128)(2,1)} %copy-done.9, ...), custom_call_target="tpu_custom_call" | custom-call | flops 1006632960 | bytes 3080192 | tf_op jit(solution)/shard_map/value/pallas_call | solution.py:233
  159.1 5.3 %collective-permute-done.15.refs_9_ = bf16[768,640]{1,0:T(8,128)(2,1)} collective-permute-done((bf16[768,640]{1,0:T(8,128)(2,1)}, bf16[768,640]{1,0:T(8,128)(2,1)}, u32[]{:S(2)}, u32[]{:S(2)}) %collective-permute-start.15) | collective-permute-done | bytes 983072 | tf_op jit(solution)/shard_map/ppermute | solution.py:551
  170.4 4.8 %all-to-all-start.1 = ((f32[4,2,512]{2,1,0:T(2,128)}), f32[4,2,512]{2,1,0:T(2,128)S(1)}, u32[]{:S(2)}, u32[]{:S(2)}) async-start(f32[4,2,512]{2,1,0:T(2,128)} %norms.1), calls=%async_computation.1 | async-start | bytes 32768 | tf_op jit(solution)/shard_map/all_to_all | solution.py:556
  175.8 5.1 %all-to-all-done.1.squares = f32[4,2,512]{2,1,0:T(2,128)S(1)} async-done(((f32[4,2,512]{2,1,0:T(2,128)}), f32[4,2,512]{2,1,0:T(2,128)S(1)}, u32[]{:S(2)}, u32[]{:S(2)}) %all-to-all-start.1) | async-done | bytes 16416 | tf_op jit(solution)/shard_map/all_to_all | solution.py:556
  185.2 7.7 %probs.1 = bf16[6,512,512]{2,1,0:T(8,128)(2,1)} custom-call(s32[5]{0:T(128)} %stack.32.place, f32[4,2,512]{2,1,0:T(2,128)} %copy-done.26, f32[384,1536]{1,0:T(8,128)} %get-tuple-element.48.first_a.refs_0_.refs_4_, f32[384,1536]{1,0:T(8,128)} %copy-done.2, f32[128,1536]{1,0:T(8,128)} %get-tuple-element.51.last_a.refs_2_.refs_6_, f32[128,1536]{1,0:T(8,128)} %copy-done.8, ...), custom_call_target="tpu_custom_call" | custom-call | flops 100663296 | bytes 2359296 | tf_op jit(solution)/shard_map/probs/pallas_call | solution.py:325
  192.9 5.0 %attend.1 = bf16[4,128,768]{2,1,0:T(8,128)(2,1)} custom-call(s32[5]{0:T(128)} %stack.32.place, bf16[6,512,512]{2,1,0:T(8,128)(2,1)} %probs.1, f32[512,768]{1,0:T(8,128)} %get-tuple-element.55.v_a, f32[512,768]{1,0:T(8,128)} %collective-permute-done.22.v_b), custom_call_target="tpu_custom_call" | custom-call | flops 100663296 | bytes 1769472 | tf_op jit(solution)/shard_map/attend/pallas_call | solution.py:354
  197.9 8.1 %collective-permute-done.24.refs_10_ = bf16[768,640]{1,0:T(8,128)(2,1)} collective-permute-done((bf16[768,640]{1,0:T(8,128)(2,1)}, bf16[768,640]{1,0:T(8,128)(2,1)}, u32[]{:S(2)}, u32[]{:S(2)}) %collective-permute-start.24) | collective-permute-done | bytes 983072 | tf_op jit(solution)/shard_map/ppermute | solution.py:551
  213.7 12.6 %all-to-all-done.2.refs_0_ = bf16[4,128,768]{2,1,0:T(8,128)(2,1)S(1)} async-done(((bf16[4,128,768]{2,1,0:T(8,128)(2,1)}), bf16[4,128,768]{2,1,0:T(8,128)(2,1)S(1)}, u32[]{:S(2)}, u32[]{:S(2)}) %all-to-all-start.2) | async-done | bytes 786464 | tf_op jit(solution)/shard_map/all_to_all | solution.py:561
  231.5 18.4 %collective-permute-done.32.refs_11_ = bf16[768,640]{1,0:T(8,128)(2,1)S(1)} collective-permute-done((bf16[768,640]{1,0:T(8,128)(2,1)}, bf16[768,640]{1,0:T(8,128)(2,1)S(1)}, u32[]{:S(2)}, u32[]{:S(2)}) %collective-permute-start.32) | collective-permute-done | bytes 983072 | tf_op jit(solution)/shard_map/ppermute | solution.py:551
  253.4 8.3 %collective-permute-done.29.refs_3_ = bf16[2,128,768]{2,1,0:T(8,128)(2,1)S(1)} collective-permute-done((bf16[2,128,768]{2,1,0:T(8,128)(2,1)S(1)}, bf16[2,128,768]{2,1,0:T(8,128)(2,1)S(1)}, u32[]{:S(2)}, u32[]{:S(2)}) %collective-permute-start.29) | collective-permute-done | bytes 393248 | tf_op jit(solution)/shard_map/ppermute | solution.py:19
  264.2 13.0 %project_out.1 = bf16[4,2,128,1280]{3,2,1,0:T(8,128)(2,1)} custom-call(s32[5]{0:T(128)} %stack.32.place, bf16[4,128,768]{2,1,0:T(8,128)(2,1)} %copy-done.13, bf16[4,128,768]{2,1,0:T(8,128)(2,1)} %copy-done.15, bf16[4,128,768]{2,1,0:T(8,128)(2,1)} %copy-done.14, bf16[2,128,768]{2,1,0:T(8,128)(2,1)} %copy-done.24, bf16[2,128,768]{2,1,0:T(8,128)(2,1)} %copy-done.25, ...), custom_call_target="tpu_custom_call" | custom-call | flops 1006632960 | bytes 3407872 | tf_op jit(solution)/shard_map/project_out/pallas_call | solution.py:453
  277.2 4.8 %all-to-all-start.3 = ((bf16[4,2,128,1280]{3,2,1,0:T(8,128)(2,1)}), bf16[4,2,128,1280]{3,2,1,0:T(8,128)(2,1)}, u32[]{:S(2)}, u32[]{:S(2)}) async-start(bf16[4,2,128,1280]{3,2,1,0:T(8,128)(2,1)} %project_out.1), calls=%async_computation.3 | async-start | bytes 5242880 | tf_op jit(solution)/shard_map/all_to_all | solution.py:570
  284.0 28.5 %all-to-all-done.3.arrived = bf16[4,2,128,1280]{3,2,1,0:T(8,128)(2,1)} async-done(((bf16[4,2,128,1280]{3,2,1,0:T(8,128)(2,1)}), bf16[4,2,128,1280]{3,2,1,0:T(8,128)(2,1)}, u32[]{:S(2)}, u32[]{:S(2)}) %all-to-all-start.3) | async-done | bytes 2621472 | tf_op jit(solution)/shard_map/all_to_all | solution.py:570
  312.5 4.8 %finish.1 = (f32[128,5120]{1,0:T(8,128)}, bf16[128,5120]{1,0:T(8,128)(2,1)}) custom-call(f32[128,5120]{1,0:T(8,128)} %select_add_fusion.base, bf16[4,2,128,1280]{3,2,1,0:T(8,128)(2,1)} %all-to-all-done.3.arrived), custom_call_target="tpu_custom_call" | custom-call | flops 163840 | bytes 2293760 | tf_op jit(solution)/shard_map/finish/pallas_call | solution.py:479
  (139 shorter events, 74.5 us)
Async XLA Ops:
  10.0 46.0 %collective-permute-start.6 = (bf16[640,1536]{1,0:T(8,128)(2,1)S(1)}, bf16[640,1536]{1,0:T(8,128)(2,1)S(1)}, u32[]{:S(2)}, u32[]{:S(2)}) collective-permute-start(bf16[640,1536]{1,0:T(8,128)(2,1)S(1)} %constant_dynamic-update-slice_fusion.refs_7_), channel_id=1, source_target_pairs={{0,16},{8,24},{16,0},{24,8},{1,17},{9,25},{17,1},{25,9},{2,18},{10... | collective-permute-start | bytes 5898248 | tf_op jit(solution)/shard_map/ppermute | solution.py:19
  12.5 44.9 %collective-permute-start.5 = (bf16[640,1536]{1,0:T(8,128)(2,1)S(1)}, bf16[640,1536]{1,0:T(8,128)(2,1)S(1)}, u32[]{:S(2)}, u32[]{:S(2)}) collective-permute-start(bf16[640,1536]{1,0:T(8,128)(2,1)S(1)} %constant_dynamic-update-slice_fusion.refs_7_), channel_id=1, source_target_pairs={{0,8},{8,0},{16,24},{24,16},{1,9},{9,1},{17,25},{25,17},{2,10},{10... | collective-permute-start | bytes 5898248 | tf_op jit(solution)/shard_map/ppermute | solution.py:19
  15.3 32.6 %collective-permute-start.3 = (bf16[2,128,2560]{2,1,0:T(8,128)(2,1)S(1)}, bf16[2,128,2560]{2,1,0:T(8,128)(2,1)S(1)}, u32[]{:S(2)}, u32[]{:S(2)}) collective-permute-start(bf16[2,128,2560]{2,1,0:T(8,128)(2,1)S(1)} %pad_maximum_fusion.refs_0_.refs_3_.refs_6_), channel_id=1, source_target_pairs={{2,0},{4,2},{6,4},{3,1},{5,3},{7,5},{10,8},{12,10},{14,12},{11,9},... | collective-permute-start | bytes 3932168 | tf_op jit(solution)/shard_map/ppermute | solution.py:508
  16.7 32.5 %collective-permute-start.1 = (bf16[2,128,2560]{2,1,0:T(8,128)(2,1)S(1)}, bf16[2,128,2560]{2,1,0:T(8,128)(2,1)S(1)}, u32[]{:S(2)}, u32[]{:S(2)}) collective-permute-start(bf16[2,128,2560]{2,1,0:T(8,128)(2,1)S(1)} %pad_maximum_fusion.refs_0_.refs_3_.refs_6_), channel_id=1, source_target_pairs={{0,2},{2,4},{4,6},{1,3},{3,5},{5,7},{8,10},{10,12},{12,14},{9,11},... | collective-permute-start | bytes 3932168 | tf_op jit(solution)/shard_map/ppermute | solution.py:507
  47.9 33.2 %collective-permute-start.4 = (bf16[2,128,2560]{2,1,0:T(8,128)(2,1)S(1)}, bf16[2,128,2560]{2,1,0:T(8,128)(2,1)}, u32[]{:S(2)}, u32[]{:S(2)}) collective-permute-start(bf16[2,128,2560]{2,1,0:T(8,128)(2,1)S(1)} %collective-permute-done.3.refs_4_), channel_id=1, source_target_pairs={{2,0},{4,2},{3,1},{5,3},{10,8},{12,10},{11,9},{13,11},{18,16},{20,... | collective-permute-start | bytes 3932168 | tf_op jit(solution)/shard_map/ppermute | solution.py:508
  49.2 32.9 %collective-permute-start.2 = (bf16[2,128,2560]{2,1,0:T(8,128)(2,1)S(1)}, bf16[2,128,2560]{2,1,0:T(8,128)(2,1)}, u32[]{:S(2)}, u32[]{:S(2)}) collective-permute-start(bf16[2,128,2560]{2,1,0:T(8,128)(2,1)S(1)} %collective-permute-done.1.refs_1_), channel_id=1, source_target_pairs={{2,4},{4,6},{3,5},{5,7},{10,12},{12,14},{11,13},{13,15},{18,20},{2... | collective-permute-start | bytes 3932168 | tf_op jit(solution)/shard_map/ppermute | solution.py:507
  57.6 23.2 %collective-permute-start.8 = (bf16[640,768]{1,0:T(8,128)(2,1)S(1)}, bf16[640,768]{1,0:T(8,128)(2,1)S(1)}, u32[]{:S(2)}, u32[]{:S(2)}) collective-permute-start(bf16[640,768]{1,0:T(8,128)(2,1)S(1)} %slice.27), channel_id=1, source_target_pairs={{0,16},{8,24},{16,0},{24,8},{1,17},{9,25},{17,1},{25,9},{2,18},{10... | collective-permute-start | bytes 2949128 | tf_op jit(solution)/shard_map/ppermute | solution.py:19
  58.0 23.1 %collective-permute-start.7 = (bf16[640,768]{1,0:T(8,128)(2,1)S(1)}, bf16[640,768]{1,0:T(8,128)(2,1)S(1)}, u32[]{:S(2)}, u32[]{:S(2)}) collective-permute-start(bf16[640,768]{1,0:T(8,128)(2,1)S(1)} %slice.26), channel_id=1, source_target_pairs={{0,8},{8,0},{16,24},{24,16},{1,9},{9,1},{17,25},{25,17},{2,10},{10... | collective-permute-start | bytes 2949128 | tf_op jit(solution)/shard_map/ppermute | solution.py:19
  82.1 27.8 %collective-permute-start.9 = (bf16[2,128,2560]{2,1,0:T(8,128)(2,1)}, bf16[2,128,2560]{2,1,0:T(8,128)(2,1)S(1)}, u32[]{:S(2)}, u32[]{:S(2)}) collective-permute-start(bf16[2,128,2560]{2,1,0:T(8,128)(2,1)} %collective-permute-done.2.refs_2_), channel_id=1, source_target_pairs={{4,6},{5,7},{12,14},{13,15},{20,22},{21,23},{28,30},{29,31}} | collective-permute-start | bytes 3932168 | tf_op jit(solution)/shard_map/ppermute | solution.py:507
  82.9 31.4 %collective-permute-start.10 = (bf16[2,128,2560]{2,1,0:T(8,128)(2,1)}, bf16[2,128,2560]{2,1,0:T(8,128)(2,1)S(1)}, u32[]{:S(2)}, u32[]{:S(2)}) collective-permute-start(bf16[2,128,2560]{2,1,0:T(8,128)(2,1)} %collective-permute-done.4.refs_5_), channel_id=1, source_target_pairs={{2,0},{3,1},{10,8},{11,9},{18,16},{19,17},{26,24},{27,25}} | collective-permute-start | bytes 3932168 | tf_op jit(solution)/shard_map/ppermute | solution.py:508
  84.2 24.5 %collective-permute-start.11 = (bf16[640,768]{1,0:T(8,128)(2,1)}, bf16[640,768]{1,0:T(8,128)(2,1)}, u32[]{:S(2)}, u32[]{:S(2)}) collective-permute-start(bf16[640,768]{1,0:T(8,128)(2,1)} %refs_7_.1), channel_id=1, source_target_pairs={{0,8},{8,0},{16,24},{24,16},{1,9},{9,1},{17,25},{25,17},{2,10},{10... | collective-permute-start | bytes 2949128 | tf_op jit(solution)/shard_map/ppermute | solution.py:19
  85.8 24.1 %collective-permute-start.12 = (bf16[640,768]{1,0:T(8,128)(2,1)}, bf16[640,768]{1,0:T(8,128)(2,1)}, u32[]{:S(2)}, u32[]{:S(2)}) collective-permute-start(bf16[640,768]{1,0:T(8,128)(2,1)} %refs_7_.1), channel_id=1, source_target_pairs={{0,16},{8,24},{16,0},{24,8},{1,17},{9,25},{17,1},{25,9},{2,18},{10... | collective-permute-start | bytes 2949128 | tf_op jit(solution)/shard_map/ppermute | solution.py:19
  115.4 49.0 %collective-permute-start.18 = (f32[384,1536]{1,0:T(8,128)}, f32[384,1536]{1,0:T(8,128)S(1)}, u32[]{:S(2)}, u32[]{:S(2)}) collective-permute-start(f32[384,1536]{1,0:T(8,128)} %get-tuple-element.59), channel_id=1, source_target_pairs={{0,1},{1,0},{2,3},{3,2},{4,5},{5,4},{6,7},{7,6},{8,9},{9,8},{10,11... | collective-permute-start | bytes 7077896 | tf_op jit(solution)/shard_map/ppermute | solution.py:19
  132.2 32.2 %all-to-all-start = ((bf16[4,144,1280]{2,1,0:T(8,128)(2,1)}), bf16[4,144,1280]{2,1,0:T(8,128)(2,1)}, u32[]{:S(2)}, u32[]{:S(2)}) async-start(bf16[4,144,1280]{2,1,0:T(8,128)(2,1)} %tell.1), calls=%async_computation | async-start | bytes 2949120 | tf_op jit(solution)/shard_map/all_to_all | solution.py:539
  136.5 22.6 %collective-permute-start.14 = (bf16[768,640]{1,0:T(8,128)(2,1)}, bf16[768,640]{1,0:T(8,128)(2,1)}, u32[]{:S(2)}, u32[]{:S(2)}) collective-permute-start(bf16[768,640]{1,0:T(8,128)(2,1)} %refs_5_.1), channel_id=1, source_target_pairs={{0,2},{2,4},{4,6},{1,3},{3,5},{5,7},{8,10},{10,12},{12,14},{9,11},... | collective-permute-start | bytes 2949128 | tf_op jit(solution)/shard_map/ppermute | solution.py:550
  139.1 25.3 %collective-permute-start.15 = (bf16[768,640]{1,0:T(8,128)(2,1)}, bf16[768,640]{1,0:T(8,128)(2,1)}, u32[]{:S(2)}, u32[]{:S(2)}) collective-permute-start(bf16[768,640]{1,0:T(8,128)(2,1)} %refs_5_.1), channel_id=1, source_target_pairs={{2,0},{4,2},{6,4},{3,1},{5,3},{7,5},{10,8},{12,10},{14,12},{11,9},... | collective-permute-start | bytes 2949128 | tf_op jit(solution)/shard_map/ppermute | solution.py:551
  158.5 34.4 %collective-permute-start.22 = (f32[512,768]{1,0:T(8,128)}, f32[512,768]{1,0:T(8,128)}, u32[]{:S(2)}, u32[]{:S(2)}) collective-permute-start(f32[512,768]{1,0:T(8,128)} %get-tuple-element.63), channel_id=1, source_target_pairs={{0,1},{1,0},{2,3},{3,2},{4,5},{5,4},{6,7},{7,6},{8,9},{9,8},{10,11... | collective-permute-start | bytes 4718600 | tf_op jit(solution)/shard_map/ppermute | solution.py:19
  182.5 23.5 %collective-permute-start.24 = (bf16[768,640]{1,0:T(8,128)(2,1)}, bf16[768,640]{1,0:T(8,128)(2,1)}, u32[]{:S(2)}, u32[]{:S(2)}) collective-permute-start(bf16[768,640]{1,0:T(8,128)(2,1)} %collective-permute-done.15.refs_9_), channel_id=1, source_target_pairs={{2,0},{4,2},{3,1},{5,3},{10,8},{12,10},{11,9},{13,11},{18,16},{20,... | collective-permute-start | bytes 2949128 | tf_op jit(solution)/shard_map/ppermute | solution.py:551
  206.0 20.3 %all-to-all-start.2 = ((bf16[4,128,768]{2,1,0:T(8,128)(2,1)}), bf16[4,128,768]{2,1,0:T(8,128)(2,1)S(1)}, u32[]{:S(2)}, u32[]{:S(2)}) async-start(bf16[4,128,768]{2,1,0:T(8,128)(2,1)} %attend.1), calls=%async_computation.2 | async-start | bytes 1572864 | tf_op jit(solution)/shard_map/all_to_all | solution.py:561
  227.0 23.0 %collective-permute-start.32 = (bf16[768,640]{1,0:T(8,128)(2,1)}, bf16[768,640]{1,0:T(8,128)(2,1)S(1)}, u32[]{:S(2)}, u32[]{:S(2)}) collective-permute-start(bf16[768,640]{1,0:T(8,128)(2,1)} %collective-permute-done.24.refs_10_), channel_id=1, source_target_pairs={{2,0},{3,1},{10,8},{11,9},{18,16},{19,17},{26,24},{27,25}} | collective-permute-start | bytes 2949128 | tf_op jit(solution)/shard_map/ppermute | solution.py:551
  228.3 21.7 %collective-permute-start.28 = (bf16[4,128,768]{2,1,0:T(8,128)(2,1)S(1)}, bf16[4,128,768]{2,1,0:T(8,128)(2,1)S(1)}, u32[]{:S(2)}, u32[]{:S(2)}) collective-permute-start(bf16[4,128,768]{2,1,0:T(8,128)(2,1)S(1)} %all-to-all-done.2.refs_0_), channel_id=1, source_target_pairs={{0,16},{8,24},{16,0},{24,8},{1,17},{9,25},{17,1},{25,9},{2,18},{10... | collective-permute-start | bytes 2359304 | tf_op jit(solution)/shard_map/ppermute | solution.py:19
  230.1 21.7 %collective-permute-start.27 = (bf16[4,128,768]{2,1,0:T(8,128)(2,1)S(1)}, bf16[4,128,768]{2,1,0:T(8,128)(2,1)S(1)}, u32[]{:S(2)}, u32[]{:S(2)}) collective-permute-start(bf16[4,128,768]{2,1,0:T(8,128)(2,1)S(1)} %all-to-all-done.2.refs_0_), channel_id=1, source_target_pairs={{0,8},{8,0},{16,24},{24,16},{1,9},{9,1},{17,25},{25,17},{2,10},{10... | collective-permute-start | bytes 2359304 | tf_op jit(solution)/shard_map/ppermute | solution.py:19
  231.5 31.6 %collective-permute-start.33 = (bf16[768,640]{1,0:T(8,128)(2,1)S(1)}, bf16[768,640]{1,0:T(8,128)(2,1)S(1)}, u32[]{:S(2)}, u32[]{:S(2)}) collective-permute-start(bf16[768,640]{1,0:T(8,128)(2,1)S(1)} %collective-permute-done.31.refs_8_), channel_id=1, source_target_pairs={{0,1},{1,0},{2,3},{3,2},{4,5},{5,4},{6,7},{7,6},{8,9},{9,8},{10,11... | collective-permute-start | bytes 2949128 | tf_op jit(solution)/shard_map/ppermute | solution.py:19
  277.2 35.2 %all-to-all-start.3 = ((bf16[4,2,128,1280]{3,2,1,0:T(8,128)(2,1)}), bf16[4,2,128,1280]{3,2,1,0:T(8,128)(2,1)}, u32[]{:S(2)}, u32[]{:S(2)}) async-start(bf16[4,2,128,1280]{3,2,1,0:T(8,128)(2,1)} %project_out.1), calls=%async_computation.3 | async-start | bytes 5242880 | tf_op jit(solution)/shard_map/all_to_all | solution.py:570
  (45 other events, 752.7 us)

commit v9 on v8

--- a/solution.py
+++ b/solution.py
@@ -364,7 +364,7 @@
     )(place, probs, *v_parts)
 
 
-def out_kernel(size, layout, place, *refs):
+def out_kernel(size, layout, first, place, *refs):
     count = 2 * size - 1
     pieces, weights = refs[: len(layout)], refs[len(layout) : len(layout) + 2 * count]
     heard, out, a_held, w_held, total, a_sems, w_sems = refs[len(layout) + 2 * count :]
@@ -379,7 +379,9 @@
             row = pl.multiple_of(jnp.bitwise_xor(step_at, offset) * tokens, tokens)
             for group in range(groups):
                 yield pltpu.make_async_copy(
-                    pieces[index].at[group], a_held.at[start + group, pl.ds(row, tokens)], a_sems.at[index, group]
+                    pieces[index].at[group, pl.ds(first, tokens)],
+                    a_held.at[start + group, pl.ds(row, tokens)],
+                    a_sems.at[index, group],
                 )
 
     def w_copy(half, away, slot):
@@ -425,20 +427,21 @@
         span = slice(half * span_width, (half + 1) * span_width)
         reached = jnp.zeros((tokens, span_width), jnp.float32)
         for step in range(steps):
-            told = heard[step, tokens : tokens + 16, span].astype(jnp.float32)
+            told = heard[step, -16:, span].astype(jnp.float32)
             gate = told[0:1] + told[1:2] + told[2:3]
             step_width = told[3:4] + told[4:5] + told[5:6]
             branch = total[half, step * tokens : (step + 1) * tokens] * gate
             out[step, 0, :, span] = branch.astype(jnp.bfloat16)
             reached += branch * step_width
             out[step, 1, :, span] = reached.astype(jnp.bfloat16)
-            reached += heard[step, :tokens, span].astype(jnp.float32)
-
-
-def project_out(place, heard, gathered, weights):
+            reached += heard[step, first : first + tokens, span].astype(jnp.float32)
+
+
+def project_out(place, heard, gathered, weights, part, parts):
     size = lax.axis_size("head")
     steps = len(gathered)
     _, tokens, inner = gathered[0][0].shape
+    tokens = tokens // parts
     width = weights[0][0].shape[1]
     layout, pieces = [], []
     for offset, held in enumerate(gathered):
@@ -451,7 +454,7 @@
     halves = 1 if width % 128 == 0 else 2
     operands = pieces + [w for half in weights for w in half]
     return pl.pallas_call(
-        functools.partial(out_kernel, size, tuple(layout)),
+        functools.partial(out_kernel, size, tuple(layout), part * tokens),
         in_specs=[SMEM] + [ANY] * len(operands) + [VMEM],
         out_specs=VMEM,
         out_shape=jax.ShapeDtypeStruct((steps, 2, tokens, 2 * width), jnp.bfloat16),
@@ -468,24 +471,26 @@
     )(place, *operands, heard)
 
 
-def finish_kernel(base, arrived, reached, update):
+def finish_kernel(base, arrived, *refs):
+    reached, update = refs[-2:]
     reached[...] = base[...] + arrived[0, 1].astype(jnp.float32)
     update[...] = arrived[0, 0]
 
 
-def finish(base, arrived):
+def finish(base, arrived, part, started):
     steps, _, tokens, width = arrived.shape
-    by_columns = pl.BlockSpec((tokens, width), lambda i: (0, i))
+    by_columns = pl.BlockSpec((tokens, width), lambda i: (part, i))
     return pl.pallas_call(
         finish_kernel,
         grid=(steps,),
-        in_specs=[by_columns, pl.BlockSpec((1, 2, tokens, width), lambda i: (i, 0, 0, 0))],
+        in_specs=[by_columns, pl.BlockSpec((1, 2, tokens, width), lambda i: (i, 0, 0, 0))] + [ANY] * len(started),
         out_specs=[by_columns, by_columns],
         out_shape=[jax.ShapeDtypeStruct(base.shape, jnp.float32), jax.ShapeDtypeStruct(base.shape, jnp.bfloat16)],
-        compiler_params=params(),
-        cost_estimate=cost(base.size, 14 * base.size),
+        input_output_aliases={2 + i: i for i in range(len(started))},
+        compiler_params=params(),
+        cost_estimate=cost(arrived.size // 2, 7 * arrived.size),
         name="finish",
-    )(base, arrived)
+    )(base, arrived, *started)
 
 
 def body(states, timesteps, lengths, modulation, w_query, w_key, w_value, w_out, q_gain, k_gain):
@@ -496,7 +501,7 @@
     place = jnp.stack([step, core, position, lengths[0], shift]).astype(jnp.int32)
 
     w_both = jnp.concatenate([w_query, w_key], axis=1)
-    mine, other = modulate(place, after(current, w_both), modulation, steps)
+    mine, other = modulate(place, current, modulation, steps)
     tokens = jnp.stack([mine, swap(other, "fsdp", 1)])
     below, above = [tokens], [tokens]
 
@@ -536,7 +541,7 @@
     parts += [last_here, swap(after(last_there, *v_last), "fsdp", 1)]
     v_here, v_there = project(after(place, last_here), line, v_shards, "all", "value")
     v_parts = [v_here, swap(v_there, "fsdp", 1)]
-    heard = lax.all_to_all(after(told, *v_last), "step", 0, 0)
+    heard = lax.all_to_all(after(told, last_here, *v_last), "step", 0, 0)
 
     below, above = [w_out], [w_out]
     for count in range(1, size):
@@ -544,7 +549,7 @@
         if count == 1:
             up, down = after((up, down), *ended, first_here)
         if count == 2:
-            up, down = after((up, down), squares)
+            up, down = after((up, down), v_here)
         if count == size - 1:
             up, down = after((up, down), quarter)
         below.append(lax.ppermute(up, "head", [(i, i + 1) for i in range(count - 1, size - 1)]))
@@ -554,10 +559,10 @@
         if count == 1:
             own_squares = norms(after(place, below[-1], above[-1], v_here, heard), parts, size)
             squares = lax.all_to_all(own_squares, "head", 0, 0)
-            ready = after(squares, *partner_below, *partner_above)
+        if count == size - 2:
+            ready = after(squares, *partner_below[:-1], *partner_above[:-1], below[-1], above[-1])
             probs = probabilities(place, ready, parts, q_gain, k_gain)
-        if count == size - 2:
-            attended = after(attend(place, probs, v_parts, size), below[-1], above[-1])
+            attended = attend(place, probs, v_parts, size)
             quarter = after(lax.all_to_all(attended, "head", 0, 0), partner_below[-1], partner_above[-1])
 
     gathered = forwarded(quarter, direct(quarter))
@@ -566,9 +571,11 @@
     out_weights = (raw, partner_below + partner_above)
     carried = step_width * current + jnp.where(step == 0, current, jnp.zeros_like(current))
 
-    sent = project_out(place, heard, gathered, out_weights)
-    arrived = lax.all_to_all(sent, "step", 0, 0)
-    reached, update = finish(carried, arrived)
+    outputs, parts_of = (), 2
+    sent = [project_out(place, heard, gathered, out_weights, part, parts_of) for part in range(parts_of)]
+    for part in range(parts_of):
+        outputs = finish(carried, lax.all_to_all(sent[part], "step", 0, 0), part, outputs)
+    reached, update = outputs
     return reached[None, None], update[None, None]
 
 

time: 319 us -> 312 us (0.978)
  waiting for transfers between devices: 166 us -> 151 us
  Pallas kernels: 74.3 us -> 82.2 us
  starting transfers between devices: 58 us -> 61.6 us
    ppermute x23, waiting for transfers between devices: 56.7 us -> 46.9 us  [swap(): lax.ppermute(x, axis, [(i, i ^ offset) for i in range(lax.axis_size(axis))])]
    ppermute x3, waiting for transfers between devices: 31.8 us -> 22.1 us  [body(): lax.ppermute(down, 'head', [(i, i - 1) for i in range(1, size - count + 1)])]
    pallas_call x1 -> x2, Pallas kernels: 13 us -> 18.8 us  [project_out(): pl.pallas_call(functools.partial(out_kernel, size, tuple(layout), part *...]
    all_to_all x2 -> x3, waiting for transfers between devices: 28.5 us -> 32.3 us  [the longest x2 17.3 us: body(): lax.all_to_all(sent[part], 'step', 0, 0)]
    all_to_all x2 -> x3, starting transfers between devices: 9.16 us -> 13 us  [the longest x2 8.62 us: body(): lax.all_to_all(sent[part], 'step', 0, 0)]
    unnamed x62 -> x70, local copies, waits for them, and re-layouts: 8.19 us -> 5.1 us
    pallas_call x1 -> x2, Pallas kernels: 4.83 us -> 7.63 us  [finish(): pl.pallas_call(finish_kernel, grid=(steps,), in_specs=[by_columns, pl.Blo...]
  transfers between devices with their start and end apart: 39 -> 40, of which waited for: 20 -> 20; matrix products, arithmetic and copies ran while one was open for 2% -> 2% of each run, Pallas kernels for 16% -> 19%
where the time goes in v9:
time: 312 us; the launch traced here: 310 us
  waiting for transfers between devices  151 us (48%)
  Pallas kernels  82.2 us (26%)
  starting transfers between devices  61.6 us (20%)
  local copies, waits for them, and re-layouts  10.2 us (3%)
  between operations  3.13 us (1%)
    ppermute x23, waiting for transfers between devices, swap(): lax.ppermute(x, axis, [(i, i ^ offset) for i in range(lax.axis_size(axis))])  46.9 us
    pallas_call x3, Pallas kernels, project(): pl.pallas_call(functools.partial(project_kernel, size, parts, shard, tupl...  31.4 us
    ppermute x3, waiting for transfers between devices, hop(): lax.ppermute(down, 'head', [(i, i - 1) for i in range(1, size - count + 1)])  31 us
    ppermute x3, waiting for transfers between devices, body(): lax.ppermute(down, 'head', [(i, i - 1) for i in range(1, size - count + 1)])  22.1 us
    pallas_call x2, Pallas kernels, project_out(): pl.pallas_call(functools.partial(out_kernel, size, tuple(layout), part *...  18.8 us
    ppermute x23, starting transfers between devices, swap(): lax.ppermute(x, axis, [(i, i ^ offset) for i in range(lax.axis_size(axis))])  17.8 us
    all_to_all x2, waiting for transfers between devices, body(): lax.all_to_all(sent[part], 'step', 0, 0)  17.3 us
    all_to_all x1, waiting for transfers between devices, body(): heard = lax.all_to_all(after(told, last_here, *v_last), 'step', 0, 0)  15 us
  transfers between devices with their start and end apart: 40, of which 20 were waited for; matrix products, arithmetic and copies ran while one was open for 2% of the time, Pallas kernels for 19%

profile of v9, /device:TPU:0, one launch (start us, length us, event | category | flops | bytes accessed | tf_op | source)
XLA Modules:
  0.0 310.1 jit_solution(8745963800165216538)
XLA Ops:
  3.5 4.6 %modulate.1 = (bf16[128,2560]{1,0:T(8,128)(2,1)}, bf16[128,2560]{1,0:T(8,128)(2,1)}) custom-call(s32[5]{0:T(128)} %stack.32.place, f32[128,5120]{1,0:T(8,128)} %bitcast.12, f32[1,3,5120]{2,1,0:T(4,128)} %copy.14.rows), custom_call_target="tpu_custom_call" | custom-call | flops 1638400 | bytes 983040 | tf_op jit(solution)/shard_map/modulate/pallas_call | solution.py:119
  14.4 4.6 %collective-permute-start.1 = (bf16[2,128,2560]{2,1,0:T(8,128)(2,1)S(1)}, bf16[2,128,2560]{2,1,0:T(8,128)(2,1)S(1)}, u32[]{:S(2)}, u32[]{:S(2)}) collective-permute-start(bf16[2,128,2560]{2,1,0:T(8,128)(2,1)S(1)} %pad_maximum_fusion.refs_0_.refs_3_.refs_6_), channel_id=1, source_target_pairs={{0,2},{2,4},{4,6},{1,3},{3,5},{5,7},{8,10},{10,12},{12,14},{9,11},... | collective-permute-start | bytes 3932168 | tf_op jit(solution)/shard_map/ppermute | solution.py:512
  19.1 26.6 %collective-permute-done.3.refs_4_ = bf16[2,128,2560]{2,1,0:T(8,128)(2,1)S(1)} collective-permute-done((bf16[2,128,2560]{2,1,0:T(8,128)(2,1)S(1)}, bf16[2,128,2560]{2,1,0:T(8,128)(2,1)S(1)}, u32[]{:S(2)}, u32[]{:S(2)}) %collective-permute-start.3) | collective-permute-done | bytes 1310752 | tf_op jit(solution)/shard_map/ppermute | solution.py:513
  48.7 6.1 %collective-permute-done.6.refs_9_ = bf16[640,1536]{1,0:T(8,128)(2,1)S(1)} collective-permute-done((bf16[640,1536]{1,0:T(8,128)(2,1)S(1)}, bf16[640,1536]{1,0:T(8,128)(2,1)S(1)}, u32[]{:S(2)}, u32[]{:S(2)}) %collective-permute-start.6) | collective-permute-done | bytes 1966112 | tf_op jit(solution)/shard_map/ppermute | solution.py:19
  58.5 21.2 %collective-permute-done.8.refs_11_ = bf16[640,768]{1,0:T(8,128)(2,1)S(1)} collective-permute-done((bf16[640,768]{1,0:T(8,128)(2,1)S(1)}, bf16[640,768]{1,0:T(8,128)(2,1)S(1)}, u32[]{:S(2)}, u32[]{:S(2)}) %collective-permute-start.8) | collective-permute-done | bytes 983072 | tf_op jit(solution)/shard_map/ppermute | solution.py:19
  90.9 13.5 %first.1 = (f32[384,1536]{1,0:T(8,128)}, f32[384,1536]{1,0:T(8,128)}) custom-call(s32[5]{0:T(128)} %stack.32.place, bf16[2,128,2560]{2,1,0:T(8,128)(2,1)} %copy-done, bf16[2,128,2560]{2,1,0:T(8,128)(2,1)} %copy-done.7, bf16[2,128,2560]{2,1,0:T(8,128)(2,1)} %collective-permute-done.2.refs_2_, bf16[2,128,2560]{2,1,0:T(8,128)(2,1)} %copy-done, ...), custom_call_target="tpu_custom_call" | custom-call | flops 1509949440 | bytes 4128768 | tf_op jit(solution)/shard_map/first/pallas_call | solution.py:233
  107.9 4.4 %collective-permute-done.10.refs_6_ = bf16[2,128,2560]{2,1,0:T(8,128)(2,1)S(1)} collective-permute-done((bf16[2,128,2560]{2,1,0:T(8,128)(2,1)}, bf16[2,128,2560]{2,1,0:T(8,128)(2,1)S(1)}, u32[]{:S(2)}, u32[]{:S(2)}) %collective-permute-start.10) | collective-permute-done | bytes 1310752 | tf_op jit(solution)/shard_map/ppermute | solution.py:513
  121.1 7.8 %last.1 = (f32[128,1536]{1,0:T(8,128)}, f32[128,1536]{1,0:T(8,128)}) custom-call(s32[5]{0:T(128)} %stack.32.place, bf16[2,128,2560]{2,1,0:T(8,128)(2,1)} %copy-done, bf16[2,128,2560]{2,1,0:T(8,128)(2,1)} %copy-done.7, bf16[2,128,2560]{2,1,0:T(8,128)(2,1)} %collective-permute-done.2.refs_2_, bf16[2,128,2560]{2,1,0:T(8,128)(2,1)} %copy-done.10, ...), custom_call_target="tpu_custom_call" | custom-call | flops 503316480 | bytes 2686976 | tf_op jit(solution)/shard_map/last/pallas_call | solution.py:233
  129.9 10.2 %value.1 = (f32[512,768]{1,0:T(8,128)}, f32[512,768]{1,0:T(8,128)}) custom-call(s32[5]{0:T(128)} %stack.32.place, bf16[2,128,2560]{2,1,0:T(8,128)(2,1)} %copy-done, bf16[2,128,2560]{2,1,0:T(8,128)(2,1)} %copy-done.7, bf16[2,128,2560]{2,1,0:T(8,128)(2,1)} %collective-permute-done.2.refs_2_, bf16[2,128,2560]{2,1,0:T(8,128)(2,1)} %copy-done.10, ...), custom_call_target="tpu_custom_call" | custom-call | flops 1006632960 | bytes 3080192 | tf_op jit(solution)/shard_map/value/pallas_call | solution.py:233
  140.2 4.3 %all-to-all-start = ((bf16[4,144,1280]{2,1,0:T(8,128)(2,1)}), bf16[4,144,1280]{2,1,0:T(8,128)(2,1)}, u32[]{:S(2)}, u32[]{:S(2)}) async-start(bf16[4,144,1280]{2,1,0:T(8,128)(2,1)} %tell.1), calls=%async_computation | async-start | bytes 2949120 | tf_op jit(solution)/shard_map/all_to_all | solution.py:544
  148.7 15.0 %all-to-all-done.refs_19_ = bf16[4,144,1280]{2,1,0:T(8,128)(2,1)} async-done(((bf16[4,144,1280]{2,1,0:T(8,128)(2,1)}), bf16[4,144,1280]{2,1,0:T(8,128)(2,1)}, u32[]{:S(2)}, u32[]{:S(2)}) %all-to-all-start) | async-done | bytes 1474592 | tf_op jit(solution)/shard_map/all_to_all | solution.py:544
  167.5 7.4 %all-to-all-start.1 = ((f32[4,2,512]{2,1,0:T(2,128)}), f32[4,2,512]{2,1,0:T(2,128)S(1)}, u32[]{:S(2)}, u32[]{:S(2)}) async-start(f32[4,2,512]{2,1,0:T(2,128)} %norms.1), calls=%async_computation.1 | async-start | bytes 32768 | tf_op jit(solution)/shard_map/all_to_all | solution.py:561
  176.3 4.2 %all-to-all-done.1.squares = f32[4,2,512]{2,1,0:T(2,128)S(1)} async-done(((f32[4,2,512]{2,1,0:T(2,128)}), f32[4,2,512]{2,1,0:T(2,128)S(1)}, u32[]{:S(2)}, u32[]{:S(2)}) %all-to-all-start.1) | async-done | bytes 16416 | tf_op jit(solution)/shard_map/all_to_all | solution.py:561
  181.1 7.0 %probs.1 = bf16[6,512,512]{2,1,0:T(8,128)(2,1)} custom-call(s32[5]{0:T(128)} %stack.32.place, f32[4,2,512]{2,1,0:T(2,128)} %copy-done.30, f32[384,1536]{1,0:T(8,128)} %get-tuple-element.47.first_a.refs_0_.refs_4_, f32[384,1536]{1,0:T(8,128)} %copy-done.2, f32[128,1536]{1,0:T(8,128)} %get-tuple-element.50.last_a.refs_2_.refs_6_, f32[128,1536]{1,0:T(8,128)} %copy-done.8, ...), custom_call_target="tpu_custom_call" | custom-call | flops 100663296 | bytes 2359296 | tf_op jit(solution)/shard_map/probs/pallas_call | solution.py:325
  188.1 5.0 %attend.1 = bf16[4,128,768]{2,1,0:T(8,128)(2,1)} custom-call(s32[5]{0:T(128)} %stack.32.place, bf16[6,512,512]{2,1,0:T(8,128)(2,1)} %probs.1, f32[512,768]{1,0:T(8,128)} %get-tuple-element.54.v_a, f32[512,768]{1,0:T(8,128)} %collective-permute-done.24.v_b), custom_call_target="tpu_custom_call" | custom-call | flops 100663296 | bytes 1769472 | tf_op jit(solution)/shard_map/attend/pallas_call | solution.py:354
  200.9 14.5 %all-to-all-done.2.refs_0_ = bf16[4,128,768]{2,1,0:T(8,128)(2,1)S(1)} async-done(((bf16[4,128,768]{2,1,0:T(8,128)(2,1)}), bf16[4,128,768]{2,1,0:T(8,128)(2,1)S(1)}, u32[]{:S(2)}, u32[]{:S(2)}) %all-to-all-start.2) | async-done | bytes 786464 | tf_op jit(solution)/shard_map/all_to_all | solution.py:566
  219.6 21.4 %collective-permute-done.32.refs_11_ = bf16[768,640]{1,0:T(8,128)(2,1)S(1)} collective-permute-done((bf16[768,640]{1,0:T(8,128)(2,1)}, bf16[768,640]{1,0:T(8,128)(2,1)S(1)}, u32[]{:S(2)}, u32[]{:S(2)}) %collective-permute-start.32) | collective-permute-done | bytes 983072 | tf_op jit(solution)/shard_map/ppermute | solution.py:556
  243.2 9.3 %collective-permute-done.29.refs_3_ = bf16[2,128,768]{2,1,0:T(8,128)(2,1)S(1)} collective-permute-done((bf16[2,128,768]{2,1,0:T(8,128)(2,1)S(1)}, bf16[2,128,768]{2,1,0:T(8,128)(2,1)S(1)}, u32[]{:S(2)}, u32[]{:S(2)}) %collective-permute-start.29) | collective-permute-done | bytes 393248 | tf_op jit(solution)/shard_map/ppermute | solution.py:19
  255.9 9.5 %project_out.3 = bf16[4,2,64,1280]{3,2,1,0:T(8,128)(2,1)} custom-call(s32[5]{0:T(128)} %stack.32.place, bf16[4,128,768]{2,1,0:T(8,128)(2,1)} %copy-done.9, bf16[4,128,768]{2,1,0:T(8,128)(2,1)} %copy-done.13, bf16[4,128,768]{2,1,0:T(8,128)(2,1)} %copy-done.12, bf16[2,128,768]{2,1,0:T(8,128)(2,1)} %copy-done.23, bf16[2,128,768]{2,1,0:T(8,128)(2,1)} %copy-done.24, ...), custom_call_target="tpu_custom_call" | custom-call | flops 503316480 | bytes 2686976 | tf_op jit(solution)/shard_map/project_out/pallas_call | solution.py:456
  265.4 4.3 %all-to-all-start.4 = ((bf16[4,2,64,1280]{3,2,1,0:T(8,128)(2,1)}), bf16[4,2,64,1280]{3,2,1,0:T(8,128)(2,1)}, u32[]{:S(2)}, u32[]{:S(2)}) async-start(bf16[4,2,64,1280]{3,2,1,0:T(8,128)(2,1)} %project_out.3), calls=%async_computation.4 | async-start | bytes 2621440 | tf_op jit(solution)/shard_map/all_to_all | solution.py:577
  269.7 9.3 %project_out.2 = bf16[4,2,64,1280]{3,2,1,0:T(8,128)(2,1)} custom-call(s32[5]{0:T(128)} %stack.32.place, bf16[4,128,768]{2,1,0:T(8,128)(2,1)} %copy-done.9, bf16[4,128,768]{2,1,0:T(8,128)(2,1)} %copy-done.13, bf16[4,128,768]{2,1,0:T(8,128)(2,1)} %copy-done.12, bf16[2,128,768]{2,1,0:T(8,128)(2,1)} %copy-done.23, bf16[2,128,768]{2,1,0:T(8,128)(2,1)} %copy-done.24, ...), custom_call_target="tpu_custom_call" | custom-call | flops 503316480 | bytes 2686976 | tf_op jit(solution)/shard_map/project_out/pallas_call | solution.py:456
  279.0 7.0 %all-to-all-done.4.arrived = bf16[4,2,64,1280]{3,2,1,0:T(8,128)(2,1)} async-done(((bf16[4,2,64,1280]{3,2,1,0:T(8,128)(2,1)}), bf16[4,2,64,1280]{3,2,1,0:T(8,128)(2,1)}, u32[]{:S(2)}, u32[]{:S(2)}) %all-to-all-start.4) | async-done | bytes 1310752 | tf_op jit(solution)/shard_map/all_to_all | solution.py:577
  286.1 4.3 %all-to-all-start.3 = ((bf16[4,2,64,1280]{3,2,1,0:T(8,128)(2,1)}), bf16[4,2,64,1280]{3,2,1,0:T(8,128)(2,1)}, u32[]{:S(2)}, u32[]{:S(2)}) async-start(bf16[4,2,64,1280]{3,2,1,0:T(8,128)(2,1)} %project_out.2), calls=%async_computation.3 | async-start | bytes 2621440 | tf_op jit(solution)/shard_map/all_to_all | solution.py:577
  296.0 10.3 %all-to-all-done.3.arrived = bf16[4,2,64,1280]{3,2,1,0:T(8,128)(2,1)} async-done(((bf16[4,2,64,1280]{3,2,1,0:T(8,128)(2,1)}), bf16[4,2,64,1280]{3,2,1,0:T(8,128)(2,1)}, u32[]{:S(2)}, u32[]{:S(2)}) %all-to-all-start.3) | async-done | bytes 1310752 | tf_op jit(solution)/shard_map/all_to_all | solution.py:577
  (151 shorter events, 75.1 us)
Async XLA Ops:
  8.8 46.1 %collective-permute-start.6 = (bf16[640,1536]{1,0:T(8,128)(2,1)S(1)}, bf16[640,1536]{1,0:T(8,128)(2,1)S(1)}, u32[]{:S(2)}, u32[]{:S(2)}) collective-permute-start(bf16[640,1536]{1,0:T(8,128)(2,1)S(1)} %constant_dynamic-update-slice_fusion.refs_7_), channel_id=1, source_target_pairs={{0,16},{8,24},{16,0},{24,8},{1,17},{9,25},{17,1},{25,9},{2,18},{10... | collective-permute-start | bytes 5898248 | tf_op jit(solution)/shard_map/ppermute | solution.py:19
  11.4 44.9 %collective-permute-start.5 = (bf16[640,1536]{1,0:T(8,128)(2,1)S(1)}, bf16[640,1536]{1,0:T(8,128)(2,1)S(1)}, u32[]{:S(2)}, u32[]{:S(2)}) collective-permute-start(bf16[640,1536]{1,0:T(8,128)(2,1)S(1)} %constant_dynamic-update-slice_fusion.refs_7_), channel_id=1, source_target_pairs={{0,8},{8,0},{16,24},{24,16},{1,9},{9,1},{17,25},{25,17},{2,10},{10... | collective-permute-start | bytes 5898248 | tf_op jit(solution)/shard_map/ppermute | solution.py:19
  13.0 32.6 %collective-permute-start.3 = (bf16[2,128,2560]{2,1,0:T(8,128)(2,1)S(1)}, bf16[2,128,2560]{2,1,0:T(8,128)(2,1)S(1)}, u32[]{:S(2)}, u32[]{:S(2)}) collective-permute-start(bf16[2,128,2560]{2,1,0:T(8,128)(2,1)S(1)} %pad_maximum_fusion.refs_0_.refs_3_.refs_6_), channel_id=1, source_target_pairs={{2,0},{4,2},{6,4},{3,1},{5,3},{7,5},{10,8},{12,10},{14,12},{11,9},... | collective-permute-start | bytes 3932168 | tf_op jit(solution)/shard_map/ppermute | solution.py:513
  14.4 32.5 %collective-permute-start.1 = (bf16[2,128,2560]{2,1,0:T(8,128)(2,1)S(1)}, bf16[2,128,2560]{2,1,0:T(8,128)(2,1)S(1)}, u32[]{:S(2)}, u32[]{:S(2)}) collective-permute-start(bf16[2,128,2560]{2,1,0:T(8,128)(2,1)S(1)} %pad_maximum_fusion.refs_0_.refs_3_.refs_6_), channel_id=1, source_target_pairs={{0,2},{2,4},{4,6},{1,3},{3,5},{5,7},{8,10},{10,12},{12,14},{9,11},... | collective-permute-start | bytes 3932168 | tf_op jit(solution)/shard_map/ppermute | solution.py:512
  45.7 34.4 %collective-permute-start.4 = (bf16[2,128,2560]{2,1,0:T(8,128)(2,1)S(1)}, bf16[2,128,2560]{2,1,0:T(8,128)(2,1)}, u32[]{:S(2)}, u32[]{:S(2)}) collective-permute-start(bf16[2,128,2560]{2,1,0:T(8,128)(2,1)S(1)} %collective-permute-done.3.refs_4_), channel_id=1, source_target_pairs={{2,0},{4,2},{3,1},{5,3},{10,8},{12,10},{11,9},{13,11},{18,16},{20,... | collective-permute-start | bytes 3932168 | tf_op jit(solution)/shard_map/ppermute | solution.py:513
  47.0 33.1 %collective-permute-start.2 = (bf16[2,128,2560]{2,1,0:T(8,128)(2,1)S(1)}, bf16[2,128,2560]{2,1,0:T(8,128)(2,1)}, u32[]{:S(2)}, u32[]{:S(2)}) collective-permute-start(bf16[2,128,2560]{2,1,0:T(8,128)(2,1)S(1)} %collective-permute-done.1.refs_1_), channel_id=1, source_target_pairs={{2,4},{4,6},{3,5},{5,7},{10,12},{12,14},{11,13},{13,15},{18,20},{2... | collective-permute-start | bytes 3932168 | tf_op jit(solution)/shard_map/ppermute | solution.py:512
  56.5 23.2 %collective-permute-start.8 = (bf16[640,768]{1,0:T(8,128)(2,1)S(1)}, bf16[640,768]{1,0:T(8,128)(2,1)S(1)}, u32[]{:S(2)}, u32[]{:S(2)}) collective-permute-start(bf16[640,768]{1,0:T(8,128)(2,1)S(1)} %slice.27), channel_id=1, source_target_pairs={{0,16},{8,24},{16,0},{24,8},{1,17},{9,25},{17,1},{25,9},{2,18},{10... | collective-permute-start | bytes 2949128 | tf_op jit(solution)/shard_map/ppermute | solution.py:19
  80.1 27.8 %collective-permute-start.9 = (bf16[2,128,2560]{2,1,0:T(8,128)(2,1)}, bf16[2,128,2560]{2,1,0:T(8,128)(2,1)S(1)}, u32[]{:S(2)}, u32[]{:S(2)}) collective-permute-start(bf16[2,128,2560]{2,1,0:T(8,128)(2,1)} %collective-permute-done.2.refs_2_), channel_id=1, source_target_pairs={{4,6},{5,7},{12,14},{13,15},{20,22},{21,23},{28,30},{29,31}} | collective-permute-start | bytes 3932168 | tf_op jit(solution)/shard_map/ppermute | solution.py:512
  80.8 31.4 %collective-permute-start.10 = (bf16[2,128,2560]{2,1,0:T(8,128)(2,1)}, bf16[2,128,2560]{2,1,0:T(8,128)(2,1)S(1)}, u32[]{:S(2)}, u32[]{:S(2)}) collective-permute-start(bf16[2,128,2560]{2,1,0:T(8,128)(2,1)} %collective-permute-done.4.refs_5_), channel_id=1, source_target_pairs={{2,0},{3,1},{10,8},{11,9},{18,16},{19,17},{26,24},{27,25}} | collective-permute-start | bytes 3932168 | tf_op jit(solution)/shard_map/ppermute | solution.py:513
  82.2 24.5 %collective-permute-start.11 = (bf16[640,768]{1,0:T(8,128)(2,1)}, bf16[640,768]{1,0:T(8,128)(2,1)}, u32[]{:S(2)}, u32[]{:S(2)}) collective-permute-start(bf16[640,768]{1,0:T(8,128)(2,1)} %refs_7_.1), channel_id=1, source_target_pairs={{0,8},{8,0},{16,24},{24,16},{1,9},{9,1},{17,25},{25,17},{2,10},{10... | collective-permute-start | bytes 2949128 | tf_op jit(solution)/shard_map/ppermute | solution.py:19
  83.7 24.1 %collective-permute-start.12 = (bf16[640,768]{1,0:T(8,128)(2,1)}, bf16[640,768]{1,0:T(8,128)(2,1)}, u32[]{:S(2)}, u32[]{:S(2)}) collective-permute-start(bf16[640,768]{1,0:T(8,128)(2,1)} %refs_7_.1), channel_id=1, source_target_pairs={{0,16},{8,24},{16,0},{24,8},{1,17},{9,25},{17,1},{25,9},{2,18},{10... | collective-permute-start | bytes 2949128 | tf_op jit(solution)/shard_map/ppermute | solution.py:19
  112.3 35.9 %collective-permute-start.18 = (f32[384,1536]{1,0:T(8,128)}, f32[384,1536]{1,0:T(8,128)S(1)}, u32[]{:S(2)}, u32[]{:S(2)}) collective-permute-start(f32[384,1536]{1,0:T(8,128)} %get-tuple-element.58), channel_id=1, source_target_pairs={{0,1},{1,0},{2,3},{3,2},{4,5},{5,4},{6,7},{7,6},{8,9},{9,8},{10,11... | collective-permute-start | bytes 7077896 | tf_op jit(solution)/shard_map/ppermute | solution.py:19
  117.3 27.2 %collective-permute-start.14 = (bf16[768,640]{1,0:T(8,128)(2,1)}, bf16[768,640]{1,0:T(8,128)(2,1)}, u32[]{:S(2)}, u32[]{:S(2)}) collective-permute-start(bf16[768,640]{1,0:T(8,128)(2,1)} %refs_5_.3), channel_id=1, source_target_pairs={{0,2},{2,4},{4,6},{1,3},{3,5},{5,7},{8,10},{10,12},{12,14},{9,11},... | collective-permute-start | bytes 2949128 | tf_op jit(solution)/shard_map/ppermute | solution.py:555
  119.8 25.2 %collective-permute-start.15 = (bf16[768,640]{1,0:T(8,128)(2,1)}, bf16[768,640]{1,0:T(8,128)(2,1)}, u32[]{:S(2)}, u32[]{:S(2)}) collective-permute-start(bf16[768,640]{1,0:T(8,128)(2,1)} %refs_5_.3), channel_id=1, source_target_pairs={{2,0},{4,2},{6,4},{3,1},{5,3},{7,5},{10,8},{12,10},{14,12},{11,9},... | collective-permute-start | bytes 2949128 | tf_op jit(solution)/shard_map/ppermute | solution.py:556
  140.1 48.0 %collective-permute-start.24 = (f32[512,768]{1,0:T(8,128)}, f32[512,768]{1,0:T(8,128)}, u32[]{:S(2)}, u32[]{:S(2)}) collective-permute-start(f32[512,768]{1,0:T(8,128)} %get-tuple-element.64), channel_id=1, source_target_pairs={{0,1},{1,0},{2,3},{3,2},{4,5},{5,4},{6,7},{7,6},{8,9},{9,8},{10,11... | collective-permute-start | bytes 4718600 | tf_op jit(solution)/shard_map/ppermute | solution.py:19
  140.2 23.5 %all-to-all-start = ((bf16[4,144,1280]{2,1,0:T(8,128)(2,1)}), bf16[4,144,1280]{2,1,0:T(8,128)(2,1)}, u32[]{:S(2)}, u32[]{:S(2)}) async-start(bf16[4,144,1280]{2,1,0:T(8,128)(2,1)} %tell.1), calls=%async_computation | async-start | bytes 2949120 | tf_op jit(solution)/shard_map/all_to_all | solution.py:544
  145.1 31.0 %collective-permute-start.22 = (bf16[768,640]{1,0:T(8,128)(2,1)}, bf16[768,640]{1,0:T(8,128)(2,1)}, u32[]{:S(2)}, u32[]{:S(2)}) collective-permute-start(bf16[768,640]{1,0:T(8,128)(2,1)} %collective-permute-done.14.refs_6_), channel_id=1, source_target_pairs={{2,4},{4,6},{3,5},{5,7},{10,12},{12,14},{11,13},{13,15},{18,20},{2... | collective-permute-start | bytes 2949128 | tf_op jit(solution)/shard_map/ppermute | solution.py:555
  146.8 29.2 %collective-permute-start.20 = (bf16[768,640]{1,0:T(8,128)(2,1)}, bf16[768,640]{1,0:T(8,128)(2,1)}, u32[]{:S(2)}, u32[]{:S(2)}) collective-permute-start(bf16[768,640]{1,0:T(8,128)(2,1)} %collective-permute-done.14.refs_6_), channel_id=1, source_target_pairs={{0,1},{1,0},{2,3},{3,2},{4,5},{5,4},{6,7},{7,6},{8,9},{9,8},{10,11... | collective-permute-start | bytes 2949128 | tf_op jit(solution)/shard_map/ppermute | solution.py:19
  146.8 29.5 %collective-permute-start.23 = (bf16[768,640]{1,0:T(8,128)(2,1)}, bf16[768,640]{1,0:T(8,128)(2,1)}, u32[]{:S(2)}, u32[]{:S(2)}) collective-permute-start(bf16[768,640]{1,0:T(8,128)(2,1)} %collective-permute-done.15.refs_9_), channel_id=1, source_target_pairs={{2,0},{4,2},{3,1},{5,3},{10,8},{12,10},{11,9},{13,11},{18,16},{20,... | collective-permute-start | bytes 2949128 | tf_op jit(solution)/shard_map/ppermute | solution.py:556
  148.1 28.2 %collective-permute-start.21 = (bf16[768,640]{1,0:T(8,128)(2,1)}, bf16[768,640]{1,0:T(8,128)(2,1)}, u32[]{:S(2)}, u32[]{:S(2)}) collective-permute-start(bf16[768,640]{1,0:T(8,128)(2,1)} %collective-permute-done.15.refs_9_), channel_id=1, source_target_pairs={{0,1},{1,0},{2,3},{3,2},{4,5},{5,4},{6,7},{7,6},{8,9},{9,8},{10,11... | collective-permute-start | bytes 2949128 | tf_op jit(solution)/shard_map/ppermute | solution.py:19
  216.1 24.8 %collective-permute-start.32 = (bf16[768,640]{1,0:T(8,128)(2,1)}, bf16[768,640]{1,0:T(8,128)(2,1)S(1)}, u32[]{:S(2)}, u32[]{:S(2)}) collective-permute-start(bf16[768,640]{1,0:T(8,128)(2,1)} %collective-permute-done.23.refs_10_), channel_id=1, source_target_pairs={{2,0},{3,1},{10,8},{11,9},{18,16},{19,17},{26,24},{27,25}} | collective-permute-start | bytes 2949128 | tf_op jit(solution)/shard_map/ppermute | solution.py:556
  217.4 23.5 %collective-permute-start.28 = (bf16[4,128,768]{2,1,0:T(8,128)(2,1)S(1)}, bf16[4,128,768]{2,1,0:T(8,128)(2,1)S(1)}, u32[]{:S(2)}, u32[]{:S(2)}) collective-permute-start(bf16[4,128,768]{2,1,0:T(8,128)(2,1)S(1)} %all-to-all-done.2.refs_0_), channel_id=1, source_target_pairs={{0,16},{8,24},{16,0},{24,8},{1,17},{9,25},{17,1},{25,9},{2,18},{10... | collective-permute-start | bytes 2359304 | tf_op jit(solution)/shard_map/ppermute | solution.py:19
  219.0 23.5 %collective-permute-start.27 = (bf16[4,128,768]{2,1,0:T(8,128)(2,1)S(1)}, bf16[4,128,768]{2,1,0:T(8,128)(2,1)S(1)}, u32[]{:S(2)}, u32[]{:S(2)}) collective-permute-start(bf16[4,128,768]{2,1,0:T(8,128)(2,1)S(1)} %all-to-all-done.2.refs_0_), channel_id=1, source_target_pairs={{0,8},{8,0},{16,24},{24,16},{1,9},{9,1},{17,25},{25,17},{2,10},{10... | collective-permute-start | bytes 2359304 | tf_op jit(solution)/shard_map/ppermute | solution.py:19
  219.6 34.2 %collective-permute-start.33 = (bf16[768,640]{1,0:T(8,128)(2,1)S(1)}, bf16[768,640]{1,0:T(8,128)(2,1)S(1)}, u32[]{:S(2)}, u32[]{:S(2)}) collective-permute-start(bf16[768,640]{1,0:T(8,128)(2,1)S(1)} %collective-permute-done.31.refs_8_), channel_id=1, source_target_pairs={{0,1},{1,0},{2,3},{3,2},{4,5},{5,4},{6,7},{7,6},{8,9},{9,8},{10,11... | collective-permute-start | bytes 2949128 | tf_op jit(solution)/shard_map/ppermute | solution.py:19
  (50 other events, 907.3 us)

commit v10 on v9

--- a/solution.py
+++ b/solution.py
@@ -471,26 +471,28 @@
     )(place, *operands, heard)
 
 
-def finish_kernel(base, arrived, *refs):
+def finish_kernel(base, *refs):
     reached, update = refs[-2:]
-    reached[...] = base[...] + arrived[0, 1].astype(jnp.float32)
-    update[...] = arrived[0, 0]
-
-
-def finish(base, arrived, part, started):
-    steps, _, tokens, width = arrived.shape
-    by_columns = pl.BlockSpec((tokens, width), lambda i: (part, i))
+    for part, arrived in enumerate(refs[:-2]):
+        tokens = arrived.shape[2]
+        rows = slice(part * tokens, (part + 1) * tokens)
+        reached[rows] = base[rows] + arrived[0, 1].astype(jnp.float32)
+        update[rows] = arrived[0, 0]
+
+
+def finish(base, parts):
+    steps, _, tokens, width = parts[0].shape
+    by_columns = pl.BlockSpec((base.shape[0], width), lambda i: (0, i))
     return pl.pallas_call(
         finish_kernel,
         grid=(steps,),
-        in_specs=[by_columns, pl.BlockSpec((1, 2, tokens, width), lambda i: (i, 0, 0, 0))] + [ANY] * len(started),
+        in_specs=[by_columns] + [pl.BlockSpec((1, 2, tokens, width), lambda i: (i, 0, 0, 0))] * len(parts),
         out_specs=[by_columns, by_columns],
         out_shape=[jax.ShapeDtypeStruct(base.shape, jnp.float32), jax.ShapeDtypeStruct(base.shape, jnp.bfloat16)],
-        input_output_aliases={2 + i: i for i in range(len(started))},
-        compiler_params=params(),
-        cost_estimate=cost(arrived.size // 2, 7 * arrived.size),
+        compiler_params=params(),
+        cost_estimate=cost(base.size, 14 * base.size),
         name="finish",
-    )(base, arrived, *started)
+    )(base, *parts)
 
 
 def body(states, timesteps, lengths, modulation, w_query, w_key, w_value, w_out, q_gain, k_gain):
@@ -554,28 +556,30 @@
             up, down = after((up, down), quarter)
         below.append(lax.ppermute(up, "head", [(i, i + 1) for i in range(count - 1, size - 1)]))
         above.append(lax.ppermute(down, "head", [(i, i - 1) for i in range(1, size - count + 1)]))
-        partner_below.append(swap(below[-1], "fsdp", 1))
-        partner_above.append(swap(above[-1], "fsdp", 1))
+        arrived = (below[-1], above[-1])
+        if count == size - 1:
+            near = direct(quarter)
+            gathered = forwarded(quarter, near)
+            arrived = after(arrived, *[piece for pieces in near.values() for piece in pieces])
+        partner_below.append(swap(arrived[0], "fsdp", 1))
+        partner_above.append(swap(arrived[1], "fsdp", 1))
         if count == 1:
-            own_squares = norms(after(place, below[-1], above[-1], v_here, heard), parts, size)
+            own_squares = norms(after(place, below[-1], above[-1], v_here), parts, size)
             squares = lax.all_to_all(own_squares, "head", 0, 0)
         if count == size - 2:
-            ready = after(squares, *partner_below[:-1], *partner_above[:-1], below[-1], above[-1])
+            ready = after(squares, *partner_below[:-1], *partner_above[:-1], below[-1], above[-1], heard)
             probs = probabilities(place, ready, parts, q_gain, k_gain)
             attended = attend(place, probs, v_parts, size)
             quarter = after(lax.all_to_all(attended, "head", 0, 0), partner_below[-1], partner_above[-1])
 
-    gathered = forwarded(quarter, direct(quarter))
-
     raw = [w_out] + below[1:] + above[1:]
     out_weights = (raw, partner_below + partner_above)
     carried = step_width * current + jnp.where(step == 0, current, jnp.zeros_like(current))
 
-    outputs, parts_of = (), 2
-    sent = [project_out(place, heard, gathered, out_weights, part, parts_of) for part in range(parts_of)]
-    for part in range(parts_of):
-        outputs = finish(carried, lax.all_to_all(sent[part], "step", 0, 0), part, outputs)
-    reached, update = outputs
+    halves = 2
+    sent = [project_out(place, heard, gathered, out_weights, part, halves) for part in range(halves)]
+    arrived = after(tuple(lax.all_to_all(part, "step", 0, 0) for part in sent), carried)
+    reached, update = finish(carried, arrived)
     return reached[None, None], update[None, None]
 
 

time: 312 us -> 311 us (level)
  starting transfers between devices: 61.6 us -> 65.5 us
    ppermute x23, waiting for transfers between devices: 46.9 us -> 62.1 us  [swap(): lax.ppermute(x, axis, [(i, i ^ offset) for i in range(lax.axis_size(axis))])]
    ppermute x3, waiting for transfers between devices: 22.1 us -> 7.57 us  [body(): lax.ppermute(down, 'head', [(i, i - 1) for i in range(1, size - count + 1)])]
    all_to_all x1, waiting for transfers between devices: 15 us -> 10.4 us  [body(): heard = lax.all_to_all(after(told, last_here, *v_last), 'step', 0, 0)]
    ppermute x23, starting transfers between devices: 17.8 us -> 21.7 us  [swap(): lax.ppermute(x, axis, [(i, i ^ offset) for i in range(lax.axis_size(axis))])]
    all_to_all x2, waiting for transfers between devices: 17.3 us -> 20.6 us  [body(): lax.all_to_all(part, 'step', 0, 0)]
    pallas_call x2 -> x1, Pallas kernels: 7.63 us -> 4.78 us  [finish(): pl.pallas_call(finish_kernel, grid=(steps,), in_specs=[by_columns] + [pl....]
  transfers between devices with their start and end apart: 40 -> 40, of which waited for: 20 -> 22; matrix products, arithmetic and copies ran while one was open for 2% -> 2% of each run, Pallas kernels for 19% -> 18%
where the time goes in v10:
time: 311 us; the launch traced here: 310 us
  waiting for transfers between devices  148 us (48%)
  Pallas kernels  79.4 us (26%)
  starting transfers between devices  65.5 us (21%)
  local copies, waits for them, and re-layouts  11.1 us (4%)
  between operations  3.2 us (1%)
    ppermute x23, waiting for transfers between devices, swap(): lax.ppermute(x, axis, [(i, i ^ offset) for i in range(lax.axis_size(axis))])  62.1 us
    pallas_call x3, Pallas kernels, project(): pl.pallas_call(functools.partial(project_kernel, size, parts, shard, tupl...  31.4 us
    ppermute x3, waiting for transfers between devices, hop(): lax.ppermute(down, 'head', [(i, i - 1) for i in range(1, size - count + 1)])  31 us
    ppermute x23, starting transfers between devices, swap(): lax.ppermute(x, axis, [(i, i ^ offset) for i in range(lax.axis_size(axis))])  21.7 us
    all_to_all x2, waiting for transfers between devices, body(): lax.all_to_all(part, 'step', 0, 0)  20.6 us
    pallas_call x2, Pallas kernels, project_out(): pl.pallas_call(functools.partial(out_kernel, size, tuple(layout), part *...  18.8 us
    all_to_all x1, waiting for transfers between devices, body(): lax.all_to_all(attended, 'head', 0, 0)  15.5 us
    all_to_all x1, waiting for transfers between devices, body(): heard = lax.all_to_all(after(told, last_here, *v_last), 'step', 0, 0)  10.4 us
  transfers between devices with their start and end apart: 40, of which 22 were waited for; matrix products, arithmetic and copies ran while one was open for 2% of the time, Pallas kernels for 18%

profile of v10, /device:TPU:0, one launch (start us, length us, event | category | flops | bytes accessed | tf_op | source)
XLA Modules:
  0.0 309.6 jit_solution(894569869602125720)
XLA Ops:
  3.5 4.6 %modulate.1 = (bf16[128,2560]{1,0:T(8,128)(2,1)}, bf16[128,2560]{1,0:T(8,128)(2,1)}) custom-call(s32[5]{0:T(128)} %stack.32.place, f32[128,5120]{1,0:T(8,128)} %bitcast.12, f32[1,3,5120]{2,1,0:T(4,128)} %copy.12.rows), custom_call_target="tpu_custom_call" | custom-call | flops 1638400 | bytes 983040 | tf_op jit(solution)/shard_map/modulate/pallas_call | solution.py:119
  14.5 4.6 %collective-permute-start.1 = (bf16[2,128,2560]{2,1,0:T(8,128)(2,1)S(1)}, bf16[2,128,2560]{2,1,0:T(8,128)(2,1)S(1)}, u32[]{:S(2)}, u32[]{:S(2)}) collective-permute-start(bf16[2,128,2560]{2,1,0:T(8,128)(2,1)S(1)} %pad_maximum_fusion.refs_0_.refs_3_.refs_6_), channel_id=1, source_target_pairs={{0,2},{2,4},{4,6},{1,3},{3,5},{5,7},{8,10},{10,12},{12,14},{9,11},... | collective-permute-start | bytes 3932168 | tf_op jit(solution)/shard_map/ppermute | solution.py:514
  19.1 26.6 %collective-permute-done.3.refs_4_ = bf16[2,128,2560]{2,1,0:T(8,128)(2,1)S(1)} collective-permute-done((bf16[2,128,2560]{2,1,0:T(8,128)(2,1)S(1)}, bf16[2,128,2560]{2,1,0:T(8,128)(2,1)S(1)}, u32[]{:S(2)}, u32[]{:S(2)}) %collective-permute-start.3) | collective-permute-done | bytes 1310752 | tf_op jit(solution)/shard_map/ppermute | solution.py:515
  48.8 6.1 %collective-permute-done.6.refs_9_ = bf16[640,1536]{1,0:T(8,128)(2,1)S(1)} collective-permute-done((bf16[640,1536]{1,0:T(8,128)(2,1)S(1)}, bf16[640,1536]{1,0:T(8,128)(2,1)S(1)}, u32[]{:S(2)}, u32[]{:S(2)}) %collective-permute-start.6) | collective-permute-done | bytes 1966112 | tf_op jit(solution)/shard_map/ppermute | solution.py:19
  58.6 21.2 %collective-permute-done.8.refs_11_ = bf16[640,768]{1,0:T(8,128)(2,1)S(1)} collective-permute-done((bf16[640,768]{1,0:T(8,128)(2,1)S(1)}, bf16[640,768]{1,0:T(8,128)(2,1)S(1)}, u32[]{:S(2)}, u32[]{:S(2)}) %collective-permute-start.8) | collective-permute-done | bytes 983072 | tf_op jit(solution)/shard_map/ppermute | solution.py:19
  91.2 13.5 %first.1 = (f32[384,1536]{1,0:T(8,128)}, f32[384,1536]{1,0:T(8,128)}) custom-call(s32[5]{0:T(128)} %stack.32.place, bf16[2,128,2560]{2,1,0:T(8,128)(2,1)} %copy-done, bf16[2,128,2560]{2,1,0:T(8,128)(2,1)} %copy-done.7, bf16[2,128,2560]{2,1,0:T(8,128)(2,1)} %collective-permute-done.2.refs_2_, bf16[2,128,2560]{2,1,0:T(8,128)(2,1)} %copy-done, ...), custom_call_target="tpu_custom_call" | custom-call | flops 1509949440 | bytes 4128768 | tf_op jit(solution)/shard_map/first/pallas_call | solution.py:233
  107.9 4.4 %collective-permute-done.10.refs_6_ = bf16[2,128,2560]{2,1,0:T(8,128)(2,1)S(1)} collective-permute-done((bf16[2,128,2560]{2,1,0:T(8,128)(2,1)}, bf16[2,128,2560]{2,1,0:T(8,128)(2,1)S(1)}, u32[]{:S(2)}, u32[]{:S(2)}) %collective-permute-start.10) | collective-permute-done | bytes 1310752 | tf_op jit(solution)/shard_map/ppermute | solution.py:515
  121.2 7.8 %last.1 = (f32[128,1536]{1,0:T(8,128)}, f32[128,1536]{1,0:T(8,128)}) custom-call(s32[5]{0:T(128)} %stack.32.place, bf16[2,128,2560]{2,1,0:T(8,128)(2,1)} %copy-done, bf16[2,128,2560]{2,1,0:T(8,128)(2,1)} %copy-done.7, bf16[2,128,2560]{2,1,0:T(8,128)(2,1)} %collective-permute-done.2.refs_2_, bf16[2,128,2560]{2,1,0:T(8,128)(2,1)} %copy-done.10, ...), custom_call_target="tpu_custom_call" | custom-call | flops 503316480 | bytes 2686976 | tf_op jit(solution)/shard_map/last/pallas_call | solution.py:233
  130.0 10.2 %value.1 = (f32[512,768]{1,0:T(8,128)}, f32[512,768]{1,0:T(8,128)}) custom-call(s32[5]{0:T(128)} %stack.32.place, bf16[2,128,2560]{2,1,0:T(8,128)(2,1)} %copy-done, bf16[2,128,2560]{2,1,0:T(8,128)(2,1)} %copy-done.7, bf16[2,128,2560]{2,1,0:T(8,128)(2,1)} %collective-permute-done.2.refs_2_, bf16[2,128,2560]{2,1,0:T(8,128)(2,1)} %copy-done.10, ...), custom_call_target="tpu_custom_call" | custom-call | flops 1006632960 | bytes 3080192 | tf_op jit(solution)/shard_map/value/pallas_call | solution.py:233
  140.2 4.3 %all-to-all-start.1 = ((bf16[4,144,1280]{2,1,0:T(8,128)(2,1)}), bf16[4,144,1280]{2,1,0:T(8,128)(2,1)}, u32[]{:S(2)}, u32[]{:S(2)}) async-start(bf16[4,144,1280]{2,1,0:T(8,128)(2,1)} %tell.1), calls=%async_computation.1 | async-start | bytes 2949120 | tf_op jit(solution)/shard_map/all_to_all | solution.py:546
  153.4 10.4 %all-to-all-done.1.refs_19_ = bf16[4,144,1280]{2,1,0:T(8,128)(2,1)} async-done(((bf16[4,144,1280]{2,1,0:T(8,128)(2,1)}), bf16[4,144,1280]{2,1,0:T(8,128)(2,1)}, u32[]{:S(2)}, u32[]{:S(2)}) %all-to-all-start.1) | async-done | bytes 1474592 | tf_op jit(solution)/shard_map/all_to_all | solution.py:546
  163.8 7.4 %all-to-all-start = ((f32[4,2,512]{2,1,0:T(2,128)}), f32[4,2,512]{2,1,0:T(2,128)S(1)}, u32[]{:S(2)}, u32[]{:S(2)}) async-start(f32[4,2,512]{2,1,0:T(2,128)} %norms.1), calls=%async_computation | async-start | bytes 32768 | tf_op jit(solution)/shard_map/all_to_all | solution.py:568
  178.4 7.0 %probs.1 = bf16[6,512,512]{2,1,0:T(8,128)(2,1)} custom-call(s32[5]{0:T(128)} %stack.32.place, f32[4,2,512]{2,1,0:T(2,128)} %copy-done.30, f32[384,1536]{1,0:T(8,128)} %get-tuple-element.49.first_a.refs_0_.refs_4_, f32[384,1536]{1,0:T(8,128)} %copy-done.2, f32[128,1536]{1,0:T(8,128)} %get-tuple-element.52.last_a.refs_2_.refs_6_, f32[128,1536]{1,0:T(8,128)} %copy-done.8, ...), custom_call_target="tpu_custom_call" | custom-call | flops 100663296 | bytes 2359296 | tf_op jit(solution)/shard_map/probs/pallas_call | solution.py:325
  185.4 5.0 %attend.1 = bf16[4,128,768]{2,1,0:T(8,128)(2,1)} custom-call(s32[5]{0:T(128)} %stack.32.place, bf16[6,512,512]{2,1,0:T(8,128)(2,1)} %probs.1, f32[512,768]{1,0:T(8,128)} %get-tuple-element.56.v_a, f32[512,768]{1,0:T(8,128)} %collective-permute-done.24.v_b), custom_call_target="tpu_custom_call" | custom-call | flops 100663296 | bytes 1769472 | tf_op jit(solution)/shard_map/attend/pallas_call | solution.py:354
  198.2 15.5 %all-to-all-done.2.refs_0_ = bf16[4,128,768]{2,1,0:T(8,128)(2,1)S(1)} async-done(((bf16[4,128,768]{2,1,0:T(8,128)(2,1)}), bf16[4,128,768]{2,1,0:T(8,128)(2,1)S(1)}, u32[]{:S(2)}, u32[]{:S(2)}) %all-to-all-start.2) | async-done | bytes 786464 | tf_op jit(solution)/shard_map/all_to_all | solution.py:573
  219.5 15.3 %collective-permute-done.28.refs_2_ = bf16[4,128,768]{2,1,0:T(8,128)(2,1)S(1)} collective-permute-done((bf16[4,128,768]{2,1,0:T(8,128)(2,1)S(1)}, bf16[4,128,768]{2,1,0:T(8,128)(2,1)S(1)}, u32[]{:S(2)}, u32[]{:S(2)}) %collective-permute-start.28) | collective-permute-done | bytes 786464 | tf_op jit(solution)/shard_map/ppermute | solution.py:19
  243.7 7.7 %collective-permute-done.29.refs_3_ = bf16[2,128,768]{2,1,0:T(8,128)(2,1)S(1)} collective-permute-done((bf16[2,128,768]{2,1,0:T(8,128)(2,1)S(1)}, bf16[2,128,768]{2,1,0:T(8,128)(2,1)S(1)}, u32[]{:S(2)}, u32[]{:S(2)}) %collective-permute-start.29) | collective-permute-done | bytes 393248 | tf_op jit(solution)/shard_map/ppermute | solution.py:19
  254.9 9.5 %project_out.2 = bf16[4,2,64,1280]{3,2,1,0:T(8,128)(2,1)} custom-call(s32[5]{0:T(128)} %stack.32.place, bf16[4,128,768]{2,1,0:T(8,128)(2,1)} %copy-done.9, bf16[4,128,768]{2,1,0:T(8,128)(2,1)} %copy-done.13, bf16[4,128,768]{2,1,0:T(8,128)(2,1)} %copy-done.12, bf16[2,128,768]{2,1,0:T(8,128)(2,1)} %copy-done.23, bf16[2,128,768]{2,1,0:T(8,128)(2,1)} %copy-done.24, ...), custom_call_target="tpu_custom_call" | custom-call | flops 503316480 | bytes 2686976 | tf_op jit(solution)/shard_map/project_out/pallas_call | solution.py:456
  264.5 4.3 %all-to-all-start.3 = ((bf16[4,2,64,1280]{3,2,1,0:T(8,128)(2,1)}), bf16[4,2,64,1280]{3,2,1,0:T(8,128)(2,1)}, u32[]{:S(2)}, u32[]{:S(2)}) async-start(bf16[4,2,64,1280]{3,2,1,0:T(8,128)(2,1)} %project_out.2), calls=%async_computation.3 | async-start | bytes 2621440 | tf_op jit(solution)/shard_map/all_to_all | solution.py:581
  268.8 9.3 %project_out.3 = bf16[4,2,64,1280]{3,2,1,0:T(8,128)(2,1)} custom-call(s32[5]{0:T(128)} %stack.32.place, bf16[4,128,768]{2,1,0:T(8,128)(2,1)} %copy-done.9, bf16[4,128,768]{2,1,0:T(8,128)(2,1)} %copy-done.13, bf16[4,128,768]{2,1,0:T(8,128)(2,1)} %copy-done.12, bf16[2,128,768]{2,1,0:T(8,128)(2,1)} %copy-done.23, bf16[2,128,768]{2,1,0:T(8,128)(2,1)} %copy-done.24, ...), custom_call_target="tpu_custom_call" | custom-call | flops 503316480 | bytes 2686976 | tf_op jit(solution)/shard_map/project_out/pallas_call | solution.py:456
  278.1 6.5 %all-to-all-done.3.refs_0_ = bf16[4,2,64,1280]{3,2,1,0:T(8,128)(2,1)} async-done(((bf16[4,2,64,1280]{3,2,1,0:T(8,128)(2,1)}), bf16[4,2,64,1280]{3,2,1,0:T(8,128)(2,1)}, u32[]{:S(2)}, u32[]{:S(2)}) %all-to-all-start.3) | async-done | bytes 1310752 | tf_op jit(solution)/shard_map/all_to_all | solution.py:581
  284.6 4.3 %all-to-all-start.4 = ((bf16[4,2,64,1280]{3,2,1,0:T(8,128)(2,1)}), bf16[4,2,64,1280]{3,2,1,0:T(8,128)(2,1)}, u32[]{:S(2)}, u32[]{:S(2)}) async-start(bf16[4,2,64,1280]{3,2,1,0:T(8,128)(2,1)} %project_out.3), calls=%async_computation.4 | async-start | bytes 2621440 | tf_op jit(solution)/shard_map/all_to_all | solution.py:581
  290.7 14.1 %all-to-all-done.4.refs_1_ = bf16[4,2,64,1280]{3,2,1,0:T(8,128)(2,1)} async-done(((bf16[4,2,64,1280]{3,2,1,0:T(8,128)(2,1)}), bf16[4,2,64,1280]{3,2,1,0:T(8,128)(2,1)}, u32[]{:S(2)}, u32[]{:S(2)}) %all-to-all-start.4) | async-done | bytes 1310752 | tf_op jit(solution)/shard_map/all_to_all | solution.py:581
  304.9 4.8 %finish.1 = (f32[128,5120]{1,0:T(8,128)}, bf16[128,5120]{1,0:T(8,128)(2,1)}) custom-call(f32[128,5120]{1,0:T(8,128)} %select_add_fusion.base, bf16[4,2,64,1280]{3,2,1,0:T(8,128)(2,1)} %all-to-all-done.3.refs_0_, bf16[4,2,64,1280]{3,2,1,0:T(8,128)(2,1)} %all-to-all-done.4.refs_1_), custom_call_target="tpu_custom_call" | custom-call | flops 163840 | bytes 2293760 | tf_op jit(solution)/shard_map/finish/pallas_call | solution.py:486
  (150 shorter events, 82.1 us)
Async XLA Ops:
  8.8 46.1 %collective-permute-start.6 = (bf16[640,1536]{1,0:T(8,128)(2,1)S(1)}, bf16[640,1536]{1,0:T(8,128)(2,1)S(1)}, u32[]{:S(2)}, u32[]{:S(2)}) collective-permute-start(bf16[640,1536]{1,0:T(8,128)(2,1)S(1)} %constant_dynamic-update-slice_fusion.refs_7_), channel_id=1, source_target_pairs={{0,16},{8,24},{16,0},{24,8},{1,17},{9,25},{17,1},{25,9},{2,18},{10... | collective-permute-start | bytes 5898248 | tf_op jit(solution)/shard_map/ppermute | solution.py:19
  11.4 44.9 %collective-permute-start.5 = (bf16[640,1536]{1,0:T(8,128)(2,1)S(1)}, bf16[640,1536]{1,0:T(8,128)(2,1)S(1)}, u32[]{:S(2)}, u32[]{:S(2)}) collective-permute-start(bf16[640,1536]{1,0:T(8,128)(2,1)S(1)} %constant_dynamic-update-slice_fusion.refs_7_), channel_id=1, source_target_pairs={{0,8},{8,0},{16,24},{24,16},{1,9},{9,1},{17,25},{25,17},{2,10},{10... | collective-permute-start | bytes 5898248 | tf_op jit(solution)/shard_map/ppermute | solution.py:19
  13.1 32.6 %collective-permute-start.3 = (bf16[2,128,2560]{2,1,0:T(8,128)(2,1)S(1)}, bf16[2,128,2560]{2,1,0:T(8,128)(2,1)S(1)}, u32[]{:S(2)}, u32[]{:S(2)}) collective-permute-start(bf16[2,128,2560]{2,1,0:T(8,128)(2,1)S(1)} %pad_maximum_fusion.refs_0_.refs_3_.refs_6_), channel_id=1, source_target_pairs={{2,0},{4,2},{6,4},{3,1},{5,3},{7,5},{10,8},{12,10},{14,12},{11,9},... | collective-permute-start | bytes 3932168 | tf_op jit(solution)/shard_map/ppermute | solution.py:515
  14.5 32.5 %collective-permute-start.1 = (bf16[2,128,2560]{2,1,0:T(8,128)(2,1)S(1)}, bf16[2,128,2560]{2,1,0:T(8,128)(2,1)S(1)}, u32[]{:S(2)}, u32[]{:S(2)}) collective-permute-start(bf16[2,128,2560]{2,1,0:T(8,128)(2,1)S(1)} %pad_maximum_fusion.refs_0_.refs_3_.refs_6_), channel_id=1, source_target_pairs={{0,2},{2,4},{4,6},{1,3},{3,5},{5,7},{8,10},{10,12},{12,14},{9,11},... | collective-permute-start | bytes 3932168 | tf_op jit(solution)/shard_map/ppermute | solution.py:514
  45.7 34.4 %collective-permute-start.4 = (bf16[2,128,2560]{2,1,0:T(8,128)(2,1)S(1)}, bf16[2,128,2560]{2,1,0:T(8,128)(2,1)}, u32[]{:S(2)}, u32[]{:S(2)}) collective-permute-start(bf16[2,128,2560]{2,1,0:T(8,128)(2,1)S(1)} %collective-permute-done.3.refs_4_), channel_id=1, source_target_pairs={{2,0},{4,2},{3,1},{5,3},{10,8},{12,10},{11,9},{13,11},{18,16},{20,... | collective-permute-start | bytes 3932168 | tf_op jit(solution)/shard_map/ppermute | solution.py:515
  47.0 33.1 %collective-permute-start.2 = (bf16[2,128,2560]{2,1,0:T(8,128)(2,1)S(1)}, bf16[2,128,2560]{2,1,0:T(8,128)(2,1)}, u32[]{:S(2)}, u32[]{:S(2)}) collective-permute-start(bf16[2,128,2560]{2,1,0:T(8,128)(2,1)S(1)} %collective-permute-done.1.refs_1_), channel_id=1, source_target_pairs={{2,4},{4,6},{3,5},{5,7},{10,12},{12,14},{11,13},{13,15},{18,20},{2... | collective-permute-start | bytes 3932168 | tf_op jit(solution)/shard_map/ppermute | solution.py:514
  56.5 23.2 %collective-permute-start.8 = (bf16[640,768]{1,0:T(8,128)(2,1)S(1)}, bf16[640,768]{1,0:T(8,128)(2,1)S(1)}, u32[]{:S(2)}, u32[]{:S(2)}) collective-permute-start(bf16[640,768]{1,0:T(8,128)(2,1)S(1)} %slice.27), channel_id=1, source_target_pairs={{0,16},{8,24},{16,0},{24,8},{1,17},{9,25},{17,1},{25,9},{2,18},{10... | collective-permute-start | bytes 2949128 | tf_op jit(solution)/shard_map/ppermute | solution.py:19
  56.9 23.2 %collective-permute-start.7 = (bf16[640,768]{1,0:T(8,128)(2,1)S(1)}, bf16[640,768]{1,0:T(8,128)(2,1)S(1)}, u32[]{:S(2)}, u32[]{:S(2)}) collective-permute-start(bf16[640,768]{1,0:T(8,128)(2,1)S(1)} %slice.26), channel_id=1, source_target_pairs={{0,8},{8,0},{16,24},{24,16},{1,9},{9,1},{17,25},{25,17},{2,10},{10... | collective-permute-start | bytes 2949128 | tf_op jit(solution)/shard_map/ppermute | solution.py:19
  80.1 27.8 %collective-permute-start.9 = (bf16[2,128,2560]{2,1,0:T(8,128)(2,1)}, bf16[2,128,2560]{2,1,0:T(8,128)(2,1)S(1)}, u32[]{:S(2)}, u32[]{:S(2)}) collective-permute-start(bf16[2,128,2560]{2,1,0:T(8,128)(2,1)} %collective-permute-done.2.refs_2_), channel_id=1, source_target_pairs={{4,6},{5,7},{12,14},{13,15},{20,22},{21,23},{28,30},{29,31}} | collective-permute-start | bytes 3932168 | tf_op jit(solution)/shard_map/ppermute | solution.py:514
  80.9 31.4 %collective-permute-start.10 = (bf16[2,128,2560]{2,1,0:T(8,128)(2,1)}, bf16[2,128,2560]{2,1,0:T(8,128)(2,1)S(1)}, u32[]{:S(2)}, u32[]{:S(2)}) collective-permute-start(bf16[2,128,2560]{2,1,0:T(8,128)(2,1)} %collective-permute-done.4.refs_5_), channel_id=1, source_target_pairs={{2,0},{3,1},{10,8},{11,9},{18,16},{19,17},{26,24},{27,25}} | collective-permute-start | bytes 3932168 | tf_op jit(solution)/shard_map/ppermute | solution.py:515
  82.3 24.5 %collective-permute-start.11 = (bf16[640,768]{1,0:T(8,128)(2,1)}, bf16[640,768]{1,0:T(8,128)(2,1)}, u32[]{:S(2)}, u32[]{:S(2)}) collective-permute-start(bf16[640,768]{1,0:T(8,128)(2,1)} %refs_7_.1), channel_id=1, source_target_pairs={{0,8},{8,0},{16,24},{24,16},{1,9},{9,1},{17,25},{25,17},{2,10},{10... | collective-permute-start | bytes 2949128 | tf_op jit(solution)/shard_map/ppermute | solution.py:19
  83.8 24.1 %collective-permute-start.12 = (bf16[640,768]{1,0:T(8,128)(2,1)}, bf16[640,768]{1,0:T(8,128)(2,1)}, u32[]{:S(2)}, u32[]{:S(2)}) collective-permute-start(bf16[640,768]{1,0:T(8,128)(2,1)} %refs_7_.1), channel_id=1, source_target_pairs={{0,16},{8,24},{16,0},{24,8},{1,17},{9,25},{17,1},{25,9},{2,18},{10... | collective-permute-start | bytes 2949128 | tf_op jit(solution)/shard_map/ppermute | solution.py:19
  112.3 35.9 %collective-permute-start.18 = (f32[384,1536]{1,0:T(8,128)}, f32[384,1536]{1,0:T(8,128)S(1)}, u32[]{:S(2)}, u32[]{:S(2)}) collective-permute-start(f32[384,1536]{1,0:T(8,128)} %get-tuple-element.59), channel_id=1, source_target_pairs={{0,1},{1,0},{2,3},{3,2},{4,5},{5,4},{6,7},{7,6},{8,9},{9,8},{10,11... | collective-permute-start | bytes 7077896 | tf_op jit(solution)/shard_map/ppermute | solution.py:19
  117.4 27.2 %collective-permute-start.14 = (bf16[768,640]{1,0:T(8,128)(2,1)}, bf16[768,640]{1,0:T(8,128)(2,1)}, u32[]{:S(2)}, u32[]{:S(2)}) collective-permute-start(bf16[768,640]{1,0:T(8,128)(2,1)} %refs_5_.3), channel_id=1, source_target_pairs={{0,2},{2,4},{4,6},{1,3},{3,5},{5,7},{8,10},{10,12},{12,14},{9,11},... | collective-permute-start | bytes 2949128 | tf_op jit(solution)/shard_map/ppermute | solution.py:557
  119.9 25.2 %collective-permute-start.15 = (bf16[768,640]{1,0:T(8,128)(2,1)}, bf16[768,640]{1,0:T(8,128)(2,1)}, u32[]{:S(2)}, u32[]{:S(2)}) collective-permute-start(bf16[768,640]{1,0:T(8,128)(2,1)} %refs_5_.3), channel_id=1, source_target_pairs={{2,0},{4,2},{6,4},{3,1},{5,3},{7,5},{10,8},{12,10},{14,12},{11,9},... | collective-permute-start | bytes 2949128 | tf_op jit(solution)/shard_map/ppermute | solution.py:558
  140.2 45.3 %collective-permute-start.24 = (f32[512,768]{1,0:T(8,128)}, f32[512,768]{1,0:T(8,128)}, u32[]{:S(2)}, u32[]{:S(2)}) collective-permute-start(f32[512,768]{1,0:T(8,128)} %get-tuple-element.66), channel_id=1, source_target_pairs={{0,1},{1,0},{2,3},{3,2},{4,5},{5,4},{6,7},{7,6},{8,9},{9,8},{10,11... | collective-permute-start | bytes 4718600 | tf_op jit(solution)/shard_map/ppermute | solution.py:19
  140.2 23.5 %all-to-all-start.1 = ((bf16[4,144,1280]{2,1,0:T(8,128)(2,1)}), bf16[4,144,1280]{2,1,0:T(8,128)(2,1)}, u32[]{:S(2)}, u32[]{:S(2)}) async-start(bf16[4,144,1280]{2,1,0:T(8,128)(2,1)} %tell.1), calls=%async_computation.1 | async-start | bytes 2949120 | tf_op jit(solution)/shard_map/all_to_all | solution.py:546
  145.1 27.2 %collective-permute-start.22 = (bf16[768,640]{1,0:T(8,128)(2,1)}, bf16[768,640]{1,0:T(8,128)(2,1)}, u32[]{:S(2)}, u32[]{:S(2)}) collective-permute-start(bf16[768,640]{1,0:T(8,128)(2,1)} %collective-permute-done.14.refs_6_), channel_id=1, source_target_pairs={{2,4},{4,6},{3,5},{5,7},{10,12},{12,14},{11,13},{13,15},{18,20},{2... | collective-permute-start | bytes 2949128 | tf_op jit(solution)/shard_map/ppermute | solution.py:557
  146.9 25.5 %collective-permute-start.20 = (bf16[768,640]{1,0:T(8,128)(2,1)}, bf16[768,640]{1,0:T(8,128)(2,1)}, u32[]{:S(2)}, u32[]{:S(2)}) collective-permute-start(bf16[768,640]{1,0:T(8,128)(2,1)} %collective-permute-done.14.refs_6_), channel_id=1, source_target_pairs={{0,1},{1,0},{2,3},{3,2},{4,5},{5,4},{6,7},{7,6},{8,9},{9,8},{10,11... | collective-permute-start | bytes 2949128 | tf_op jit(solution)/shard_map/ppermute | solution.py:19
  146.9 29.6 %collective-permute-start.23 = (bf16[768,640]{1,0:T(8,128)(2,1)}, bf16[768,640]{1,0:T(8,128)(2,1)}, u32[]{:S(2)}, u32[]{:S(2)}) collective-permute-start(bf16[768,640]{1,0:T(8,128)(2,1)} %collective-permute-done.15.refs_9_), channel_id=1, source_target_pairs={{2,0},{4,2},{3,1},{5,3},{10,8},{12,10},{11,9},{13,11},{18,16},{20,... | collective-permute-start | bytes 2949128 | tf_op jit(solution)/shard_map/ppermute | solution.py:558
  148.2 28.3 %collective-permute-start.21 = (bf16[768,640]{1,0:T(8,128)(2,1)}, bf16[768,640]{1,0:T(8,128)(2,1)}, u32[]{:S(2)}, u32[]{:S(2)}) collective-permute-start(bf16[768,640]{1,0:T(8,128)(2,1)} %collective-permute-done.15.refs_9_), channel_id=1, source_target_pairs={{0,1},{1,0},{2,3},{3,2},{4,5},{5,4},{6,7},{7,6},{8,9},{9,8},{10,11... | collective-permute-start | bytes 2949128 | tf_op jit(solution)/shard_map/ppermute | solution.py:19
  190.4 23.2 %all-to-all-start.2 = ((bf16[4,128,768]{2,1,0:T(8,128)(2,1)}), bf16[4,128,768]{2,1,0:T(8,128)(2,1)S(1)}, u32[]{:S(2)}, u32[]{:S(2)}) async-start(bf16[4,128,768]{2,1,0:T(8,128)(2,1)} %attend.1), calls=%async_computation.2 | async-start | bytes 1572864 | tf_op jit(solution)/shard_map/all_to_all | solution.py:573
  213.6 22.6 %collective-permute-start.31 = (bf16[768,640]{1,0:T(8,128)(2,1)}, bf16[768,640]{1,0:T(8,128)(2,1)S(1)}, u32[]{:S(2)}, u32[]{:S(2)}) collective-permute-start(bf16[768,640]{1,0:T(8,128)(2,1)} %collective-permute-done.22.refs_7_), channel_id=1, source_target_pairs={{4,6},{5,7},{12,14},{13,15},{20,22},{21,23},{28,30},{29,31}} | collective-permute-start | bytes 2949128 | tf_op jit(solution)/shard_map/ppermute | solution.py:557
  214.4 24.8 %collective-permute-start.32 = (bf16[768,640]{1,0:T(8,128)(2,1)}, bf16[768,640]{1,0:T(8,128)(2,1)S(1)}, u32[]{:S(2)}, u32[]{:S(2)}) collective-permute-start(bf16[768,640]{1,0:T(8,128)(2,1)} %collective-permute-done.23.refs_10_), channel_id=1, source_target_pairs={{2,0},{3,1},{10,8},{11,9},{18,16},{19,17},{26,24},{27,25}} | collective-permute-start | bytes 2949128 | tf_op jit(solution)/shard_map/ppermute | solution.py:558
  (50 other events, 871.5 us)

commit v11 on v10

--- a/solution.py
+++ b/solution.py
@@ -535,21 +535,22 @@
     partner_below, partner_above = [swap(after(w_out, below[1], above[1]), "fsdp", 1)], []
     first_here, first_there = project(after(place, told, *partner_below), early, both_shards, "first", "first")
     ended = (below[-1], above[-1]) + last_round
-    first_there = after(first_there, *ended)
+    second_round = (both_shards[-1][0], both_shards[-2][0], early[0][-2], early[1][-2])
+    heard = lax.all_to_all(after(told, *second_round), "step", 0, 0)
+    first_there = after(first_there, heard, *ended)
     v_shards = finished(*ended, first_here)
     v_last = (v_shards[-1][0], v_shards[-2][0])
     parts = [first_here, swap(first_there, "fsdp", 1)]
-    last_here, last_there = project(place, line, both_shards, "last", "last")
+    last_here, last_there = project(after(place, heard), line, both_shards, "last", "last")
     parts += [last_here, swap(after(last_there, *v_last), "fsdp", 1)]
     v_here, v_there = project(after(place, last_here), line, v_shards, "all", "value")
     v_parts = [v_here, swap(v_there, "fsdp", 1)]
-    heard = lax.all_to_all(after(told, last_here, *v_last), "step", 0, 0)
 
     below, above = [w_out], [w_out]
     for count in range(1, size):
         up, down = below[-1], above[-1]
         if count == 1:
-            up, down = after((up, down), *ended, first_here)
+            up, down = after((up, down), line[0][-1], line[1][-1], first_here)
         if count == 2:
             up, down = after((up, down), v_here)
         if count == size - 1:
@@ -567,7 +568,7 @@
             own_squares = norms(after(place, below[-1], above[-1], v_here), parts, size)
             squares = lax.all_to_all(own_squares, "head", 0, 0)
         if count == size - 2:
-            ready = after(squares, *partner_below[:-1], *partner_above[:-1], below[-1], above[-1], heard)
+            ready = after(squares, *partner_below[:-1], *partner_above[:-1], below[-1], above[-1])
             probs = probabilities(place, ready, parts, q_gain, k_gain)
             attended = attend(place, probs, v_parts, size)
             quarter = after(lax.all_to_all(attended, "head", 0, 0), partner_below[-1], partner_above[-1])
@@ -576,7 +577,7 @@
     out_weights = (raw, partner_below + partner_above)
     carried = step_width * current + jnp.where(step == 0, current, jnp.zeros_like(current))
 
-    halves = 2
+    halves = 1
     sent = [project_out(place, heard, gathered, out_weights, part, halves) for part in range(halves)]
     arrived = after(tuple(lax.all_to_all(part, "step", 0, 0) for part in sent), carried)
     reached, update = finish(carried, arrived)

time: 311 us -> 332 us (1.068)
  waiting for transfers between devices: 148 us -> 175 us
  Pallas kernels: 79.4 us -> 73.9 us
  local copies, waits for them, and re-layouts: 11.1 us -> 16 us
  starting transfers between devices: 65.5 us -> 60.9 us
    ppermute x23, waiting for transfers between devices: 62.1 us -> 82.6 us  [swap(): lax.ppermute(x, axis, [(i, i ^ offset) for i in range(lax.axis_size(axis))])]
    ppermute x3, waiting for transfers between devices: 7.57 us -> 21 us  [body(): lax.ppermute(down, 'head', [(i, i - 1) for i in range(1, size - count + 1)])]
    all_to_all x1, waiting for transfers between devices: 10.4 us -> 0.01 us  [body(): heard = lax.all_to_all(after(told, *second_round), 'step', 0, 0)]
    all_to_all x2 -> x1, waiting for transfers between devices: 20.6 us -> 27.9 us  [body(): lax.all_to_all(part, 'step', 0, 0)]
    pallas_call x2 -> x1, Pallas kernels: 18.8 us -> 13 us  [project_out(): pl.pallas_call(functools.partial(out_kernel, size, tuple(layout), part *...]
    ppermute x3, waiting for transfers between devices: 31 us -> 26.6 us  [hop(): lax.ppermute(down, 'head', [(i, i - 1) for i in range(1, size - count + 1)])]
    all_to_all x2 -> x1, starting transfers between devices: 8.63 us -> 4.87 us  [body(): lax.all_to_all(part, 'step', 0, 0)]
    unnamed x70, local copies, waits for them, and re-layouts: 5.91 us -> 9.37 us
  transfers between devices with their start and end apart: 40 -> 39, of which waited for: 22 -> 18; matrix products, arithmetic and copies ran while one was open for 2% -> 2% of each run, Pallas kernels for 18% -> 14%
where the time goes in v11:
time: 332 us; the launch traced here: 331 us
  waiting for transfers between devices  175 us (53%)
  Pallas kernels  73.9 us (22%)
  starting transfers between devices  60.9 us (18%)
  local copies, waits for them, and re-layouts  16 us (5%)
    ppermute x23, waiting for transfers between devices, swap(): lax.ppermute(x, axis, [(i, i ^ offset) for i in range(lax.axis_size(axis))])  82.6 us
    pallas_call x3, Pallas kernels, project(): pl.pallas_call(functools.partial(project_kernel, size, parts, shard, tupl...  31.7 us
    all_to_all x1, waiting for transfers between devices, body(): lax.all_to_all(part, 'step', 0, 0)  27.9 us
    ppermute x3, waiting for transfers between devices, hop(): lax.ppermute(down, 'head', [(i, i - 1) for i in range(1, size - count + 1)])  26.6 us
    ppermute x3, waiting for transfers between devices, body(): lax.ppermute(down, 'head', [(i, i - 1) for i in range(1, size - count + 1)])  21 us
    ppermute x23, starting transfers between devices, swap(): lax.ppermute(x, axis, [(i, i ^ offset) for i in range(lax.axis_size(axis))])  18.5 us
    all_to_all x1, waiting for transfers between devices, body(): lax.all_to_all(attended, 'head', 0, 0)  15.5 us
    pallas_call x1, Pallas kernels, project_out(): pl.pallas_call(functools.partial(out_kernel, size, tuple(layout), part *...  13 us
  transfers between devices with their start and end apart: 39, of which 18 were waited for; matrix products, arithmetic and copies ran while one was open for 2% of the time, Pallas kernels for 14%

profile of v11, /device:TPU:0, one launch (start us, length us, event | category | flops | bytes accessed | tf_op | source)
XLA Modules:
  0.0 330.9 jit_solution(5645007771080621145)
XLA Ops:
  3.5 4.6 %modulate.1 = (bf16[128,2560]{1,0:T(8,128)(2,1)}, bf16[128,2560]{1,0:T(8,128)(2,1)}) custom-call(s32[5]{0:T(128)} %stack.32.place, f32[128,5120]{1,0:T(8,128)} %bitcast.12, f32[1,3,5120]{2,1,0:T(4,128)} %copy.12.rows), custom_call_target="tpu_custom_call" | custom-call | flops 1638400 | bytes 983040 | tf_op jit(solution)/shard_map/modulate/pallas_call | solution.py:119
  14.5 4.6 %collective-permute-start.1 = (bf16[2,128,2560]{2,1,0:T(8,128)(2,1)S(1)}, bf16[2,128,2560]{2,1,0:T(8,128)(2,1)S(1)}, u32[]{:S(2)}, u32[]{:S(2)}) collective-permute-start(bf16[2,128,2560]{2,1,0:T(8,128)(2,1)S(1)} %pad_maximum_fusion.refs_0_.refs_3_.refs_6_), channel_id=1, source_target_pairs={{0,2},{2,4},{4,6},{1,3},{3,5},{5,7},{8,10},{10,12},{12,14},{9,11},... | collective-permute-start | bytes 3932168 | tf_op jit(solution)/shard_map/ppermute | solution.py:514
  19.1 26.6 %collective-permute-done.3.refs_4_ = bf16[2,128,2560]{2,1,0:T(8,128)(2,1)S(1)} collective-permute-done((bf16[2,128,2560]{2,1,0:T(8,128)(2,1)S(1)}, bf16[2,128,2560]{2,1,0:T(8,128)(2,1)S(1)}, u32[]{:S(2)}, u32[]{:S(2)}) %collective-permute-start.3) | collective-permute-done | bytes 1310752 | tf_op jit(solution)/shard_map/ppermute | solution.py:515
  48.8 6.1 %collective-permute-done.6.refs_9_ = bf16[640,1536]{1,0:T(8,128)(2,1)S(1)} collective-permute-done((bf16[640,1536]{1,0:T(8,128)(2,1)S(1)}, bf16[640,1536]{1,0:T(8,128)(2,1)S(1)}, u32[]{:S(2)}, u32[]{:S(2)}) %collective-permute-start.6) | collective-permute-done | bytes 1966112 | tf_op jit(solution)/shard_map/ppermute | solution.py:19
  58.6 21.2 %collective-permute-done.8.refs_11_ = bf16[640,768]{1,0:T(8,128)(2,1)S(1)} collective-permute-done((bf16[640,768]{1,0:T(8,128)(2,1)S(1)}, bf16[640,768]{1,0:T(8,128)(2,1)S(1)}, u32[]{:S(2)}, u32[]{:S(2)}) %collective-permute-start.8) | collective-permute-done | bytes 983072 | tf_op jit(solution)/shard_map/ppermute | solution.py:19
  84.8 4.0 %tell.1 = bf16[4,144,1280]{2,1,0:T(8,128)(2,1)} custom-call(s32[5]{0:T(128)} %stack.32.place, f32[1]{0:T(128)} %bitcast.8.step_width, f32[128,5120]{1,0:T(8,128)} %bitcast.13, f32[1,3,5120]{2,1,0:T(4,128)} %copy.12.rows), custom_call_target="tpu_custom_call" | custom-call | flops 655360 | bytes 983040 | tf_op jit(solution)/shard_map/tell/pallas_call | solution.py:151
  95.8 13.7 %first.1 = (f32[384,1536]{1,0:T(8,128)}, f32[384,1536]{1,0:T(8,128)}) custom-call(s32[5]{0:T(128)} %stack.32.place, bf16[2,128,2560]{2,1,0:T(8,128)(2,1)} %copy-done, bf16[2,128,2560]{2,1,0:T(8,128)(2,1)} %copy-done.7, bf16[2,128,2560]{2,1,0:T(8,128)(2,1)} %collective-permute-done.2.refs_2_, bf16[2,128,2560]{2,1,0:T(8,128)(2,1)} %copy-done, ...), custom_call_target="tpu_custom_call" | custom-call | flops 1509949440 | bytes 4128768 | tf_op jit(solution)/shard_map/first/pallas_call | solution.py:233
  109.5 23.0 %collective-permute-done.14.refs_8_ = bf16[640,768]{1,0:T(8,128)(2,1)S(1)} collective-permute-done((bf16[640,768]{1,0:T(8,128)(2,1)}, bf16[640,768]{1,0:T(8,128)(2,1)S(1)}, u32[]{:S(2)}, u32[]{:S(2)}) %collective-permute-start.14) | collective-permute-done | bytes 983072 | tf_op jit(solution)/shard_map/ppermute | solution.py:19
  138.2 6.5 %collective-permute-start.12 = (bf16[768,640]{1,0:T(8,128)(2,1)}, bf16[768,640]{1,0:T(8,128)(2,1)}, u32[]{:S(2)}, u32[]{:S(2)}) collective-permute-start(bf16[768,640]{1,0:T(8,128)(2,1)} %refs_5_.1), channel_id=1, source_target_pairs={{0,2},{2,4},{4,6},{1,3},{3,5},{5,7},{8,10},{10,12},{12,14},{9,11},... | collective-permute-start | bytes 2949128 | tf_op jit(solution)/shard_map/ppermute | solution.py:558
  146.0 7.8 %last.1 = (f32[128,1536]{1,0:T(8,128)}, f32[128,1536]{1,0:T(8,128)}) custom-call(s32[5]{0:T(128)} %stack.32.place, bf16[2,128,2560]{2,1,0:T(8,128)(2,1)} %copy-done, bf16[2,128,2560]{2,1,0:T(8,128)(2,1)} %copy-done.7, bf16[2,128,2560]{2,1,0:T(8,128)(2,1)} %collective-permute-done.2.refs_2_, bf16[2,128,2560]{2,1,0:T(8,128)(2,1)} %copy-done.10, ...), custom_call_target="tpu_custom_call" | custom-call | flops 503316480 | bytes 2686976 | tf_op jit(solution)/shard_map/last/pallas_call | solution.py:233
  154.8 10.2 %value.1 = (f32[512,768]{1,0:T(8,128)}, f32[512,768]{1,0:T(8,128)}) custom-call(s32[5]{0:T(128)} %stack.32.place, bf16[2,128,2560]{2,1,0:T(8,128)(2,1)} %copy-done, bf16[2,128,2560]{2,1,0:T(8,128)(2,1)} %copy-done.7, bf16[2,128,2560]{2,1,0:T(8,128)(2,1)} %collective-permute-done.2.refs_2_, bf16[2,128,2560]{2,1,0:T(8,128)(2,1)} %copy-done.10, ...), custom_call_target="tpu_custom_call" | custom-call | flops 1006632960 | bytes 3080192 | tf_op jit(solution)/shard_map/value/pallas_call | solution.py:233
  165.1 5.0 %collective-permute-done.13.refs_9_ = bf16[768,640]{1,0:T(8,128)(2,1)} collective-permute-done((bf16[768,640]{1,0:T(8,128)(2,1)}, bf16[768,640]{1,0:T(8,128)(2,1)}, u32[]{:S(2)}, u32[]{:S(2)}) %collective-permute-start.13) | collective-permute-done | bytes 983072 | tf_op jit(solution)/shard_map/ppermute | solution.py:559
  177.4 7.6 %all-to-all-start.1 = ((f32[4,2,512]{2,1,0:T(2,128)}), f32[4,2,512]{2,1,0:T(2,128)S(1)}, u32[]{:S(2)}, u32[]{:S(2)}) async-start(f32[4,2,512]{2,1,0:T(2,128)} %norms.1), calls=%async_computation.1 | async-start | bytes 32768 | tf_op jit(solution)/shard_map/all_to_all | solution.py:569
  187.5 11.3 %collective-permute-done.23.refs_10_ = bf16[768,640]{1,0:T(8,128)(2,1)} collective-permute-done((bf16[768,640]{1,0:T(8,128)(2,1)}, bf16[768,640]{1,0:T(8,128)(2,1)}, u32[]{:S(2)}, u32[]{:S(2)}) %collective-permute-start.23) | collective-permute-done | bytes 983072 | tf_op jit(solution)/shard_map/ppermute | solution.py:559
  200.8 7.0 %probs.1 = bf16[6,512,512]{2,1,0:T(8,128)(2,1)} custom-call(s32[5]{0:T(128)} %stack.32.place, f32[4,2,512]{2,1,0:T(2,128)} %copy-done.32, f32[384,1536]{1,0:T(8,128)} %get-tuple-element.47.first_a.refs_0_.refs_4_, f32[384,1536]{1,0:T(8,128)} %copy-done.2, f32[128,1536]{1,0:T(8,128)} %get-tuple-element.52.last_a.refs_2_.refs_6_, f32[128,1536]{1,0:T(8,128)} %copy-done.8, ...), custom_call_target="tpu_custom_call" | custom-call | flops 100663296 | bytes 2359296 | tf_op jit(solution)/shard_map/probs/pallas_call | solution.py:325
  208.9 5.0 %attend.1 = bf16[4,128,768]{2,1,0:T(8,128)(2,1)} custom-call(s32[5]{0:T(128)} %stack.32.place, bf16[6,512,512]{2,1,0:T(8,128)(2,1)} %probs.1, f32[512,768]{1,0:T(8,128)} %get-tuple-element.58.v_a, f32[512,768]{1,0:T(8,128)} %copy-done.17), custom_call_target="tpu_custom_call" | custom-call | flops 100663296 | bytes 1769472 | tf_op jit(solution)/shard_map/attend/pallas_call | solution.py:354
  221.9 15.5 %all-to-all-done.2.refs_0_ = bf16[4,128,768]{2,1,0:T(8,128)(2,1)S(1)} async-done(((bf16[4,128,768]{2,1,0:T(8,128)(2,1)}), bf16[4,128,768]{2,1,0:T(8,128)(2,1)S(1)}, u32[]{:S(2)}, u32[]{:S(2)}) %all-to-all-start.2) | async-done | bytes 786464 | tf_op jit(solution)/shard_map/all_to_all | solution.py:574
  241.6 16.4 %collective-permute-done.28.refs_2_ = bf16[4,128,768]{2,1,0:T(8,128)(2,1)S(1)} collective-permute-done((bf16[4,128,768]{2,1,0:T(8,128)(2,1)S(1)}, bf16[4,128,768]{2,1,0:T(8,128)(2,1)S(1)}, u32[]{:S(2)}, u32[]{:S(2)}) %collective-permute-start.28) | collective-permute-done | bytes 786464 | tf_op jit(solution)/shard_map/ppermute | solution.py:19
  258.2 4.7 %collective-permute-done.32.refs_11_ = bf16[768,640]{1,0:T(8,128)(2,1)S(1)} collective-permute-done((bf16[768,640]{1,0:T(8,128)(2,1)}, bf16[768,640]{1,0:T(8,128)(2,1)S(1)}, u32[]{:S(2)}, u32[]{:S(2)}) %collective-permute-start.32) | collective-permute-done | bytes 983072 | tf_op jit(solution)/shard_map/ppermute | solution.py:559
  265.7 8.8 %collective-permute-done.29.refs_3_ = bf16[2,128,768]{2,1,0:T(8,128)(2,1)S(1)} collective-permute-done((bf16[2,128,768]{2,1,0:T(8,128)(2,1)S(1)}, bf16[2,128,768]{2,1,0:T(8,128)(2,1)S(1)}, u32[]{:S(2)}, u32[]{:S(2)}) %collective-permute-start.29) | collective-permute-done | bytes 393248 | tf_op jit(solution)/shard_map/ppermute | solution.py:19
  278.4 13.0 %project_out.1 = bf16[4,2,128,1280]{3,2,1,0:T(8,128)(2,1)} custom-call(s32[5]{0:T(128)} %stack.32.place, bf16[4,128,768]{2,1,0:T(8,128)(2,1)} %copy-done.13, bf16[4,128,768]{2,1,0:T(8,128)(2,1)} %copy-done.16, bf16[4,128,768]{2,1,0:T(8,128)(2,1)} %copy-done.15, bf16[2,128,768]{2,1,0:T(8,128)(2,1)} %copy-done.30, bf16[2,128,768]{2,1,0:T(8,128)(2,1)} %copy-done.31, ...), custom_call_target="tpu_custom_call" | custom-call | flops 1006632960 | bytes 3407872 | tf_op jit(solution)/shard_map/project_out/pallas_call | solution.py:456
  291.4 4.9 %all-to-all-start.3 = ((bf16[4,2,128,1280]{3,2,1,0:T(8,128)(2,1)}), bf16[4,2,128,1280]{3,2,1,0:T(8,128)(2,1)}, u32[]{:S(2)}, u32[]{:S(2)}) async-start(bf16[4,2,128,1280]{3,2,1,0:T(8,128)(2,1)} %project_out.1), calls=%async_computation.3 | async-start | bytes 5242880 | tf_op jit(solution)/shard_map/all_to_all | solution.py:582
  298.2 27.9 %all-to-all-done.3.refs_0_ = bf16[4,2,128,1280]{3,2,1,0:T(8,128)(2,1)} async-done(((bf16[4,2,128,1280]{3,2,1,0:T(8,128)(2,1)}), bf16[4,2,128,1280]{3,2,1,0:T(8,128)(2,1)}, u32[]{:S(2)}, u32[]{:S(2)}) %all-to-all-start.3) | async-done | bytes 2621472 | tf_op jit(solution)/shard_map/all_to_all | solution.py:582
  326.1 4.8 %finish.1 = (f32[128,5120]{1,0:T(8,128)}, bf16[128,5120]{1,0:T(8,128)(2,1)}) custom-call(f32[128,5120]{1,0:T(8,128)} %select_add_fusion.base, bf16[4,2,128,1280]{3,2,1,0:T(8,128)(2,1)} %all-to-all-done.3.refs_0_), custom_call_target="tpu_custom_call" | custom-call | flops 163840 | bytes 2293760 | tf_op jit(solution)/shard_map/finish/pallas_call | solution.py:486
  (147 shorter events, 67.4 us)
Async XLA Ops:
  8.8 46.1 %collective-permute-start.6 = (bf16[640,1536]{1,0:T(8,128)(2,1)S(1)}, bf16[640,1536]{1,0:T(8,128)(2,1)S(1)}, u32[]{:S(2)}, u32[]{:S(2)}) collective-permute-start(bf16[640,1536]{1,0:T(8,128)(2,1)S(1)} %constant_dynamic-update-slice_fusion.refs_7_), channel_id=1, source_target_pairs={{0,16},{8,24},{16,0},{24,8},{1,17},{9,25},{17,1},{25,9},{2,18},{10... | collective-permute-start | bytes 5898248 | tf_op jit(solution)/shard_map/ppermute | solution.py:19
  11.4 44.9 %collective-permute-start.5 = (bf16[640,1536]{1,0:T(8,128)(2,1)S(1)}, bf16[640,1536]{1,0:T(8,128)(2,1)S(1)}, u32[]{:S(2)}, u32[]{:S(2)}) collective-permute-start(bf16[640,1536]{1,0:T(8,128)(2,1)S(1)} %constant_dynamic-update-slice_fusion.refs_7_), channel_id=1, source_target_pairs={{0,8},{8,0},{16,24},{24,16},{1,9},{9,1},{17,25},{25,17},{2,10},{10... | collective-permute-start | bytes 5898248 | tf_op jit(solution)/shard_map/ppermute | solution.py:19
  13.1 32.6 %collective-permute-start.3 = (bf16[2,128,2560]{2,1,0:T(8,128)(2,1)S(1)}, bf16[2,128,2560]{2,1,0:T(8,128)(2,1)S(1)}, u32[]{:S(2)}, u32[]{:S(2)}) collective-permute-start(bf16[2,128,2560]{2,1,0:T(8,128)(2,1)S(1)} %pad_maximum_fusion.refs_0_.refs_3_.refs_6_), channel_id=1, source_target_pairs={{2,0},{4,2},{6,4},{3,1},{5,3},{7,5},{10,8},{12,10},{14,12},{11,9},... | collective-permute-start | bytes 3932168 | tf_op jit(solution)/shard_map/ppermute | solution.py:515
  14.5 32.5 %collective-permute-start.1 = (bf16[2,128,2560]{2,1,0:T(8,128)(2,1)S(1)}, bf16[2,128,2560]{2,1,0:T(8,128)(2,1)S(1)}, u32[]{:S(2)}, u32[]{:S(2)}) collective-permute-start(bf16[2,128,2560]{2,1,0:T(8,128)(2,1)S(1)} %pad_maximum_fusion.refs_0_.refs_3_.refs_6_), channel_id=1, source_target_pairs={{0,2},{2,4},{4,6},{1,3},{3,5},{5,7},{8,10},{10,12},{12,14},{9,11},... | collective-permute-start | bytes 3932168 | tf_op jit(solution)/shard_map/ppermute | solution.py:514
  45.7 34.4 %collective-permute-start.4 = (bf16[2,128,2560]{2,1,0:T(8,128)(2,1)S(1)}, bf16[2,128,2560]{2,1,0:T(8,128)(2,1)}, u32[]{:S(2)}, u32[]{:S(2)}) collective-permute-start(bf16[2,128,2560]{2,1,0:T(8,128)(2,1)S(1)} %collective-permute-done.3.refs_4_), channel_id=1, source_target_pairs={{2,0},{4,2},{3,1},{5,3},{10,8},{12,10},{11,9},{13,11},{18,16},{20,... | collective-permute-start | bytes 3932168 | tf_op jit(solution)/shard_map/ppermute | solution.py:515
  47.0 33.1 %collective-permute-start.2 = (bf16[2,128,2560]{2,1,0:T(8,128)(2,1)S(1)}, bf16[2,128,2560]{2,1,0:T(8,128)(2,1)}, u32[]{:S(2)}, u32[]{:S(2)}) collective-permute-start(bf16[2,128,2560]{2,1,0:T(8,128)(2,1)S(1)} %collective-permute-done.1.refs_1_), channel_id=1, source_target_pairs={{2,4},{4,6},{3,5},{5,7},{10,12},{12,14},{11,13},{13,15},{18,20},{2... | collective-permute-start | bytes 3932168 | tf_op jit(solution)/shard_map/ppermute | solution.py:514
  56.5 23.2 %collective-permute-start.8 = (bf16[640,768]{1,0:T(8,128)(2,1)S(1)}, bf16[640,768]{1,0:T(8,128)(2,1)S(1)}, u32[]{:S(2)}, u32[]{:S(2)}) collective-permute-start(bf16[640,768]{1,0:T(8,128)(2,1)S(1)} %slice.27), channel_id=1, source_target_pairs={{0,16},{8,24},{16,0},{24,8},{1,17},{9,25},{17,1},{25,9},{2,18},{10... | collective-permute-start | bytes 2949128 | tf_op jit(solution)/shard_map/ppermute | solution.py:19
  56.9 23.2 %collective-permute-start.7 = (bf16[640,768]{1,0:T(8,128)(2,1)S(1)}, bf16[640,768]{1,0:T(8,128)(2,1)S(1)}, u32[]{:S(2)}, u32[]{:S(2)}) collective-permute-start(bf16[640,768]{1,0:T(8,128)(2,1)S(1)} %slice.26), channel_id=1, source_target_pairs={{0,8},{8,0},{16,24},{24,16},{1,9},{9,1},{17,25},{25,17},{2,10},{10... | collective-permute-start | bytes 2949128 | tf_op jit(solution)/shard_map/ppermute | solution.py:19
  80.8 52.7 %collective-permute-start.9 = (bf16[2,128,2560]{2,1,0:T(8,128)(2,1)}, bf16[2,128,2560]{2,1,0:T(8,128)(2,1)S(1)}, u32[]{:S(2)}, u32[]{:S(2)}) collective-permute-start(bf16[2,128,2560]{2,1,0:T(8,128)(2,1)} %collective-permute-done.2.refs_2_), channel_id=1, source_target_pairs={{4,6},{5,7},{12,14},{13,15},{20,22},{21,23},{28,30},{29,31}} | collective-permute-start | bytes 3932168 | tf_op jit(solution)/shard_map/ppermute | solution.py:514
  81.5 52.0 %collective-permute-start.10 = (bf16[2,128,2560]{2,1,0:T(8,128)(2,1)}, bf16[2,128,2560]{2,1,0:T(8,128)(2,1)}, u32[]{:S(2)}, u32[]{:S(2)}) collective-permute-start(bf16[2,128,2560]{2,1,0:T(8,128)(2,1)} %collective-permute-done.4.refs_5_), channel_id=1, source_target_pairs={{2,0},{3,1},{10,8},{11,9},{18,16},{19,17},{26,24},{27,25}} | collective-permute-start | bytes 3932168 | tf_op jit(solution)/shard_map/ppermute | solution.py:515
  88.8 44.7 %all-to-all-start = ((bf16[4,144,1280]{2,1,0:T(8,128)(2,1)}), bf16[4,144,1280]{2,1,0:T(8,128)(2,1)S(1)}, u32[]{:S(2)}, u32[]{:S(2)}) async-start(bf16[4,144,1280]{2,1,0:T(8,128)(2,1)} %tell.1), calls=%async_computation | async-start | bytes 2949120 | tf_op jit(solution)/shard_map/all_to_all | solution.py:539
  92.3 40.2 %collective-permute-start.14 = (bf16[640,768]{1,0:T(8,128)(2,1)}, bf16[640,768]{1,0:T(8,128)(2,1)S(1)}, u32[]{:S(2)}, u32[]{:S(2)}) collective-permute-start(bf16[640,768]{1,0:T(8,128)(2,1)} %refs_7_.1), channel_id=1, source_target_pairs={{0,8},{8,0},{16,24},{24,16},{1,9},{9,1},{17,25},{25,17},{2,10},{10... | collective-permute-start | bytes 2949128 | tf_op jit(solution)/shard_map/ppermute | solution.py:19
  94.3 39.1 %collective-permute-start.15 = (bf16[640,768]{1,0:T(8,128)(2,1)}, bf16[640,768]{1,0:T(8,128)(2,1)}, u32[]{:S(2)}, u32[]{:S(2)}) collective-permute-start(bf16[640,768]{1,0:T(8,128)(2,1)} %refs_7_.1), channel_id=1, source_target_pairs={{0,16},{8,24},{16,0},{24,8},{1,17},{9,25},{17,1},{25,9},{2,18},{10... | collective-permute-start | bytes 2949128 | tf_op jit(solution)/shard_map/ppermute | solution.py:19
  133.5 38.7 %collective-permute-start.18 = (f32[384,1536]{1,0:T(8,128)}, f32[384,1536]{1,0:T(8,128)S(1)}, u32[]{:S(2)}, u32[]{:S(2)}) collective-permute-start(f32[384,1536]{1,0:T(8,128)} %get-tuple-element.61), channel_id=1, source_target_pairs={{0,1},{1,0},{2,3},{3,2},{4,5},{5,4},{6,7},{7,6},{8,9},{9,8},{10,11... | collective-permute-start | bytes 7077896 | tf_op jit(solution)/shard_map/ppermute | solution.py:19
  138.2 26.9 %collective-permute-start.12 = (bf16[768,640]{1,0:T(8,128)(2,1)}, bf16[768,640]{1,0:T(8,128)(2,1)}, u32[]{:S(2)}, u32[]{:S(2)}) collective-permute-start(bf16[768,640]{1,0:T(8,128)(2,1)} %refs_5_.1), channel_id=1, source_target_pairs={{0,2},{2,4},{4,6},{1,3},{3,5},{5,7},{8,10},{10,12},{12,14},{9,11},... | collective-permute-start | bytes 2949128 | tf_op jit(solution)/shard_map/ppermute | solution.py:558
  144.7 25.3 %collective-permute-start.13 = (bf16[768,640]{1,0:T(8,128)(2,1)}, bf16[768,640]{1,0:T(8,128)(2,1)}, u32[]{:S(2)}, u32[]{:S(2)}) collective-permute-start(bf16[768,640]{1,0:T(8,128)(2,1)} %refs_5_.1), channel_id=1, source_target_pairs={{2,0},{4,2},{6,4},{3,1},{5,3},{7,5},{10,8},{12,10},{14,12},{11,9},... | collective-permute-start | bytes 2949128 | tf_op jit(solution)/shard_map/ppermute | solution.py:559
  165.0 42.8 %collective-permute-start.24 = (f32[512,768]{1,0:T(8,128)}, f32[512,768]{1,0:T(8,128)S(1)}, u32[]{:S(2)}, u32[]{:S(2)}) collective-permute-start(f32[512,768]{1,0:T(8,128)} %get-tuple-element.67), channel_id=1, source_target_pairs={{0,1},{1,0},{2,3},{3,2},{4,5},{5,4},{6,7},{7,6},{8,9},{9,8},{10,11... | collective-permute-start | bytes 4718600 | tf_op jit(solution)/shard_map/ppermute | solution.py:19
  170.9 28.0 %collective-permute-start.23 = (bf16[768,640]{1,0:T(8,128)(2,1)}, bf16[768,640]{1,0:T(8,128)(2,1)}, u32[]{:S(2)}, u32[]{:S(2)}) collective-permute-start(bf16[768,640]{1,0:T(8,128)(2,1)} %collective-permute-done.13.refs_9_), channel_id=1, source_target_pairs={{2,0},{4,2},{3,1},{5,3},{10,8},{12,10},{11,9},{13,11},{18,16},{20,... | collective-permute-start | bytes 2949128 | tf_op jit(solution)/shard_map/ppermute | solution.py:559
  172.2 26.7 %collective-permute-start.21 = (bf16[768,640]{1,0:T(8,128)(2,1)}, bf16[768,640]{1,0:T(8,128)(2,1)}, u32[]{:S(2)}, u32[]{:S(2)}) collective-permute-start(bf16[768,640]{1,0:T(8,128)(2,1)} %collective-permute-done.13.refs_9_), channel_id=1, source_target_pairs={{0,1},{1,0},{2,3},{3,2},{4,5},{5,4},{6,7},{7,6},{8,9},{9,8},{10,11... | collective-permute-start | bytes 2949128 | tf_op jit(solution)/shard_map/ppermute | solution.py:19
  177.4 22.8 %all-to-all-start.1 = ((f32[4,2,512]{2,1,0:T(2,128)}), f32[4,2,512]{2,1,0:T(2,128)S(1)}, u32[]{:S(2)}, u32[]{:S(2)}) async-start(f32[4,2,512]{2,1,0:T(2,128)} %norms.1), calls=%async_computation.1 | async-start | bytes 32768 | tf_op jit(solution)/shard_map/all_to_all | solution.py:569
  214.0 23.4 %all-to-all-start.2 = ((bf16[4,128,768]{2,1,0:T(8,128)(2,1)}), bf16[4,128,768]{2,1,0:T(8,128)(2,1)S(1)}, u32[]{:S(2)}, u32[]{:S(2)}) async-start(bf16[4,128,768]{2,1,0:T(8,128)(2,1)} %attend.1), calls=%async_computation.2 | async-start | bytes 1572864 | tf_op jit(solution)/shard_map/all_to_all | solution.py:574
  237.4 20.8 %collective-permute-start.31 = (bf16[768,640]{1,0:T(8,128)(2,1)S(1)}, bf16[768,640]{1,0:T(8,128)(2,1)S(1)}, u32[]{:S(2)}, u32[]{:S(2)}) collective-permute-start(bf16[768,640]{1,0:T(8,128)(2,1)S(1)} %collective-permute-done.22.refs_7_), channel_id=1, source_target_pairs={{4,6},{5,7},{12,14},{13,15},{20,22},{21,23},{28,30},{29,31}} | collective-permute-start | bytes 2949128 | tf_op jit(solution)/shard_map/ppermute | solution.py:558
  238.1 24.8 %collective-permute-start.32 = (bf16[768,640]{1,0:T(8,128)(2,1)}, bf16[768,640]{1,0:T(8,128)(2,1)S(1)}, u32[]{:S(2)}, u32[]{:S(2)}) collective-permute-start(bf16[768,640]{1,0:T(8,128)(2,1)} %collective-permute-done.23.refs_10_), channel_id=1, source_target_pairs={{2,0},{3,1},{10,8},{11,9},{18,16},{19,17},{26,24},{27,25}} | collective-permute-start | bytes 2949128 | tf_op jit(solution)/shard_map/ppermute | solution.py:559
  291.4 34.7 %all-to-all-start.3 = ((bf16[4,2,128,1280]{3,2,1,0:T(8,128)(2,1)}), bf16[4,2,128,1280]{3,2,1,0:T(8,128)(2,1)}, u32[]{:S(2)}, u32[]{:S(2)}) async-start(bf16[4,2,128,1280]{3,2,1,0:T(8,128)(2,1)} %project_out.1), calls=%async_computation.3 | async-start | bytes 5242880 | tf_op jit(solution)/shard_map/all_to_all | solution.py:582
  (49 other events, 818.2 us)

commit v12 on v10

--- a/solution.py
+++ b/solution.py
@@ -564,8 +564,11 @@
         partner_below.append(swap(arrived[0], "fsdp", 1))
         partner_above.append(swap(arrived[1], "fsdp", 1))
         if count == 1:
-            own_squares = norms(after(place, below[-1], above[-1], v_here), parts, size)
-            squares = lax.all_to_all(own_squares, "head", 0, 0)
+            own_squares = norms(after(place, below[-1], above[-1], v_here), parts, 1)
+            squares = [own_squares]
+            for away in range(1, size):
+                squares.append(lax.ppermute(own_squares, "head", [(i, (i + away) % size) for i in range(size)]))
+            squares = jnp.concatenate(squares)
         if count == size - 2:
             ready = after(squares, *partner_below[:-1], *partner_above[:-1], below[-1], above[-1], heard)
             probs = probabilities(place, ready, parts, q_gain, k_gain)
@@ -576,7 +579,7 @@
     out_weights = (raw, partner_below + partner_above)
     carried = step_width * current + jnp.where(step == 0, current, jnp.zeros_like(current))
 
-    halves = 2
+    halves = 1
     sent = [project_out(place, heard, gathered, out_weights, part, halves) for part in range(halves)]
     arrived = after(tuple(lax.all_to_all(part, "step", 0, 0) for part in sent), carried)
     reached, update = finish(carried, arrived)

time: 311 us -> 315 us (1.013)
  waiting for transfers between devices: 148 us -> 165 us
  starting transfers between devices: 65.5 us -> 58.4 us
  Pallas kernels: 79.4 us -> 73.7 us
    ppermute x3, waiting for transfers between devices: 7.57 us -> 25.1 us  [body(): lax.ppermute(down, 'head', [(i, i - 1) for i in range(1, size - count + 1)])]
    all_to_all x1, waiting for transfers between devices: 10.4 us -> 0.01 us  [body(): heard = lax.all_to_all(after(told, last_here, *v_last), 'step', 0, 0)]
    all_to_all x1 -> x0, starting transfers between devices: 7.38 us -> none  [body(): squares = lax.all_to_all(own_squares, 'head', 0, 0)]
    all_to_all x2 -> x1, waiting for transfers between devices: 20.6 us -> 28 us  [body(): lax.all_to_all(part, 'step', 0, 0)]
    ppermute x0 -> x3, starting transfers between devices: none -> 6.14 us  [body(): lax.ppermute(own_squares, 'head', [(i, (i + away) % size) for i in range(...]
    pallas_call x2 -> x1, Pallas kernels: 18.8 us -> 13 us  [project_out(): pl.pallas_call(functools.partial(out_kernel, size, tuple(layout), part *...]
    all_to_all x2 -> x1, starting transfers between devices: 8.63 us -> 4.86 us  [body(): lax.all_to_all(part, 'step', 0, 0)]
    ppermute x0 -> x3, waiting for transfers between devices: none -> 3.43 us  [body(): lax.ppermute(own_squares, 'head', [(i, (i + away) % size) for i in range(...]
  transfers between devices with their start and end apart: 40 -> 41, of which waited for: 22 -> 21; matrix products, arithmetic and copies ran while one was open for 2% -> 2% of each run, Pallas kernels for 18% -> 15%
where the time goes in v12:
time: 315 us; the launch traced here: 314 us
  waiting for transfers between devices  165 us (52%)
  Pallas kernels  73.7 us (23%)
  starting transfers between devices  58.4 us (19%)
  local copies, waits for them, and re-layouts  10.9 us (3%)
  other arithmetic  3.26 us (1%)
  between operations  3.23 us (1%)
    ppermute x23, waiting for transfers between devices, swap(): lax.ppermute(x, axis, [(i, i ^ offset) for i in range(lax.axis_size(axis))])  62.2 us
    pallas_call x3, Pallas kernels, project(): pl.pallas_call(functools.partial(project_kernel, size, parts, shard, tupl...  31.5 us
    ppermute x3, waiting for transfers between devices, hop(): lax.ppermute(down, 'head', [(i, i - 1) for i in range(1, size - count + 1)])  31 us
    all_to_all x1, waiting for transfers between devices, body(): lax.all_to_all(part, 'step', 0, 0)  28 us
    ppermute x3, waiting for transfers between devices, body(): lax.ppermute(down, 'head', [(i, i - 1) for i in range(1, size - count + 1)])  25.1 us
    ppermute x23, starting transfers between devices, swap(): lax.ppermute(x, axis, [(i, i ^ offset) for i in range(lax.axis_size(axis))])  20.5 us
    all_to_all x1, waiting for transfers between devices, body(): lax.all_to_all(attended, 'head', 0, 0)  15.1 us
    pallas_call x1, Pallas kernels, project_out(): pl.pallas_call(functools.partial(out_kernel, size, tuple(layout), part *...  13 us
  transfers between devices with their start and end apart: 41, of which 21 were waited for; matrix products, arithmetic and copies ran while one was open for 2% of the time, Pallas kernels for 15%

profile of v12, /device:TPU:0, one launch (start us, length us, event | category | flops | bytes accessed | tf_op | source)
XLA Modules:
  0.0 314.3 jit_solution(4369514618687397591)
XLA Ops:
  3.4 4.6 %modulate.1 = (bf16[128,2560]{1,0:T(8,128)(2,1)}, bf16[128,2560]{1,0:T(8,128)(2,1)}) custom-call(s32[5]{0:T(128)} %stack.32.place, f32[128,5120]{1,0:T(8,128)} %bitcast.12, f32[1,3,5120]{2,1,0:T(4,128)} %copy.12.rows), custom_call_target="tpu_custom_call" | custom-call | flops 1638400 | bytes 983040 | tf_op jit(solution)/shard_map/modulate/pallas_call | solution.py:119
  14.4 4.6 %collective-permute-start.1 = (bf16[2,128,2560]{2,1,0:T(8,128)(2,1)S(1)}, bf16[2,128,2560]{2,1,0:T(8,128)(2,1)S(1)}, u32[]{:S(2)}, u32[]{:S(2)}) collective-permute-start(bf16[2,128,2560]{2,1,0:T(8,128)(2,1)S(1)} %pad_maximum_fusion.refs_0_.refs_3_.refs_6_), channel_id=1, source_target_pairs={{0,2},{2,4},{4,6},{1,3},{3,5},{5,7},{8,10},{10,12},{12,14},{9,11},... | collective-permute-start | bytes 3932168 | tf_op jit(solution)/shard_map/ppermute | solution.py:514
  19.0 26.6 %collective-permute-done.3.refs_4_ = bf16[2,128,2560]{2,1,0:T(8,128)(2,1)S(1)} collective-permute-done((bf16[2,128,2560]{2,1,0:T(8,128)(2,1)S(1)}, bf16[2,128,2560]{2,1,0:T(8,128)(2,1)S(1)}, u32[]{:S(2)}, u32[]{:S(2)}) %collective-permute-start.3) | collective-permute-done | bytes 1310752 | tf_op jit(solution)/shard_map/ppermute | solution.py:515
  48.7 6.1 %collective-permute-done.6.refs_9_ = bf16[640,1536]{1,0:T(8,128)(2,1)S(1)} collective-permute-done((bf16[640,1536]{1,0:T(8,128)(2,1)S(1)}, bf16[640,1536]{1,0:T(8,128)(2,1)S(1)}, u32[]{:S(2)}, u32[]{:S(2)}) %collective-permute-start.6) | collective-permute-done | bytes 1966112 | tf_op jit(solution)/shard_map/ppermute | solution.py:19
  58.5 21.2 %collective-permute-done.8.refs_11_ = bf16[640,768]{1,0:T(8,128)(2,1)S(1)} collective-permute-done((bf16[640,768]{1,0:T(8,128)(2,1)S(1)}, bf16[640,768]{1,0:T(8,128)(2,1)S(1)}, u32[]{:S(2)}, u32[]{:S(2)}) %collective-permute-start.8) | collective-permute-done | bytes 983072 | tf_op jit(solution)/shard_map/ppermute | solution.py:19
  87.0 4.0 %tell.1 = bf16[4,144,1280]{2,1,0:T(8,128)(2,1)} custom-call(s32[5]{0:T(128)} %stack.32.place, f32[1]{0:T(128)} %bitcast.8.step_width, f32[128,5120]{1,0:T(8,128)} %bitcast.13, f32[1,3,5120]{2,1,0:T(4,128)} %copy.12.rows), custom_call_target="tpu_custom_call" | custom-call | flops 655360 | bytes 983040 | tf_op jit(solution)/shard_map/tell/pallas_call | solution.py:151
  91.0 13.5 %first.1 = (f32[384,1536]{1,0:T(8,128)}, f32[384,1536]{1,0:T(8,128)}) custom-call(s32[5]{0:T(128)} %stack.32.place, bf16[2,128,2560]{2,1,0:T(8,128)(2,1)} %copy-done, bf16[2,128,2560]{2,1,0:T(8,128)(2,1)} %copy-done.7, bf16[2,128,2560]{2,1,0:T(8,128)(2,1)} %collective-permute-done.2.refs_2_, bf16[2,128,2560]{2,1,0:T(8,128)(2,1)} %copy-done, ...), custom_call_target="tpu_custom_call" | custom-call | flops 1509949440 | bytes 4128768 | tf_op jit(solution)/shard_map/first/pallas_call | solution.py:233
  107.8 4.4 %collective-permute-done.10.refs_6_ = bf16[2,128,2560]{2,1,0:T(8,128)(2,1)S(1)} collective-permute-done((bf16[2,128,2560]{2,1,0:T(8,128)(2,1)}, bf16[2,128,2560]{2,1,0:T(8,128)(2,1)S(1)}, u32[]{:S(2)}, u32[]{:S(2)}) %collective-permute-start.10) | collective-permute-done | bytes 1310752 | tf_op jit(solution)/shard_map/ppermute | solution.py:515
  120.1 7.8 %last.1 = (f32[128,1536]{1,0:T(8,128)}, f32[128,1536]{1,0:T(8,128)}) custom-call(s32[5]{0:T(128)} %stack.32.place, bf16[2,128,2560]{2,1,0:T(8,128)(2,1)} %copy-done, bf16[2,128,2560]{2,1,0:T(8,128)(2,1)} %copy-done.7, bf16[2,128,2560]{2,1,0:T(8,128)(2,1)} %collective-permute-done.2.refs_2_, bf16[2,128,2560]{2,1,0:T(8,128)(2,1)} %copy-done.9, ...), custom_call_target="tpu_custom_call" | custom-call | flops 503316480 | bytes 2686976 | tf_op jit(solution)/shard_map/last/pallas_call | solution.py:233
  128.9 10.2 %value.1 = (f32[512,768]{1,0:T(8,128)}, f32[512,768]{1,0:T(8,128)}) custom-call(s32[5]{0:T(128)} %stack.32.place, bf16[2,128,2560]{2,1,0:T(8,128)(2,1)} %copy-done, bf16[2,128,2560]{2,1,0:T(8,128)(2,1)} %copy-done.7, bf16[2,128,2560]{2,1,0:T(8,128)(2,1)} %collective-permute-done.2.refs_2_, bf16[2,128,2560]{2,1,0:T(8,128)(2,1)} %copy-done.9, ...), custom_call_target="tpu_custom_call" | custom-call | flops 1006632960 | bytes 3080192 | tf_op jit(solution)/shard_map/value/pallas_call | solution.py:233
  139.1 4.3 %all-to-all-start = ((bf16[4,144,1280]{2,1,0:T(8,128)(2,1)}), bf16[4,144,1280]{2,1,0:T(8,128)(2,1)}, u32[]{:S(2)}, u32[]{:S(2)}) async-start(bf16[4,144,1280]{2,1,0:T(8,128)(2,1)} %tell.1), calls=%async_computation | async-start | bytes 2949120 | tf_op jit(solution)/shard_map/all_to_all | solution.py:546
  146.2 3.8 %norms.1 = f32[1,2,512]{2,1,0:T(2,128)} custom-call(s32[5]{0:T(128)} %stack.32.place, f32[384,1536]{1,0:T(8,128)} %get-tuple-element.48.first_a.refs_0_.refs_4_, f32[384,1536]{1,0:T(8,128)} %copy-done.2, f32[128,1536]{1,0:T(8,128)} %get-tuple-element.51.last_a.refs_2_.refs_6_, f32[128,1536]{1,0:T(8,128)} %copy-done.8), custom_call_target="tpu_custom_call" | custom-call | flops 786432 | bytes 1572864 | tf_op jit(solution)/shard_map/norms/pallas_call | solution.py:271
  150.0 5.6 %collective-permute-start.22 = (f32[1,2,512]{2,1,0:T(2,128)}, f32[1,2,512]{2,1,0:T(2,128)S(1)}, u32[]{:S(2)}, u32[]{:S(2)}) collective-permute-start(f32[1,2,512]{2,1,0:T(2,128)} %norms.1), channel_id=1, source_target_pairs={{0,6},{2,0},{4,2},{6,4},{1,7},{3,1},{5,3},{7,5},{8,14},{10,8},{12,... | collective-permute-start | bytes 12296 | tf_op jit(solution)/shard_map/ppermute | solution.py:570
  164.4 21.4 %collective-permute-done.26.refs_10_ = bf16[768,640]{1,0:T(8,128)(2,1)} collective-permute-done((bf16[768,640]{1,0:T(8,128)(2,1)}, bf16[768,640]{1,0:T(8,128)(2,1)}, u32[]{:S(2)}, u32[]{:S(2)}) %collective-permute-start.26) | collective-permute-done | bytes 983072 | tf_op jit(solution)/shard_map/ppermute | solution.py:558
  185.8 7.0 %probs.1 = bf16[6,512,512]{2,1,0:T(8,128)(2,1)} custom-call(s32[5]{0:T(128)} %stack.32.place, f32[4,2,512]{2,1,0:T(2,128)} %pad_maximum_fusion.1.squares, f32[384,1536]{1,0:T(8,128)} %get-tuple-element.48.first_a.refs_0_.refs_4_, f32[384,1536]{1,0:T(8,128)} %copy-done.2, f32[128,1536]{1,0:T(8,128)} %get-tuple-element.51.last_a.refs_2_.refs_6_, ...), custom_call_target="tpu_custom_call" | custom-call | flops 100663296 | bytes 2359296 | tf_op jit(solution)/shard_map/probs/pallas_call | solution.py:325
  192.8 5.0 %attend.1 = bf16[4,128,768]{2,1,0:T(8,128)(2,1)} custom-call(s32[5]{0:T(128)} %stack.32.place, bf16[6,512,512]{2,1,0:T(8,128)(2,1)} %probs.1, f32[512,768]{1,0:T(8,128)} %get-tuple-element.55.v_a, f32[512,768]{1,0:T(8,128)} %collective-permute-done.27.v_b), custom_call_target="tpu_custom_call" | custom-call | flops 100663296 | bytes 1769472 | tf_op jit(solution)/shard_map/attend/pallas_call | solution.py:354
  197.8 3.5 %all-to-all-start.1 = ((bf16[4,128,768]{2,1,0:T(8,128)(2,1)}), bf16[4,128,768]{2,1,0:T(8,128)(2,1)S(1)}, u32[]{:S(2)}, u32[]{:S(2)}) async-start(bf16[4,128,768]{2,1,0:T(8,128)(2,1)} %attend.1), calls=%async_computation.1 | async-start | bytes 1572864 | tf_op jit(solution)/shard_map/all_to_all | solution.py:576
  205.7 15.1 %all-to-all-done.1.refs_0_ = bf16[4,128,768]{2,1,0:T(8,128)(2,1)S(1)} async-done(((bf16[4,128,768]{2,1,0:T(8,128)(2,1)}), bf16[4,128,768]{2,1,0:T(8,128)(2,1)S(1)}, u32[]{:S(2)}, u32[]{:S(2)}) %all-to-all-start.1) | async-done | bytes 786464 | tf_op jit(solution)/shard_map/all_to_all | solution.py:576
  226.3 15.3 %collective-permute-done.31.refs_2_ = bf16[4,128,768]{2,1,0:T(8,128)(2,1)S(1)} collective-permute-done((bf16[4,128,768]{2,1,0:T(8,128)(2,1)S(1)}, bf16[4,128,768]{2,1,0:T(8,128)(2,1)S(1)}, u32[]{:S(2)}, u32[]{:S(2)}) %collective-permute-start.31) | collective-permute-done | bytes 786464 | tf_op jit(solution)/shard_map/ppermute | solution.py:19
  250.4 7.7 %collective-permute-done.32.refs_3_ = bf16[2,128,768]{2,1,0:T(8,128)(2,1)S(1)} collective-permute-done((bf16[2,128,768]{2,1,0:T(8,128)(2,1)S(1)}, bf16[2,128,768]{2,1,0:T(8,128)(2,1)S(1)}, u32[]{:S(2)}, u32[]{:S(2)}) %collective-permute-start.32) | collective-permute-done | bytes 393248 | tf_op jit(solution)/shard_map/ppermute | solution.py:19
  261.8 13.0 %project_out.1 = bf16[4,2,128,1280]{3,2,1,0:T(8,128)(2,1)} custom-call(s32[5]{0:T(128)} %stack.32.place, bf16[4,128,768]{2,1,0:T(8,128)(2,1)} %copy-done.13, bf16[4,128,768]{2,1,0:T(8,128)(2,1)} %copy-done.16, bf16[4,128,768]{2,1,0:T(8,128)(2,1)} %copy-done.15, bf16[2,128,768]{2,1,0:T(8,128)(2,1)} %copy-done.29, bf16[2,128,768]{2,1,0:T(8,128)(2,1)} %copy-done.30, ...), custom_call_target="tpu_custom_call" | custom-call | flops 1006632960 | bytes 3407872 | tf_op jit(solution)/shard_map/project_out/pallas_call | solution.py:456
  274.8 4.9 %all-to-all-start.2 = ((bf16[4,2,128,1280]{3,2,1,0:T(8,128)(2,1)}), bf16[4,2,128,1280]{3,2,1,0:T(8,128)(2,1)}, u32[]{:S(2)}, u32[]{:S(2)}) async-start(bf16[4,2,128,1280]{3,2,1,0:T(8,128)(2,1)} %project_out.1), calls=%async_computation.2 | async-start | bytes 5242880 | tf_op jit(solution)/shard_map/all_to_all | solution.py:584
  281.5 28.0 %all-to-all-done.2.refs_0_ = bf16[4,2,128,1280]{3,2,1,0:T(8,128)(2,1)} async-done(((bf16[4,2,128,1280]{3,2,1,0:T(8,128)(2,1)}), bf16[4,2,128,1280]{3,2,1,0:T(8,128)(2,1)}, u32[]{:S(2)}, u32[]{:S(2)}) %all-to-all-start.2) | async-done | bytes 2621472 | tf_op jit(solution)/shard_map/all_to_all | solution.py:584
  309.5 4.8 %finish.1 = (f32[128,5120]{1,0:T(8,128)}, bf16[128,5120]{1,0:T(8,128)(2,1)}) custom-call(f32[128,5120]{1,0:T(8,128)} %select_add_fusion.base, bf16[4,2,128,1280]{3,2,1,0:T(8,128)(2,1)} %all-to-all-done.2.refs_0_), custom_call_target="tpu_custom_call" | custom-call | flops 163840 | bytes 2293760 | tf_op jit(solution)/shard_map/finish/pallas_call | solution.py:486
  (152 shorter events, 68.8 us)
Async XLA Ops:
  8.7 46.1 %collective-permute-start.6 = (bf16[640,1536]{1,0:T(8,128)(2,1)S(1)}, bf16[640,1536]{1,0:T(8,128)(2,1)S(1)}, u32[]{:S(2)}, u32[]{:S(2)}) collective-permute-start(bf16[640,1536]{1,0:T(8,128)(2,1)S(1)} %constant_dynamic-update-slice_fusion.refs_7_), channel_id=1, source_target_pairs={{0,16},{8,24},{16,0},{24,8},{1,17},{9,25},{17,1},{25,9},{2,18},{10... | collective-permute-start | bytes 5898248 | tf_op jit(solution)/shard_map/ppermute | solution.py:19
  11.3 44.9 %collective-permute-start.5 = (bf16[640,1536]{1,0:T(8,128)(2,1)S(1)}, bf16[640,1536]{1,0:T(8,128)(2,1)S(1)}, u32[]{:S(2)}, u32[]{:S(2)}) collective-permute-start(bf16[640,1536]{1,0:T(8,128)(2,1)S(1)} %constant_dynamic-update-slice_fusion.refs_7_), channel_id=1, source_target_pairs={{0,8},{8,0},{16,24},{24,16},{1,9},{9,1},{17,25},{25,17},{2,10},{10... | collective-permute-start | bytes 5898248 | tf_op jit(solution)/shard_map/ppermute | solution.py:19
  13.0 32.6 %collective-permute-start.3 = (bf16[2,128,2560]{2,1,0:T(8,128)(2,1)S(1)}, bf16[2,128,2560]{2,1,0:T(8,128)(2,1)S(1)}, u32[]{:S(2)}, u32[]{:S(2)}) collective-permute-start(bf16[2,128,2560]{2,1,0:T(8,128)(2,1)S(1)} %pad_maximum_fusion.refs_0_.refs_3_.refs_6_), channel_id=1, source_target_pairs={{2,0},{4,2},{6,4},{3,1},{5,3},{7,5},{10,8},{12,10},{14,12},{11,9},... | collective-permute-start | bytes 3932168 | tf_op jit(solution)/shard_map/ppermute | solution.py:515
  14.4 32.5 %collective-permute-start.1 = (bf16[2,128,2560]{2,1,0:T(8,128)(2,1)S(1)}, bf16[2,128,2560]{2,1,0:T(8,128)(2,1)S(1)}, u32[]{:S(2)}, u32[]{:S(2)}) collective-permute-start(bf16[2,128,2560]{2,1,0:T(8,128)(2,1)S(1)} %pad_maximum_fusion.refs_0_.refs_3_.refs_6_), channel_id=1, source_target_pairs={{0,2},{2,4},{4,6},{1,3},{3,5},{5,7},{8,10},{10,12},{12,14},{9,11},... | collective-permute-start | bytes 3932168 | tf_op jit(solution)/shard_map/ppermute | solution.py:514
  45.6 34.4 %collective-permute-start.4 = (bf16[2,128,2560]{2,1,0:T(8,128)(2,1)S(1)}, bf16[2,128,2560]{2,1,0:T(8,128)(2,1)}, u32[]{:S(2)}, u32[]{:S(2)}) collective-permute-start(bf16[2,128,2560]{2,1,0:T(8,128)(2,1)S(1)} %collective-permute-done.3.refs_4_), channel_id=1, source_target_pairs={{2,0},{4,2},{3,1},{5,3},{10,8},{12,10},{11,9},{13,11},{18,16},{20,... | collective-permute-start | bytes 3932168 | tf_op jit(solution)/shard_map/ppermute | solution.py:515
  46.9 33.1 %collective-permute-start.2 = (bf16[2,128,2560]{2,1,0:T(8,128)(2,1)S(1)}, bf16[2,128,2560]{2,1,0:T(8,128)(2,1)}, u32[]{:S(2)}, u32[]{:S(2)}) collective-permute-start(bf16[2,128,2560]{2,1,0:T(8,128)(2,1)S(1)} %collective-permute-done.1.refs_1_), channel_id=1, source_target_pairs={{2,4},{4,6},{3,5},{5,7},{10,12},{12,14},{11,13},{13,15},{18,20},{2... | collective-permute-start | bytes 3932168 | tf_op jit(solution)/shard_map/ppermute | solution.py:514
  56.4 23.2 %collective-permute-start.8 = (bf16[640,768]{1,0:T(8,128)(2,1)S(1)}, bf16[640,768]{1,0:T(8,128)(2,1)S(1)}, u32[]{:S(2)}, u32[]{:S(2)}) collective-permute-start(bf16[640,768]{1,0:T(8,128)(2,1)S(1)} %slice.27), channel_id=1, source_target_pairs={{0,16},{8,24},{16,0},{24,8},{1,17},{9,25},{17,1},{25,9},{2,18},{10... | collective-permute-start | bytes 2949128 | tf_op jit(solution)/shard_map/ppermute | solution.py:19
  56.8 23.2 %collective-permute-start.7 = (bf16[640,768]{1,0:T(8,128)(2,1)S(1)}, bf16[640,768]{1,0:T(8,128)(2,1)S(1)}, u32[]{:S(2)}, u32[]{:S(2)}) collective-permute-start(bf16[640,768]{1,0:T(8,128)(2,1)S(1)} %slice.26), channel_id=1, source_target_pairs={{0,8},{8,0},{16,24},{24,16},{1,9},{9,1},{17,25},{25,17},{2,10},{10... | collective-permute-start | bytes 2949128 | tf_op jit(solution)/shard_map/ppermute | solution.py:19
  80.0 27.8 %collective-permute-start.9 = (bf16[2,128,2560]{2,1,0:T(8,128)(2,1)}, bf16[2,128,2560]{2,1,0:T(8,128)(2,1)S(1)}, u32[]{:S(2)}, u32[]{:S(2)}) collective-permute-start(bf16[2,128,2560]{2,1,0:T(8,128)(2,1)} %collective-permute-done.2.refs_2_), channel_id=1, source_target_pairs={{4,6},{5,7},{12,14},{13,15},{20,22},{21,23},{28,30},{29,31}} | collective-permute-start | bytes 3932168 | tf_op jit(solution)/shard_map/ppermute | solution.py:514
  80.8 31.4 %collective-permute-start.10 = (bf16[2,128,2560]{2,1,0:T(8,128)(2,1)}, bf16[2,128,2560]{2,1,0:T(8,128)(2,1)S(1)}, u32[]{:S(2)}, u32[]{:S(2)}) collective-permute-start(bf16[2,128,2560]{2,1,0:T(8,128)(2,1)} %collective-permute-done.4.refs_5_), channel_id=1, source_target_pairs={{2,0},{3,1},{10,8},{11,9},{18,16},{19,17},{26,24},{27,25}} | collective-permute-start | bytes 3932168 | tf_op jit(solution)/shard_map/ppermute | solution.py:515
  82.2 24.4 %collective-permute-start.11 = (bf16[640,768]{1,0:T(8,128)(2,1)}, bf16[640,768]{1,0:T(8,128)(2,1)S(1)}, u32[]{:S(2)}, u32[]{:S(2)}) collective-permute-start(bf16[640,768]{1,0:T(8,128)(2,1)} %refs_7_.1), channel_id=1, source_target_pairs={{0,8},{8,0},{16,24},{24,16},{1,9},{9,1},{17,25},{25,17},{2,10},{10... | collective-permute-start | bytes 2949128 | tf_op jit(solution)/shard_map/ppermute | solution.py:19
  83.7 24.1 %collective-permute-start.12 = (bf16[640,768]{1,0:T(8,128)(2,1)}, bf16[640,768]{1,0:T(8,128)(2,1)}, u32[]{:S(2)}, u32[]{:S(2)}) collective-permute-start(bf16[640,768]{1,0:T(8,128)(2,1)} %refs_7_.1), channel_id=1, source_target_pairs={{0,16},{8,24},{16,0},{24,8},{1,17},{9,25},{17,1},{25,9},{2,18},{10... | collective-permute-start | bytes 2949128 | tf_op jit(solution)/shard_map/ppermute | solution.py:19
  112.2 31.8 %collective-permute-start.18 = (f32[384,1536]{1,0:T(8,128)}, f32[384,1536]{1,0:T(8,128)S(1)}, u32[]{:S(2)}, u32[]{:S(2)}) collective-permute-start(f32[384,1536]{1,0:T(8,128)} %get-tuple-element.58), channel_id=1, source_target_pairs={{0,1},{1,0},{2,3},{3,2},{4,5},{5,4},{6,7},{7,6},{8,9},{9,8},{10,11... | collective-permute-start | bytes 7077896 | tf_op jit(solution)/shard_map/ppermute | solution.py:19
  116.3 27.2 %collective-permute-start.14 = (bf16[768,640]{1,0:T(8,128)(2,1)}, bf16[768,640]{1,0:T(8,128)(2,1)}, u32[]{:S(2)}, u32[]{:S(2)}) collective-permute-start(bf16[768,640]{1,0:T(8,128)(2,1)} %refs_5_.1), channel_id=1, source_target_pairs={{0,2},{2,4},{4,6},{1,3},{3,5},{5,7},{8,10},{10,12},{12,14},{9,11},... | collective-permute-start | bytes 2949128 | tf_op jit(solution)/shard_map/ppermute | solution.py:557
  118.8 25.2 %collective-permute-start.15 = (bf16[768,640]{1,0:T(8,128)(2,1)}, bf16[768,640]{1,0:T(8,128)(2,1)}, u32[]{:S(2)}, u32[]{:S(2)}) collective-permute-start(bf16[768,640]{1,0:T(8,128)(2,1)} %refs_5_.1), channel_id=1, source_target_pairs={{2,0},{4,2},{6,4},{3,1},{5,3},{7,5},{10,8},{12,10},{14,12},{11,9},... | collective-permute-start | bytes 2949128 | tf_op jit(solution)/shard_map/ppermute | solution.py:558
  139.0 53.7 %collective-permute-start.27 = (f32[512,768]{1,0:T(8,128)}, f32[512,768]{1,0:T(8,128)}, u32[]{:S(2)}, u32[]{:S(2)}) collective-permute-start(f32[512,768]{1,0:T(8,128)} %get-tuple-element.65), channel_id=1, source_target_pairs={{0,1},{1,0},{2,3},{3,2},{4,5},{5,4},{6,7},{7,6},{8,9},{9,8},{10,11... | collective-permute-start | bytes 4718600 | tf_op jit(solution)/shard_map/ppermute | solution.py:19
  139.1 25.2 %all-to-all-start = ((bf16[4,144,1280]{2,1,0:T(8,128)(2,1)}), bf16[4,144,1280]{2,1,0:T(8,128)(2,1)}, u32[]{:S(2)}, u32[]{:S(2)}) async-start(bf16[4,144,1280]{2,1,0:T(8,128)(2,1)} %tell.1), calls=%async_computation | async-start | bytes 2949120 | tf_op jit(solution)/shard_map/all_to_all | solution.py:546
  160.3 25.5 %collective-permute-start.26 = (bf16[768,640]{1,0:T(8,128)(2,1)}, bf16[768,640]{1,0:T(8,128)(2,1)}, u32[]{:S(2)}, u32[]{:S(2)}) collective-permute-start(bf16[768,640]{1,0:T(8,128)(2,1)} %collective-permute-done.15.refs_9_), channel_id=1, source_target_pairs={{2,0},{4,2},{3,1},{5,3},{10,8},{12,10},{11,9},{13,11},{18,16},{20,... | collective-permute-start | bytes 2949128 | tf_op jit(solution)/shard_map/ppermute | solution.py:558
  161.8 24.0 %collective-permute-start.24 = (bf16[768,640]{1,0:T(8,128)(2,1)}, bf16[768,640]{1,0:T(8,128)(2,1)}, u32[]{:S(2)}, u32[]{:S(2)}) collective-permute-start(bf16[768,640]{1,0:T(8,128)(2,1)} %collective-permute-done.15.refs_9_), channel_id=1, source_target_pairs={{0,1},{1,0},{2,3},{3,2},{4,5},{5,4},{6,7},{7,6},{8,9},{9,8},{10,11... | collective-permute-start | bytes 2949128 | tf_op jit(solution)/shard_map/ppermute | solution.py:19
  197.8 23.0 %all-to-all-start.1 = ((bf16[4,128,768]{2,1,0:T(8,128)(2,1)}), bf16[4,128,768]{2,1,0:T(8,128)(2,1)S(1)}, u32[]{:S(2)}, u32[]{:S(2)}) async-start(bf16[4,128,768]{2,1,0:T(8,128)(2,1)} %attend.1), calls=%async_computation.1 | async-start | bytes 1572864 | tf_op jit(solution)/shard_map/all_to_all | solution.py:576
  220.8 22.3 %collective-permute-start.34 = (bf16[768,640]{1,0:T(8,128)(2,1)S(1)}, bf16[768,640]{1,0:T(8,128)(2,1)S(1)}, u32[]{:S(2)}, u32[]{:S(2)}) collective-permute-start(bf16[768,640]{1,0:T(8,128)(2,1)S(1)} %collective-permute-done.25.refs_7_), channel_id=1, source_target_pairs={{4,6},{5,7},{12,14},{13,15},{20,22},{21,23},{28,30},{29,31}} | collective-permute-start | bytes 2949128 | tf_op jit(solution)/shard_map/ppermute | solution.py:557
  221.5 24.8 %collective-permute-start.35 = (bf16[768,640]{1,0:T(8,128)(2,1)}, bf16[768,640]{1,0:T(8,128)(2,1)S(1)}, u32[]{:S(2)}, u32[]{:S(2)}) collective-permute-start(bf16[768,640]{1,0:T(8,128)(2,1)} %collective-permute-done.26.refs_10_), channel_id=1, source_target_pairs={{2,0},{3,1},{10,8},{11,9},{18,16},{19,17},{26,24},{27,25}} | collective-permute-start | bytes 2949128 | tf_op jit(solution)/shard_map/ppermute | solution.py:558
  222.8 18.8 %collective-permute-start.31 = (bf16[4,128,768]{2,1,0:T(8,128)(2,1)S(1)}, bf16[4,128,768]{2,1,0:T(8,128)(2,1)S(1)}, u32[]{:S(2)}, u32[]{:S(2)}) collective-permute-start(bf16[4,128,768]{2,1,0:T(8,128)(2,1)S(1)} %all-to-all-done.1.refs_0_), channel_id=1, source_target_pairs={{0,16},{8,24},{16,0},{24,8},{1,17},{9,25},{17,1},{25,9},{2,18},{10... | collective-permute-start | bytes 2359304 | tf_op jit(solution)/shard_map/ppermute | solution.py:19
  274.8 34.7 %all-to-all-start.2 = ((bf16[4,2,128,1280]{3,2,1,0:T(8,128)(2,1)}), bf16[4,2,128,1280]{3,2,1,0:T(8,128)(2,1)}, u32[]{:S(2)}, u32[]{:S(2)}) async-start(bf16[4,2,128,1280]{3,2,1,0:T(8,128)(2,1)} %project_out.1), calls=%async_computation.2 | async-start | bytes 5242880 | tf_op jit(solution)/shard_map/all_to_all | solution.py:584
  (51 other events, 877.9 us)

commit v13 on v12

--- a/solution.py
+++ b/solution.py
@@ -570,9 +570,9 @@
                 squares.append(lax.ppermute(own_squares, "head", [(i, (i + away) % size) for i in range(size)]))
             squares = jnp.concatenate(squares)
         if count == size - 2:
-            ready = after(squares, *partner_below[:-1], *partner_above[:-1], below[-1], above[-1], heard)
+            ready = after(squares, *partner_below[:-1], *partner_above[:-1], heard)
             probs = probabilities(place, ready, parts, q_gain, k_gain)
-            attended = attend(place, probs, v_parts, size)
+            attended = after(attend(place, probs, v_parts, size), below[-1], above[-1])
             quarter = after(lax.all_to_all(attended, "head", 0, 0), partner_below[-1], partner_above[-1])
 
     raw = [w_out] + below[1:] + above[1:]

time: 315 us -> 302 us (0.959)
  waiting for transfers between devices: 165 us -> 152 us
    ppermute x3, waiting for transfers between devices: 25.1 us -> 12 us  [body(): lax.ppermute(down, 'head', [(i, i - 1) for i in range(1, size - count + 1)])]
    ppermute x3, waiting for transfers between devices: 3.43 us -> 6.68 us  [body(): lax.ppermute(own_squares, 'head', [(i, (i + away) % size) for i in range(...]
    unnamed x70 -> x68, local copies, waits for them, and re-layouts: 6.76 us -> 6.9 us
  transfers between devices with their start and end apart: 41 -> 41, of which waited for: 21 -> 20; matrix products, arithmetic and copies ran while one was open for 2% -> 2% of each run, Pallas kernels for 15% -> 17%
where the time goes in v13:
time: 302 us; the launch traced here: 301 us
  waiting for transfers between devices  152 us (50%)
  Pallas kernels  74 us (25%)
  starting transfers between devices  57.5 us (19%)
  local copies, waits for them, and re-layouts  11 us (4%)
  other arithmetic  3.26 us (1%)
  between operations  3.13 us (1%)
    ppermute x23, waiting for transfers between devices, swap(): lax.ppermute(x, axis, [(i, i ^ offset) for i in range(lax.axis_size(axis))])  60.5 us
    pallas_call x3, Pallas kernels, project(): pl.pallas_call(functools.partial(project_kernel, size, parts, shard, tupl...  31.7 us
    ppermute x3, waiting for transfers between devices, hop(): lax.ppermute(down, 'head', [(i, i - 1) for i in range(1, size - count + 1)])  31 us
    all_to_all x1, waiting for transfers between devices, body(): lax.all_to_all(part, 'step', 0, 0)  27.9 us
    ppermute x23, starting transfers between devices, swap(): lax.ppermute(x, axis, [(i, i ^ offset) for i in range(lax.axis_size(axis))])  19.7 us
    all_to_all x1, waiting for transfers between devices, body(): lax.all_to_all(attended, 'head', 0, 0)  13.8 us
    pallas_call x1, Pallas kernels, project_out(): pl.pallas_call(functools.partial(out_kernel, size, tuple(layout), part *...  13 us
    ppermute x3, waiting for transfers between devices, body(): lax.ppermute(down, 'head', [(i, i - 1) for i in range(1, size - count + 1)])  12 us
  transfers between devices with their start and end apart: 41, of which 20 were waited for; matrix products, arithmetic and copies ran while one was open for 2% of the time, Pallas kernels for 17%

profile of v13, /device:TPU:0, one launch (start us, length us, event | category | flops | bytes accessed | tf_op | source)
XLA Modules:
  0.0 300.7 jit_solution(15606734223688910576)
XLA Ops:
  3.5 4.6 %modulate.1 = (bf16[128,2560]{1,0:T(8,128)(2,1)}, bf16[128,2560]{1,0:T(8,128)(2,1)}) custom-call(s32[5]{0:T(128)} %stack.32.place, f32[128,5120]{1,0:T(8,128)} %bitcast.12, f32[1,3,5120]{2,1,0:T(4,128)} %copy.12.rows), custom_call_target="tpu_custom_call" | custom-call | flops 1638400 | bytes 983040 | tf_op jit(solution)/shard_map/modulate/pallas_call | solution.py:119
  14.4 4.6 %collective-permute-start.1 = (bf16[2,128,2560]{2,1,0:T(8,128)(2,1)S(1)}, bf16[2,128,2560]{2,1,0:T(8,128)(2,1)S(1)}, u32[]{:S(2)}, u32[]{:S(2)}) collective-permute-start(bf16[2,128,2560]{2,1,0:T(8,128)(2,1)S(1)} %pad_maximum_fusion.refs_0_.refs_3_.refs_6_), channel_id=1, source_target_pairs={{0,2},{2,4},{4,6},{1,3},{3,5},{5,7},{8,10},{10,12},{12,14},{9,11},... | collective-permute-start | bytes 3932168 | tf_op jit(solution)/shard_map/ppermute | solution.py:514
  19.1 26.6 %collective-permute-done.3.refs_4_ = bf16[2,128,2560]{2,1,0:T(8,128)(2,1)S(1)} collective-permute-done((bf16[2,128,2560]{2,1,0:T(8,128)(2,1)S(1)}, bf16[2,128,2560]{2,1,0:T(8,128)(2,1)S(1)}, u32[]{:S(2)}, u32[]{:S(2)}) %collective-permute-start.3) | collective-permute-done | bytes 1310752 | tf_op jit(solution)/shard_map/ppermute | solution.py:515
  48.7 6.1 %collective-permute-done.6.refs_9_ = bf16[640,1536]{1,0:T(8,128)(2,1)S(1)} collective-permute-done((bf16[640,1536]{1,0:T(8,128)(2,1)S(1)}, bf16[640,1536]{1,0:T(8,128)(2,1)S(1)}, u32[]{:S(2)}, u32[]{:S(2)}) %collective-permute-start.6) | collective-permute-done | bytes 1966112 | tf_op jit(solution)/shard_map/ppermute | solution.py:19
  58.5 21.2 %collective-permute-done.8.refs_11_ = bf16[640,768]{1,0:T(8,128)(2,1)S(1)} collective-permute-done((bf16[640,768]{1,0:T(8,128)(2,1)S(1)}, bf16[640,768]{1,0:T(8,128)(2,1)S(1)}, u32[]{:S(2)}, u32[]{:S(2)}) %collective-permute-start.8) | collective-permute-done | bytes 983072 | tf_op jit(solution)/shard_map/ppermute | solution.py:19
  86.9 4.0 %tell.1 = bf16[4,144,1280]{2,1,0:T(8,128)(2,1)} custom-call(s32[5]{0:T(128)} %stack.32.place, f32[1]{0:T(128)} %bitcast.8.step_width, f32[128,5120]{1,0:T(8,128)} %bitcast.13, f32[1,3,5120]{2,1,0:T(4,128)} %copy.12.rows), custom_call_target="tpu_custom_call" | custom-call | flops 655360 | bytes 983040 | tf_op jit(solution)/shard_map/tell/pallas_call | solution.py:151
  90.9 13.6 %first.1 = (f32[384,1536]{1,0:T(8,128)}, f32[384,1536]{1,0:T(8,128)}) custom-call(s32[5]{0:T(128)} %stack.32.place, bf16[2,128,2560]{2,1,0:T(8,128)(2,1)} %copy-done, bf16[2,128,2560]{2,1,0:T(8,128)(2,1)} %copy-done.7, bf16[2,128,2560]{2,1,0:T(8,128)(2,1)} %collective-permute-done.2.refs_2_, bf16[2,128,2560]{2,1,0:T(8,128)(2,1)} %copy-done, ...), custom_call_target="tpu_custom_call" | custom-call | flops 1509949440 | bytes 4128768 | tf_op jit(solution)/shard_map/first/pallas_call | solution.py:233
  107.8 4.4 %collective-permute-done.10.refs_6_ = bf16[2,128,2560]{2,1,0:T(8,128)(2,1)S(1)} collective-permute-done((bf16[2,128,2560]{2,1,0:T(8,128)(2,1)}, bf16[2,128,2560]{2,1,0:T(8,128)(2,1)S(1)}, u32[]{:S(2)}, u32[]{:S(2)}) %collective-permute-start.10) | collective-permute-done | bytes 1310752 | tf_op jit(solution)/shard_map/ppermute | solution.py:515
  120.1 7.8 %last.1 = (f32[128,1536]{1,0:T(8,128)}, f32[128,1536]{1,0:T(8,128)}) custom-call(s32[5]{0:T(128)} %stack.32.place, bf16[2,128,2560]{2,1,0:T(8,128)(2,1)} %copy-done, bf16[2,128,2560]{2,1,0:T(8,128)(2,1)} %copy-done.7, bf16[2,128,2560]{2,1,0:T(8,128)(2,1)} %collective-permute-done.2.refs_2_, bf16[2,128,2560]{2,1,0:T(8,128)(2,1)} %copy-done.9, ...), custom_call_target="tpu_custom_call" | custom-call | flops 503316480 | bytes 2686976 | tf_op jit(solution)/shard_map/last/pallas_call | solution.py:233
  129.0 10.2 %value.1 = (f32[512,768]{1,0:T(8,128)}, f32[512,768]{1,0:T(8,128)}) custom-call(s32[5]{0:T(128)} %stack.32.place, bf16[2,128,2560]{2,1,0:T(8,128)(2,1)} %copy-done, bf16[2,128,2560]{2,1,0:T(8,128)(2,1)} %copy-done.7, bf16[2,128,2560]{2,1,0:T(8,128)(2,1)} %collective-permute-done.2.refs_2_, bf16[2,128,2560]{2,1,0:T(8,128)(2,1)} %copy-done.9, ...), custom_call_target="tpu_custom_call" | custom-call | flops 1006632960 | bytes 3080192 | tf_op jit(solution)/shard_map/value/pallas_call | solution.py:233
  139.3 4.4 %all-to-all-start = ((bf16[4,144,1280]{2,1,0:T(8,128)(2,1)}), bf16[4,144,1280]{2,1,0:T(8,128)(2,1)}, u32[]{:S(2)}, u32[]{:S(2)}) async-start(bf16[4,144,1280]{2,1,0:T(8,128)(2,1)} %tell.1), calls=%async_computation | async-start | bytes 2949120 | tf_op jit(solution)/shard_map/all_to_all | solution.py:546
  146.7 3.8 %norms.1 = f32[1,2,512]{2,1,0:T(2,128)} custom-call(s32[5]{0:T(128)} %stack.32.place, f32[384,1536]{1,0:T(8,128)} %get-tuple-element.49.first_a.refs_0_.refs_4_, f32[384,1536]{1,0:T(8,128)} %copy-done.2, f32[128,1536]{1,0:T(8,128)} %get-tuple-element.52.last_a.refs_2_.refs_6_, f32[128,1536]{1,0:T(8,128)} %copy-done.8), custom_call_target="tpu_custom_call" | custom-call | flops 786432 | bytes 1572864 | tf_op jit(solution)/shard_map/norms/pallas_call | solution.py:271
  150.4 6.0 %collective-permute-start.22 = (f32[1,2,512]{2,1,0:T(2,128)}, f32[1,2,512]{2,1,0:T(2,128)S(1)}, u32[]{:S(2)}, u32[]{:S(2)}) collective-permute-start(f32[1,2,512]{2,1,0:T(2,128)} %norms.1), channel_id=1, source_target_pairs={{0,6},{2,0},{4,2},{6,4},{1,7},{3,1},{5,3},{7,5},{8,14},{10,8},{12,... | collective-permute-start | bytes 12296 | tf_op jit(solution)/shard_map/ppermute | solution.py:570
  167.7 7.1 %probs.1 = bf16[6,512,512]{2,1,0:T(8,128)(2,1)} custom-call(s32[5]{0:T(128)} %stack.32.place, f32[4,2,512]{2,1,0:T(2,128)} %pad_maximum_fusion.1.squares, f32[384,1536]{1,0:T(8,128)} %get-tuple-element.49.first_a.refs_0_.refs_4_, f32[384,1536]{1,0:T(8,128)} %copy-done.2, f32[128,1536]{1,0:T(8,128)} %get-tuple-element.52.last_a.refs_2_.refs_6_, ...), custom_call_target="tpu_custom_call" | custom-call | flops 100663296 | bytes 2359296 | tf_op jit(solution)/shard_map/probs/pallas_call | solution.py:325
  174.9 5.0 %attend.1 = bf16[4,128,768]{2,1,0:T(8,128)(2,1)} custom-call(s32[5]{0:T(128)} %stack.32.place, bf16[6,512,512]{2,1,0:T(8,128)(2,1)} %probs.1, f32[512,768]{1,0:T(8,128)} %get-tuple-element.56.v_a, f32[512,768]{1,0:T(8,128)} %collective-permute-done.25.v_b), custom_call_target="tpu_custom_call" | custom-call | flops 100663296 | bytes 1769472 | tf_op jit(solution)/shard_map/attend/pallas_call | solution.py:354
  179.9 8.1 %collective-permute-done.27.refs_10_ = bf16[768,640]{1,0:T(8,128)(2,1)S(1)} collective-permute-done((bf16[768,640]{1,0:T(8,128)(2,1)}, bf16[768,640]{1,0:T(8,128)(2,1)S(1)}, u32[]{:S(2)}, u32[]{:S(2)}) %collective-permute-start.27) | collective-permute-done | bytes 983072 | tf_op jit(solution)/shard_map/ppermute | solution.py:558
  195.7 13.8 %all-to-all-done.1.refs_0_ = bf16[4,128,768]{2,1,0:T(8,128)(2,1)S(1)} async-done(((bf16[4,128,768]{2,1,0:T(8,128)(2,1)}), bf16[4,128,768]{2,1,0:T(8,128)(2,1)S(1)}, u32[]{:S(2)}, u32[]{:S(2)}) %all-to-all-start.1) | async-done | bytes 786464 | tf_op jit(solution)/shard_map/all_to_all | solution.py:576
  214.4 15.3 %collective-permute-done.31.refs_2_ = bf16[4,128,768]{2,1,0:T(8,128)(2,1)S(1)} collective-permute-done((bf16[4,128,768]{2,1,0:T(8,128)(2,1)S(1)}, bf16[4,128,768]{2,1,0:T(8,128)(2,1)S(1)}, u32[]{:S(2)}, u32[]{:S(2)}) %collective-permute-start.31) | collective-permute-done | bytes 786464 | tf_op jit(solution)/shard_map/ppermute | solution.py:19
  230.6 3.9 %collective-permute-done.35.refs_11_ = bf16[768,640]{1,0:T(8,128)(2,1)S(1)} collective-permute-done((bf16[768,640]{1,0:T(8,128)(2,1)S(1)}, bf16[768,640]{1,0:T(8,128)(2,1)S(1)}, u32[]{:S(2)}, u32[]{:S(2)}) %collective-permute-start.35) | collective-permute-done | bytes 983072 | tf_op jit(solution)/shard_map/ppermute | solution.py:558
  237.8 8.3 %collective-permute-done.32.refs_3_ = bf16[2,128,768]{2,1,0:T(8,128)(2,1)S(1)} collective-permute-done((bf16[2,128,768]{2,1,0:T(8,128)(2,1)S(1)}, bf16[2,128,768]{2,1,0:T(8,128)(2,1)S(1)}, u32[]{:S(2)}, u32[]{:S(2)}) %collective-permute-start.32) | collective-permute-done | bytes 393248 | tf_op jit(solution)/shard_map/ppermute | solution.py:19
  248.2 13.0 %project_out.1 = bf16[4,2,128,1280]{3,2,1,0:T(8,128)(2,1)} custom-call(s32[5]{0:T(128)} %stack.32.place, bf16[4,128,768]{2,1,0:T(8,128)(2,1)} %copy-done.13, bf16[4,128,768]{2,1,0:T(8,128)(2,1)} %copy-done.16, bf16[4,128,768]{2,1,0:T(8,128)(2,1)} %copy-done.15, bf16[2,128,768]{2,1,0:T(8,128)(2,1)} %copy-done.28, bf16[2,128,768]{2,1,0:T(8,128)(2,1)} %copy-done.29, ...), custom_call_target="tpu_custom_call" | custom-call | flops 1006632960 | bytes 3407872 | tf_op jit(solution)/shard_map/project_out/pallas_call | solution.py:456
  261.2 4.9 %all-to-all-start.2 = ((bf16[4,2,128,1280]{3,2,1,0:T(8,128)(2,1)}), bf16[4,2,128,1280]{3,2,1,0:T(8,128)(2,1)}, u32[]{:S(2)}, u32[]{:S(2)}) async-start(bf16[4,2,128,1280]{3,2,1,0:T(8,128)(2,1)} %project_out.1), calls=%async_computation.2 | async-start | bytes 5242880 | tf_op jit(solution)/shard_map/all_to_all | solution.py:584
  267.9 27.9 %all-to-all-done.2.refs_0_ = bf16[4,2,128,1280]{3,2,1,0:T(8,128)(2,1)} async-done(((bf16[4,2,128,1280]{3,2,1,0:T(8,128)(2,1)}), bf16[4,2,128,1280]{3,2,1,0:T(8,128)(2,1)}, u32[]{:S(2)}, u32[]{:S(2)}) %all-to-all-start.2) | async-done | bytes 2621472 | tf_op jit(solution)/shard_map/all_to_all | solution.py:584
  295.9 4.8 %finish.1 = (f32[128,5120]{1,0:T(8,128)}, bf16[128,5120]{1,0:T(8,128)(2,1)}) custom-call(f32[128,5120]{1,0:T(8,128)} %select_add_fusion.base, bf16[4,2,128,1280]{3,2,1,0:T(8,128)(2,1)} %all-to-all-done.2.refs_0_), custom_call_target="tpu_custom_call" | custom-call | flops 163840 | bytes 2293760 | tf_op jit(solution)/shard_map/finish/pallas_call | solution.py:486
  (150 shorter events, 68.2 us)
Async XLA Ops:
  8.7 46.1 %collective-permute-start.6 = (bf16[640,1536]{1,0:T(8,128)(2,1)S(1)}, bf16[640,1536]{1,0:T(8,128)(2,1)S(1)}, u32[]{:S(2)}, u32[]{:S(2)}) collective-permute-start(bf16[640,1536]{1,0:T(8,128)(2,1)S(1)} %constant_dynamic-update-slice_fusion.refs_7_), channel_id=1, source_target_pairs={{0,16},{8,24},{16,0},{24,8},{1,17},{9,25},{17,1},{25,9},{2,18},{10... | collective-permute-start | bytes 5898248 | tf_op jit(solution)/shard_map/ppermute | solution.py:19
  11.3 44.9 %collective-permute-start.5 = (bf16[640,1536]{1,0:T(8,128)(2,1)S(1)}, bf16[640,1536]{1,0:T(8,128)(2,1)S(1)}, u32[]{:S(2)}, u32[]{:S(2)}) collective-permute-start(bf16[640,1536]{1,0:T(8,128)(2,1)S(1)} %constant_dynamic-update-slice_fusion.refs_7_), channel_id=1, source_target_pairs={{0,8},{8,0},{16,24},{24,16},{1,9},{9,1},{17,25},{25,17},{2,10},{10... | collective-permute-start | bytes 5898248 | tf_op jit(solution)/shard_map/ppermute | solution.py:19
  13.0 32.6 %collective-permute-start.3 = (bf16[2,128,2560]{2,1,0:T(8,128)(2,1)S(1)}, bf16[2,128,2560]{2,1,0:T(8,128)(2,1)S(1)}, u32[]{:S(2)}, u32[]{:S(2)}) collective-permute-start(bf16[2,128,2560]{2,1,0:T(8,128)(2,1)S(1)} %pad_maximum_fusion.refs_0_.refs_3_.refs_6_), channel_id=1, source_target_pairs={{2,0},{4,2},{6,4},{3,1},{5,3},{7,5},{10,8},{12,10},{14,12},{11,9},... | collective-permute-start | bytes 3932168 | tf_op jit(solution)/shard_map/ppermute | solution.py:515
  14.4 32.5 %collective-permute-start.1 = (bf16[2,128,2560]{2,1,0:T(8,128)(2,1)S(1)}, bf16[2,128,2560]{2,1,0:T(8,128)(2,1)S(1)}, u32[]{:S(2)}, u32[]{:S(2)}) collective-permute-start(bf16[2,128,2560]{2,1,0:T(8,128)(2,1)S(1)} %pad_maximum_fusion.refs_0_.refs_3_.refs_6_), channel_id=1, source_target_pairs={{0,2},{2,4},{4,6},{1,3},{3,5},{5,7},{8,10},{10,12},{12,14},{9,11},... | collective-permute-start | bytes 3932168 | tf_op jit(solution)/shard_map/ppermute | solution.py:514
  45.6 34.4 %collective-permute-start.4 = (bf16[2,128,2560]{2,1,0:T(8,128)(2,1)S(1)}, bf16[2,128,2560]{2,1,0:T(8,128)(2,1)}, u32[]{:S(2)}, u32[]{:S(2)}) collective-permute-start(bf16[2,128,2560]{2,1,0:T(8,128)(2,1)S(1)} %collective-permute-done.3.refs_4_), channel_id=1, source_target_pairs={{2,0},{4,2},{3,1},{5,3},{10,8},{12,10},{11,9},{13,11},{18,16},{20,... | collective-permute-start | bytes 3932168 | tf_op jit(solution)/shard_map/ppermute | solution.py:515
  46.9 33.1 %collective-permute-start.2 = (bf16[2,128,2560]{2,1,0:T(8,128)(2,1)S(1)}, bf16[2,128,2560]{2,1,0:T(8,128)(2,1)}, u32[]{:S(2)}, u32[]{:S(2)}) collective-permute-start(bf16[2,128,2560]{2,1,0:T(8,128)(2,1)S(1)} %collective-permute-done.1.refs_1_), channel_id=1, source_target_pairs={{2,4},{4,6},{3,5},{5,7},{10,12},{12,14},{11,13},{13,15},{18,20},{2... | collective-permute-start | bytes 3932168 | tf_op jit(solution)/shard_map/ppermute | solution.py:514
  56.4 23.2 %collective-permute-start.8 = (bf16[640,768]{1,0:T(8,128)(2,1)S(1)}, bf16[640,768]{1,0:T(8,128)(2,1)S(1)}, u32[]{:S(2)}, u32[]{:S(2)}) collective-permute-start(bf16[640,768]{1,0:T(8,128)(2,1)S(1)} %slice.27), channel_id=1, source_target_pairs={{0,16},{8,24},{16,0},{24,8},{1,17},{9,25},{17,1},{25,9},{2,18},{10... | collective-permute-start | bytes 2949128 | tf_op jit(solution)/shard_map/ppermute | solution.py:19
  56.9 23.2 %collective-permute-start.7 = (bf16[640,768]{1,0:T(8,128)(2,1)S(1)}, bf16[640,768]{1,0:T(8,128)(2,1)S(1)}, u32[]{:S(2)}, u32[]{:S(2)}) collective-permute-start(bf16[640,768]{1,0:T(8,128)(2,1)S(1)} %slice.26), channel_id=1, source_target_pairs={{0,8},{8,0},{16,24},{24,16},{1,9},{9,1},{17,25},{25,17},{2,10},{10... | collective-permute-start | bytes 2949128 | tf_op jit(solution)/shard_map/ppermute | solution.py:19
  80.1 27.8 %collective-permute-start.9 = (bf16[2,128,2560]{2,1,0:T(8,128)(2,1)}, bf16[2,128,2560]{2,1,0:T(8,128)(2,1)S(1)}, u32[]{:S(2)}, u32[]{:S(2)}) collective-permute-start(bf16[2,128,2560]{2,1,0:T(8,128)(2,1)} %collective-permute-done.2.refs_2_), channel_id=1, source_target_pairs={{4,6},{5,7},{12,14},{13,15},{20,22},{21,23},{28,30},{29,31}} | collective-permute-start | bytes 3932168 | tf_op jit(solution)/shard_map/ppermute | solution.py:514
  80.8 31.4 %collective-permute-start.10 = (bf16[2,128,2560]{2,1,0:T(8,128)(2,1)}, bf16[2,128,2560]{2,1,0:T(8,128)(2,1)S(1)}, u32[]{:S(2)}, u32[]{:S(2)}) collective-permute-start(bf16[2,128,2560]{2,1,0:T(8,128)(2,1)} %collective-permute-done.4.refs_5_), channel_id=1, source_target_pairs={{2,0},{3,1},{10,8},{11,9},{18,16},{19,17},{26,24},{27,25}} | collective-permute-start | bytes 3932168 | tf_op jit(solution)/shard_map/ppermute | solution.py:515
  82.2 24.4 %collective-permute-start.11 = (bf16[640,768]{1,0:T(8,128)(2,1)}, bf16[640,768]{1,0:T(8,128)(2,1)S(1)}, u32[]{:S(2)}, u32[]{:S(2)}) collective-permute-start(bf16[640,768]{1,0:T(8,128)(2,1)} %refs_7_.1), channel_id=1, source_target_pairs={{0,8},{8,0},{16,24},{24,16},{1,9},{9,1},{17,25},{25,17},{2,10},{10... | collective-permute-start | bytes 2949128 | tf_op jit(solution)/shard_map/ppermute | solution.py:19
  83.7 24.1 %collective-permute-start.12 = (bf16[640,768]{1,0:T(8,128)(2,1)}, bf16[640,768]{1,0:T(8,128)(2,1)}, u32[]{:S(2)}, u32[]{:S(2)}) collective-permute-start(bf16[640,768]{1,0:T(8,128)(2,1)} %refs_7_.1), channel_id=1, source_target_pairs={{0,16},{8,24},{16,0},{24,8},{1,17},{9,25},{17,1},{25,9},{2,18},{10... | collective-permute-start | bytes 2949128 | tf_op jit(solution)/shard_map/ppermute | solution.py:19
  112.2 32.1 %collective-permute-start.18 = (f32[384,1536]{1,0:T(8,128)}, f32[384,1536]{1,0:T(8,128)S(1)}, u32[]{:S(2)}, u32[]{:S(2)}) collective-permute-start(f32[384,1536]{1,0:T(8,128)} %get-tuple-element.59), channel_id=1, source_target_pairs={{0,1},{1,0},{2,3},{3,2},{4,5},{5,4},{6,7},{7,6},{8,9},{9,8},{10,11... | collective-permute-start | bytes 7077896 | tf_op jit(solution)/shard_map/ppermute | solution.py:19
  116.3 27.4 %collective-permute-start.14 = (bf16[768,640]{1,0:T(8,128)(2,1)}, bf16[768,640]{1,0:T(8,128)(2,1)}, u32[]{:S(2)}, u32[]{:S(2)}) collective-permute-start(bf16[768,640]{1,0:T(8,128)(2,1)} %refs_5_.1), channel_id=1, source_target_pairs={{0,2},{2,4},{4,6},{1,3},{3,5},{5,7},{8,10},{10,12},{12,14},{9,11},... | collective-permute-start | bytes 2949128 | tf_op jit(solution)/shard_map/ppermute | solution.py:557
  118.8 25.4 %collective-permute-start.15 = (bf16[768,640]{1,0:T(8,128)(2,1)}, bf16[768,640]{1,0:T(8,128)(2,1)}, u32[]{:S(2)}, u32[]{:S(2)}) collective-permute-start(bf16[768,640]{1,0:T(8,128)(2,1)} %refs_5_.1), channel_id=1, source_target_pairs={{2,0},{4,2},{6,4},{3,1},{5,3},{7,5},{10,8},{12,10},{14,12},{11,9},... | collective-permute-start | bytes 2949128 | tf_op jit(solution)/shard_map/ppermute | solution.py:558
  139.2 35.6 %collective-permute-start.25 = (f32[512,768]{1,0:T(8,128)}, f32[512,768]{1,0:T(8,128)}, u32[]{:S(2)}, u32[]{:S(2)}) collective-permute-start(f32[512,768]{1,0:T(8,128)} %get-tuple-element.64), channel_id=1, source_target_pairs={{0,1},{1,0},{2,3},{3,2},{4,5},{5,4},{6,7},{7,6},{8,9},{9,8},{10,11... | collective-permute-start | bytes 4718600 | tf_op jit(solution)/shard_map/ppermute | solution.py:19
  139.3 28.4 %all-to-all-start = ((bf16[4,144,1280]{2,1,0:T(8,128)(2,1)}), bf16[4,144,1280]{2,1,0:T(8,128)(2,1)}, u32[]{:S(2)}, u32[]{:S(2)}) async-start(bf16[4,144,1280]{2,1,0:T(8,128)(2,1)} %tell.1), calls=%async_computation | async-start | bytes 2949120 | tf_op jit(solution)/shard_map/all_to_all | solution.py:546
  143.7 24.1 %collective-permute-start.23 = (bf16[768,640]{1,0:T(8,128)(2,1)}, bf16[768,640]{1,0:T(8,128)(2,1)}, u32[]{:S(2)}, u32[]{:S(2)}) collective-permute-start(bf16[768,640]{1,0:T(8,128)(2,1)} %collective-permute-done.14.refs_6_), channel_id=1, source_target_pairs={{0,1},{1,0},{2,3},{3,2},{4,5},{5,4},{6,7},{7,6},{8,9},{9,8},{10,11... | collective-permute-start | bytes 2949128 | tf_op jit(solution)/shard_map/ppermute | solution.py:19
  144.2 23.5 %collective-permute-start.24 = (bf16[768,640]{1,0:T(8,128)(2,1)}, bf16[768,640]{1,0:T(8,128)(2,1)}, u32[]{:S(2)}, u32[]{:S(2)}) collective-permute-start(bf16[768,640]{1,0:T(8,128)(2,1)} %collective-permute-done.15.refs_9_), channel_id=1, source_target_pairs={{0,1},{1,0},{2,3},{3,2},{4,5},{5,4},{6,7},{7,6},{8,9},{9,8},{10,11... | collective-permute-start | bytes 2949128 | tf_op jit(solution)/shard_map/ppermute | solution.py:19
  163.8 24.2 %collective-permute-start.27 = (bf16[768,640]{1,0:T(8,128)(2,1)}, bf16[768,640]{1,0:T(8,128)(2,1)S(1)}, u32[]{:S(2)}, u32[]{:S(2)}) collective-permute-start(bf16[768,640]{1,0:T(8,128)(2,1)} %collective-permute-done.15.refs_9_), channel_id=1, source_target_pairs={{2,0},{4,2},{3,1},{5,3},{10,8},{12,10},{11,9},{13,11},{18,16},{20,... | collective-permute-start | bytes 2949128 | tf_op jit(solution)/shard_map/ppermute | solution.py:558
  188.0 21.5 %all-to-all-start.1 = ((bf16[4,128,768]{2,1,0:T(8,128)(2,1)}), bf16[4,128,768]{2,1,0:T(8,128)(2,1)S(1)}, u32[]{:S(2)}, u32[]{:S(2)}) async-start(bf16[4,128,768]{2,1,0:T(8,128)(2,1)} %attend.1), calls=%async_computation.1 | async-start | bytes 1572864 | tf_op jit(solution)/shard_map/all_to_all | solution.py:576
  209.5 21.1 %collective-permute-start.34 = (bf16[768,640]{1,0:T(8,128)(2,1)S(1)}, bf16[768,640]{1,0:T(8,128)(2,1)S(1)}, u32[]{:S(2)}, u32[]{:S(2)}) collective-permute-start(bf16[768,640]{1,0:T(8,128)(2,1)S(1)} %collective-permute-done.26.refs_7_), channel_id=1, source_target_pairs={{4,6},{5,7},{12,14},{13,15},{20,22},{21,23},{28,30},{29,31}} | collective-permute-start | bytes 2949128 | tf_op jit(solution)/shard_map/ppermute | solution.py:557
  210.2 24.2 %collective-permute-start.35 = (bf16[768,640]{1,0:T(8,128)(2,1)S(1)}, bf16[768,640]{1,0:T(8,128)(2,1)S(1)}, u32[]{:S(2)}, u32[]{:S(2)}) collective-permute-start(bf16[768,640]{1,0:T(8,128)(2,1)S(1)} %collective-permute-done.27.refs_10_), channel_id=1, source_target_pairs={{2,0},{3,1},{10,8},{11,9},{18,16},{19,17},{26,24},{27,25}} | collective-permute-start | bytes 2949128 | tf_op jit(solution)/shard_map/ppermute | solution.py:558
  261.2 34.7 %all-to-all-start.2 = ((bf16[4,2,128,1280]{3,2,1,0:T(8,128)(2,1)}), bf16[4,2,128,1280]{3,2,1,0:T(8,128)(2,1)}, u32[]{:S(2)}, u32[]{:S(2)}) async-start(bf16[4,2,128,1280]{3,2,1,0:T(8,128)(2,1)} %project_out.1), calls=%async_computation.2 | async-start | bytes 5242880 | tf_op jit(solution)/shard_map/all_to_all | solution.py:584
  (50 other events, 885.1 us)

commit v14 on v13

--- a/solution.py
+++ b/solution.py
@@ -543,7 +543,6 @@
     parts += [last_here, swap(after(last_there, *v_last), "fsdp", 1)]
     v_here, v_there = project(after(place, last_here), line, v_shards, "all", "value")
     v_parts = [v_here, swap(v_there, "fsdp", 1)]
-    heard = lax.all_to_all(after(told, last_here, *v_last), "step", 0, 0)
 
     below, above = [w_out], [w_out]
     for count in range(1, size):
@@ -565,14 +564,15 @@
         partner_above.append(swap(arrived[1], "fsdp", 1))
         if count == 1:
             own_squares = norms(after(place, below[-1], above[-1], v_here), parts, 1)
+            heard = lax.all_to_all(after(told, own_squares), "step", 0, 0)
             squares = [own_squares]
             for away in range(1, size):
                 squares.append(lax.ppermute(own_squares, "head", [(i, (i + away) % size) for i in range(size)]))
             squares = jnp.concatenate(squares)
         if count == size - 2:
-            ready = after(squares, *partner_below[:-1], *partner_above[:-1], heard)
+            ready = after(squares, *partner_below[:-1], *partner_above[:-1])
             probs = probabilities(place, ready, parts, q_gain, k_gain)
-            attended = after(attend(place, probs, v_parts, size), below[-1], above[-1])
+            attended = after(attend(place, probs, v_parts, size), below[-1], above[-1], heard)
             quarter = after(lax.all_to_all(attended, "head", 0, 0), partner_below[-1], partner_above[-1])
 
     raw = [w_out] + below[1:] + above[1:]

time: 302 us -> 304 us (level)
  local copies, waits for them, and re-layouts: 11 us -> 14.2 us
    unnamed x68 -> x76, local copies, waits for them, and re-layouts: 6.9 us -> 8.4 us
  transfers between devices with their start and end apart: 41 -> 41, of which waited for: 20 -> 24; matrix products, arithmetic and copies ran while one was open for 2% -> 3% of each run, Pallas kernels for 17% -> 17%
where the time goes in v14:
time: 304 us; the launch traced here: 303 us
  waiting for transfers between devices  153 us (50%)
  Pallas kernels  73.8 us (24%)
  starting transfers between devices  56.6 us (19%)
  local copies, waits for them, and re-layouts  14.2 us (5%)
  between operations  3.15 us (1%)
    ppermute x23, waiting for transfers between devices, swap(): lax.ppermute(x, axis, [(i, i ^ offset) for i in range(lax.axis_size(axis))])  61.6 us
    pallas_call x3, Pallas kernels, project(): pl.pallas_call(functools.partial(project_kernel, size, parts, shard, tupl...  31.6 us
    ppermute x3, waiting for transfers between devices, hop(): lax.ppermute(down, 'head', [(i, i - 1) for i in range(1, size - count + 1)])  31 us
    all_to_all x1, waiting for transfers between devices, body(): lax.all_to_all(part, 'step', 0, 0)  28 us
    ppermute x23, starting transfers between devices, swap(): lax.ppermute(x, axis, [(i, i ^ offset) for i in range(lax.axis_size(axis))])  20.9 us
    ppermute x3, waiting for transfers between devices, body(): lax.ppermute(down, 'head', [(i, i - 1) for i in range(1, size - count + 1)])  14.9 us
    all_to_all x1, waiting for transfers between devices, body(): lax.all_to_all(attended, 'head', 0, 0)  13.4 us
    pallas_call x1, Pallas kernels, project_out(): pl.pallas_call(functools.partial(out_kernel, size, tuple(layout), part *...  13 us
  transfers between devices with their start and end apart: 41, of which 24 were waited for; matrix products, arithmetic and copies ran while one was open for 3% of the time, Pallas kernels for 17%

profile of v14, /device:TPU:0, one launch (start us, length us, event | category | flops | bytes accessed | tf_op | source)
XLA Modules:
  0.0 303.1 jit_solution(13286384160403424101)
XLA Ops:
  3.5 4.6 %modulate.1 = (bf16[128,2560]{1,0:T(8,128)(2,1)}, bf16[128,2560]{1,0:T(8,128)(2,1)}) custom-call(s32[5]{0:T(128)} %stack.32.place, f32[128,5120]{1,0:T(8,128)} %bitcast.12, f32[1,3,5120]{2,1,0:T(4,128)} %copy.12.rows), custom_call_target="tpu_custom_call" | custom-call | flops 1638400 | bytes 983040 | tf_op jit(solution)/shard_map/modulate/pallas_call | solution.py:119
  14.5 4.6 %collective-permute-start.1 = (bf16[2,128,2560]{2,1,0:T(8,128)(2,1)S(1)}, bf16[2,128,2560]{2,1,0:T(8,128)(2,1)S(1)}, u32[]{:S(2)}, u32[]{:S(2)}) collective-permute-start(bf16[2,128,2560]{2,1,0:T(8,128)(2,1)S(1)} %pad_maximum_fusion.refs_0_.refs_3_.refs_6_), channel_id=1, source_target_pairs={{0,2},{2,4},{4,6},{1,3},{3,5},{5,7},{8,10},{10,12},{12,14},{9,11},... | collective-permute-start | bytes 3932168 | tf_op jit(solution)/shard_map/ppermute | solution.py:514
  19.1 26.6 %collective-permute-done.3.refs_4_ = bf16[2,128,2560]{2,1,0:T(8,128)(2,1)S(1)} collective-permute-done((bf16[2,128,2560]{2,1,0:T(8,128)(2,1)S(1)}, bf16[2,128,2560]{2,1,0:T(8,128)(2,1)S(1)}, u32[]{:S(2)}, u32[]{:S(2)}) %collective-permute-start.3) | collective-permute-done | bytes 1310752 | tf_op jit(solution)/shard_map/ppermute | solution.py:515
  48.7 6.1 %collective-permute-done.6.refs_9_ = bf16[640,1536]{1,0:T(8,128)(2,1)S(1)} collective-permute-done((bf16[640,1536]{1,0:T(8,128)(2,1)S(1)}, bf16[640,1536]{1,0:T(8,128)(2,1)S(1)}, u32[]{:S(2)}, u32[]{:S(2)}) %collective-permute-start.6) | collective-permute-done | bytes 1966112 | tf_op jit(solution)/shard_map/ppermute | solution.py:19
  58.5 21.2 %collective-permute-done.8.refs_11_ = bf16[640,768]{1,0:T(8,128)(2,1)S(1)} collective-permute-done((bf16[640,768]{1,0:T(8,128)(2,1)S(1)}, bf16[640,768]{1,0:T(8,128)(2,1)S(1)}, u32[]{:S(2)}, u32[]{:S(2)}) %collective-permute-start.8) | collective-permute-done | bytes 983072 | tf_op jit(solution)/shard_map/ppermute | solution.py:19
  87.1 4.0 %tell.1 = bf16[4,144,1280]{2,1,0:T(8,128)(2,1)} custom-call(s32[5]{0:T(128)} %stack.32.place, f32[1]{0:T(128)} %bitcast.8.step_width, f32[128,5120]{1,0:T(8,128)} %bitcast.13, f32[1,3,5120]{2,1,0:T(4,128)} %copy.12.rows), custom_call_target="tpu_custom_call" | custom-call | flops 655360 | bytes 983040 | tf_op jit(solution)/shard_map/tell/pallas_call | solution.py:151
  91.1 13.6 %first.1 = (f32[384,1536]{1,0:T(8,128)}, f32[384,1536]{1,0:T(8,128)}) custom-call(s32[5]{0:T(128)} %stack.32.place, bf16[2,128,2560]{2,1,0:T(8,128)(2,1)} %copy-done, bf16[2,128,2560]{2,1,0:T(8,128)(2,1)} %copy-done.7, bf16[2,128,2560]{2,1,0:T(8,128)(2,1)} %collective-permute-done.2.refs_2_, bf16[2,128,2560]{2,1,0:T(8,128)(2,1)} %copy-done, ...), custom_call_target="tpu_custom_call" | custom-call | flops 1509949440 | bytes 4128768 | tf_op jit(solution)/shard_map/first/pallas_call | solution.py:233
  107.9 4.4 %collective-permute-done.10.refs_6_ = bf16[2,128,2560]{2,1,0:T(8,128)(2,1)S(1)} collective-permute-done((bf16[2,128,2560]{2,1,0:T(8,128)(2,1)}, bf16[2,128,2560]{2,1,0:T(8,128)(2,1)S(1)}, u32[]{:S(2)}, u32[]{:S(2)}) %collective-permute-start.10) | collective-permute-done | bytes 1310752 | tf_op jit(solution)/shard_map/ppermute | solution.py:515
  120.8 7.8 %last.1 = (f32[128,1536]{1,0:T(8,128)}, f32[128,1536]{1,0:T(8,128)}) custom-call(s32[5]{0:T(128)} %stack.32.place, bf16[2,128,2560]{2,1,0:T(8,128)(2,1)} %copy-done, bf16[2,128,2560]{2,1,0:T(8,128)(2,1)} %copy-done.7, bf16[2,128,2560]{2,1,0:T(8,128)(2,1)} %collective-permute-done.2.refs_2_, bf16[2,128,2560]{2,1,0:T(8,128)(2,1)} %copy-done.10, ...), custom_call_target="tpu_custom_call" | custom-call | flops 503316480 | bytes 2686976 | tf_op jit(solution)/shard_map/last/pallas_call | solution.py:233
  130.5 10.3 %value.1 = (f32[512,768]{1,0:T(8,128)}, f32[512,768]{1,0:T(8,128)}) custom-call(s32[5]{0:T(128)} %stack.32.place, bf16[2,128,2560]{2,1,0:T(8,128)(2,1)} %copy-done, bf16[2,128,2560]{2,1,0:T(8,128)(2,1)} %copy-done.7, bf16[2,128,2560]{2,1,0:T(8,128)(2,1)} %collective-permute-done.2.refs_2_, bf16[2,128,2560]{2,1,0:T(8,128)(2,1)} %copy-done.10, ...), custom_call_target="tpu_custom_call" | custom-call | flops 1006632960 | bytes 3080192 | tf_op jit(solution)/shard_map/value/pallas_call | solution.py:233
  141.3 3.6 %collective-permute-done.15.refs_9_ = bf16[768,640]{1,0:T(8,128)(2,1)} collective-permute-done((bf16[768,640]{1,0:T(8,128)(2,1)}, bf16[768,640]{1,0:T(8,128)(2,1)}, u32[]{:S(2)}, u32[]{:S(2)}) %collective-permute-start.15) | collective-permute-done | bytes 983072 | tf_op jit(solution)/shard_map/ppermute | solution.py:557
  147.2 3.8 %norms.1 = f32[1,2,512]{2,1,0:T(2,128)} custom-call(s32[5]{0:T(128)} %stack.32.place, f32[384,1536]{1,0:T(8,128)} %get-tuple-element.49.first_a.refs_0_.refs_4_, f32[384,1536]{1,0:T(8,128)} %copy-done.2, f32[128,1536]{1,0:T(8,128)} %get-tuple-element.52.last_a.refs_2_.refs_6_, f32[128,1536]{1,0:T(8,128)} %copy-done.8), custom_call_target="tpu_custom_call" | custom-call | flops 786432 | bytes 1572864 | tf_op jit(solution)/shard_map/norms/pallas_call | solution.py:271
  151.0 3.7 %all-to-all-start = ((bf16[4,144,1280]{2,1,0:T(8,128)(2,1)}), bf16[4,144,1280]{2,1,0:T(8,128)(2,1)S(1)}, u32[]{:S(2)}, u32[]{:S(2)}) async-start(bf16[4,144,1280]{2,1,0:T(8,128)(2,1)} %tell.1), calls=%async_computation | async-start | bytes 2949120 | tf_op jit(solution)/shard_map/all_to_all | solution.py:567
  169.7 7.0 %probs.1 = bf16[6,512,512]{2,1,0:T(8,128)(2,1)} custom-call(s32[5]{0:T(128)} %stack.32.place, f32[4,2,512]{2,1,0:T(2,128)} %pad_maximum_fusion.1.squares, f32[384,1536]{1,0:T(8,128)} %get-tuple-element.49.first_a.refs_0_.refs_4_, f32[384,1536]{1,0:T(8,128)} %copy-done.2, f32[128,1536]{1,0:T(8,128)} %get-tuple-element.52.last_a.refs_2_.refs_6_, ...), custom_call_target="tpu_custom_call" | custom-call | flops 100663296 | bytes 2359296 | tf_op jit(solution)/shard_map/probs/pallas_call | solution.py:325
  176.8 5.0 %attend.1 = bf16[4,128,768]{2,1,0:T(8,128)(2,1)} custom-call(s32[5]{0:T(128)} %stack.32.place, bf16[6,512,512]{2,1,0:T(8,128)(2,1)} %probs.1, f32[512,768]{1,0:T(8,128)} %get-tuple-element.56.v_a, f32[512,768]{1,0:T(8,128)} %collective-permute-done.25.v_b), custom_call_target="tpu_custom_call" | custom-call | flops 100663296 | bytes 1769472 | tf_op jit(solution)/shard_map/attend/pallas_call | solution.py:354
  181.8 7.7 %collective-permute-done.27.refs_10_ = bf16[768,640]{1,0:T(8,128)(2,1)} collective-permute-done((bf16[768,640]{1,0:T(8,128)(2,1)}, bf16[768,640]{1,0:T(8,128)(2,1)}, u32[]{:S(2)}, u32[]{:S(2)}) %collective-permute-start.27) | collective-permute-done | bytes 983072 | tf_op jit(solution)/shard_map/ppermute | solution.py:557
  197.4 13.4 %all-to-all-done.1.refs_0_ = bf16[4,128,768]{2,1,0:T(8,128)(2,1)S(1)} async-done(((bf16[4,128,768]{2,1,0:T(8,128)(2,1)}), bf16[4,128,768]{2,1,0:T(8,128)(2,1)S(1)}, u32[]{:S(2)}, u32[]{:S(2)}) %all-to-all-start.1) | async-done | bytes 786464 | tf_op jit(solution)/shard_map/all_to_all | solution.py:576
  216.1 14.6 %collective-permute-done.31.refs_2_ = bf16[4,128,768]{2,1,0:T(8,128)(2,1)S(1)} collective-permute-done((bf16[4,128,768]{2,1,0:T(8,128)(2,1)S(1)}, bf16[4,128,768]{2,1,0:T(8,128)(2,1)S(1)}, u32[]{:S(2)}, u32[]{:S(2)}) %collective-permute-start.31) | collective-permute-done | bytes 786464 | tf_op jit(solution)/shard_map/ppermute | solution.py:19
  232.1 3.5 %collective-permute-done.35.refs_11_ = bf16[768,640]{1,0:T(8,128)(2,1)S(1)} collective-permute-done((bf16[768,640]{1,0:T(8,128)(2,1)}, bf16[768,640]{1,0:T(8,128)(2,1)S(1)}, u32[]{:S(2)}, u32[]{:S(2)}) %collective-permute-start.35) | collective-permute-done | bytes 983072 | tf_op jit(solution)/shard_map/ppermute | solution.py:557
  239.5 7.8 %collective-permute-done.32.refs_3_ = bf16[2,128,768]{2,1,0:T(8,128)(2,1)S(1)} collective-permute-done((bf16[2,128,768]{2,1,0:T(8,128)(2,1)S(1)}, bf16[2,128,768]{2,1,0:T(8,128)(2,1)S(1)}, u32[]{:S(2)}, u32[]{:S(2)}) %collective-permute-start.32) | collective-permute-done | bytes 393248 | tf_op jit(solution)/shard_map/ppermute | solution.py:19
  250.5 13.0 %project_out.1 = bf16[4,2,128,1280]{3,2,1,0:T(8,128)(2,1)} custom-call(s32[5]{0:T(128)} %stack.32.place, bf16[4,128,768]{2,1,0:T(8,128)(2,1)} %copy-done.14, bf16[4,128,768]{2,1,0:T(8,128)(2,1)} %copy-done.17, bf16[4,128,768]{2,1,0:T(8,128)(2,1)} %copy-done.16, bf16[2,128,768]{2,1,0:T(8,128)(2,1)} %copy-done.31, bf16[2,128,768]{2,1,0:T(8,128)(2,1)} %copy-done.32, ...), custom_call_target="tpu_custom_call" | custom-call | flops 1006632960 | bytes 3407872 | tf_op jit(solution)/shard_map/project_out/pallas_call | solution.py:456
  263.6 4.8 %all-to-all-start.2 = ((bf16[4,2,128,1280]{3,2,1,0:T(8,128)(2,1)}), bf16[4,2,128,1280]{3,2,1,0:T(8,128)(2,1)}, u32[]{:S(2)}, u32[]{:S(2)}) async-start(bf16[4,2,128,1280]{3,2,1,0:T(8,128)(2,1)} %project_out.1), calls=%async_computation.2 | async-start | bytes 5242880 | tf_op jit(solution)/shard_map/all_to_all | solution.py:584
  270.3 28.0 %all-to-all-done.2.refs_0_ = bf16[4,2,128,1280]{3,2,1,0:T(8,128)(2,1)} async-done(((bf16[4,2,128,1280]{3,2,1,0:T(8,128)(2,1)}), bf16[4,2,128,1280]{3,2,1,0:T(8,128)(2,1)}, u32[]{:S(2)}, u32[]{:S(2)}) %all-to-all-start.2) | async-done | bytes 2621472 | tf_op jit(solution)/shard_map/all_to_all | solution.py:584
  298.2 4.8 %finish.1 = (f32[128,5120]{1,0:T(8,128)}, bf16[128,5120]{1,0:T(8,128)(2,1)}) custom-call(f32[128,5120]{1,0:T(8,128)} %select_add_fusion.base, bf16[4,2,128,1280]{3,2,1,0:T(8,128)(2,1)} %all-to-all-done.2.refs_0_), custom_call_target="tpu_custom_call" | custom-call | flops 163840 | bytes 2293760 | tf_op jit(solution)/shard_map/finish/pallas_call | solution.py:486
  (158 shorter events, 76.0 us)
Async XLA Ops:
  8.8 46.1 %collective-permute-start.6 = (bf16[640,1536]{1,0:T(8,128)(2,1)S(1)}, bf16[640,1536]{1,0:T(8,128)(2,1)S(1)}, u32[]{:S(2)}, u32[]{:S(2)}) collective-permute-start(bf16[640,1536]{1,0:T(8,128)(2,1)S(1)} %constant_dynamic-update-slice_fusion.refs_7_), channel_id=1, source_target_pairs={{0,16},{8,24},{16,0},{24,8},{1,17},{9,25},{17,1},{25,9},{2,18},{10... | collective-permute-start | bytes 5898248 | tf_op jit(solution)/shard_map/ppermute | solution.py:19
  11.4 44.9 %collective-permute-start.5 = (bf16[640,1536]{1,0:T(8,128)(2,1)S(1)}, bf16[640,1536]{1,0:T(8,128)(2,1)S(1)}, u32[]{:S(2)}, u32[]{:S(2)}) collective-permute-start(bf16[640,1536]{1,0:T(8,128)(2,1)S(1)} %constant_dynamic-update-slice_fusion.refs_7_), channel_id=1, source_target_pairs={{0,8},{8,0},{16,24},{24,16},{1,9},{9,1},{17,25},{25,17},{2,10},{10... | collective-permute-start | bytes 5898248 | tf_op jit(solution)/shard_map/ppermute | solution.py:19
  13.0 32.6 %collective-permute-start.3 = (bf16[2,128,2560]{2,1,0:T(8,128)(2,1)S(1)}, bf16[2,128,2560]{2,1,0:T(8,128)(2,1)S(1)}, u32[]{:S(2)}, u32[]{:S(2)}) collective-permute-start(bf16[2,128,2560]{2,1,0:T(8,128)(2,1)S(1)} %pad_maximum_fusion.refs_0_.refs_3_.refs_6_), channel_id=1, source_target_pairs={{2,0},{4,2},{6,4},{3,1},{5,3},{7,5},{10,8},{12,10},{14,12},{11,9},... | collective-permute-start | bytes 3932168 | tf_op jit(solution)/shard_map/ppermute | solution.py:515
  14.5 32.5 %collective-permute-start.1 = (bf16[2,128,2560]{2,1,0:T(8,128)(2,1)S(1)}, bf16[2,128,2560]{2,1,0:T(8,128)(2,1)S(1)}, u32[]{:S(2)}, u32[]{:S(2)}) collective-permute-start(bf16[2,128,2560]{2,1,0:T(8,128)(2,1)S(1)} %pad_maximum_fusion.refs_0_.refs_3_.refs_6_), channel_id=1, source_target_pairs={{0,2},{2,4},{4,6},{1,3},{3,5},{5,7},{8,10},{10,12},{12,14},{9,11},... | collective-permute-start | bytes 3932168 | tf_op jit(solution)/shard_map/ppermute | solution.py:514
  45.7 34.4 %collective-permute-start.4 = (bf16[2,128,2560]{2,1,0:T(8,128)(2,1)S(1)}, bf16[2,128,2560]{2,1,0:T(8,128)(2,1)}, u32[]{:S(2)}, u32[]{:S(2)}) collective-permute-start(bf16[2,128,2560]{2,1,0:T(8,128)(2,1)S(1)} %collective-permute-done.3.refs_4_), channel_id=1, source_target_pairs={{2,0},{4,2},{3,1},{5,3},{10,8},{12,10},{11,9},{13,11},{18,16},{20,... | collective-permute-start | bytes 3932168 | tf_op jit(solution)/shard_map/ppermute | solution.py:515
  47.0 33.1 %collective-permute-start.2 = (bf16[2,128,2560]{2,1,0:T(8,128)(2,1)S(1)}, bf16[2,128,2560]{2,1,0:T(8,128)(2,1)}, u32[]{:S(2)}, u32[]{:S(2)}) collective-permute-start(bf16[2,128,2560]{2,1,0:T(8,128)(2,1)S(1)} %collective-permute-done.1.refs_1_), channel_id=1, source_target_pairs={{2,4},{4,6},{3,5},{5,7},{10,12},{12,14},{11,13},{13,15},{18,20},{2... | collective-permute-start | bytes 3932168 | tf_op jit(solution)/shard_map/ppermute | solution.py:514
  56.5 23.2 %collective-permute-start.8 = (bf16[640,768]{1,0:T(8,128)(2,1)S(1)}, bf16[640,768]{1,0:T(8,128)(2,1)S(1)}, u32[]{:S(2)}, u32[]{:S(2)}) collective-permute-start(bf16[640,768]{1,0:T(8,128)(2,1)S(1)} %slice.27), channel_id=1, source_target_pairs={{0,16},{8,24},{16,0},{24,8},{1,17},{9,25},{17,1},{25,9},{2,18},{10... | collective-permute-start | bytes 2949128 | tf_op jit(solution)/shard_map/ppermute | solution.py:19
  56.9 23.2 %collective-permute-start.7 = (bf16[640,768]{1,0:T(8,128)(2,1)S(1)}, bf16[640,768]{1,0:T(8,128)(2,1)S(1)}, u32[]{:S(2)}, u32[]{:S(2)}) collective-permute-start(bf16[640,768]{1,0:T(8,128)(2,1)S(1)} %slice.26), channel_id=1, source_target_pairs={{0,8},{8,0},{16,24},{24,16},{1,9},{9,1},{17,25},{25,17},{2,10},{10... | collective-permute-start | bytes 2949128 | tf_op jit(solution)/shard_map/ppermute | solution.py:19
  80.1 27.8 %collective-permute-start.9 = (bf16[2,128,2560]{2,1,0:T(8,128)(2,1)}, bf16[2,128,2560]{2,1,0:T(8,128)(2,1)S(1)}, u32[]{:S(2)}, u32[]{:S(2)}) collective-permute-start(bf16[2,128,2560]{2,1,0:T(8,128)(2,1)} %collective-permute-done.2.refs_2_), channel_id=1, source_target_pairs={{4,6},{5,7},{12,14},{13,15},{20,22},{21,23},{28,30},{29,31}} | collective-permute-start | bytes 3932168 | tf_op jit(solution)/shard_map/ppermute | solution.py:514
  80.9 31.4 %collective-permute-start.10 = (bf16[2,128,2560]{2,1,0:T(8,128)(2,1)}, bf16[2,128,2560]{2,1,0:T(8,128)(2,1)S(1)}, u32[]{:S(2)}, u32[]{:S(2)}) collective-permute-start(bf16[2,128,2560]{2,1,0:T(8,128)(2,1)} %collective-permute-done.4.refs_5_), channel_id=1, source_target_pairs={{2,0},{3,1},{10,8},{11,9},{18,16},{19,17},{26,24},{27,25}} | collective-permute-start | bytes 3932168 | tf_op jit(solution)/shard_map/ppermute | solution.py:515
  82.3 24.4 %collective-permute-start.11 = (bf16[640,768]{1,0:T(8,128)(2,1)}, bf16[640,768]{1,0:T(8,128)(2,1)S(1)}, u32[]{:S(2)}, u32[]{:S(2)}) collective-permute-start(bf16[640,768]{1,0:T(8,128)(2,1)} %refs_7_.1), channel_id=1, source_target_pairs={{0,8},{8,0},{16,24},{24,16},{1,9},{9,1},{17,25},{25,17},{2,10},{10... | collective-permute-start | bytes 2949128 | tf_op jit(solution)/shard_map/ppermute | solution.py:19
  83.7 24.1 %collective-permute-start.12 = (bf16[640,768]{1,0:T(8,128)(2,1)}, bf16[640,768]{1,0:T(8,128)(2,1)}, u32[]{:S(2)}, u32[]{:S(2)}) collective-permute-start(bf16[640,768]{1,0:T(8,128)(2,1)} %refs_7_.1), channel_id=1, source_target_pairs={{0,16},{8,24},{16,0},{24,8},{1,17},{9,25},{17,1},{25,9},{2,18},{10... | collective-permute-start | bytes 2949128 | tf_op jit(solution)/shard_map/ppermute | solution.py:19
  112.3 32.7 %collective-permute-start.18 = (f32[384,1536]{1,0:T(8,128)}, f32[384,1536]{1,0:T(8,128)S(1)}, u32[]{:S(2)}, u32[]{:S(2)}) collective-permute-start(f32[384,1536]{1,0:T(8,128)} %get-tuple-element.59), channel_id=1, source_target_pairs={{0,1},{1,0},{2,3},{3,2},{4,5},{5,4},{6,7},{7,6},{8,9},{9,8},{10,11... | collective-permute-start | bytes 7077896 | tf_op jit(solution)/shard_map/ppermute | solution.py:19
  117.8 23.5 %collective-permute-start.14 = (bf16[768,640]{1,0:T(8,128)(2,1)}, bf16[768,640]{1,0:T(8,128)(2,1)S(1)}, u32[]{:S(2)}, u32[]{:S(2)}) collective-permute-start(bf16[768,640]{1,0:T(8,128)(2,1)} %refs_5_.1), channel_id=1, source_target_pairs={{0,2},{2,4},{4,6},{1,3},{3,5},{5,7},{8,10},{10,12},{12,14},{9,11},... | collective-permute-start | bytes 2949128 | tf_op jit(solution)/shard_map/ppermute | solution.py:556
  119.5 25.5 %collective-permute-start.15 = (bf16[768,640]{1,0:T(8,128)(2,1)}, bf16[768,640]{1,0:T(8,128)(2,1)}, u32[]{:S(2)}, u32[]{:S(2)}) collective-permute-start(bf16[768,640]{1,0:T(8,128)(2,1)} %refs_5_.1), channel_id=1, source_target_pairs={{2,0},{4,2},{6,4},{3,1},{5,3},{7,5},{10,8},{12,10},{14,12},{11,9},... | collective-permute-start | bytes 2949128 | tf_op jit(solution)/shard_map/ppermute | solution.py:557
  140.7 36.0 %collective-permute-start.25 = (f32[512,768]{1,0:T(8,128)}, f32[512,768]{1,0:T(8,128)}, u32[]{:S(2)}, u32[]{:S(2)}) collective-permute-start(f32[512,768]{1,0:T(8,128)} %get-tuple-element.63), channel_id=1, source_target_pairs={{0,1},{1,0},{2,3},{3,2},{4,5},{5,4},{6,7},{7,6},{8,9},{9,8},{10,11... | collective-permute-start | bytes 4718600 | tf_op jit(solution)/shard_map/ppermute | solution.py:19
  151.0 38.5 %all-to-all-start = ((bf16[4,144,1280]{2,1,0:T(8,128)(2,1)}), bf16[4,144,1280]{2,1,0:T(8,128)(2,1)S(1)}, u32[]{:S(2)}, u32[]{:S(2)}) async-start(bf16[4,144,1280]{2,1,0:T(8,128)(2,1)} %tell.1), calls=%async_computation | async-start | bytes 2949120 | tf_op jit(solution)/shard_map/all_to_all | solution.py:567
  163.0 18.8 %collective-permute-start.26 = (bf16[768,640]{1,0:T(8,128)(2,1)S(1)}, bf16[768,640]{1,0:T(8,128)(2,1)S(1)}, u32[]{:S(2)}, u32[]{:S(2)}) collective-permute-start(bf16[768,640]{1,0:T(8,128)(2,1)S(1)} %copy-done.21), channel_id=1, source_target_pairs={{2,4},{4,6},{3,5},{5,7},{10,12},{12,14},{11,13},{13,15},{18,20},{2... | collective-permute-start | bytes 2949128 | tf_op jit(solution)/shard_map/ppermute | solution.py:556
  165.5 24.0 %collective-permute-start.27 = (bf16[768,640]{1,0:T(8,128)(2,1)}, bf16[768,640]{1,0:T(8,128)(2,1)}, u32[]{:S(2)}, u32[]{:S(2)}) collective-permute-start(bf16[768,640]{1,0:T(8,128)(2,1)} %collective-permute-done.15.refs_9_), channel_id=1, source_target_pairs={{2,0},{4,2},{3,1},{5,3},{10,8},{12,10},{11,9},{13,11},{18,16},{20,... | collective-permute-start | bytes 2949128 | tf_op jit(solution)/shard_map/ppermute | solution.py:557
  189.5 21.3 %all-to-all-start.1 = ((bf16[4,128,768]{2,1,0:T(8,128)(2,1)}), bf16[4,128,768]{2,1,0:T(8,128)(2,1)S(1)}, u32[]{:S(2)}, u32[]{:S(2)}) async-start(bf16[4,128,768]{2,1,0:T(8,128)(2,1)} %attend.1), calls=%async_computation.1 | async-start | bytes 1572864 | tf_op jit(solution)/shard_map/all_to_all | solution.py:576
  210.7 21.4 %collective-permute-start.34 = (bf16[768,640]{1,0:T(8,128)(2,1)S(1)}, bf16[768,640]{1,0:T(8,128)(2,1)S(1)}, u32[]{:S(2)}, u32[]{:S(2)}) collective-permute-start(bf16[768,640]{1,0:T(8,128)(2,1)S(1)} %collective-permute-done.26.refs_7_), channel_id=1, source_target_pairs={{4,6},{5,7},{12,14},{13,15},{20,22},{21,23},{28,30},{29,31}} | collective-permute-start | bytes 2949128 | tf_op jit(solution)/shard_map/ppermute | solution.py:556
  211.5 24.2 %collective-permute-start.35 = (bf16[768,640]{1,0:T(8,128)(2,1)}, bf16[768,640]{1,0:T(8,128)(2,1)S(1)}, u32[]{:S(2)}, u32[]{:S(2)}) collective-permute-start(bf16[768,640]{1,0:T(8,128)(2,1)} %collective-permute-done.27.refs_10_), channel_id=1, source_target_pairs={{2,0},{3,1},{10,8},{11,9},{18,16},{19,17},{26,24},{27,25}} | collective-permute-start | bytes 2949128 | tf_op jit(solution)/shard_map/ppermute | solution.py:557
  212.8 17.9 %collective-permute-start.31 = (bf16[4,128,768]{2,1,0:T(8,128)(2,1)S(1)}, bf16[4,128,768]{2,1,0:T(8,128)(2,1)S(1)}, u32[]{:S(2)}, u32[]{:S(2)}) collective-permute-start(bf16[4,128,768]{2,1,0:T(8,128)(2,1)S(1)} %all-to-all-done.1.refs_0_), channel_id=1, source_target_pairs={{0,16},{8,24},{16,0},{24,8},{1,17},{9,25},{17,1},{25,9},{2,18},{10... | collective-permute-start | bytes 2359304 | tf_op jit(solution)/shard_map/ppermute | solution.py:19
  263.6 34.7 %all-to-all-start.2 = ((bf16[4,2,128,1280]{3,2,1,0:T(8,128)(2,1)}), bf16[4,2,128,1280]{3,2,1,0:T(8,128)(2,1)}, u32[]{:S(2)}, u32[]{:S(2)}) async-start(bf16[4,2,128,1280]{3,2,1,0:T(8,128)(2,1)} %project_out.1), calls=%async_computation.2 | async-start | bytes 5242880 | tf_op jit(solution)/shard_map/all_to_all | solution.py:584
  (54 other events, 885.4 us)

commit v15 on v13

--- a/solution.py
+++ b/solution.py
@@ -113,7 +113,7 @@
 
 def modulate(place, states, rows, steps):
     tokens, width = states.shape
-    tile = 32
+    tile = min(tokens, 64)
     out = jax.ShapeDtypeStruct((tokens, width // 2), jnp.bfloat16)
     spec = pl.BlockSpec((tile, width // 2), lambda i: (i, 0))
     return pl.pallas_call(
@@ -482,11 +482,14 @@
 
 def finish(base, parts):
     steps, _, tokens, width = parts[0].shape
+    cuts = 2 if width % 256 == 0 else 1
+    width = width // cuts
     by_columns = pl.BlockSpec((base.shape[0], width), lambda i: (0, i))
+    by_step = pl.BlockSpec((1, 2, tokens, width), lambda i: (i // cuts, 0, 0, i % cuts))
     return pl.pallas_call(
         finish_kernel,
-        grid=(steps,),
-        in_specs=[by_columns] + [pl.BlockSpec((1, 2, tokens, width), lambda i: (i, 0, 0, 0))] * len(parts),
+        grid=(steps * cuts,),
+        in_specs=[by_columns] + [by_step] * len(parts),
         out_specs=[by_columns, by_columns],
         out_shape=[jax.ShapeDtypeStruct(base.shape, jnp.float32), jax.ShapeDtypeStruct(base.shape, jnp.bfloat16)],
         compiler_params=params(),

time: 302 us -> 303 us (level)
  no operation moved by 1% of the time
where the time goes in v15:
time: 303 us; the launch traced here: 302 us
  waiting for transfers between devices  152 us (50%)
  Pallas kernels  74.8 us (25%)
  starting transfers between devices  57.5 us (19%)
  local copies, waits for them, and re-layouts  11 us (4%)
  other arithmetic  3.26 us (1%)
  between operations  3.13 us (1%)
    ppermute x23, waiting for transfers between devices, swap(): lax.ppermute(x, axis, [(i, i ^ offset) for i in range(lax.axis_size(axis))])  60.5 us
    pallas_call x3, Pallas kernels, project(): pl.pallas_call(functools.partial(project_kernel, size, parts, shard, tupl...  31.7 us
    ppermute x3, waiting for transfers between devices, hop(): lax.ppermute(down, 'head', [(i, i - 1) for i in range(1, size - count + 1)])  31 us
    all_to_all x1, waiting for transfers between devices, body(): lax.all_to_all(part, 'step', 0, 0)  27.9 us
    ppermute x23, starting transfers between devices, swap(): lax.ppermute(x, axis, [(i, i ^ offset) for i in range(lax.axis_size(axis))])  19.7 us
    all_to_all x1, waiting for transfers between devices, body(): lax.all_to_all(attended, 'head', 0, 0)  13.8 us
    pallas_call x1, Pallas kernels, project_out(): pl.pallas_call(functools.partial(out_kernel, size, tuple(layout), part *...  13 us
    ppermute x3, waiting for transfers between devices, body(): lax.ppermute(down, 'head', [(i, i - 1) for i in range(1, size - count + 1)])  12 us
  transfers between devices with their start and end apart: 41, of which 20 were waited for; matrix products, arithmetic and copies ran while one was open for 2% of the time, Pallas kernels for 17%

profile of v15, /device:TPU:0, one launch (start us, length us, event | category | flops | bytes accessed | tf_op | source)
XLA Modules:
  0.0 301.5 jit_solution(6690162628992731786)
XLA Ops:
  3.5 3.6 %modulate.1 = (bf16[128,2560]{1,0:T(8,128)(2,1)}, bf16[128,2560]{1,0:T(8,128)(2,1)}) custom-call(s32[5]{0:T(128)} %stack.32.place, f32[128,5120]{1,0:T(8,128)} %bitcast.12, f32[1,3,5120]{2,1,0:T(4,128)} %copy.12.rows), custom_call_target="tpu_custom_call" | custom-call | flops 1638400 | bytes 983040 | tf_op jit(solution)/shard_map/modulate/pallas_call | solution.py:119
  13.4 4.6 %collective-permute-start.1 = (bf16[2,128,2560]{2,1,0:T(8,128)(2,1)S(1)}, bf16[2,128,2560]{2,1,0:T(8,128)(2,1)S(1)}, u32[]{:S(2)}, u32[]{:S(2)}) collective-permute-start(bf16[2,128,2560]{2,1,0:T(8,128)(2,1)S(1)} %pad_maximum_fusion.refs_0_.refs_3_.refs_6_), channel_id=1, source_target_pairs={{0,2},{2,4},{4,6},{1,3},{3,5},{5,7},{8,10},{10,12},{12,14},{9,11},... | collective-permute-start | bytes 3932168 | tf_op jit(solution)/shard_map/ppermute | solution.py:517
  18.0 26.6 %collective-permute-done.3.refs_4_ = bf16[2,128,2560]{2,1,0:T(8,128)(2,1)S(1)} collective-permute-done((bf16[2,128,2560]{2,1,0:T(8,128)(2,1)S(1)}, bf16[2,128,2560]{2,1,0:T(8,128)(2,1)S(1)}, u32[]{:S(2)}, u32[]{:S(2)}) %collective-permute-start.3) | collective-permute-done | bytes 1310752 | tf_op jit(solution)/shard_map/ppermute | solution.py:518
  47.6 6.1 %collective-permute-done.6.refs_9_ = bf16[640,1536]{1,0:T(8,128)(2,1)S(1)} collective-permute-done((bf16[640,1536]{1,0:T(8,128)(2,1)S(1)}, bf16[640,1536]{1,0:T(8,128)(2,1)S(1)}, u32[]{:S(2)}, u32[]{:S(2)}) %collective-permute-start.6) | collective-permute-done | bytes 1966112 | tf_op jit(solution)/shard_map/ppermute | solution.py:19
  57.5 21.2 %collective-permute-done.8.refs_11_ = bf16[640,768]{1,0:T(8,128)(2,1)S(1)} collective-permute-done((bf16[640,768]{1,0:T(8,128)(2,1)S(1)}, bf16[640,768]{1,0:T(8,128)(2,1)S(1)}, u32[]{:S(2)}, u32[]{:S(2)}) %collective-permute-start.8) | collective-permute-done | bytes 983072 | tf_op jit(solution)/shard_map/ppermute | solution.py:19
  85.9 4.0 %tell.1 = bf16[4,144,1280]{2,1,0:T(8,128)(2,1)} custom-call(s32[5]{0:T(128)} %stack.32.place, f32[1]{0:T(128)} %bitcast.8.step_width, f32[128,5120]{1,0:T(8,128)} %bitcast.13, f32[1,3,5120]{2,1,0:T(4,128)} %copy.12.rows), custom_call_target="tpu_custom_call" | custom-call | flops 655360 | bytes 983040 | tf_op jit(solution)/shard_map/tell/pallas_call | solution.py:151
  89.9 13.6 %first.1 = (f32[384,1536]{1,0:T(8,128)}, f32[384,1536]{1,0:T(8,128)}) custom-call(s32[5]{0:T(128)} %stack.32.place, bf16[2,128,2560]{2,1,0:T(8,128)(2,1)} %copy-done, bf16[2,128,2560]{2,1,0:T(8,128)(2,1)} %copy-done.7, bf16[2,128,2560]{2,1,0:T(8,128)(2,1)} %collective-permute-done.2.refs_2_, bf16[2,128,2560]{2,1,0:T(8,128)(2,1)} %copy-done, ...), custom_call_target="tpu_custom_call" | custom-call | flops 1509949440 | bytes 4128768 | tf_op jit(solution)/shard_map/first/pallas_call | solution.py:233
  106.8 4.4 %collective-permute-done.10.refs_6_ = bf16[2,128,2560]{2,1,0:T(8,128)(2,1)S(1)} collective-permute-done((bf16[2,128,2560]{2,1,0:T(8,128)(2,1)}, bf16[2,128,2560]{2,1,0:T(8,128)(2,1)S(1)}, u32[]{:S(2)}, u32[]{:S(2)}) %collective-permute-start.10) | collective-permute-done | bytes 1310752 | tf_op jit(solution)/shard_map/ppermute | solution.py:518
  119.1 7.8 %last.1 = (f32[128,1536]{1,0:T(8,128)}, f32[128,1536]{1,0:T(8,128)}) custom-call(s32[5]{0:T(128)} %stack.32.place, bf16[2,128,2560]{2,1,0:T(8,128)(2,1)} %copy-done, bf16[2,128,2560]{2,1,0:T(8,128)(2,1)} %copy-done.7, bf16[2,128,2560]{2,1,0:T(8,128)(2,1)} %collective-permute-done.2.refs_2_, bf16[2,128,2560]{2,1,0:T(8,128)(2,1)} %copy-done.9, ...), custom_call_target="tpu_custom_call" | custom-call | flops 503316480 | bytes 2686976 | tf_op jit(solution)/shard_map/last/pallas_call | solution.py:233
  128.0 10.2 %value.1 = (f32[512,768]{1,0:T(8,128)}, f32[512,768]{1,0:T(8,128)}) custom-call(s32[5]{0:T(128)} %stack.32.place, bf16[2,128,2560]{2,1,0:T(8,128)(2,1)} %copy-done, bf16[2,128,2560]{2,1,0:T(8,128)(2,1)} %copy-done.7, bf16[2,128,2560]{2,1,0:T(8,128)(2,1)} %collective-permute-done.2.refs_2_, bf16[2,128,2560]{2,1,0:T(8,128)(2,1)} %copy-done.9, ...), custom_call_target="tpu_custom_call" | custom-call | flops 1006632960 | bytes 3080192 | tf_op jit(solution)/shard_map/value/pallas_call | solution.py:233
  138.3 4.4 %all-to-all-start = ((bf16[4,144,1280]{2,1,0:T(8,128)(2,1)}), bf16[4,144,1280]{2,1,0:T(8,128)(2,1)}, u32[]{:S(2)}, u32[]{:S(2)}) async-start(bf16[4,144,1280]{2,1,0:T(8,128)(2,1)} %tell.1), calls=%async_computation | async-start | bytes 2949120 | tf_op jit(solution)/shard_map/all_to_all | solution.py:549
  145.6 3.8 %norms.1 = f32[1,2,512]{2,1,0:T(2,128)} custom-call(s32[5]{0:T(128)} %stack.32.place, f32[384,1536]{1,0:T(8,128)} %get-tuple-element.49.first_a.refs_0_.refs_4_, f32[384,1536]{1,0:T(8,128)} %copy-done.2, f32[128,1536]{1,0:T(8,128)} %get-tuple-element.52.last_a.refs_2_.refs_6_, f32[128,1536]{1,0:T(8,128)} %copy-done.8), custom_call_target="tpu_custom_call" | custom-call | flops 786432 | bytes 1572864 | tf_op jit(solution)/shard_map/norms/pallas_call | solution.py:271
  149.4 6.0 %collective-permute-start.22 = (f32[1,2,512]{2,1,0:T(2,128)}, f32[1,2,512]{2,1,0:T(2,128)S(1)}, u32[]{:S(2)}, u32[]{:S(2)}) collective-permute-start(f32[1,2,512]{2,1,0:T(2,128)} %norms.1), channel_id=1, source_target_pairs={{0,6},{2,0},{4,2},{6,4},{1,7},{3,1},{5,3},{7,5},{8,14},{10,8},{12,... | collective-permute-start | bytes 12296 | tf_op jit(solution)/shard_map/ppermute | solution.py:573
  166.7 7.1 %probs.1 = bf16[6,512,512]{2,1,0:T(8,128)(2,1)} custom-call(s32[5]{0:T(128)} %stack.32.place, f32[4,2,512]{2,1,0:T(2,128)} %pad_maximum_fusion.1.squares, f32[384,1536]{1,0:T(8,128)} %get-tuple-element.49.first_a.refs_0_.refs_4_, f32[384,1536]{1,0:T(8,128)} %copy-done.2, f32[128,1536]{1,0:T(8,128)} %get-tuple-element.52.last_a.refs_2_.refs_6_, ...), custom_call_target="tpu_custom_call" | custom-call | flops 100663296 | bytes 2359296 | tf_op jit(solution)/shard_map/probs/pallas_call | solution.py:325
  173.8 5.0 %attend.1 = bf16[4,128,768]{2,1,0:T(8,128)(2,1)} custom-call(s32[5]{0:T(128)} %stack.32.place, bf16[6,512,512]{2,1,0:T(8,128)(2,1)} %probs.1, f32[512,768]{1,0:T(8,128)} %get-tuple-element.56.v_a, f32[512,768]{1,0:T(8,128)} %collective-permute-done.25.v_b), custom_call_target="tpu_custom_call" | custom-call | flops 100663296 | bytes 1769472 | tf_op jit(solution)/shard_map/attend/pallas_call | solution.py:354
  178.8 8.1 %collective-permute-done.27.refs_10_ = bf16[768,640]{1,0:T(8,128)(2,1)S(1)} collective-permute-done((bf16[768,640]{1,0:T(8,128)(2,1)}, bf16[768,640]{1,0:T(8,128)(2,1)S(1)}, u32[]{:S(2)}, u32[]{:S(2)}) %collective-permute-start.27) | collective-permute-done | bytes 983072 | tf_op jit(solution)/shard_map/ppermute | solution.py:561
  194.7 13.8 %all-to-all-done.1.refs_0_ = bf16[4,128,768]{2,1,0:T(8,128)(2,1)S(1)} async-done(((bf16[4,128,768]{2,1,0:T(8,128)(2,1)}), bf16[4,128,768]{2,1,0:T(8,128)(2,1)S(1)}, u32[]{:S(2)}, u32[]{:S(2)}) %all-to-all-start.1) | async-done | bytes 786464 | tf_op jit(solution)/shard_map/all_to_all | solution.py:579
  213.4 15.3 %collective-permute-done.31.refs_2_ = bf16[4,128,768]{2,1,0:T(8,128)(2,1)S(1)} collective-permute-done((bf16[4,128,768]{2,1,0:T(8,128)(2,1)S(1)}, bf16[4,128,768]{2,1,0:T(8,128)(2,1)S(1)}, u32[]{:S(2)}, u32[]{:S(2)}) %collective-permute-start.31) | collective-permute-done | bytes 786464 | tf_op jit(solution)/shard_map/ppermute | solution.py:19
  229.5 3.9 %collective-permute-done.35.refs_11_ = bf16[768,640]{1,0:T(8,128)(2,1)S(1)} collective-permute-done((bf16[768,640]{1,0:T(8,128)(2,1)S(1)}, bf16[768,640]{1,0:T(8,128)(2,1)S(1)}, u32[]{:S(2)}, u32[]{:S(2)}) %collective-permute-start.35) | collective-permute-done | bytes 983072 | tf_op jit(solution)/shard_map/ppermute | solution.py:561
  236.7 8.3 %collective-permute-done.32.refs_3_ = bf16[2,128,768]{2,1,0:T(8,128)(2,1)S(1)} collective-permute-done((bf16[2,128,768]{2,1,0:T(8,128)(2,1)S(1)}, bf16[2,128,768]{2,1,0:T(8,128)(2,1)S(1)}, u32[]{:S(2)}, u32[]{:S(2)}) %collective-permute-start.32) | collective-permute-done | bytes 393248 | tf_op jit(solution)/shard_map/ppermute | solution.py:19
  247.1 13.0 %project_out.1 = bf16[4,2,128,1280]{3,2,1,0:T(8,128)(2,1)} custom-call(s32[5]{0:T(128)} %stack.32.place, bf16[4,128,768]{2,1,0:T(8,128)(2,1)} %copy-done.13, bf16[4,128,768]{2,1,0:T(8,128)(2,1)} %copy-done.16, bf16[4,128,768]{2,1,0:T(8,128)(2,1)} %copy-done.15, bf16[2,128,768]{2,1,0:T(8,128)(2,1)} %copy-done.28, bf16[2,128,768]{2,1,0:T(8,128)(2,1)} %copy-done.29, ...), custom_call_target="tpu_custom_call" | custom-call | flops 1006632960 | bytes 3407872 | tf_op jit(solution)/shard_map/project_out/pallas_call | solution.py:456
  260.1 4.9 %all-to-all-start.2 = ((bf16[4,2,128,1280]{3,2,1,0:T(8,128)(2,1)}), bf16[4,2,128,1280]{3,2,1,0:T(8,128)(2,1)}, u32[]{:S(2)}, u32[]{:S(2)}) async-start(bf16[4,2,128,1280]{3,2,1,0:T(8,128)(2,1)} %project_out.1), calls=%async_computation.2 | async-start | bytes 5242880 | tf_op jit(solution)/shard_map/all_to_all | solution.py:587
  266.9 27.9 %all-to-all-done.2.refs_0_ = bf16[4,2,128,1280]{3,2,1,0:T(8,128)(2,1)} async-done(((bf16[4,2,128,1280]{3,2,1,0:T(8,128)(2,1)}), bf16[4,2,128,1280]{3,2,1,0:T(8,128)(2,1)}, u32[]{:S(2)}, u32[]{:S(2)}) %all-to-all-start.2) | async-done | bytes 2621472 | tf_op jit(solution)/shard_map/all_to_all | solution.py:587
  294.8 6.7 %finish.1 = (f32[128,5120]{1,0:T(8,128)}, bf16[128,5120]{1,0:T(8,128)(2,1)}) custom-call(f32[128,5120]{1,0:T(8,128)} %select_add_fusion.base, bf16[4,2,128,1280]{3,2,1,0:T(8,128)(2,1)} %all-to-all-done.2.refs_0_), custom_call_target="tpu_custom_call" | custom-call | flops 163840 | bytes 2293760 | tf_op jit(solution)/shard_map/finish/pallas_call | solution.py:489
  (150 shorter events, 68.2 us)
Async XLA Ops:
  7.7 46.1 %collective-permute-start.6 = (bf16[640,1536]{1,0:T(8,128)(2,1)S(1)}, bf16[640,1536]{1,0:T(8,128)(2,1)S(1)}, u32[]{:S(2)}, u32[]{:S(2)}) collective-permute-start(bf16[640,1536]{1,0:T(8,128)(2,1)S(1)} %constant_dynamic-update-slice_fusion.refs_7_), channel_id=1, source_target_pairs={{0,16},{8,24},{16,0},{24,8},{1,17},{9,25},{17,1},{25,9},{2,18},{10... | collective-permute-start | bytes 5898248 | tf_op jit(solution)/shard_map/ppermute | solution.py:19
  10.3 44.9 %collective-permute-start.5 = (bf16[640,1536]{1,0:T(8,128)(2,1)S(1)}, bf16[640,1536]{1,0:T(8,128)(2,1)S(1)}, u32[]{:S(2)}, u32[]{:S(2)}) collective-permute-start(bf16[640,1536]{1,0:T(8,128)(2,1)S(1)} %constant_dynamic-update-slice_fusion.refs_7_), channel_id=1, source_target_pairs={{0,8},{8,0},{16,24},{24,16},{1,9},{9,1},{17,25},{25,17},{2,10},{10... | collective-permute-start | bytes 5898248 | tf_op jit(solution)/shard_map/ppermute | solution.py:19
  11.9 32.6 %collective-permute-start.3 = (bf16[2,128,2560]{2,1,0:T(8,128)(2,1)S(1)}, bf16[2,128,2560]{2,1,0:T(8,128)(2,1)S(1)}, u32[]{:S(2)}, u32[]{:S(2)}) collective-permute-start(bf16[2,128,2560]{2,1,0:T(8,128)(2,1)S(1)} %pad_maximum_fusion.refs_0_.refs_3_.refs_6_), channel_id=1, source_target_pairs={{2,0},{4,2},{6,4},{3,1},{5,3},{7,5},{10,8},{12,10},{14,12},{11,9},... | collective-permute-start | bytes 3932168 | tf_op jit(solution)/shard_map/ppermute | solution.py:518
  13.4 32.5 %collective-permute-start.1 = (bf16[2,128,2560]{2,1,0:T(8,128)(2,1)S(1)}, bf16[2,128,2560]{2,1,0:T(8,128)(2,1)S(1)}, u32[]{:S(2)}, u32[]{:S(2)}) collective-permute-start(bf16[2,128,2560]{2,1,0:T(8,128)(2,1)S(1)} %pad_maximum_fusion.refs_0_.refs_3_.refs_6_), channel_id=1, source_target_pairs={{0,2},{2,4},{4,6},{1,3},{3,5},{5,7},{8,10},{10,12},{12,14},{9,11},... | collective-permute-start | bytes 3932168 | tf_op jit(solution)/shard_map/ppermute | solution.py:517
  44.6 34.4 %collective-permute-start.4 = (bf16[2,128,2560]{2,1,0:T(8,128)(2,1)S(1)}, bf16[2,128,2560]{2,1,0:T(8,128)(2,1)}, u32[]{:S(2)}, u32[]{:S(2)}) collective-permute-start(bf16[2,128,2560]{2,1,0:T(8,128)(2,1)S(1)} %collective-permute-done.3.refs_4_), channel_id=1, source_target_pairs={{2,0},{4,2},{3,1},{5,3},{10,8},{12,10},{11,9},{13,11},{18,16},{20,... | collective-permute-start | bytes 3932168 | tf_op jit(solution)/shard_map/ppermute | solution.py:518
  45.9 33.1 %collective-permute-start.2 = (bf16[2,128,2560]{2,1,0:T(8,128)(2,1)S(1)}, bf16[2,128,2560]{2,1,0:T(8,128)(2,1)}, u32[]{:S(2)}, u32[]{:S(2)}) collective-permute-start(bf16[2,128,2560]{2,1,0:T(8,128)(2,1)S(1)} %collective-permute-done.1.refs_1_), channel_id=1, source_target_pairs={{2,4},{4,6},{3,5},{5,7},{10,12},{12,14},{11,13},{13,15},{18,20},{2... | collective-permute-start | bytes 3932168 | tf_op jit(solution)/shard_map/ppermute | solution.py:517
  55.4 23.2 %collective-permute-start.8 = (bf16[640,768]{1,0:T(8,128)(2,1)S(1)}, bf16[640,768]{1,0:T(8,128)(2,1)S(1)}, u32[]{:S(2)}, u32[]{:S(2)}) collective-permute-start(bf16[640,768]{1,0:T(8,128)(2,1)S(1)} %slice.27), channel_id=1, source_target_pairs={{0,16},{8,24},{16,0},{24,8},{1,17},{9,25},{17,1},{25,9},{2,18},{10... | collective-permute-start | bytes 2949128 | tf_op jit(solution)/shard_map/ppermute | solution.py:19
  55.8 23.2 %collective-permute-start.7 = (bf16[640,768]{1,0:T(8,128)(2,1)S(1)}, bf16[640,768]{1,0:T(8,128)(2,1)S(1)}, u32[]{:S(2)}, u32[]{:S(2)}) collective-permute-start(bf16[640,768]{1,0:T(8,128)(2,1)S(1)} %slice.26), channel_id=1, source_target_pairs={{0,8},{8,0},{16,24},{24,16},{1,9},{9,1},{17,25},{25,17},{2,10},{10... | collective-permute-start | bytes 2949128 | tf_op jit(solution)/shard_map/ppermute | solution.py:19
  79.0 27.8 %collective-permute-start.9 = (bf16[2,128,2560]{2,1,0:T(8,128)(2,1)}, bf16[2,128,2560]{2,1,0:T(8,128)(2,1)S(1)}, u32[]{:S(2)}, u32[]{:S(2)}) collective-permute-start(bf16[2,128,2560]{2,1,0:T(8,128)(2,1)} %collective-permute-done.2.refs_2_), channel_id=1, source_target_pairs={{4,6},{5,7},{12,14},{13,15},{20,22},{21,23},{28,30},{29,31}} | collective-permute-start | bytes 3932168 | tf_op jit(solution)/shard_map/ppermute | solution.py:517
  79.8 31.4 %collective-permute-start.10 = (bf16[2,128,2560]{2,1,0:T(8,128)(2,1)}, bf16[2,128,2560]{2,1,0:T(8,128)(2,1)S(1)}, u32[]{:S(2)}, u32[]{:S(2)}) collective-permute-start(bf16[2,128,2560]{2,1,0:T(8,128)(2,1)} %collective-permute-done.4.refs_5_), channel_id=1, source_target_pairs={{2,0},{3,1},{10,8},{11,9},{18,16},{19,17},{26,24},{27,25}} | collective-permute-start | bytes 3932168 | tf_op jit(solution)/shard_map/ppermute | solution.py:518
  81.2 24.4 %collective-permute-start.11 = (bf16[640,768]{1,0:T(8,128)(2,1)}, bf16[640,768]{1,0:T(8,128)(2,1)S(1)}, u32[]{:S(2)}, u32[]{:S(2)}) collective-permute-start(bf16[640,768]{1,0:T(8,128)(2,1)} %refs_7_.1), channel_id=1, source_target_pairs={{0,8},{8,0},{16,24},{24,16},{1,9},{9,1},{17,25},{25,17},{2,10},{10... | collective-permute-start | bytes 2949128 | tf_op jit(solution)/shard_map/ppermute | solution.py:19
  82.6 24.1 %collective-permute-start.12 = (bf16[640,768]{1,0:T(8,128)(2,1)}, bf16[640,768]{1,0:T(8,128)(2,1)}, u32[]{:S(2)}, u32[]{:S(2)}) collective-permute-start(bf16[640,768]{1,0:T(8,128)(2,1)} %refs_7_.1), channel_id=1, source_target_pairs={{0,16},{8,24},{16,0},{24,8},{1,17},{9,25},{17,1},{25,9},{2,18},{10... | collective-permute-start | bytes 2949128 | tf_op jit(solution)/shard_map/ppermute | solution.py:19
  111.2 32.1 %collective-permute-start.18 = (f32[384,1536]{1,0:T(8,128)}, f32[384,1536]{1,0:T(8,128)S(1)}, u32[]{:S(2)}, u32[]{:S(2)}) collective-permute-start(f32[384,1536]{1,0:T(8,128)} %get-tuple-element.59), channel_id=1, source_target_pairs={{0,1},{1,0},{2,3},{3,2},{4,5},{5,4},{6,7},{7,6},{8,9},{9,8},{10,11... | collective-permute-start | bytes 7077896 | tf_op jit(solution)/shard_map/ppermute | solution.py:19
  115.2 27.4 %collective-permute-start.14 = (bf16[768,640]{1,0:T(8,128)(2,1)}, bf16[768,640]{1,0:T(8,128)(2,1)}, u32[]{:S(2)}, u32[]{:S(2)}) collective-permute-start(bf16[768,640]{1,0:T(8,128)(2,1)} %refs_5_.1), channel_id=1, source_target_pairs={{0,2},{2,4},{4,6},{1,3},{3,5},{5,7},{8,10},{10,12},{12,14},{9,11},... | collective-permute-start | bytes 2949128 | tf_op jit(solution)/shard_map/ppermute | solution.py:560
  117.8 25.4 %collective-permute-start.15 = (bf16[768,640]{1,0:T(8,128)(2,1)}, bf16[768,640]{1,0:T(8,128)(2,1)}, u32[]{:S(2)}, u32[]{:S(2)}) collective-permute-start(bf16[768,640]{1,0:T(8,128)(2,1)} %refs_5_.1), channel_id=1, source_target_pairs={{2,0},{4,2},{6,4},{3,1},{5,3},{7,5},{10,8},{12,10},{14,12},{11,9},... | collective-permute-start | bytes 2949128 | tf_op jit(solution)/shard_map/ppermute | solution.py:561
  138.2 35.6 %collective-permute-start.25 = (f32[512,768]{1,0:T(8,128)}, f32[512,768]{1,0:T(8,128)}, u32[]{:S(2)}, u32[]{:S(2)}) collective-permute-start(f32[512,768]{1,0:T(8,128)} %get-tuple-element.64), channel_id=1, source_target_pairs={{0,1},{1,0},{2,3},{3,2},{4,5},{5,4},{6,7},{7,6},{8,9},{9,8},{10,11... | collective-permute-start | bytes 4718600 | tf_op jit(solution)/shard_map/ppermute | solution.py:19
  138.3 28.4 %all-to-all-start = ((bf16[4,144,1280]{2,1,0:T(8,128)(2,1)}), bf16[4,144,1280]{2,1,0:T(8,128)(2,1)}, u32[]{:S(2)}, u32[]{:S(2)}) async-start(bf16[4,144,1280]{2,1,0:T(8,128)(2,1)} %tell.1), calls=%async_computation | async-start | bytes 2949120 | tf_op jit(solution)/shard_map/all_to_all | solution.py:549
  142.6 24.1 %collective-permute-start.23 = (bf16[768,640]{1,0:T(8,128)(2,1)}, bf16[768,640]{1,0:T(8,128)(2,1)}, u32[]{:S(2)}, u32[]{:S(2)}) collective-permute-start(bf16[768,640]{1,0:T(8,128)(2,1)} %collective-permute-done.14.refs_6_), channel_id=1, source_target_pairs={{0,1},{1,0},{2,3},{3,2},{4,5},{5,4},{6,7},{7,6},{8,9},{9,8},{10,11... | collective-permute-start | bytes 2949128 | tf_op jit(solution)/shard_map/ppermute | solution.py:19
  143.2 23.5 %collective-permute-start.24 = (bf16[768,640]{1,0:T(8,128)(2,1)}, bf16[768,640]{1,0:T(8,128)(2,1)}, u32[]{:S(2)}, u32[]{:S(2)}) collective-permute-start(bf16[768,640]{1,0:T(8,128)(2,1)} %collective-permute-done.15.refs_9_), channel_id=1, source_target_pairs={{0,1},{1,0},{2,3},{3,2},{4,5},{5,4},{6,7},{7,6},{8,9},{9,8},{10,11... | collective-permute-start | bytes 2949128 | tf_op jit(solution)/shard_map/ppermute | solution.py:19
  162.8 24.2 %collective-permute-start.27 = (bf16[768,640]{1,0:T(8,128)(2,1)}, bf16[768,640]{1,0:T(8,128)(2,1)S(1)}, u32[]{:S(2)}, u32[]{:S(2)}) collective-permute-start(bf16[768,640]{1,0:T(8,128)(2,1)} %collective-permute-done.15.refs_9_), channel_id=1, source_target_pairs={{2,0},{4,2},{3,1},{5,3},{10,8},{12,10},{11,9},{13,11},{18,16},{20,... | collective-permute-start | bytes 2949128 | tf_op jit(solution)/shard_map/ppermute | solution.py:561
  186.9 21.5 %all-to-all-start.1 = ((bf16[4,128,768]{2,1,0:T(8,128)(2,1)}), bf16[4,128,768]{2,1,0:T(8,128)(2,1)S(1)}, u32[]{:S(2)}, u32[]{:S(2)}) async-start(bf16[4,128,768]{2,1,0:T(8,128)(2,1)} %attend.1), calls=%async_computation.1 | async-start | bytes 1572864 | tf_op jit(solution)/shard_map/all_to_all | solution.py:579
  208.4 21.1 %collective-permute-start.34 = (bf16[768,640]{1,0:T(8,128)(2,1)S(1)}, bf16[768,640]{1,0:T(8,128)(2,1)S(1)}, u32[]{:S(2)}, u32[]{:S(2)}) collective-permute-start(bf16[768,640]{1,0:T(8,128)(2,1)S(1)} %collective-permute-done.26.refs_7_), channel_id=1, source_target_pairs={{4,6},{5,7},{12,14},{13,15},{20,22},{21,23},{28,30},{29,31}} | collective-permute-start | bytes 2949128 | tf_op jit(solution)/shard_map/ppermute | solution.py:560
  209.2 24.2 %collective-permute-start.35 = (bf16[768,640]{1,0:T(8,128)(2,1)S(1)}, bf16[768,640]{1,0:T(8,128)(2,1)S(1)}, u32[]{:S(2)}, u32[]{:S(2)}) collective-permute-start(bf16[768,640]{1,0:T(8,128)(2,1)S(1)} %collective-permute-done.27.refs_10_), channel_id=1, source_target_pairs={{2,0},{3,1},{10,8},{11,9},{18,16},{19,17},{26,24},{27,25}} | collective-permute-start | bytes 2949128 | tf_op jit(solution)/shard_map/ppermute | solution.py:561
  260.1 34.7 %all-to-all-start.2 = ((bf16[4,2,128,1280]{3,2,1,0:T(8,128)(2,1)}), bf16[4,2,128,1280]{3,2,1,0:T(8,128)(2,1)}, u32[]{:S(2)}, u32[]{:S(2)}) async-start(bf16[4,2,128,1280]{3,2,1,0:T(8,128)(2,1)} %project_out.1), calls=%async_computation.2 | async-start | bytes 5242880 | tf_op jit(solution)/shard_map/all_to_all | solution.py:587
  (50 other events, 883.0 us)
